TPU v7x, 256 devices: a whole 4x4x8 slice. The times are simulated.
256 devices in a mesh: dp: 64 (over y, x_lo, z), tensor: 4 (over x_hi, core).
Axes of the slice: x: 4 (x_hi: 2, x_lo: 2; x = x_hi * 2 + x_lo), y: 4, z: 8, core: 2. Of those that a mesh axis runs over, the one named last changes fastest.
Arguments:
- hidden: bfloat16 [128, 2, 256, 4096], P('dp', None, None, 'tensor'), may hold values from -6 to 6
- lengths: int32 [128, 2], P('dp'), may hold values from 1 to 256, as said below
- norm_gain: float32 [4096], replicated, may hold values from 0.25 to 1.75
- q_norm_gain: float32 [128], replicated, may hold values from 0.5 to 2
- k_norm_gain: float32 [128], replicated, may hold values from 0.5 to 2
- query_weight: bfloat16 [4096, 4096], P('dp', 'tensor'), may hold values from -0.09375 to 0.09375
- key_weight: bfloat16 [4096, 1024], P('dp', 'tensor'), may hold values from -0.09375 to 0.09375
- value_weight: bfloat16 [4096, 1024], P('dp', 'tensor'), may hold values from -0.09375 to 0.09375
Outputs:
- embeddings: bfloat16 [128, 2, 4096], P('dp', None, 'tensor')
- pair_loss: float32 [128], P('dp')
- loss: float32 [], replicated
Inputs may be any that keep to these rules, and one draw needn't show every extreme that they name: `lengths`: every token slot below the length is valid; some passage has all 256 slots valid.
All inputs are finite; a program needn't handle non-finite values.
Results may differ from a plain program's by a relative error of at most 0.0071.
The roundings to bfloat16 on the way count: a program that leaves them out, or rounds other values in their place, can miss the bound.
Values may be sent and summed in bfloat16 or wider, within the bound.
No kernel may reach another device: no remote copies, remote signals or barrier semaphores. Data moves between devices by JAX's collectives and lax.ppermute only.
A program may use at most 128 MiB of HBM per device.

v0:
```python
import math

import jax
import jax.numpy as jnp
from jax import lax
from jax.sharding import PartitionSpec as P

HEAD_DIM = 128


EPS = 1e-06
SCORE_SCALE = 20.0


def rms_rows(values):
    return values * lax.rsqrt(jnp.mean(values * values, axis=-1, keepdims=True) + EPS)


def attend(query_proj, key_proj, value_proj, seq_lengths, q_norm_gain, k_norm_gain):
    seq_count, seq_slots, kv_local, head_size = key_proj.shape
    query_heads = (
        rms_rows(query_proj.reshape(seq_count, kv_local, -1, head_size)) * q_norm_gain
    ).astype(jnp.bfloat16)
    key_heads = (rms_rows(key_proj) * k_norm_gain).astype(jnp.bfloat16)
    value_heads = value_proj.astype(jnp.bfloat16)
    scores = jnp.einsum(
        "skgd,slkd->skgl", query_heads, key_heads, preferred_element_type=jnp.float32
    ) / math.sqrt(head_size)
    positions = jnp.arange(seq_slots, dtype=jnp.int32)
    valid = positions[None, :] < seq_lengths[:, None]
    scores = jnp.where(valid[:, None, None, :], scores, -1e30)
    peak = jnp.max(scores, axis=-1, keepdims=True)
    expo = jnp.exp(scores - peak)
    attn_weights = (expo / jnp.sum(expo, axis=-1, keepdims=True)).astype(jnp.bfloat16)
    mixed = jnp.einsum(
        "skgl,slkd->skgd", attn_weights, value_heads, preferred_element_type=jnp.float32
    )
    return mixed.reshape(seq_count, -1)


def body(
    hidden, lengths, norm_gain, q_norm_gain, k_norm_gain, query_weight, key_weight, value_weight
):
    gathered = lax.all_gather(hidden, "tensor", axis=3, tiled=True)
    pair_count, _, seq_slots, model_width = gathered.shape
    seq_count = 2 * pair_count
    flat_rows = gathered.reshape(-1, model_width).astype(jnp.float32)
    normed = (rms_rows(flat_rows) * norm_gain).astype(jnp.bfloat16)
    kv_width = key_weight.shape[1]
    incoming = (
        lax.all_gather(key_weight, "dp", axis=0, tiled=True),
        lax.all_gather(value_weight, "dp", axis=0, tiled=True),
    )
    columns = normed
    key_proj = jnp.dot(columns, incoming[0], preferred_element_type=jnp.float32)
    value_proj = jnp.dot(columns, incoming[1], preferred_element_type=jnp.float32)
    head_size = HEAD_DIM
    kv_local = kv_width // head_size
    key_proj = key_proj.reshape(seq_count, seq_slots, kv_local, head_size)
    value_proj = value_proj.reshape(seq_count, seq_slots, kv_local, head_size)
    seq_lengths = lengths.reshape(-1)
    last_index = seq_lengths - 1
    normed_seqs = normed.reshape(seq_count, seq_slots, model_width)
    last_rows = jnp.take_along_axis(normed_seqs, last_index[:, None, None], axis=1)[:, 0]
    query_width = query_weight.shape[1]
    columns = last_rows
    query_proj = jnp.dot(
        columns,
        lax.all_gather(query_weight, "dp", axis=0, tiled=True),
        preferred_element_type=jnp.float32,
    )
    mixed = attend(query_proj, key_proj, value_proj, seq_lengths, q_norm_gain, k_norm_gain)
    squares = lax.psum(jnp.sum(mixed * mixed, axis=-1), "tensor")
    emb_local = (mixed * lax.rsqrt(squares + EPS)[:, None]).astype(jnp.bfloat16)
    emb_full = lax.all_gather(emb_local, "tensor", axis=1, tiled=True)
    emb_pairs = emb_full.reshape(pair_count, 2, model_width)
    query_emb = emb_pairs[:, 0]
    passage_emb = emb_pairs[:, 1]
    positive = SCORE_SCALE * jnp.sum(
        query_emb.astype(jnp.float32) * passage_emb.astype(jnp.float32), axis=-1
    )
    low_start = jnp.full((pair_count,), -1e30, jnp.float32)
    incoming = lax.all_gather(emb_pairs, "dp", axis=0, tiled=True)
    row_peak = low_start
    col_peak = low_start
    row_sim = SCORE_SCALE * jnp.dot(query_emb, incoming[:, 1].T, preferred_element_type=jnp.float32)
    col_sim = SCORE_SCALE * jnp.dot(
        passage_emb, incoming[:, 0].T, preferred_element_type=jnp.float32
    )
    row_new = jnp.maximum(row_peak, jnp.max(row_sim, axis=-1))
    col_new = jnp.maximum(col_peak, jnp.max(col_sim, axis=-1))
    row_sum = jnp.sum(jnp.exp(row_sim - row_new[:, None]), axis=-1)
    col_sum = jnp.sum(jnp.exp(col_sim - col_new[:, None]), axis=-1)
    row_peak, row_sum, col_peak, col_sum = (row_new, row_sum, col_new, col_sum)
    pair_loss = 0.5 * (row_peak + jnp.log(row_sum) + col_peak + jnp.log(col_sum)) - positive
    loss = lax.psum(jnp.sum(pair_loss), "dp") / (pair_count * lax.axis_size("dp"))
    embeddings = emb_local.reshape(pair_count, 2, query_width)
    return (embeddings, pair_loss, loss)


def solution(mesh):
    in_specs = (
        P("dp", None, None, "tensor"),
        P("dp", None),
        P(),
        P(),
        P(),
        P("dp", "tensor"),
        P("dp", "tensor"),
        P("dp", "tensor"),
    )
    out_specs = (P("dp", None, "tensor"), P("dp"), P())
    return jax.shard_map(body, mesh=mesh, in_specs=in_specs, out_specs=out_specs, check_vma=False)
```

profile of v0, /device:TPU:32, one launch (start us, length us, event | category | flops | bytes accessed | tf_op | source)
XLA Modules:
  0.0 1495.4 jit_solution(7932595372664853019)
XLA Ops:
  7.2 0.0 all-gather.10.cloned.1.call-start
  7.2 0.7 all-gather.10.cloned.1.call-update
  7.9 0.0 all-gather.12.cloned.1.call-start
  7.9 0.7 all-gather.12.cloned.1.call-update
  8.6 0.0 all-gather.6.cloned.1.call-start
  8.7 0.7 all-gather.6.cloned.1.call-update
  9.4 0.0 all-gather.8.cloned.1.call-start
  9.4 0.5 all-gather.8.cloned.1.call-update
  10.0 0.0 all-gather.14.cloned.1.call-start
  10.0 0.8 lt.37
  10.8 0.7 broadcast_add_fusion.1
  11.4 0.1 add.97
  11.5 0.1 sub.36
  11.6 0.1 iota_compare_fusion
  11.7 299.7 %all-gather.10.cloned.1.call-done = bf16[4096,256]{1,0:T(8,128)(2,1)} async-done(((bf16[64,256]{1,0:T(8,128)(2,1)}), bf16[4096,256]{1,0:T(8,128)(2,1)}) %all-gather.10.cloned.1.call-update) | async-done | bytes 2097168 | tf_op jit(solution)/shard_map/all_gather | solution.py:51
  311.4 0.0 copy-start
  311.4 4.1 copy.31
  315.5 294.6 %all-gather.12.cloned.1.call-done = bf16[4096,256]{1,0:T(8,128)(2,1)} async-done(((bf16[64,256]{1,0:T(8,128)(2,1)}), bf16[4096,256]{1,0:T(8,128)(2,1)}) %all-gather.12.cloned.1.call-update) | async-done | bytes 2097168 | tf_op jit(solution)/shard_map/all_gather | solution.py:52
  610.1 2.9 copy.34
  613.0 61.8 %all-gather.6.cloned.1.call-done = bf16[2,2,256,4096]{3,2,1,0:T(8,128)(2,1)} async-done(((bf16[2,2,256,1024]{3,2,1,0:T(8,128)(2,1)}), bf16[2,2,256,4096]{3,2,1,0:T(8,128)(2,1)}) %all-gather.6.cloned.1.call-update) | async-done | bytes 8388624 | tf_op jit(solution)/shard_map/all_gather | solution.py:44
  674.8 5.1 multiply_reduce_fusion
  679.9 0.0 copy-done
  679.9 10.3 fusion.2
  690.3 1.5 gather_fusion
  691.8 10.3 multiply_convert_fusion
  702.1 6.4 multiply_reduce_fusion.1
  708.5 277.9 %all-gather.8.cloned.1.call-done = bf16[4096,1024]{1,0:T(8,128)(2,1)} async-done(((bf16[64,1024]{1,0:T(8,128)(2,1)}), bf16[4096,1024]{1,0:T(8,128)(2,1)}) %all-gather.8.cloned.1.call-update) | async-done | bytes 8388624 | tf_op jit(solution)/shard_map/all_gather | solution.py:69
  986.4 11.5 copy.30
  997.9 0.0 copy-start.1
  997.9 0.0 copy-start.2
  997.9 5.7 multiply_reduce_fusion.4
  1003.7 0.0 copy-done.1
  1003.7 0.1 multiply_convert_fusion.5
  1003.8 0.0 copy-done.2
  1003.8 0.4 fusion.23
  1004.2 6.1 multiply_reduce_fusion.3
  1010.4 7.2 psum.14
  1017.5 0.1 multiply_convert_fusion.3
  1017.6 6.7 all_gather.22
  1024.3 0.6 reshape.228
  1024.9 0.0 all-gather.14.cloned.1.call-update
  1025.0 0.1 mul.140
  1025.1 0.9 fusion.22
  1026.0 0.2 multiply_reduce_fusion.2
  1026.1 0.7 multiply_convert_fusion.4
  1026.8 295.8 %all-gather.14.cloned.1.call-done = bf16[128,2,4096]{2,1,0:T(2,128)(2,1)} async-done(((bf16[2,2,4096]{2,1,0:T(2,128)(2,1)}), bf16[128,2,4096]{2,1,0:T(2,128)(2,1)}) %all-gather.14.cloned.1.call-update) | async-done | bytes 2097168 | tf_op jit(solution)/shard_map/all_gather | solution.py:83
  1322.6 6.1 fusion.21
  1328.8 1.3 fusion.25
  1330.1 1.3 fusion.24
  1331.4 0.2 exponential_reduce_fusion
  1331.7 1.1 fusion.20
  1332.8 154.3 %psum.15 = f32[]{:T(128)} all-reduce(f32[]{:T(128)} %get-tuple-element.3), channel_id=1, replica_groups=mesh['dp'=64,'tensor'=4] {'dp'}, use_global_device_ids=true, to_apply=%region_13.14 | all-reduce | flops 1 | bytes 8 | tf_op jit(solution)/shard_map/psum | solution.py:96
  (14 shorter events, 0.2 us)
Async XLA Ops:
  7.2 304.2 %all-gather.10.cloned.1.call-start = ((), (), s32[]{:S(2)}) async-start(), calls=%async_computation.2 | async-start | bytes 2129920 | tf_op jit(solution)/shard_map/all_gather | solution.py:51
  7.9 602.2 %all-gather.12.cloned.1.call-start = ((), (), s32[]{:S(2)}) async-start(), calls=%async_computation.3 | async-start | bytes 2129920 | tf_op jit(solution)/shard_map/all_gather | solution.py:52
  8.6 666.2 %all-gather.6.cloned.1.call-start = ((), (), s32[]{:S(2)}) async-start(), calls=%async_computation | async-start | bytes 10485760 | tf_op jit(solution)/shard_map/all_gather | solution.py:44
  9.4 977.0 %all-gather.8.cloned.1.call-start = ((), (), s32[]{:S(2)}) async-start(), calls=%async_computation.1 | async-start | bytes 8519680 | tf_op jit(solution)/shard_map/all_gather | solution.py:69
  10.0 1312.7 %all-gather.14.cloned.1.call-start = ((), (), s32[]{:S(2)}) async-start(), calls=%async_computation.4 | async-start | bytes 2129920 | tf_op jit(solution)/shard_map/all_gather | solution.py:83
  311.4 368.6 %copy-start = (f32[4096]{0:T(1024)S(1)}, f32[4096]{0:T(1024)}, u32[]{:S(2)}) copy-start(f32[4096]{0:T(1024)} %param.10) | copy-start | bytes 49156
  997.9 5.8 copy-start.1
  997.9 5.9 copy-start.2
Sparse Core Ops, SparseCore 0:
  9.8 301.5 all-gather.9
  313.2 296.9 all-gather.11
  612.0 62.8 all-gather.5
  676.5 309.8 all-gather.7
  1025.1 297.5 all-gather.13
where the time goes:
time: 1500 us
  waiting for transfers between devices  1230 us (82%)
  blocking collectives  168 us (11%)
  other arithmetic  28.9 us (2%)
  local copies, waits for them, and re-layouts  28.7 us (2%)
  matrix products  21.3 us (1%)
  between operations  15.7 us (1%)
    all_gather x1, waiting for transfers between devices, body(): lax.all_gather(key_weight, 'dp', axis=0, tiled=True)  300 us
    all_gather x1, waiting for transfers between devices, body(): incoming = lax.all_gather(emb_pairs, 'dp', axis=0, tiled=True)  296 us
    all_gather x1, waiting for transfers between devices, body(): lax.all_gather(value_weight, 'dp', axis=0, tiled=True)  295 us
    all_gather x1, waiting for transfers between devices, body(): lax.all_gather(query_weight, 'dp', axis=0, tiled=True)  278 us
    psum x1, blocking collectives, body(): lax.psum(jnp.sum(pair_loss), 'dp') / (pair_count * lax.axis_size('dp'))  154 us
    all_gather x1, waiting for transfers between devices, body(): gathered = lax.all_gather(hidden, 'tensor', axis=3, tiled=True)  61.8 us
  transfers between devices with their start and end apart: 5, of which 5 were waited for; matrix products, arithmetic and copies ran while one was open for 3% of the time, Pallas kernels for 0%

commit v1 on v0

v1 whole, which is shorter than its diff:
```python
import math

import jax
import jax.numpy as jnp
from jax import lax
from jax.experimental import pallas as pl
from jax.experimental.pallas import tpu as pltpu
from jax.sharding import PartitionSpec as P

HEAD_DIM = 128
EPS = 1e-06
SCORE_SCALE = 20.0

Y, XLO, Z = 4, 2, 8
XHI, CORES = 2, 2
GROUPS = Y * XLO
Z_GROUPS = [[g * Z + z for z in range(Z)] for g in range(GROUPS)]


def rms_rows(values):
    return values * lax.rsqrt(jnp.mean(values * values, axis=-1, keepdims=True) + EPS)


def shift(array, dx=0, dy=0, dz=0):
    pairs = []
    for y in range(Y):
        for x in range(XHI * XLO):
            for z in range(Z):
                for core in range(CORES):

                    def at(x, y, z):
                        x_hi, x_lo = divmod(x, XLO)
                        dp = (y * XLO + x_lo) * Z + z
                        return dp * (XHI * CORES) + x_hi * CORES + core

                    there = at((x + dx) % (XHI * XLO), (y + dy) % Y, (z + dz) % Z)
                    pairs.append((at(x, y, z), there))
    return lax.ppermute(array, ("dp", "tensor"), pairs)


def swap_tensor(array, mask):
    size = XHI * CORES
    return lax.ppermute(array, "tensor", [(i, i ^ mask) for i in range(size)])


def swap_x_lo(array):
    pairs = [(i, (i // Z ^ 1) * Z + i % Z) for i in range(GROUPS * Z)]
    return lax.ppermute(array, "dp", pairs)


def exchange(chunks, groups):
    return lax.all_to_all(
        chunks, "dp", split_axis=0, concat_axis=0, tiled=True, axis_index_groups=groups
    )


def last_rows_kernel(at_ref, r0, r1, r2, r3, gain_ref, out_ref, raw_ref, row_ref):
    y_at, x_lo_at, tensor_at = at_ref[0], at_ref[1], at_ref[2]
    refs = [r0, r1, r2, r3]
    seq_count, width = r0.shape
    rows = width // (XLO * Z)
    squares = None
    for k, ref in enumerate(refs):
        x = ref[...].astype(jnp.float32)
        raw_ref[k] = x
        part = jnp.sum(x * x, axis=-1, keepdims=True)
        squares = part if squares is None else squares + part
    scale = lax.rsqrt(squares / (len(refs) * width) + EPS)
    row_ref[...] = jnp.zeros_like(row_ref)
    for step in range(Y):
        slice_at = (y_at + step) & (Y - 1)
        normed = raw_ref[slice_at ^ tensor_at] * scale * gain_ref[pl.ds(slice_at, 1), :]
        normed = normed.astype(jnp.bfloat16).astype(jnp.float32)
        halves = [normed[:, : Z * rows], normed[:, Z * rows :]]
        row, lane = (0, step * XLO * rows) if step < Y - 1 else (8, 0)
        for x in range(XLO):
            half = jnp.where(x_lo_at == x, halves[0], halves[1])
            for z in range(Z):
                at = lane + x * rows
                row_ref[z, row : row + seq_count, at : at + rows] = half[
                    :, z * rows : (z + 1) * rows
                ]
    out_ref[...] = row_ref[...].astype(jnp.bfloat16)


def query_kernel(rows_ref, w0, w1, w2, w3, out_ref, acc_ref):
    depth, _ = w0.shape
    rows = rows_ref[...].astype(jnp.float32)
    total = None
    for step, w_ref in enumerate([w0, w1, w2, w3]):
        row, lane = (0, step * depth) if step < Y - 1 else (8, 0)
        lhs = rows[:, row : row + 8, lane : lane + depth].reshape(Z * 8, depth)
        part = jnp.dot(
            lhs.astype(jnp.bfloat16), w_ref[:, HEAD_DIM:], preferred_element_type=jnp.float32
        )
        total = part if total is None else total + part
    high = total.astype(jnp.bfloat16).astype(jnp.float32)
    low = (total - high).astype(jnp.bfloat16).astype(jnp.float32)
    both = high + pltpu.roll(low, 4, 0)
    for head in range(both.shape[1] // HEAD_DIM):
        block = both[:, head * HEAD_DIM : (head + 1) * HEAD_DIM]
        acc_ref[:, head * 8 : (head + 1) * 8, :] = block.reshape(Z, 8, HEAD_DIM)
    out_ref[...] = acc_ref[...].astype(jnp.bfloat16)


def kv_attend_kernel(
    at_ref,
    len_ref,
    x0_ref,
    x1_ref,
    x2_ref,
    x3_ref,
    own_ref,
    up_ref,
    far_ref,
    down_ref,
    last_ref,
    gain_ref,
    qg_ref,
    kg_ref,
    out_ref,
    wk_ref,
    wv_ref,
    query_ref,
):
    x_refs = [x0_ref, x1_ref, x2_ref, x3_ref]
    _, slots, width = x0_ref.shape
    slices = len(x_refs)
    rows = width // (XLO * Z)
    seq = pl.program_id(0)
    heads = out_ref.shape[1]
    y_at, x_lo_at, tensor_at = at_ref[0], at_ref[1], at_ref[2]

    @pl.when(seq == 0)
    def _():
        for step, piece in enumerate([own_ref, up_ref, far_ref, down_ref]):
            base = ((y_at + step) & (Y - 1)) * width
            for x in range(XLO):
                half = base + (x_lo_at ^ x) * (Z * rows)
                for z in range(Z):
                    at = pl.ds(pl.multiple_of(half + z * rows, rows), rows)
                    block = slice(x * rows, (x + 1) * rows)
                    wk_ref[at, :] = piece[z, block, : 2 * HEAD_DIM]
                    wv_ref[at, :HEAD_DIM] = piece[z, block, 2 * HEAD_DIM :]
                    start = (step * XLO + x) * rows
                    wv_ref[at, HEAD_DIM:] = last_ref[z, start : start + rows, :]
        parts = last_ref[:, Y * XLO * rows :, :].astype(jnp.float32)
        parts = jnp.sum(parts, axis=0)
        query_ref[...] = parts + pltpu.roll(parts, parts.shape[0] - 4, 0)

    squares = None
    for k in range(slices):
        x = x_refs[k][0].astype(jnp.float32)
        part = jnp.sum(x * x, axis=-1, keepdims=True)
        squares = part if squares is None else squares + part
    scale = lax.rsqrt(squares / (slices * width) + EPS)
    key_proj = value_proj = None
    for k in range(slices):
        x = x_refs[k][0].astype(jnp.float32)
        slice_at = tensor_at ^ k
        normed = (x * scale * gain_ref[pl.ds(slice_at, 1), :]).astype(jnp.bfloat16)
        at = pl.ds(pl.multiple_of(slice_at * width, width), width)
        kp = jnp.dot(normed, wk_ref[at, :], preferred_element_type=jnp.float32)
        vp = jnp.dot(normed, wv_ref[at, :], preferred_element_type=jnp.float32)
        key_proj = kp if key_proj is None else key_proj + kp
        value_proj = vp if value_proj is None else value_proj + vp
    query = query_ref[pl.ds(seq, heads, stride=8), :]
    query = (rms_rows(query) * qg_ref[...]).astype(jnp.bfloat16)
    first = lax.broadcasted_iota(jnp.int32, (heads, 1), 0) < heads // 2
    scores = []
    for h in range(2):
        key = key_proj[:, h * HEAD_DIM : (h + 1) * HEAD_DIM]
        key = (rms_rows(key) * kg_ref[...]).astype(jnp.bfloat16)
        scores.append(
            lax.dot_general(
                query, key, (((1,), (1,)), ((), ())), preferred_element_type=jnp.float32
            )
        )
    scores = jnp.where(first, scores[0], scores[1]) / math.sqrt(HEAD_DIM)
    positions = lax.broadcasted_iota(jnp.int32, (1, slots), 1)
    scores = jnp.where(positions < len_ref[seq], scores, -1e30)
    expo = jnp.exp(scores - jnp.max(scores, axis=-1, keepdims=True))
    weights = (expo / jnp.sum(expo, axis=-1, keepdims=True)).astype(jnp.bfloat16)
    value = value_proj.astype(jnp.bfloat16)
    mixed = jnp.dot(weights, value, preferred_element_type=jnp.float32)
    out_ref[0] = jnp.where(first, mixed[:, :HEAD_DIM], mixed[:, HEAD_DIM:])


SMEM = pl.BlockSpec(memory_space=pltpu.SMEM)
VMEM = pl.BlockSpec(memory_space=pltpu.VMEM)


def last_rows_call(at, raw, gains):
    seq_count, width = raw[0].shape
    shape = (Z, 16, (Y - 1) * XLO * (width // (XLO * Z)))
    return pl.pallas_call(
        last_rows_kernel,
        in_specs=[SMEM] + [VMEM] * (len(raw) + 1),
        out_specs=VMEM,
        out_shape=jax.ShapeDtypeStruct(shape, jnp.bfloat16),
        scratch_shapes=[
            pltpu.VMEM((len(raw), seq_count, width), jnp.float32),
            pltpu.VMEM(shape, jnp.float32),
        ],
    )(at, *raw, gains)


def query_call(z_own, rest):
    shape = (Z, (rest[0].shape[1] // HEAD_DIM - 1) * 8, HEAD_DIM)
    tail = z_own.shape[1] // 16 - 1
    return pl.pallas_call(
        query_kernel,
        grid=(1,),
        in_specs=[pl.BlockSpec((Z, 16, z_own.shape[2]), lambda i: (0, tail, 0))]
        + [VMEM] * len(rest),
        out_specs=VMEM,
        out_shape=jax.ShapeDtypeStruct(shape, jnp.bfloat16),
        scratch_shapes=[pltpu.VMEM(shape, jnp.float32)],
    )(z_own, *rest)


def kv_attend(at, lengths, slices, pieces, last, gains, heads, qg, kg):
    seq_count, slots, width = slices[0].shape
    model_width = gains.size
    kv_width = 2 * HEAD_DIM
    x_spec = pl.BlockSpec((1, slots, width), lambda seq: (seq, 0, 0))
    return pl.pallas_call(
        kv_attend_kernel,
        grid=(seq_count,),
        in_specs=[SMEM, SMEM] + [x_spec] * len(slices) + [VMEM] * (len(pieces) + 4),
        out_specs=pl.BlockSpec((1, heads, HEAD_DIM), lambda seq: (seq, 0, 0)),
        out_shape=jax.ShapeDtypeStruct((seq_count, heads, HEAD_DIM), jnp.float32),
        scratch_shapes=[pltpu.VMEM((model_width, kv_width), jnp.bfloat16)] * 2
        + [pltpu.VMEM((heads * 8, HEAD_DIM), jnp.float32)],
        compiler_params=pltpu.CompilerParams(vmem_limit_bytes=40 * 1024 * 1024),
        cost_estimate=pl.CostEstimate(
            flops=4 * seq_count * slots * model_width * kv_width,
            bytes_accessed=2 * seq_count * slots * model_width + 4 * model_width * kv_width,
            transcendentals=seq_count * heads * slots,
        ),
    )(at, lengths, *slices, *pieces, last, gains, qg, kg)


def body(
    hidden, lengths, norm_gain, q_norm_gain, k_norm_gain, query_weight, key_weight, value_weight
):
    tensor_size = lax.axis_size("tensor")
    tensor_at = lax.axis_index("tensor")
    dp_at = lax.axis_index("dp")
    x_lo_at = (dp_at >> (Z.bit_length() - 1)) & (XLO - 1)
    y_at = dp_at >> ((Z * XLO).bit_length() - 1)
    at = jnp.stack([y_at, x_lo_at, tensor_at]).astype(jnp.int32)

    pair_count, _, seq_slots, width_local = hidden.shape
    seq_count = 2 * pair_count
    own = hidden.reshape(seq_count, seq_slots, width_local)
    seq_lengths = lengths.reshape(-1)
    rows_local, kv_width = key_weight.shape
    query_width = query_weight.shape[1]
    gains = norm_gain.reshape(tensor_size, width_local)

    kv_weight = jnp.concatenate([key_weight, value_weight], axis=1)
    kv_both = jnp.concatenate([kv_weight, swap_x_lo(kv_weight)])
    query_other = swap_x_lo(query_weight)
    last_own = jnp.take_along_axis(own, (seq_lengths - 1)[:, None, None], axis=1)[:, 0]
    last_raw = [last_own] + [swap_tensor(last_own, k) for k in range(1, tensor_size)]

    peer = swap_tensor(own, 1)
    sent_own = lax.optimization_barrier((own, kv_both, query_other, *last_raw))[0]
    far = swap_tensor(sent_own, 2)

    block = kv_both[:, : kv_width + HEAD_DIM]
    rows = last_rows_call(at, last_raw, gains)
    z_own = exchange(
        jnp.concatenate([jnp.broadcast_to(block[None], (Z,) + block.shape), rows], axis=1),
        Z_GROUPS,
    )
    pieces = [z_own] + [shift(z_own, dy=-step) for step in range(1, Y)]

    rest = jnp.concatenate(
        [kv_both[:, kv_width + HEAD_DIM :], jnp.concatenate([query_weight, query_other])], axis=1
    )
    rest = [rest] + [shift(rest, dy=-step) for step in range(1, Y)]
    partial_q = query_call(z_own, rest)
    head = jnp.concatenate([array[:, :HEAD_DIM] for array in rest])
    last = exchange(
        jnp.concatenate([jnp.broadcast_to(head[None], (Z,) + head.shape), partial_q], axis=1),
        Z_GROUPS,
    )
    far_peer = swap_tensor(lax.optimization_barrier((far, last, *pieces))[0], 1)

    mixed = kv_attend(
        at,
        seq_lengths,
        [own, peer, far, far_peer],
        pieces,
        last,
        gains,
        query_width // HEAD_DIM,
        q_norm_gain[None],
        k_norm_gain[None],
    ).reshape(seq_count, width_local)

    sent = mixed.astype(jnp.bfloat16)
    every = exchange(jnp.broadcast_to(sent[None], (GROUPS * Z,) + sent.shape), None)
    every = every.reshape(-1, 2, width_local)
    dots = jnp.dot(every[:, 0], every[:, 1].T, preferred_element_type=jnp.float32)
    every_f32 = every.astype(jnp.float32)
    norms = jnp.sum(every_f32 * every_f32, axis=-1).T
    part = jnp.concatenate([dots, norms], axis=0)
    parts = [part] + [swap_tensor(part, k) for k in range(1, tensor_size)]
    total = (parts[0] + parts[1]) + (parts[2] + parts[3])
    pairs = dots.shape[0]
    scales = lax.rsqrt(total[pairs:] + EPS)
    sim = SCORE_SCALE * total[:pairs] * scales[0][:, None] * scales[1][None, :]
    row_lse = jax.nn.logsumexp(sim, axis=1)
    col_lse = jax.nn.logsumexp(sim, axis=0)
    positive = jnp.sum(jnp.where(jnp.eye(pairs, dtype=bool), sim, 0.0), axis=0)
    all_loss = 0.5 * (row_lse + col_lse) - positive
    loss = jnp.mean(all_loss)
    pair_loss = lax.dynamic_slice_in_dim(all_loss, dp_at * pair_count, pair_count)
    own_scale = lax.dynamic_slice_in_dim(scales, dp_at * pair_count, pair_count, axis=1)
    embeddings = (mixed.reshape(pair_count, 2, width_local) * own_scale.T[:, :, None]).astype(
        jnp.bfloat16
    )
    return (embeddings, pair_loss, loss)


def solution(mesh):
    in_specs = (
        P("dp", None, None, "tensor"),
        P("dp", None),
        P(),
        P(),
        P(),
        P("dp", "tensor"),
        P("dp", "tensor"),
        P("dp", "tensor"),
    )
    out_specs = (P("dp", None, "tensor"), P("dp"), P())
    return jax.shard_map(body, mesh=mesh, in_specs=in_specs, out_specs=out_specs, check_vma=False)
```

time: 1500 us -> 165 us (0.11)
  waiting for transfers between devices: 1230 us -> 60.2 us
  blocking collectives: 168 us -> 27.5 us
  starting transfers between devices: 0.19 us -> 37.2 us
  other arithmetic: 28.9 us -> 7.69 us
  matrix products: 21.3 us -> 0.26 us
  local copies, waits for them, and re-layouts: 28.7 us -> 13.7 us
    all_gather x5 -> x0, waiting for transfers between devices: 1230 us -> none  [the longest x1 300 us: body(): lax.all_gather(key_weight, 'dp', axis=0, tiled=True)]
    psum x2 -> x0, blocking collectives: 161 us -> none  [the longest x1 154 us: body(): lax.psum(jnp.sum(pair_loss), 'dp') / (pair_count * lax.axis_size('dp'))]
    ppermute x0 -> x17, waiting for transfers between devices: none -> 57.7 us  [the longest x9 26.6 us: swap_tensor(): return lax.ppermute(array, 'tensor', [(i, i ^ mask) for i in range(size)])]
    all_to_all x0 -> x1, blocking collectives: none -> 27.5 us  [exchange(): lax.all_to_all(chunks, 'dp', split_axis=0, concat_axis=0, tiled=True, axi...]
    ppermute x0 -> x17, starting transfers between devices: none -> 23.1 us  [the longest x6 11.2 us: shift(): return lax.ppermute(array, ('dp', 'tensor'), pairs)]
    convert_element_type x5 -> x1, other arithmetic: 21.5 us -> 0.67 us  [body(): (mixed.reshape(pair_count, 2, width_local) * own_scale.T[:, :, None]).ast...]
    dot_general x5 -> x1, matrix products: 20.9 us -> 0.26 us  [body(): jnp.dot(every[:, 0], every[:, 1].T, preferred_element_type=jnp.float32)]
    dot_general x3 -> x0, local copies, waits for them, and re-layouts: 18.5 us -> none  [the longest x1 11.5 us: body(): jnp.dot(columns, lax.all_gather(query_weight, 'dp', axis=0, tiled=True),...]
  transfers between devices with their start and end apart: 5 -> 19, of which waited for: 5 -> 9; matrix products, arithmetic and copies ran while one was open for 3% -> 4% of each run, Pallas kernels for 0% -> 2%
where the time goes in v1:
time: 165 us; the launch traced here: 164 us
  waiting for transfers between devices  60.2 us (36%)
  starting transfers between devices  37.2 us (23%)
  blocking collectives  27.5 us (17%)
  Pallas kernels  14.7 us (9%)
  local copies, waits for them, and re-layouts  13.7 us (8%)
  other arithmetic  7.69 us (5%)
  between operations  2.7 us (2%)
    all_to_all x1, blocking collectives, exchange(): lax.all_to_all(chunks, 'dp', split_axis=0, concat_axis=0, tiled=True, axi...  27.5 us
    ppermute x9, waiting for transfers between devices, swap_tensor(): return lax.ppermute(array, 'tensor', [(i, i ^ mask) for i in range(size)])  26.6 us
    ppermute x6, waiting for transfers between devices, shift(): return lax.ppermute(array, ('dp', 'tensor'), pairs)  26.6 us
    all_to_all x2, starting transfers between devices, exchange(): lax.all_to_all(chunks, 'dp', split_axis=0, concat_axis=0, tiled=True, axi...  14 us
    ppermute x6, starting transfers between devices, shift(): return lax.ppermute(array, ('dp', 'tensor'), pairs)  11.2 us
    pallas_call x1, Pallas kernels, kv_attend(): pl.pallas_call(kv_attend_kernel, grid=(seq_count,), in_specs=[SMEM, SMEM]...  10.8 us
    ppermute x9, starting transfers between devices, swap_tensor(): return lax.ppermute(array, 'tensor', [(i, i ^ mask) for i in range(size)])  9.9 us
    unnamed x41, local copies, waits for them, and re-layouts  7.09 us
  transfers between devices with their start and end apart: 19, of which 9 were waited for; matrix products, arithmetic and copies ran while one was open for 4% of the time, Pallas kernels for 2%

profile of v1, /device:TPU:32, one launch (start us, length us, event | category | flops | bytes accessed | tf_op | source)
XLA Modules:
  0.0 163.9 jit_solution(2272484324215871213)
XLA Ops:
  0.6 0.8 reshape.88.len_ref
  1.4 0.7 broadcast_add_fusion.1
  2.1 0.1 sub.28
  2.2 0.1 add.72
  2.3 1.4 gather_fusion
  3.7 0.1 broadcast_select_fusion.r0
  3.8 2.5 %collective-permute-start.5 = (bf16[4,1024]{1,0:T(4,128)(2,1)S(1)}, bf16[4,1024]{1,0:T(4,128)(2,1)S(1)}, u32[]{:S(2)}, u32[]{:S(2)}) collective-permute-start(bf16[4,1024]{1,0:T(4,128)(2,1)S(1)} %broadcast_select_fusion.r0), channel_id=1, source_target_pairs={{0,3},{1,2},{2,1},{3,0},{4,7},{5,6},{6,5},{7,4},{8,11},{9,10},{10,... | collective-permute-start | bytes 24584 | tf_op jit(solution)/shard_map/ppermute | solution.py:43
  6.3 0.7 collective-permute-start.4
  7.0 0.2 collective-permute-start.3
  7.2 0.8 constant_dynamic-update-slice_fusion.1
  8.0 0.8 constant_dynamic-update-slice_fusion
  8.7 1.5 collective-permute-start.1
  10.2 0.7 pad_add_fusion.at_ref
  10.9 1.3 reshape.90.gain_ref
  12.3 0.6 copy-done.16
  12.8 0.6 copy-done.18
  13.4 1.7 %shard_map.103 = bf16[8,16,384]{2,1,0:T(8,128)(2,1)} custom-call(s32[3]{0:T(128)} %pad_add_fusion.at_ref, bf16[4,1024]{1,0:T(4,128)(2,1)} %copy-done.15, bf16[4,1024]{1,0:T(4,128)(2,1)} %copy-done.18, bf16[4,1024]{1,0:T(4,128)(2,1)} %copy-done.17, bf16[4,1024]{1,0:T(4,128)(2,1)} %copy-done.16, f32[4,1024]{1,0:T(4,128)} %reshape.90.gain_ref), custom_call_target="tpu_custom_call" | custom-call | tf_op jit(solution)/shard_map/pallas_call | solution.py:196
  15.1 0.1 broadcast_in_dim.43
  15.2 1.9 %pad_maximum_fusion.1 = bf16[8,144,384]{2,1,0:T(8,128)(2,1)} fusion(bf16[8,16,384]{2,1,0:T(8,128)(2,1)} %shard_map.103, bf16[8,128,384]{2,1,0:T(8,128)(2,1)S(1)} %broadcast_in_dim.43), kind=kLoop, calls=%fused_computation.3 | loop fusion | flops 1769472 | bytes 1769472 | tf_op jit(solution)/shard_map/concatenate | solution.py:275
  17.1 8.6 %all-to-all-start = ((bf16[8,144,384]{2,1,0:T(8,128)(2,1)}), bf16[8,144,384]{2,1,0:T(8,128)(2,1)S(1)}, u32[]{:S(2)}, u32[]{:S(2)}) async-start(bf16[8,144,384]{2,1,0:T(8,128)(2,1)} %pad_maximum_fusion.1), calls=%async_computation | async-start | bytes 1769472 | tf_op jit(solution)/shard_map/all_to_all | solution.py:52
  25.7 0.5 collective-permute-start.2
  26.2 4.4 %collective-permute-done.2 = bf16[64,1024]{1,0:T(8,128)(2,1)S(1)} collective-permute-done((bf16[64,1024]{1,0:T(8,128)(2,1)S(1)}, bf16[64,1024]{1,0:T(8,128)(2,1)S(1)}, u32[]{:S(2)}, u32[]{:S(2)}) %collective-permute-start.2) | collective-permute-done | bytes 131104 | tf_op jit(solution)/shard_map/ppermute | solution.py:48
  30.7 1.7 %collective-permute-start.9 = (bf16[128,1152]{1,0:T(8,128)(2,1)S(1)}, bf16[128,1152]{1,0:T(8,128)(2,1)S(1)}, u32[]{:S(2)}, u32[]{:S(2)}) collective-permute-start(bf16[128,1152]{1,0:T(8,128)(2,1)S(1)} %maximum_maximum_fusion.w0), channel_id=1, source_target_pairs={{0,64},{1,65},{4,68},{5,69},{8,72},{9,73},{12,76},{13,77},{16,80},... | collective-permute-start | bytes 884744 | tf_op jit(solution)/shard_map/ppermute | solution.py:38
  32.3 2.9 %collective-permute-start.8 = (bf16[128,1152]{1,0:T(8,128)(2,1)S(1)}, bf16[128,1152]{1,0:T(8,128)(2,1)S(1)}, u32[]{:S(2)}, u32[]{:S(2)}) collective-permute-start(bf16[128,1152]{1,0:T(8,128)(2,1)S(1)} %maximum_maximum_fusion.w0), channel_id=1, source_target_pairs={{0,128},{1,129},{4,132},{5,133},{8,136},{9,137},{12,140},{13,141},... | collective-permute-start | bytes 884744 | tf_op jit(solution)/shard_map/ppermute | solution.py:38
  35.2 1.3 collective-permute-start.7
  36.6 2.7 %collective-permute-start.6 = (bf16[4,256,1024]{2,1,0:T(8,128)(2,1)}, bf16[4,256,1024]{2,1,0:T(8,128)(2,1)}, u32[]{:S(2)}, u32[]{:S(2)}) collective-permute-start(bf16[4,256,1024]{2,1,0:T(8,128)(2,1)} %bitcast.3.x0_ref), channel_id=1, source_target_pairs={{0,2},{1,3},{2,0},{3,1},{4,6},{5,7},{6,4},{7,5},{8,10},{9,11},{10,... | collective-permute-start | bytes 6291464 | tf_op jit(solution)/shard_map/ppermute | solution.py:43
  39.3 1.5 collective-permute-done.9.w3
  40.8 6.1 %collective-permute-done.8.w2 = bf16[128,1152]{1,0:T(8,128)(2,1)S(1)} collective-permute-done((bf16[128,1152]{1,0:T(8,128)(2,1)S(1)}, bf16[128,1152]{1,0:T(8,128)(2,1)S(1)}, u32[]{:S(2)}, u32[]{:S(2)}) %collective-permute-start.8) | collective-permute-done | bytes 294944 | tf_op jit(solution)/shard_map/ppermute | solution.py:38
  46.9 2.5 %all-to-all-done.rows_ref.own_ref = bf16[8,144,384]{2,1,0:T(8,128)(2,1)S(1)} async-done(((bf16[8,144,384]{2,1,0:T(8,128)(2,1)}), bf16[8,144,384]{2,1,0:T(8,128)(2,1)S(1)}, u32[]{:S(2)}, u32[]{:S(2)}) %all-to-all-start) | async-done | bytes 884768 | tf_op jit(solution)/shard_map/all_to_all | solution.py:52
  49.5 0.9 copy-done
  50.4 2.3 %shard_map.104 = bf16[8,64,128]{2,1,0:T(8,128)(2,1)} custom-call(bf16[8,144,384]{2,1,0:T(8,128)(2,1)} %copy-done, bf16[128,1152]{1,0:T(8,128)(2,1)} %copy-done.10, bf16[128,1152]{1,0:T(8,128)(2,1)} %copy-done.13, bf16[128,1152]{1,0:T(8,128)(2,1)} %copy-done.12, bf16[128,1152]{1,0:T(8,128)(2,1)} %copy-done.11), custom_call_target="tpu_custom_call" | custom-call | tf_op jit(solution)/shard_map/pallas_call | solution.py:211
  52.6 0.1 broadcast_in_dim.42
  52.8 2.1 %pad_maximum_fusion = bf16[8,576,128]{2,1,0:T(8,128)(2,1)} fusion(bf16[8,64,128]{2,1,0:T(8,128)(2,1)} %shard_map.104, bf16[8,512,128]{2,1,0:T(8,128)(2,1)S(1)} %broadcast_in_dim.42), kind=kLoop, calls=%fused_computation.1 | loop fusion | flops 2359296 | bytes 2359296 | tf_op jit(solution)/shard_map/concatenate | solution.py:287
  55.0 5.4 %all-to-all-start.1 = ((bf16[8,576,128]{2,1,0:T(8,128)(2,1)}), bf16[8,576,128]{2,1,0:T(8,128)(2,1)S(1)}, u32[]{:S(2)}, u32[]{:S(2)}) async-start(bf16[8,576,128]{2,1,0:T(8,128)(2,1)} %pad_maximum_fusion), calls=%async_computation.1 | async-start | bytes 2359296 | tf_op jit(solution)/shard_map/all_to_all | solution.py:52
  60.4 1.1 collective-permute-start.12
  61.5 2.8 %collective-permute-start.11 = (bf16[8,144,384]{2,1,0:T(8,128)(2,1)S(1)}, bf16[8,144,384]{2,1,0:T(8,128)(2,1)S(1)}, u32[]{:S(2)}, u32[]{:S(2)}) collective-permute-start(bf16[8,144,384]{2,1,0:T(8,128)(2,1)S(1)} %copy-done.1), channel_id=1, source_target_pairs={{0,128},{1,129},{4,132},{5,133},{8,136},{9,137},{12,140},{13,141},... | collective-permute-start | bytes 2654216 | tf_op jit(solution)/shard_map/ppermute | solution.py:38
  64.4 1.4 collective-permute-start.10
  65.7 17.8 %collective-permute-done.6.x2_ref = bf16[4,256,1024]{2,1,0:T(8,128)(2,1)} collective-permute-done((bf16[4,256,1024]{2,1,0:T(8,128)(2,1)}, bf16[4,256,1024]{2,1,0:T(8,128)(2,1)}, u32[]{:S(2)}, u32[]{:S(2)}) %collective-permute-start.6) | collective-permute-done | bytes 2097184 | tf_op jit(solution)/shard_map/ppermute | solution.py:43
  83.5 19.1 %collective-permute-done.11.far_ref = bf16[8,144,384]{2,1,0:T(8,128)(2,1)S(1)} collective-permute-done((bf16[8,144,384]{2,1,0:T(8,128)(2,1)S(1)}, bf16[8,144,384]{2,1,0:T(8,128)(2,1)S(1)}, u32[]{:S(2)}, u32[]{:S(2)}) %collective-permute-start.11) | collective-permute-done | bytes 884768 | tf_op jit(solution)/shard_map/ppermute | solution.py:38
  102.6 0.9 copy-done.4
  103.5 0.9 copy-done.6
  104.4 4.4 %collective-permute-done.13.x3_ref = bf16[4,256,1024]{2,1,0:T(8,128)(2,1)S(1)} collective-permute-done((bf16[4,256,1024]{2,1,0:T(8,128)(2,1)}, bf16[4,256,1024]{2,1,0:T(8,128)(2,1)S(1)}, u32[]{:S(2)}, u32[]{:S(2)}) %collective-permute-start.13) | collective-permute-done | bytes 2097184 | tf_op jit(solution)/shard_map/ppermute | solution.py:43
  108.8 1.2 copy-done.5
  110.0 1.2 copy-done.7
  111.2 10.8 %shard_map.105 = f32[4,8,128]{2,1,0:T(8,128)S(1)} custom-call(s32[3]{0:T(128)S(1)} %copy-done.3, s32[4]{0:T(128)S(1)} %reshape.88.len_ref, bf16[4,256,1024]{2,1,0:T(8,128)(2,1)} %bitcast.3.x0_ref, bf16[4,256,1024]{2,1,0:T(8,128)(2,1)} %collective-permute-done.x1_ref, bf16[4,256,1024]{2,1,0:T(8,128)(2,1)} %collective-permute-done.6.x2_ref, ...), custom_call_target="tpu_custom_call" | custom-call | flops 4294967296 | bytes 12582912 | tf_op jit(solution)/shard_map/pallas_call | solution.py:227
  122.0 0.1 broadcast_in_dim.46
  122.2 27.5 %all_to_all.15 = bf16[64,4,1024]{2,1,0:T(4,128)(2,1)S(1)} all-to-all(bf16[64,4,1024]{2,1,0:T(4,128)(2,1)S(1)} %broadcast_in_dim.46), channel_id=1, replica_groups=mesh['dp'=64,'tensor'=4] {'dp'}, dimensions={0} | all-to-all | bytes 1048576 | tf_op jit(solution)/shard_map/all_to_all | solution.py:52
  149.6 0.3 multiply_reduce_fusion
  150.0 0.1 reduce_sum.48
  150.1 0.2 reshape.91
  150.3 0.7 fusion.12
  151.1 0.3 fusion
  151.4 3.0 %collective-permute-start.15 = (f32[130,128]{1,0:T(8,128)S(1)}, f32[130,128]{1,0:T(8,128)S(1)}, u32[]{:S(2)}, u32[]{:S(2)}) collective-permute-start(f32[130,128]{1,0:T(8,128)S(1)} %pad_maximum_fusion.4), channel_id=1, source_target_pairs={{0,2},{1,3},{2,0},{3,1},{4,6},{5,7},{6,4},{7,5},{8,10},{9,11},{10,... | collective-permute-start | bytes 199688 | tf_op jit(solution)/shard_map/ppermute | solution.py:43
  154.3 0.8 collective-permute-start.14
  155.1 2.2 %collective-permute-done.15 = f32[130,128]{1,0:T(8,128)S(1)} collective-permute-done((f32[130,128]{1,0:T(8,128)S(1)}, f32[130,128]{1,0:T(8,128)S(1)}, u32[]{:S(2)}, u32[]{:S(2)}) %collective-permute-start.15) | collective-permute-done | bytes 66592 | tf_op jit(solution)/shard_map/ppermute | solution.py:43
  157.3 2.3 %collective-permute-done.16 = f32[130,128]{1,0:T(8,128)S(1)} collective-permute-done((f32[130,128]{1,0:T(8,128)S(1)}, f32[130,128]{1,0:T(8,128)S(1)}, u32[]{:S(2)}, u32[]{:S(2)}) %collective-permute-start.16) | collective-permute-done | bytes 66592 | tf_op jit(solution)/shard_map/ppermute | solution.py:43
  159.6 0.1 dynamic-slice_bitcast_fusion
  159.7 0.1 copy.15
  159.8 0.2 fusion.10
  160.0 0.2 exponential_reduce_fusion.1
  160.2 0.1 exponential_reduce_fusion
  160.3 0.6 fusion.11
  160.9 0.6 dynamic_slice.7
  161.5 0.7 multiply_convert_fusion
  (66 shorter events, 0.4 us)
Async XLA Ops:
  3.8 8.5 %copy-start.15 = (bf16[4,1024]{1,0:T(4,128)(2,1)}, bf16[4,1024]{1,0:T(4,128)(2,1)S(1)}, u32[]{:S(2)}) copy-start(bf16[4,1024]{1,0:T(4,128)(2,1)S(1)} %broadcast_select_fusion.r0) | copy-start | bytes 24580
  3.8 8.4 %collective-permute-start.5 = (bf16[4,1024]{1,0:T(4,128)(2,1)S(1)}, bf16[4,1024]{1,0:T(4,128)(2,1)S(1)}, u32[]{:S(2)}, u32[]{:S(2)}) collective-permute-start(bf16[4,1024]{1,0:T(4,128)(2,1)S(1)} %broadcast_select_fusion.r0), channel_id=1, source_target_pairs={{0,3},{1,2},{2,1},{3,0},{4,7},{5,6},{6,5},{7,4},{8,11},{9,10},{10,... | collective-permute-start | bytes 24584 | tf_op jit(solution)/shard_map/ppermute | solution.py:43
  6.3 5.9 %collective-permute-start.4 = (bf16[4,1024]{1,0:T(4,128)(2,1)S(1)}, bf16[4,1024]{1,0:T(4,128)(2,1)S(1)}, u32[]{:S(2)}, u32[]{:S(2)}) collective-permute-start(bf16[4,1024]{1,0:T(4,128)(2,1)S(1)} %broadcast_select_fusion.r0), channel_id=1, source_target_pairs={{0,2},{1,3},{2,0},{3,1},{4,6},{5,7},{6,4},{7,5},{8,10},{9,11},{10,... | collective-permute-start | bytes 24584 | tf_op jit(solution)/shard_map/ppermute | solution.py:43
  7.0 5.3 %collective-permute-start.3 = (bf16[4,1024]{1,0:T(4,128)(2,1)S(1)}, bf16[4,1024]{1,0:T(4,128)(2,1)S(1)}, u32[]{:S(2)}, u32[]{:S(2)}) collective-permute-start(bf16[4,1024]{1,0:T(4,128)(2,1)S(1)} %broadcast_select_fusion.r0), channel_id=1, source_target_pairs={{0,1},{1,0},{2,3},{3,2},{4,5},{5,4},{6,7},{7,6},{8,9},{9,8},{10,11... | collective-permute-start | bytes 24584 | tf_op jit(solution)/shard_map/ppermute | solution.py:43
  8.7 6.3 %collective-permute-start.1 = (bf16[64,512]{1,0:T(8,128)(2,1)S(1)}, bf16[64,512]{1,0:T(8,128)(2,1)S(1)}, u32[]{:S(2)}, u32[]{:S(2)}) collective-permute-start(bf16[64,512]{1,0:T(8,128)(2,1)S(1)} %constant_dynamic-update-slice_fusion), channel_id=1, source_target_pairs={{0,32},{4,36},{8,40},{12,44},{16,48},{20,52},{24,56},{28,60},{32,0... | collective-permute-start | bytes 196616 | tf_op jit(solution)/shard_map/ppermute | solution.py:48
  12.2 0.6 copy-start.16
  12.2 0.6 copy-start.17
  12.8 0.6 copy-start.18
  15.1 10.6 %copy-start.14 = (bf16[64,1024]{1,0:T(8,128)(2,1)S(1)}, bf16[64,1024]{1,0:T(8,128)(2,1)}, u32[]{:S(2)}) copy-start(bf16[64,1024]{1,0:T(8,128)(2,1)} %param.13) | copy-start | bytes 393220
  17.1 32.3 %all-to-all-start = ((bf16[8,144,384]{2,1,0:T(8,128)(2,1)}), bf16[8,144,384]{2,1,0:T(8,128)(2,1)S(1)}, u32[]{:S(2)}, u32[]{:S(2)}) async-start(bf16[8,144,384]{2,1,0:T(8,128)(2,1)} %pad_maximum_fusion.1), calls=%async_computation | async-start | bytes 1769472 | tf_op jit(solution)/shard_map/all_to_all | solution.py:52
  25.7 5.0 %collective-permute-start.2 = (bf16[64,1024]{1,0:T(8,128)(2,1)S(1)}, bf16[64,1024]{1,0:T(8,128)(2,1)S(1)}, u32[]{:S(2)}, u32[]{:S(2)}) collective-permute-start(bf16[64,1024]{1,0:T(8,128)(2,1)S(1)} %copy-done.14), channel_id=1, source_target_pairs={{0,32},{4,36},{8,40},{12,44},{16,48},{20,52},{24,56},{28,60},{32,0... | collective-permute-start | bytes 393224 | tf_op jit(solution)/shard_map/ppermute | solution.py:48
  30.7 18.8 %copy-start.10 = (bf16[128,1152]{1,0:T(8,128)(2,1)}, bf16[128,1152]{1,0:T(8,128)(2,1)S(1)}, u32[]{:S(2)}) copy-start(bf16[128,1152]{1,0:T(8,128)(2,1)S(1)} %maximum_maximum_fusion.w0) | copy-start | bytes 884740
  30.7 10.1 %collective-permute-start.9 = (bf16[128,1152]{1,0:T(8,128)(2,1)S(1)}, bf16[128,1152]{1,0:T(8,128)(2,1)S(1)}, u32[]{:S(2)}, u32[]{:S(2)}) collective-permute-start(bf16[128,1152]{1,0:T(8,128)(2,1)S(1)} %maximum_maximum_fusion.w0), channel_id=1, source_target_pairs={{0,64},{1,65},{4,68},{5,69},{8,72},{9,73},{12,76},{13,77},{16,80},... | collective-permute-start | bytes 884744 | tf_op jit(solution)/shard_map/ppermute | solution.py:38
  32.3 14.5 %collective-permute-start.8 = (bf16[128,1152]{1,0:T(8,128)(2,1)S(1)}, bf16[128,1152]{1,0:T(8,128)(2,1)S(1)}, u32[]{:S(2)}, u32[]{:S(2)}) collective-permute-start(bf16[128,1152]{1,0:T(8,128)(2,1)S(1)} %maximum_maximum_fusion.w0), channel_id=1, source_target_pairs={{0,128},{1,129},{4,132},{5,133},{8,136},{9,137},{12,140},{13,141},... | collective-permute-start | bytes 884744 | tf_op jit(solution)/shard_map/ppermute | solution.py:38
  35.2 11.6 %collective-permute-start.7 = (bf16[128,1152]{1,0:T(8,128)(2,1)S(1)}, bf16[128,1152]{1,0:T(8,128)(2,1)S(1)}, u32[]{:S(2)}, u32[]{:S(2)}) collective-permute-start(bf16[128,1152]{1,0:T(8,128)(2,1)S(1)} %maximum_maximum_fusion.w0), channel_id=1, source_target_pairs={{0,192},{1,193},{4,196},{5,197},{8,200},{9,201},{12,204},{13,205},... | collective-permute-start | bytes 884744 | tf_op jit(solution)/shard_map/ppermute | solution.py:38
  36.6 46.9 %collective-permute-start.6 = (bf16[4,256,1024]{2,1,0:T(8,128)(2,1)}, bf16[4,256,1024]{2,1,0:T(8,128)(2,1)}, u32[]{:S(2)}, u32[]{:S(2)}) collective-permute-start(bf16[4,256,1024]{2,1,0:T(8,128)(2,1)} %bitcast.3.x0_ref), channel_id=1, source_target_pairs={{0,2},{1,3},{2,0},{3,1},{4,6},{5,7},{6,4},{7,5},{8,10},{9,11},{10,... | collective-permute-start | bytes 6291464 | tf_op jit(solution)/shard_map/ppermute | solution.py:43
  40.8 8.6 %copy-start.11 = (bf16[128,1152]{1,0:T(8,128)(2,1)}, bf16[128,1152]{1,0:T(8,128)(2,1)S(1)}, u32[]{:S(2)}) copy-start(bf16[128,1152]{1,0:T(8,128)(2,1)S(1)} %collective-permute-done.9.w3) | copy-start | bytes 884740
  46.9 2.6 %copy-start.12 = (bf16[128,1152]{1,0:T(8,128)(2,1)}, bf16[128,1152]{1,0:T(8,128)(2,1)S(1)}, u32[]{:S(2)}) copy-start(bf16[128,1152]{1,0:T(8,128)(2,1)S(1)} %collective-permute-done.8.w2) | copy-start | bytes 884740
  46.9 2.6 %copy-start.13 = (bf16[128,1152]{1,0:T(8,128)(2,1)}, bf16[128,1152]{1,0:T(8,128)(2,1)S(1)}, u32[]{:S(2)}) copy-start(bf16[128,1152]{1,0:T(8,128)(2,1)S(1)} %collective-permute-done.7.w1) | copy-start | bytes 884740
  49.4 0.9 copy-start
  52.8 7.6 %copy-start.1 = (bf16[8,144,384]{2,1,0:T(8,128)(2,1)S(1)}, bf16[8,144,384]{2,1,0:T(8,128)(2,1)}, u32[]{:S(2)}) copy-start(bf16[8,144,384]{2,1,0:T(8,128)(2,1)} %copy-done) | copy-start | bytes 2654212
  52.8 56.0 %copy-start.2 = (f32[4,1024]{1,0:T(4,128)S(1)}, f32[4,1024]{1,0:T(4,128)}, u32[]{:S(2)}) copy-start(f32[4,1024]{1,0:T(4,128)} %reshape.90.gain_ref) | copy-start | bytes 49156
  52.8 56.0 %copy-start.3 = (s32[3]{0:T(128)S(1)}, s32[3]{0:T(128)}, u32[]{:S(2)}) copy-start(s32[3]{0:T(128)} %pad_add_fusion.at_ref) | copy-start | bytes 40
  52.8 56.0 %copy-start.8 = (f32[128]{0:T(128)S(1)}, f32[128]{0:T(128)}, u32[]{:S(2)}) copy-start(f32[128]{0:T(128)} %param.11) | copy-start | bytes 1540
  52.8 56.0 %copy-start.9 = (f32[128]{0:T(128)S(1)}, f32[128]{0:T(128)}, u32[]{:S(2)}) copy-start(f32[128]{0:T(128)} %param.12) | copy-start | bytes 1540
  55.0 49.5 %all-to-all-start.1 = ((bf16[8,576,128]{2,1,0:T(8,128)(2,1)}), bf16[8,576,128]{2,1,0:T(8,128)(2,1)S(1)}, u32[]{:S(2)}, u32[]{:S(2)}) async-start(bf16[8,576,128]{2,1,0:T(8,128)(2,1)} %pad_maximum_fusion), calls=%async_computation.1 | async-start | bytes 2359296 | tf_op jit(solution)/shard_map/all_to_all | solution.py:52
  60.4 23.1 %collective-permute-start.12 = (bf16[8,144,384]{2,1,0:T(8,128)(2,1)S(1)}, bf16[8,144,384]{2,1,0:T(8,128)(2,1)S(1)}, u32[]{:S(2)}, u32[]{:S(2)}) collective-permute-start(bf16[8,144,384]{2,1,0:T(8,128)(2,1)S(1)} %copy-done.1), channel_id=1, source_target_pairs={{0,64},{1,65},{4,68},{5,69},{8,72},{9,73},{12,76},{13,77},{16,80},... | collective-permute-start | bytes 2654216 | tf_op jit(solution)/shard_map/ppermute | solution.py:38
  61.5 41.1 %collective-permute-start.11 = (bf16[8,144,384]{2,1,0:T(8,128)(2,1)S(1)}, bf16[8,144,384]{2,1,0:T(8,128)(2,1)S(1)}, u32[]{:S(2)}, u32[]{:S(2)}) collective-permute-start(bf16[8,144,384]{2,1,0:T(8,128)(2,1)S(1)} %copy-done.1), channel_id=1, source_target_pairs={{0,128},{1,129},{4,132},{5,133},{8,136},{9,137},{12,140},{13,141},... | collective-permute-start | bytes 2654216 | tf_op jit(solution)/shard_map/ppermute | solution.py:38
  64.4 39.1 %collective-permute-start.10 = (bf16[8,144,384]{2,1,0:T(8,128)(2,1)S(1)}, bf16[8,144,384]{2,1,0:T(8,128)(2,1)S(1)}, u32[]{:S(2)}, u32[]{:S(2)}) collective-permute-start(bf16[8,144,384]{2,1,0:T(8,128)(2,1)S(1)} %copy-done.1), channel_id=1, source_target_pairs={{0,192},{1,193},{4,196},{5,197},{8,200},{9,201},{12,204},{13,205},... | collective-permute-start | bytes 2654216 | tf_op jit(solution)/shard_map/ppermute | solution.py:38
  65.7 38.7 %collective-permute-start = (bf16[4,256,1024]{2,1,0:T(8,128)(2,1)}, bf16[4,256,1024]{2,1,0:T(8,128)(2,1)}, u32[]{:S(2)}, u32[]{:S(2)}) collective-permute-start(bf16[4,256,1024]{2,1,0:T(8,128)(2,1)} %bitcast.3.x0_ref), channel_id=1, source_target_pairs={{0,1},{1,0},{2,3},{3,2},{4,5},{5,4},{6,7},{7,6},{8,9},{9,8},{10,11... | collective-permute-start | bytes 6291464 | tf_op jit(solution)/shard_map/ppermute | solution.py:43
  102.6 0.9 copy-start.4
  103.5 0.9 copy-start.6
  104.4 4.4 %collective-permute-start.13 = (bf16[4,256,1024]{2,1,0:T(8,128)(2,1)}, bf16[4,256,1024]{2,1,0:T(8,128)(2,1)S(1)}, u32[]{:S(2)}, u32[]{:S(2)}) collective-permute-start(bf16[4,256,1024]{2,1,0:T(8,128)(2,1)} %collective-permute-done.6.x2_ref), channel_id=1, source_target_pairs={{0,1},{1,0},{2,3},{3,2},{4,5},{5,4},{6,7},{7,6},{8,9},{9,8},{10,11... | collective-permute-start | bytes 6291464 | tf_op jit(solution)/shard_map/ppermute | solution.py:43
  108.8 1.2 copy-start.5
  110.0 1.2 copy-start.7
  151.4 5.9 %collective-permute-start.15 = (f32[130,128]{1,0:T(8,128)S(1)}, f32[130,128]{1,0:T(8,128)S(1)}, u32[]{:S(2)}, u32[]{:S(2)}) collective-permute-start(f32[130,128]{1,0:T(8,128)S(1)} %pad_maximum_fusion.4), channel_id=1, source_target_pairs={{0,2},{1,3},{2,0},{3,1},{4,6},{5,7},{6,4},{7,5},{8,10},{9,11},{10,... | collective-permute-start | bytes 199688 | tf_op jit(solution)/shard_map/ppermute | solution.py:43
  154.3 5.2 %collective-permute-start.16 = (f32[130,128]{1,0:T(8,128)S(1)}, f32[130,128]{1,0:T(8,128)S(1)}, u32[]{:S(2)}, u32[]{:S(2)}) collective-permute-start(f32[130,128]{1,0:T(8,128)S(1)} %pad_maximum_fusion.4), channel_id=1, source_target_pairs={{0,3},{1,2},{2,1},{3,0},{4,7},{5,6},{6,5},{7,4},{8,11},{9,10},{10,... | collective-permute-start | bytes 199688 | tf_op jit(solution)/shard_map/ppermute | solution.py:43
  154.3 5.2 %collective-permute-start.14 = (f32[130,128]{1,0:T(8,128)S(1)}, f32[130,128]{1,0:T(8,128)S(1)}, u32[]{:S(2)}, u32[]{:S(2)}) collective-permute-start(f32[130,128]{1,0:T(8,128)S(1)} %pad_maximum_fusion.4), channel_id=1, source_target_pairs={{0,1},{1,0},{2,3},{3,2},{4,5},{5,4},{6,7},{7,6},{8,9},{9,8},{10,11... | collective-permute-start | bytes 199688 | tf_op jit(solution)/shard_map/ppermute | solution.py:43

commit v2 on v1

--- a/solution.py
+++ b/solution.py
@@ -52,6 +52,27 @@
     return lax.all_to_all(
         chunks, "dp", split_axis=0, concat_axis=0, tiled=True, axis_index_groups=groups
     )
+
+
+def take_last_kernel(len_ref, hidden_ref, out_ref, tile_ref, sem):
+    seq_count, depth, width = tile_ref.shape
+    spots = [len_ref[seq // 2, seq % 2] - 1 for seq in range(seq_count)]
+    copies = []
+    for seq, spot in enumerate(spots):
+        rows = pl.ds(pl.multiple_of(spot & -depth, depth), depth)
+        copies.append(
+            pltpu.make_async_copy(hidden_ref.at[seq, rows, :], tile_ref.at[seq], sem.at[seq])
+        )
+        copies[-1].start()
+    row_at = lax.broadcasted_iota(jnp.int32, (depth, width), 0)
+    seq_at = lax.broadcasted_iota(jnp.int32, (seq_count, width), 0)
+    rows = jnp.zeros((seq_count, width), jnp.float32)
+    for seq, spot in enumerate(spots):
+        copies[seq].wait()
+        tile = tile_ref[seq].astype(jnp.float32)
+        row = jnp.sum(jnp.where(row_at == (spot & (depth - 1)), tile, 0.0), axis=0, keepdims=True)
+        rows = jnp.where(seq_at == seq, row, rows)
+    out_ref[...] = rows.astype(jnp.bfloat16)
 
 
 def last_rows_kernel(at_ref, r0, r1, r2, r3, gain_ref, out_ref, raw_ref, row_ref):
@@ -69,7 +90,9 @@
     row_ref[...] = jnp.zeros_like(row_ref)
     for step in range(Y):
         slice_at = (y_at + step) & (Y - 1)
-        normed = raw_ref[slice_at ^ tensor_at] * scale * gain_ref[pl.ds(slice_at, 1), :]
+        normed = raw_ref[slice_at ^ tensor_at] * scale * gain_ref[
+            :, pl.ds(pl.multiple_of(slice_at * width, width), width)
+        ]
         normed = normed.astype(jnp.bfloat16).astype(jnp.float32)
         halves = [normed[:, : Z * rows], normed[:, Z * rows :]]
         row, lane = (0, step * XLO * rows) if step < Y - 1 else (8, 0)
@@ -112,8 +135,9 @@
     x3_ref,
     own_ref,
     up_ref,
-    far_ref,
     down_ref,
+    far_low_ref,
+    far_high_ref,
     last_ref,
     gain_ref,
     qg_ref,
@@ -133,15 +157,24 @@
 
     @pl.when(seq == 0)
     def _():
-        for step, piece in enumerate([own_ref, up_ref, far_ref, down_ref]):
+        low = Z // 2
+        for step, parts in enumerate(
+            [
+                [own_ref.at[:low], own_ref.at[low:]],
+                [up_ref.at[:low], up_ref.at[low:]],
+                [far_low_ref, far_high_ref],
+                [down_ref.at[:low], down_ref.at[low:]],
+            ]
+        ):
             base = ((y_at + step) & (Y - 1)) * width
             for x in range(XLO):
                 half = base + (x_lo_at ^ x) * (Z * rows)
                 for z in range(Z):
                     at = pl.ds(pl.multiple_of(half + z * rows, rows), rows)
                     block = slice(x * rows, (x + 1) * rows)
-                    wk_ref[at, :] = piece[z, block, : 2 * HEAD_DIM]
-                    wv_ref[at, :HEAD_DIM] = piece[z, block, 2 * HEAD_DIM :]
+                    piece = parts[z // low].at[z % low]
+                    wk_ref[at, :] = piece[block, : 2 * HEAD_DIM]
+                    wv_ref[at, :HEAD_DIM] = piece[block, 2 * HEAD_DIM :]
                     start = (step * XLO + x) * rows
                     wv_ref[at, HEAD_DIM:] = last_ref[z, start : start + rows, :]
         parts = last_ref[:, Y * XLO * rows :, :].astype(jnp.float32)
@@ -158,8 +191,8 @@
     for k in range(slices):
         x = x_refs[k][0].astype(jnp.float32)
         slice_at = tensor_at ^ k
-        normed = (x * scale * gain_ref[pl.ds(slice_at, 1), :]).astype(jnp.bfloat16)
         at = pl.ds(pl.multiple_of(slice_at * width, width), width)
+        normed = (x * scale * gain_ref[:, at]).astype(jnp.bfloat16)
         kp = jnp.dot(normed, wk_ref[at, :], preferred_element_type=jnp.float32)
         vp = jnp.dot(normed, wv_ref[at, :], preferred_element_type=jnp.float32)
         key_proj = kp if key_proj is None else key_proj + kp
@@ -178,7 +211,7 @@
         )
     scores = jnp.where(first, scores[0], scores[1]) / math.sqrt(HEAD_DIM)
     positions = lax.broadcasted_iota(jnp.int32, (1, slots), 1)
-    scores = jnp.where(positions < len_ref[seq], scores, -1e30)
+    scores = jnp.where(positions < len_ref[seq >> 1, seq & 1], scores, -1e30)
     expo = jnp.exp(scores - jnp.max(scores, axis=-1, keepdims=True))
     weights = (expo / jnp.sum(expo, axis=-1, keepdims=True)).astype(jnp.bfloat16)
     value = value_proj.astype(jnp.bfloat16)
@@ -188,6 +221,20 @@
 
 SMEM = pl.BlockSpec(memory_space=pltpu.SMEM)
 VMEM = pl.BlockSpec(memory_space=pltpu.VMEM)
+
+
+def take_last_call(lengths, own):
+    seq_count, _, width = own.shape
+    return pl.pallas_call(
+        take_last_kernel,
+        in_specs=[SMEM, pl.BlockSpec(memory_space=pl.ANY)],
+        out_specs=VMEM,
+        out_shape=jax.ShapeDtypeStruct((seq_count, width), own.dtype),
+        scratch_shapes=[
+            pltpu.VMEM((seq_count, 16, width), own.dtype),
+            pltpu.SemaphoreType.DMA((seq_count,)),
+        ],
+    )(lengths, own)
 
 
 def last_rows_call(at, raw, gains):
@@ -205,18 +252,18 @@
     )(at, *raw, gains)
 
 
-def query_call(z_own, rest):
+def query_call(z_all, rest):
     shape = (Z, (rest[0].shape[1] // HEAD_DIM - 1) * 8, HEAD_DIM)
-    tail = z_own.shape[1] // 16 - 1
+    tail = z_all.shape[1] // 16 - 1
     return pl.pallas_call(
         query_kernel,
         grid=(1,),
-        in_specs=[pl.BlockSpec((Z, 16, z_own.shape[2]), lambda i: (0, tail, 0))]
+        in_specs=[pl.BlockSpec((Z, 16, z_all.shape[2]), lambda i: (0, tail, 0))]
         + [VMEM] * len(rest),
         out_specs=VMEM,
         out_shape=jax.ShapeDtypeStruct(shape, jnp.bfloat16),
         scratch_shapes=[pltpu.VMEM(shape, jnp.float32)],
-    )(z_own, *rest)
+    )(z_all, *rest)
 
 
 def kv_attend(at, lengths, slices, pieces, last, gains, heads, qg, kg):
@@ -254,34 +301,38 @@
     pair_count, _, seq_slots, width_local = hidden.shape
     seq_count = 2 * pair_count
     own = hidden.reshape(seq_count, seq_slots, width_local)
-    seq_lengths = lengths.reshape(-1)
     rows_local, kv_width = key_weight.shape
     query_width = query_weight.shape[1]
-    gains = norm_gain.reshape(tensor_size, width_local)
+    gains = norm_gain[None]
 
     kv_weight = jnp.concatenate([key_weight, value_weight], axis=1)
     kv_both = jnp.concatenate([kv_weight, swap_x_lo(kv_weight)])
     query_other = swap_x_lo(query_weight)
-    last_own = jnp.take_along_axis(own, (seq_lengths - 1)[:, None, None], axis=1)[:, 0]
+    last_own = take_last_call(lengths, own)
     last_raw = [last_own] + [swap_tensor(last_own, k) for k in range(1, tensor_size)]
 
-    peer = swap_tensor(own, 1)
     sent_own = lax.optimization_barrier((own, kv_both, query_other, *last_raw))[0]
     far = swap_tensor(sent_own, 2)
+    peer = swap_tensor(sent_own, 1)
 
     block = kv_both[:, : kv_width + HEAD_DIM]
     rows = last_rows_call(at, last_raw, gains)
-    z_own = exchange(
+    z_all = exchange(
         jnp.concatenate([jnp.broadcast_to(block[None], (Z,) + block.shape), rows], axis=1),
         Z_GROUPS,
     )
-    pieces = [z_own] + [shift(z_own, dy=-step) for step in range(1, Y)]
+    z_own = z_all[:, : block.shape[0]]
+    z_up = shift(z_own, dy=-1)
+    z_down = shift(z_own, dy=1)
+    far_low = shift(z_up[: Z // 2], dy=-1)
+    far_high = shift(z_down[Z // 2 :], dy=1)
+    pieces = [z_own, z_up, z_down, far_low, far_high]
 
     rest = jnp.concatenate(
         [kv_both[:, kv_width + HEAD_DIM :], jnp.concatenate([query_weight, query_other])], axis=1
     )
     rest = [rest] + [shift(rest, dy=-step) for step in range(1, Y)]
-    partial_q = query_call(z_own, rest)
+    partial_q = query_call(z_all, rest)
     head = jnp.concatenate([array[:, :HEAD_DIM] for array in rest])
     last = exchange(
         jnp.concatenate([jnp.broadcast_to(head[None], (Z,) + head.shape), partial_q], axis=1),
@@ -291,7 +342,7 @@
 
     mixed = kv_attend(
         at,
-        seq_lengths,
+        lengths,
         [own, peer, far, far_peer],
         pieces,
         last,

time: 165 us -> 156 us (0.945)
  waiting for transfers between devices: 60.2 us -> 48.8 us
  Pallas kernels: 14.7 us -> 16.7 us
    ppermute x9, waiting for transfers between devices: 26.6 us -> 10.3 us  [swap_tensor(): return lax.ppermute(array, 'tensor', [(i, i ^ mask) for i in range(size)])]
    ppermute x6 -> x7, waiting for transfers between devices: 26.6 us -> 32.1 us  [shift(): return lax.ppermute(array, ('dp', 'tensor'), pairs)]
    unnamed x41 -> x56, local copies, waits for them, and re-layouts: 7.09 us -> 10.2 us
    pallas_call x0 -> x1, Pallas kernels: none -> 2.28 us  [take_last_call(): pl.pallas_call(take_last_kernel, in_specs=[SMEM, pl.BlockSpec(memory_spac...]
    reshape x2 -> x0, local copies, waits for them, and re-layouts: 2.09 us -> none  [the longest x1 1.33 us: body(): gains = norm_gain.reshape(tensor_size, width_local)]
    ppermute x9, starting transfers between devices: 9.9 us -> 7.86 us  [swap_tensor(): return lax.ppermute(array, 'tensor', [(i, i ^ mask) for i in range(size)])]
    ppermute x6 -> x7, starting transfers between devices: 11.2 us -> 12.5 us  [shift(): return lax.ppermute(array, ('dp', 'tensor'), pairs)]
  transfers between devices with their start and end apart: 19 -> 20, of which waited for: 9 -> 10; matrix products, arithmetic and copies ran while one was open for 4% -> 3% of each run, Pallas kernels for 2% -> 3%
where the time goes in v2:
time: 156 us; the launch traced here: 155 us
  waiting for transfers between devices  48.8 us (31%)
  starting transfers between devices  36.6 us (23%)
  blocking collectives  28.9 us (19%)
  Pallas kernels  16.7 us (11%)
  local copies, waits for them, and re-layouts  13.8 us (9%)
  other arithmetic  6.91 us (4%)
  between operations  2.73 us (2%)
    ppermute x7, waiting for transfers between devices, shift(): return lax.ppermute(array, ('dp', 'tensor'), pairs)  32.1 us
    all_to_all x1, blocking collectives, exchange(): lax.all_to_all(chunks, 'dp', split_axis=0, concat_axis=0, tiled=True, axi...  28.9 us
    all_to_all x2, starting transfers between devices, exchange(): lax.all_to_all(chunks, 'dp', split_axis=0, concat_axis=0, tiled=True, axi...  14.1 us
    ppermute x7, starting transfers between devices, shift(): return lax.ppermute(array, ('dp', 'tensor'), pairs)  12.5 us
    pallas_call x1, Pallas kernels, kv_attend(): pl.pallas_call(kv_attend_kernel, grid=(seq_count,), in_specs=[SMEM, SMEM]...  10.4 us
    ppermute x9, waiting for transfers between devices, swap_tensor(): return lax.ppermute(array, 'tensor', [(i, i ^ mask) for i in range(size)])  10.3 us
    unnamed x56, local copies, waits for them, and re-layouts  10.2 us
    ppermute x9, starting transfers between devices, swap_tensor(): return lax.ppermute(array, 'tensor', [(i, i ^ mask) for i in range(size)])  7.86 us
  transfers between devices with their start and end apart: 20, of which 10 were waited for; matrix products, arithmetic and copies ran while one was open for 3% of the time, Pallas kernels for 3%

profile of v2, /device:TPU:32, one launch (start us, length us, event | category | flops | bytes accessed | tf_op | source)
XLA Modules:
  0.0 154.6 jit_solution(8535708645314940598)
XLA Ops:
  0.7 2.3 %shard_map.103.r0 = bf16[4,1024]{1,0:T(4,128)(2,1)} custom-call(s32[2,2]{1,0:T(2,128)} %len_ref.3, bf16[4,256,1024]{2,1,0:T(8,128)(2,1)} %bitcast.25), custom_call_target="tpu_custom_call" | custom-call | tf_op jit(solution)/shard_map/pallas_call | solution.py:228
  2.9 2.5 %collective-permute-start.4 = (bf16[4,1024]{1,0:T(4,128)(2,1)}, bf16[4,1024]{1,0:T(4,128)(2,1)S(1)}, u32[]{:S(2)}, u32[]{:S(2)}) collective-permute-start(bf16[4,1024]{1,0:T(4,128)(2,1)} %shard_map.103.r0), channel_id=1, source_target_pairs={{0,3},{1,2},{2,1},{3,0},{4,7},{5,6},{6,5},{7,4},{8,11},{9,10},{10,... | collective-permute-start | bytes 24584 | tf_op jit(solution)/shard_map/ppermute | solution.py:43
  5.5 0.7 collective-permute-start.3
  6.2 0.2 collective-permute-start.2
  6.4 1.6 %collective-permute-start = (bf16[64,512]{1,0:T(8,128)(2,1)S(1)}, bf16[64,512]{1,0:T(8,128)(2,1)S(1)}, u32[]{:S(2)}, u32[]{:S(2)}) collective-permute-start(bf16[64,512]{1,0:T(8,128)(2,1)S(1)} %constant_dynamic-update-slice_fusion), channel_id=1, source_target_pairs={{0,32},{4,36},{8,40},{12,44},{16,48},{20,52},{24,56},{28,60},{32,0... | collective-permute-start | bytes 196616 | tf_op jit(solution)/shard_map/ppermute | solution.py:48
  8.0 0.6 pad_add_fusion.at_ref
  8.6 2.3 %collective-permute-done.3.r2 = bf16[4,1024]{1,0:T(4,128)(2,1)S(1)} collective-permute-done((bf16[4,1024]{1,0:T(4,128)(2,1)}, bf16[4,1024]{1,0:T(4,128)(2,1)S(1)}, u32[]{:S(2)}, u32[]{:S(2)}) %collective-permute-start.3) | collective-permute-done | bytes 8224 | tf_op jit(solution)/shard_map/ppermute | solution.py:43
  10.9 0.6 copy-done.25
  11.5 1.7 %shard_map.104 = bf16[8,16,384]{2,1,0:T(8,128)(2,1)} custom-call(s32[3]{0:T(128)} %pad_add_fusion.at_ref, bf16[4,1024]{1,0:T(4,128)(2,1)} %shard_map.103.r0, bf16[4,1024]{1,0:T(4,128)(2,1)} %copy-done.26, bf16[4,1024]{1,0:T(4,128)(2,1)} %copy-done.25, bf16[4,1024]{1,0:T(4,128)(2,1)} %copy-done.24, f32[1,4096]{1,0:T(1,128)} %bitcast.29), custom_call_target="tpu_custom_call" | custom-call | tf_op jit(solution)/shard_map/pallas_call | solution.py:243
  13.1 0.1 broadcast_in_dim.16
  13.2 2.1 %pad_maximum_fusion.1 = bf16[8,144,384]{2,1,0:T(8,128)(2,1)} fusion(bf16[8,16,384]{2,1,0:T(8,128)(2,1)} %shard_map.104, bf16[8,128,384]{2,1,0:T(8,128)(2,1)S(1)} %broadcast_in_dim.16), kind=kLoop, calls=%fused_computation.2 | loop fusion | flops 1769472 | bytes 1769472 | tf_op jit(solution)/shard_map/concatenate | solution.py:321
  15.3 8.6 %all-to-all-start = ((bf16[8,144,384]{2,1,0:T(8,128)(2,1)}), bf16[8,144,384]{2,1,0:T(8,128)(2,1)S(1)}, u32[]{:S(2)}, u32[]{:S(2)}) async-start(bf16[8,144,384]{2,1,0:T(8,128)(2,1)} %pad_maximum_fusion.1), calls=%async_computation | async-start | bytes 1769472 | tf_op jit(solution)/shard_map/all_to_all | solution.py:52
  23.9 0.6 collective-permute-start.1
  24.5 4.4 %collective-permute-done.1 = bf16[64,1024]{1,0:T(8,128)(2,1)S(1)} collective-permute-done((bf16[64,1024]{1,0:T(8,128)(2,1)S(1)}, bf16[64,1024]{1,0:T(8,128)(2,1)S(1)}, u32[]{:S(2)}, u32[]{:S(2)}) %collective-permute-start.1) | collective-permute-done | bytes 131104 | tf_op jit(solution)/shard_map/ppermute | solution.py:48
  28.9 1.7 %collective-permute-start.9 = (bf16[128,1152]{1,0:T(8,128)(2,1)S(1)}, bf16[128,1152]{1,0:T(8,128)(2,1)S(1)}, u32[]{:S(2)}, u32[]{:S(2)}) collective-permute-start(bf16[128,1152]{1,0:T(8,128)(2,1)S(1)} %maximum_maximum_fusion.w0), channel_id=1, source_target_pairs={{0,64},{1,65},{4,68},{5,69},{8,72},{9,73},{12,76},{13,77},{16,80},... | collective-permute-start | bytes 884744 | tf_op jit(solution)/shard_map/ppermute | solution.py:38
  30.6 2.9 %collective-permute-start.8 = (bf16[128,1152]{1,0:T(8,128)(2,1)S(1)}, bf16[128,1152]{1,0:T(8,128)(2,1)S(1)}, u32[]{:S(2)}, u32[]{:S(2)}) collective-permute-start(bf16[128,1152]{1,0:T(8,128)(2,1)S(1)} %maximum_maximum_fusion.w0), channel_id=1, source_target_pairs={{0,128},{1,129},{4,132},{5,133},{8,136},{9,137},{12,140},{13,141},... | collective-permute-start | bytes 884744 | tf_op jit(solution)/shard_map/ppermute | solution.py:38
  33.5 1.3 collective-permute-start.7
  34.8 0.7 collective-permute-start.6
  35.5 3.5 %collective-permute-done.9.w3 = bf16[128,1152]{1,0:T(8,128)(2,1)S(1)} collective-permute-done((bf16[128,1152]{1,0:T(8,128)(2,1)S(1)}, bf16[128,1152]{1,0:T(8,128)(2,1)S(1)}, u32[]{:S(2)}, u32[]{:S(2)}) %collective-permute-start.9) | collective-permute-done | bytes 294944 | tf_op jit(solution)/shard_map/ppermute | solution.py:38
  39.0 5.5 %collective-permute-done.8.w2 = bf16[128,1152]{1,0:T(8,128)(2,1)S(1)} collective-permute-done((bf16[128,1152]{1,0:T(8,128)(2,1)S(1)}, bf16[128,1152]{1,0:T(8,128)(2,1)S(1)}, u32[]{:S(2)}, u32[]{:S(2)}) %collective-permute-start.8) | collective-permute-done | bytes 294944 | tf_op jit(solution)/shard_map/ppermute | solution.py:38
  44.5 0.7 copy-done.19
  45.2 0.1 copy-done.20
  45.3 2.0 %all-to-all-done.rows_ref = bf16[8,144,384]{2,1,0:T(8,128)(2,1)S(1)} async-done(((bf16[8,144,384]{2,1,0:T(8,128)(2,1)}), bf16[8,144,384]{2,1,0:T(8,128)(2,1)S(1)}, u32[]{:S(2)}, u32[]{:S(2)}) %all-to-all-start) | async-done | bytes 884768 | tf_op jit(solution)/shard_map/all_to_all | solution.py:52
  47.3 0.9 copy-done.16
  48.3 2.3 %shard_map.105 = bf16[8,64,128]{2,1,0:T(8,128)(2,1)} custom-call(bf16[8,144,384]{2,1,0:T(8,128)(2,1)} %copy-done.16, bf16[128,1152]{1,0:T(8,128)(2,1)} %copy-done.17, bf16[128,1152]{1,0:T(8,128)(2,1)} %copy-done.20, bf16[128,1152]{1,0:T(8,128)(2,1)} %copy-done.19, bf16[128,1152]{1,0:T(8,128)(2,1)} %copy-done.18), custom_call_target="tpu_custom_call" | custom-call | tf_op jit(solution)/shard_map/pallas_call | solution.py:258
  50.5 0.1 broadcast_in_dim.15
  50.7 2.0 %pad_maximum_fusion = bf16[8,576,128]{2,1,0:T(8,128)(2,1)} fusion(bf16[8,64,128]{2,1,0:T(8,128)(2,1)} %shard_map.105, bf16[8,512,128]{2,1,0:T(8,128)(2,1)S(1)} %broadcast_in_dim.15), kind=kLoop, calls=%fused_computation | loop fusion | flops 2359296 | bytes 2359296 | tf_op jit(solution)/shard_map/concatenate | solution.py:338
  52.7 5.5 %all-to-all-start.1 = ((bf16[8,576,128]{2,1,0:T(8,128)(2,1)}), bf16[8,576,128]{2,1,0:T(8,128)(2,1)S(1)}, u32[]{:S(2)}, u32[]{:S(2)}) async-start(bf16[8,576,128]{2,1,0:T(8,128)(2,1)} %pad_maximum_fusion), calls=%async_computation.1 | async-start | bytes 2359296 | tf_op jit(solution)/shard_map/all_to_all | solution.py:52
  58.3 1.2 slice.63.own_ref
  59.5 1.2 collective-permute-start.11
  60.7 2.1 %collective-permute-start.10 = (bf16[8,128,384]{2,1,0:T(8,128)(2,1)S(1)}, bf16[8,128,384]{2,1,0:T(8,128)(2,1)S(1)}, u32[]{:S(2)}, u32[]{:S(2)}) collective-permute-start(bf16[8,128,384]{2,1,0:T(8,128)(2,1)S(1)} %slice.63.own_ref), channel_id=1, source_target_pairs={{0,192},{1,193},{4,196},{5,197},{8,200},{9,201},{12,204},{13,205},... | collective-permute-start | bytes 2359304 | tf_op jit(solution)/shard_map/ppermute | solution.py:38
  62.8 16.7 %collective-permute-done.11.down_ref = bf16[8,128,384]{2,1,0:T(8,128)(2,1)S(1)} collective-permute-done((bf16[8,128,384]{2,1,0:T(8,128)(2,1)S(1)}, bf16[8,128,384]{2,1,0:T(8,128)(2,1)S(1)}, u32[]{:S(2)}, u32[]{:S(2)}) %collective-permute-start.11) | collective-permute-done | bytes 786464 | tf_op jit(solution)/shard_map/ppermute | solution.py:38
  79.5 0.4 collective-permute-start.13
  80.0 0.9 copy-done.5
  80.9 2.9 %collective-permute-start.12 = (bf16[4,128,384]{2,1,0:T(8,128)(2,1)S(1)}, bf16[4,128,384]{2,1,0:T(8,128)(2,1)S(1)}, u32[]{:S(2)}, u32[]{:S(2)}) collective-permute-start(bf16[4,128,384]{2,1,0:T(8,128)(2,1)S(1)} %slice.64), channel_id=1, source_target_pairs={{0,192},{1,193},{4,196},{5,197},{8,200},{9,201},{12,204},{13,205},... | collective-permute-start | bytes 1179656 | tf_op jit(solution)/shard_map/ppermute | solution.py:38
  83.8 6.5 %collective-permute-done.13.far_high_ref = bf16[4,128,384]{2,1,0:T(8,128)(2,1)S(1)} collective-permute-done((bf16[4,128,384]{2,1,0:T(8,128)(2,1)S(1)}, bf16[4,128,384]{2,1,0:T(8,128)(2,1)S(1)}, u32[]{:S(2)}, u32[]{:S(2)}) %collective-permute-start.13) | collective-permute-done | bytes 393248 | tf_op jit(solution)/shard_map/ppermute | solution.py:38
  90.3 0.8 copy-done.10
  91.0 0.8 copy-done.12
  91.9 4.4 %collective-permute-done.14.x3_ref = bf16[4,256,1024]{2,1,0:T(8,128)(2,1)S(1)} collective-permute-done((bf16[4,256,1024]{2,1,0:T(8,128)(2,1)}, bf16[4,256,1024]{2,1,0:T(8,128)(2,1)S(1)}, u32[]{:S(2)}, u32[]{:S(2)}) %collective-permute-start.14) | collective-permute-done | bytes 2097184 | tf_op jit(solution)/shard_map/ppermute | solution.py:43
  96.3 1.1 copy-done.2
  97.4 1.1 copy-done.4
  98.5 1.1 copy-done.6
  99.7 1.0 copy-done.11
  100.7 1.0 copy-done.13
  101.7 10.4 %shard_map.106 = f32[4,8,128]{2,1,0:T(8,128)S(1)} custom-call(s32[3]{0:T(128)S(1)} %copy-done.8, s32[2,2]{1,0:T(2,128)S(1)} %copy-done.9, bf16[4,256,1024]{2,1,0:T(8,128)(2,1)S(1)} %bitcast.28, bf16[4,256,1024]{2,1,0:T(8,128)(2,1)} %collective-permute-done.5.x1_ref, bf16[4,256,1024]{2,1,0:T(8,128)(2,1)} %collective-permute-done.6.x2_ref, ...), custom_call_target="tpu_custom_call" | custom-call | flops 4294967296 | bytes 12582912 | tf_op jit(solution)/shard_map/pallas_call | solution.py:274
  112.1 0.1 broadcast_in_dim.39
  112.3 28.9 %all_to_all.15 = bf16[64,4,1024]{2,1,0:T(4,128)(2,1)S(1)} all-to-all(bf16[64,4,1024]{2,1,0:T(4,128)(2,1)S(1)} %broadcast_in_dim.39), channel_id=1, replica_groups=mesh['dp'=64,'tensor'=4] {'dp'}, dimensions={0} | all-to-all | bytes 1048576 | tf_op jit(solution)/shard_map/all_to_all | solution.py:52
  141.2 0.3 multiply_reduce_fusion
  141.5 0.1 reduce_sum.48
  141.6 0.2 reshape.35
  141.9 0.7 fusion.12
  142.6 0.3 fusion
  142.9 2.1 %collective-permute-start.16 = (f32[130,128]{1,0:T(8,128)S(1)}, f32[130,128]{1,0:T(8,128)S(1)}, u32[]{:S(2)}, u32[]{:S(2)}) collective-permute-start(f32[130,128]{1,0:T(8,128)S(1)} %pad_maximum_fusion.4), channel_id=1, source_target_pairs={{0,2},{1,3},{2,0},{3,1},{4,6},{5,7},{6,4},{7,5},{8,10},{9,11},{10,... | collective-permute-start | bytes 199688 | tf_op jit(solution)/shard_map/ppermute | solution.py:43
  145.0 1.6 %collective-permute-start.15 = (f32[130,128]{1,0:T(8,128)S(1)}, f32[130,128]{1,0:T(8,128)S(1)}, u32[]{:S(2)}, u32[]{:S(2)}) collective-permute-start(f32[130,128]{1,0:T(8,128)S(1)} %pad_maximum_fusion.4), channel_id=1, source_target_pairs={{0,1},{1,0},{2,3},{3,2},{4,5},{5,4},{6,7},{7,6},{8,9},{9,8},{10,11... | collective-permute-start | bytes 199688 | tf_op jit(solution)/shard_map/ppermute | solution.py:43
  146.6 2.2 %collective-permute-done.16 = f32[130,128]{1,0:T(8,128)S(1)} collective-permute-done((f32[130,128]{1,0:T(8,128)S(1)}, f32[130,128]{1,0:T(8,128)S(1)}, u32[]{:S(2)}, u32[]{:S(2)}) %collective-permute-start.16) | collective-permute-done | bytes 66592 | tf_op jit(solution)/shard_map/ppermute | solution.py:43
  148.8 1.5 collective-permute-done.17
  150.3 0.1 dynamic-slice_bitcast_fusion
  150.4 0.1 copy.15
  150.5 0.2 fusion.10
  150.7 0.2 exponential_reduce_fusion.1
  150.9 0.1 exponential_reduce_fusion
  151.0 0.6 fusion.11
  151.6 0.6 dynamic_slice.7
  152.2 0.7 multiply_convert_fusion
  (76 shorter events, 0.5 us)
Async XLA Ops:
  0.6 5.8 %copy-start.22 = (bf16[64,256]{1,0:T(8,128)(2,1)S(1)}, bf16[64,256]{1,0:T(8,128)(2,1)}, u32[]{:S(2)}) copy-start(bf16[64,256]{1,0:T(8,128)(2,1)} %param.14) | copy-start | bytes 98308
  0.6 5.8 %copy-start.23 = (bf16[64,256]{1,0:T(8,128)(2,1)S(1)}, bf16[64,256]{1,0:T(8,128)(2,1)}, u32[]{:S(2)}) copy-start(bf16[64,256]{1,0:T(8,128)(2,1)} %param.15) | copy-start | bytes 98308
  2.9 5.6 %collective-permute-start.4 = (bf16[4,1024]{1,0:T(4,128)(2,1)}, bf16[4,1024]{1,0:T(4,128)(2,1)S(1)}, u32[]{:S(2)}, u32[]{:S(2)}) collective-permute-start(bf16[4,1024]{1,0:T(4,128)(2,1)} %shard_map.103.r0), channel_id=1, source_target_pairs={{0,3},{1,2},{2,1},{3,0},{4,7},{5,6},{6,5},{7,4},{8,11},{9,10},{10,... | collective-permute-start | bytes 24584 | tf_op jit(solution)/shard_map/ppermute | solution.py:43
  5.5 5.4 %collective-permute-start.3 = (bf16[4,1024]{1,0:T(4,128)(2,1)}, bf16[4,1024]{1,0:T(4,128)(2,1)S(1)}, u32[]{:S(2)}, u32[]{:S(2)}) collective-permute-start(bf16[4,1024]{1,0:T(4,128)(2,1)} %shard_map.103.r0), channel_id=1, source_target_pairs={{0,2},{1,3},{2,0},{3,1},{4,6},{5,7},{6,4},{7,5},{8,10},{9,11},{10,... | collective-permute-start | bytes 24584 | tf_op jit(solution)/shard_map/ppermute | solution.py:43
  6.2 4.7 %collective-permute-start.2 = (bf16[4,1024]{1,0:T(4,128)(2,1)}, bf16[4,1024]{1,0:T(4,128)(2,1)S(1)}, u32[]{:S(2)}, u32[]{:S(2)}) collective-permute-start(bf16[4,1024]{1,0:T(4,128)(2,1)} %shard_map.103.r0), channel_id=1, source_target_pairs={{0,1},{1,0},{2,3},{3,2},{4,5},{5,4},{6,7},{7,6},{8,9},{9,8},{10,11... | collective-permute-start | bytes 24584 | tf_op jit(solution)/shard_map/ppermute | solution.py:43
  6.4 6.7 %collective-permute-start = (bf16[64,512]{1,0:T(8,128)(2,1)S(1)}, bf16[64,512]{1,0:T(8,128)(2,1)S(1)}, u32[]{:S(2)}, u32[]{:S(2)}) collective-permute-start(bf16[64,512]{1,0:T(8,128)(2,1)S(1)} %constant_dynamic-update-slice_fusion), channel_id=1, source_target_pairs={{0,32},{4,36},{8,40},{12,44},{16,48},{20,52},{24,56},{28,60},{32,0... | collective-permute-start | bytes 196616 | tf_op jit(solution)/shard_map/ppermute | solution.py:48
  8.6 2.3 %copy-start.24 = (bf16[4,1024]{1,0:T(4,128)(2,1)}, bf16[4,1024]{1,0:T(4,128)(2,1)S(1)}, u32[]{:S(2)}) copy-start(bf16[4,1024]{1,0:T(4,128)(2,1)S(1)} %collective-permute-done.4.r3) | copy-start | bytes 24580
  10.9 0.6 copy-start.25
  10.9 0.6 copy-start.26
  13.2 10.7 %copy-start.21 = (bf16[64,1024]{1,0:T(8,128)(2,1)S(1)}, bf16[64,1024]{1,0:T(8,128)(2,1)}, u32[]{:S(2)}) copy-start(bf16[64,1024]{1,0:T(8,128)(2,1)} %param.13) | copy-start | bytes 393220
  13.2 21.6 %copy-start = (bf16[2,2,256,1024]{3,2,1,0:T(8,128)(2,1)S(1)}, bf16[2,2,256,1024]{3,2,1,0:T(8,128)(2,1)}, u32[]{:S(2)}) copy-start(bf16[2,2,256,1024]{3,2,1,0:T(8,128)(2,1)} %param.8) | copy-start | bytes 6291460
  15.3 32.0 %all-to-all-start = ((bf16[8,144,384]{2,1,0:T(8,128)(2,1)}), bf16[8,144,384]{2,1,0:T(8,128)(2,1)S(1)}, u32[]{:S(2)}, u32[]{:S(2)}) async-start(bf16[8,144,384]{2,1,0:T(8,128)(2,1)} %pad_maximum_fusion.1), calls=%async_computation | async-start | bytes 1769472 | tf_op jit(solution)/shard_map/all_to_all | solution.py:52
  23.9 5.0 %collective-permute-start.1 = (bf16[64,1024]{1,0:T(8,128)(2,1)S(1)}, bf16[64,1024]{1,0:T(8,128)(2,1)S(1)}, u32[]{:S(2)}, u32[]{:S(2)}) collective-permute-start(bf16[64,1024]{1,0:T(8,128)(2,1)S(1)} %copy-done.21), channel_id=1, source_target_pairs={{0,32},{4,36},{8,40},{12,44},{16,48},{20,52},{24,56},{28,60},{32,0... | collective-permute-start | bytes 393224 | tf_op jit(solution)/shard_map/ppermute | solution.py:48
  28.9 18.4 %copy-start.17 = (bf16[128,1152]{1,0:T(8,128)(2,1)}, bf16[128,1152]{1,0:T(8,128)(2,1)S(1)}, u32[]{:S(2)}) copy-start(bf16[128,1152]{1,0:T(8,128)(2,1)S(1)} %maximum_maximum_fusion.w0) | copy-start | bytes 884740
  28.9 10.1 %collective-permute-start.9 = (bf16[128,1152]{1,0:T(8,128)(2,1)S(1)}, bf16[128,1152]{1,0:T(8,128)(2,1)S(1)}, u32[]{:S(2)}, u32[]{:S(2)}) collective-permute-start(bf16[128,1152]{1,0:T(8,128)(2,1)S(1)} %maximum_maximum_fusion.w0), channel_id=1, source_target_pairs={{0,64},{1,65},{4,68},{5,69},{8,72},{9,73},{12,76},{13,77},{16,80},... | collective-permute-start | bytes 884744 | tf_op jit(solution)/shard_map/ppermute | solution.py:38
  30.6 13.9 %collective-permute-start.8 = (bf16[128,1152]{1,0:T(8,128)(2,1)S(1)}, bf16[128,1152]{1,0:T(8,128)(2,1)S(1)}, u32[]{:S(2)}, u32[]{:S(2)}) collective-permute-start(bf16[128,1152]{1,0:T(8,128)(2,1)S(1)} %maximum_maximum_fusion.w0), channel_id=1, source_target_pairs={{0,128},{1,129},{4,132},{5,133},{8,136},{9,137},{12,140},{13,141},... | collective-permute-start | bytes 884744 | tf_op jit(solution)/shard_map/ppermute | solution.py:38
  33.5 11.0 %collective-permute-start.7 = (bf16[128,1152]{1,0:T(8,128)(2,1)S(1)}, bf16[128,1152]{1,0:T(8,128)(2,1)S(1)}, u32[]{:S(2)}, u32[]{:S(2)}) collective-permute-start(bf16[128,1152]{1,0:T(8,128)(2,1)S(1)} %maximum_maximum_fusion.w0), channel_id=1, source_target_pairs={{0,192},{1,193},{4,196},{5,197},{8,200},{9,201},{12,204},{13,205},... | collective-permute-start | bytes 884744 | tf_op jit(solution)/shard_map/ppermute | solution.py:38
  34.8 49.0 %collective-permute-start.6 = (bf16[4,256,1024]{2,1,0:T(8,128)(2,1)S(1)}, bf16[4,256,1024]{2,1,0:T(8,128)(2,1)}, u32[]{:S(2)}, u32[]{:S(2)}) collective-permute-start(bf16[4,256,1024]{2,1,0:T(8,128)(2,1)S(1)} %bitcast.26), channel_id=1, source_target_pairs={{0,2},{1,3},{2,0},{3,1},{4,6},{5,7},{6,4},{7,5},{8,10},{9,11},{10,... | collective-permute-start | bytes 6291464 | tf_op jit(solution)/shard_map/ppermute | solution.py:43
  39.0 5.5 %copy-start.18 = (bf16[128,1152]{1,0:T(8,128)(2,1)}, bf16[128,1152]{1,0:T(8,128)(2,1)S(1)}, u32[]{:S(2)}) copy-start(bf16[128,1152]{1,0:T(8,128)(2,1)S(1)} %collective-permute-done.9.w3) | copy-start | bytes 884740
  44.5 0.7 copy-start.19
  44.5 0.8 copy-start.20
  47.3 0.9 copy-start.16
  52.7 39.1 %all-to-all-start.1 = ((bf16[8,576,128]{2,1,0:T(8,128)(2,1)}), bf16[8,576,128]{2,1,0:T(8,128)(2,1)S(1)}, u32[]{:S(2)}, u32[]{:S(2)}) async-start(bf16[8,576,128]{2,1,0:T(8,128)(2,1)} %pad_maximum_fusion), calls=%async_computation.1 | async-start | bytes 2359296 | tf_op jit(solution)/shard_map/all_to_all | solution.py:52
  58.2 38.0 %copy-start.7 = (f32[4096]{0:T(1024)S(1)}, f32[4096]{0:T(1024)}, u32[]{:S(2)}) copy-start(f32[4096]{0:T(1024)} %param.10) | copy-start | bytes 49156
  58.2 38.0 %copy-start.8 = (s32[3]{0:T(128)S(1)}, s32[3]{0:T(128)}, u32[]{:S(2)}) copy-start(s32[3]{0:T(128)} %pad_add_fusion.at_ref) | copy-start | bytes 40
  58.2 38.0 %copy-start.9 = (s32[2,2]{1,0:T(2,128)S(1)}, s32[2,2]{1,0:T(2,128)}, u32[]{:S(2)}) copy-start(s32[2,2]{1,0:T(2,128)} %len_ref.3) | copy-start | bytes 52
  58.2 38.0 %copy-start.14 = (f32[128]{0:T(128)S(1)}, f32[128]{0:T(128)}, u32[]{:S(2)}) copy-start(f32[128]{0:T(128)} %param.11) | copy-start | bytes 1540
  58.2 38.0 %copy-start.15 = (f32[128]{0:T(128)S(1)}, f32[128]{0:T(128)}, u32[]{:S(2)}) copy-start(f32[128]{0:T(128)} %param.12) | copy-start | bytes 1540
  59.5 30.8 %copy-start.1 = (bf16[8,128,384]{2,1,0:T(8,128)(2,1)}, bf16[8,128,384]{2,1,0:T(8,128)(2,1)S(1)}, u32[]{:S(2)}) copy-start(bf16[8,128,384]{2,1,0:T(8,128)(2,1)S(1)} %slice.63.own_ref) | copy-start | bytes 2359300
  59.5 20.0 %collective-permute-start.11 = (bf16[8,128,384]{2,1,0:T(8,128)(2,1)S(1)}, bf16[8,128,384]{2,1,0:T(8,128)(2,1)S(1)}, u32[]{:S(2)}, u32[]{:S(2)}) collective-permute-start(bf16[8,128,384]{2,1,0:T(8,128)(2,1)S(1)} %slice.63.own_ref), channel_id=1, source_target_pairs={{0,64},{1,65},{4,68},{5,69},{8,72},{9,73},{12,76},{13,77},{16,80},... | collective-permute-start | bytes 2359304 | tf_op jit(solution)/shard_map/ppermute | solution.py:38
  60.7 19.2 %collective-permute-start.10 = (bf16[8,128,384]{2,1,0:T(8,128)(2,1)S(1)}, bf16[8,128,384]{2,1,0:T(8,128)(2,1)S(1)}, u32[]{:S(2)}, u32[]{:S(2)}) collective-permute-start(bf16[8,128,384]{2,1,0:T(8,128)(2,1)S(1)} %slice.63.own_ref), channel_id=1, source_target_pairs={{0,192},{1,193},{4,196},{5,197},{8,200},{9,201},{12,204},{13,205},... | collective-permute-start | bytes 2359304 | tf_op jit(solution)/shard_map/ppermute | solution.py:38
  79.5 10.8 %copy-start.3 = (bf16[8,128,384]{2,1,0:T(8,128)(2,1)}, bf16[8,128,384]{2,1,0:T(8,128)(2,1)S(1)}, u32[]{:S(2)}) copy-start(bf16[8,128,384]{2,1,0:T(8,128)(2,1)S(1)} %collective-permute-done.11.down_ref) | copy-start | bytes 2359300
  79.5 10.7 %collective-permute-start.13 = (bf16[4,128,384]{2,1,0:T(8,128)(2,1)S(1)}, bf16[4,128,384]{2,1,0:T(8,128)(2,1)S(1)}, u32[]{:S(2)}, u32[]{:S(2)}) collective-permute-start(bf16[4,128,384]{2,1,0:T(8,128)(2,1)S(1)} %slice.65), channel_id=1, source_target_pairs={{0,64},{1,65},{4,68},{5,69},{8,72},{9,73},{12,76},{13,77},{16,80},... | collective-permute-start | bytes 1179656 | tf_op jit(solution)/shard_map/ppermute | solution.py:38
  80.0 0.9 copy-start.5
  80.9 10.2 %collective-permute-start.12 = (bf16[4,128,384]{2,1,0:T(8,128)(2,1)S(1)}, bf16[4,128,384]{2,1,0:T(8,128)(2,1)S(1)}, u32[]{:S(2)}, u32[]{:S(2)}) collective-permute-start(bf16[4,128,384]{2,1,0:T(8,128)(2,1)S(1)} %slice.64), channel_id=1, source_target_pairs={{0,192},{1,193},{4,196},{5,197},{8,200},{9,201},{12,204},{13,205},... | collective-permute-start | bytes 1179656 | tf_op jit(solution)/shard_map/ppermute | solution.py:38
  83.8 8.1 %collective-permute-start.5 = (bf16[4,256,1024]{2,1,0:T(8,128)(2,1)S(1)}, bf16[4,256,1024]{2,1,0:T(8,128)(2,1)}, u32[]{:S(2)}, u32[]{:S(2)}) collective-permute-start(bf16[4,256,1024]{2,1,0:T(8,128)(2,1)S(1)} %bitcast.27), channel_id=1, source_target_pairs={{0,1},{1,0},{2,3},{3,2},{4,5},{5,4},{6,7},{7,6},{8,9},{9,8},{10,11... | collective-permute-start | bytes 6291464 | tf_op jit(solution)/shard_map/ppermute | solution.py:43
  90.3 0.8 copy-start.10
  91.0 0.8 copy-start.12
  91.9 4.4 %collective-permute-start.14 = (bf16[4,256,1024]{2,1,0:T(8,128)(2,1)}, bf16[4,256,1024]{2,1,0:T(8,128)(2,1)S(1)}, u32[]{:S(2)}, u32[]{:S(2)}) collective-permute-start(bf16[4,256,1024]{2,1,0:T(8,128)(2,1)} %collective-permute-done.6.x2_ref), channel_id=1, source_target_pairs={{0,1},{1,0},{2,3},{3,2},{4,5},{5,4},{6,7},{7,6},{8,9},{9,8},{10,11... | collective-permute-start | bytes 6291464 | tf_op jit(solution)/shard_map/ppermute | solution.py:43
  96.3 1.1 copy-start.2
  97.4 1.1 copy-start.4
  98.5 1.1 copy-start.6
  99.7 1.0 copy-start.11
  100.7 1.0 copy-start.13
  142.9 5.9 %collective-permute-start.16 = (f32[130,128]{1,0:T(8,128)S(1)}, f32[130,128]{1,0:T(8,128)S(1)}, u32[]{:S(2)}, u32[]{:S(2)}) collective-permute-start(f32[130,128]{1,0:T(8,128)S(1)} %pad_maximum_fusion.4), channel_id=1, source_target_pairs={{0,2},{1,3},{2,0},{3,1},{4,6},{5,7},{6,4},{7,5},{8,10},{9,11},{10,... | collective-permute-start | bytes 199688 | tf_op jit(solution)/shard_map/ppermute | solution.py:43
  145.0 5.3 %collective-permute-start.17 = (f32[130,128]{1,0:T(8,128)S(1)}, f32[130,128]{1,0:T(8,128)S(1)}, u32[]{:S(2)}, u32[]{:S(2)}) collective-permute-start(f32[130,128]{1,0:T(8,128)S(1)} %pad_maximum_fusion.4), channel_id=1, source_target_pairs={{0,3},{1,2},{2,1},{3,0},{4,7},{5,6},{6,5},{7,4},{8,11},{9,10},{10,... | collective-permute-start | bytes 199688 | tf_op jit(solution)/shard_map/ppermute | solution.py:43
  145.0 5.3 %collective-permute-start.15 = (f32[130,128]{1,0:T(8,128)S(1)}, f32[130,128]{1,0:T(8,128)S(1)}, u32[]{:S(2)}, u32[]{:S(2)}) collective-permute-start(f32[130,128]{1,0:T(8,128)S(1)} %pad_maximum_fusion.4), channel_id=1, source_target_pairs={{0,1},{1,0},{2,3},{3,2},{4,5},{5,4},{6,7},{7,6},{8,9},{9,8},{10,11... | collective-permute-start | bytes 199688 | tf_op jit(solution)/shard_map/ppermute | solution.py:43

commit v3 on v2

--- a/solution.py
+++ b/solution.py
@@ -145,7 +145,9 @@
     out_ref,
     wk_ref,
     wv_ref,
+    parts_ref,
     query_ref,
+    sem,
 ):
     x_refs = [x0_ref, x1_ref, x2_ref, x3_ref]
     _, slots, width = x0_ref.shape
@@ -158,27 +160,33 @@
     @pl.when(seq == 0)
     def _():
         low = Z // 2
-        for step, parts in enumerate(
-            [
-                [own_ref.at[:low], own_ref.at[low:]],
-                [up_ref.at[:low], up_ref.at[low:]],
-                [far_low_ref, far_high_ref],
-                [down_ref.at[:low], down_ref.at[low:]],
-            ]
+        copies = []
+
+        def start(source, target):
+            copy = pltpu.make_async_copy(source, target, sem.at[len(copies)])
+            copy.start()
+            copies.append(copy)
+
+        tail = pl.ds(Y * XLO * rows, parts_ref.shape[1])
+        start(last_ref.at[:, tail, :], parts_ref)
+        for step, halves in enumerate(
+            [[own_ref], [up_ref], [far_low_ref, far_high_ref], [down_ref]]
         ):
-            base = ((y_at + step) & (Y - 1)) * width
+            y = (y_at + step) & (Y - 1)
             for x in range(XLO):
-                half = base + (x_lo_at ^ x) * (Z * rows)
-                for z in range(Z):
-                    at = pl.ds(pl.multiple_of(half + z * rows, rows), rows)
-                    block = slice(x * rows, (x + 1) * rows)
-                    piece = parts[z // low].at[z % low]
-                    wk_ref[at, :] = piece[block, : 2 * HEAD_DIM]
-                    wv_ref[at, :HEAD_DIM] = piece[block, 2 * HEAD_DIM :]
-                    start = (step * XLO + x) * rows
-                    wv_ref[at, HEAD_DIM:] = last_ref[z, start : start + rows, :]
-        parts = last_ref[:, Y * XLO * rows :, :].astype(jnp.float32)
-        parts = jnp.sum(parts, axis=0)
+                block = pl.ds(x * rows, rows)
+                for half, piece in enumerate(halves):
+                    zs = pl.ds(half * low, piece.shape[0])
+                    wk_at = wk_ref.at[y, x_lo_at ^ x, zs]
+                    start(piece.at[:, block, pl.ds(0, 2 * HEAD_DIM)], wk_at)
+                    wv_at = wv_ref.at[y, x_lo_at ^ x, zs, :, pl.ds(0, HEAD_DIM)]
+                    start(piece.at[:, block, pl.ds(2 * HEAD_DIM, HEAD_DIM)], wv_at)
+                block = pl.ds((step * XLO + x) * rows, rows)
+                wv_at = wv_ref.at[y, x_lo_at ^ x, :, :, pl.ds(HEAD_DIM, HEAD_DIM)]
+                start(last_ref.at[:, block, :], wv_at)
+        for copy in copies:
+            copy.wait()
+        parts = jnp.sum(parts_ref[...].astype(jnp.float32), axis=0)
         query_ref[...] = parts + pltpu.roll(parts, parts.shape[0] - 4, 0)
 
     squares = None
@@ -193,8 +201,10 @@
         slice_at = tensor_at ^ k
         at = pl.ds(pl.multiple_of(slice_at * width, width), width)
         normed = (x * scale * gain_ref[:, at]).astype(jnp.bfloat16)
-        kp = jnp.dot(normed, wk_ref[at, :], preferred_element_type=jnp.float32)
-        vp = jnp.dot(normed, wv_ref[at, :], preferred_element_type=jnp.float32)
+        wk = wk_ref[slice_at].reshape(width, -1)
+        wv = wv_ref[slice_at].reshape(width, -1)
+        kp = jnp.dot(normed, wk, preferred_element_type=jnp.float32)
+        vp = jnp.dot(normed, wv, preferred_element_type=jnp.float32)
         key_proj = kp if key_proj is None else key_proj + kp
         value_proj = vp if value_proj is None else value_proj + vp
     query = query_ref[pl.ds(seq, heads, stride=8), :]
@@ -270,15 +280,23 @@
     seq_count, slots, width = slices[0].shape
     model_width = gains.size
     kv_width = 2 * HEAD_DIM
+    rows = model_width // (Y * XLO * Z)
     x_spec = pl.BlockSpec((1, slots, width), lambda seq: (seq, 0, 0))
     return pl.pallas_call(
         kv_attend_kernel,
         grid=(seq_count,),
-        in_specs=[SMEM, SMEM] + [x_spec] * len(slices) + [VMEM] * (len(pieces) + 4),
+        in_specs=[SMEM, SMEM]
+        + [x_spec] * len(slices)
+        + [pl.BlockSpec(memory_space=pltpu.HBM)] * (len(pieces) + 1)
+        + [VMEM] * 3,
         out_specs=pl.BlockSpec((1, heads, HEAD_DIM), lambda seq: (seq, 0, 0)),
         out_shape=jax.ShapeDtypeStruct((seq_count, heads, HEAD_DIM), jnp.float32),
-        scratch_shapes=[pltpu.VMEM((model_width, kv_width), jnp.bfloat16)] * 2
-        + [pltpu.VMEM((heads * 8, HEAD_DIM), jnp.float32)],
+        scratch_shapes=[pltpu.VMEM((Y, XLO, Z, rows, kv_width), jnp.bfloat16)] * 2
+        + [
+            pltpu.VMEM((Z, heads * 8, HEAD_DIM), jnp.bfloat16),
+            pltpu.VMEM((heads * 8, HEAD_DIM), jnp.float32),
+            pltpu.SemaphoreType.DMA((1 + XLO * (3 * Y + 2),)),
+        ],
         compiler_params=pltpu.CompilerParams(vmem_limit_bytes=40 * 1024 * 1024),
         cost_estimate=pl.CostEstimate(
             flops=4 * seq_count * slots * model_width * kv_width,
@@ -317,28 +335,34 @@
 
     block = kv_both[:, : kv_width + HEAD_DIM]
     rows = last_rows_call(at, last_raw, gains)
+    rows, _ = lax.optimization_barrier((rows, query_other))
     z_all = exchange(
         jnp.concatenate([jnp.broadcast_to(block[None], (Z,) + block.shape), rows], axis=1),
         Z_GROUPS,
     )
-    z_own = z_all[:, : block.shape[0]]
+
+    rest = jnp.concatenate(
+        [kv_both[:, kv_width + HEAD_DIM :], jnp.concatenate([query_weight, query_other])], axis=1
+    )
+    rest = [rest] + [shift(rest, dy=-step) for step in range(1, Y)]
+    partial_q = query_call(z_all, rest)
+    head = jnp.concatenate([array[:, :HEAD_DIM] for array in rest])
+
+    z_own = lax.optimization_barrier((z_all[:, : block.shape[0]], *rest))[0]
     z_up = shift(z_own, dy=-1)
     z_down = shift(z_own, dy=1)
     far_low = shift(z_up[: Z // 2], dy=-1)
     far_high = shift(z_down[Z // 2 :], dy=1)
     pieces = [z_own, z_up, z_down, far_low, far_high]
 
-    rest = jnp.concatenate(
-        [kv_both[:, kv_width + HEAD_DIM :], jnp.concatenate([query_weight, query_other])], axis=1
-    )
-    rest = [rest] + [shift(rest, dy=-step) for step in range(1, Y)]
-    partial_q = query_call(z_all, rest)
-    head = jnp.concatenate([array[:, :HEAD_DIM] for array in rest])
+    corner = swap_tensor(z_own[:, :16, :HEAD_DIM], 1)
     last = exchange(
-        jnp.concatenate([jnp.broadcast_to(head[None], (Z,) + head.shape), partial_q], axis=1),
+        jnp.concatenate(
+            [jnp.broadcast_to(head[None], (Z,) + head.shape), partial_q, corner], axis=1
+        ),
         Z_GROUPS,
     )
-    far_peer = swap_tensor(lax.optimization_barrier((far, last, *pieces))[0], 1)
+    far_peer = swap_tensor(lax.optimization_barrier((far, z_up, z_down))[0], 1)
 
     mixed = kv_attend(
         at,

time: 156 us -> 152 us (0.974)
  waiting for transfers between devices: 48.8 us -> 43 us
  blocking collectives: 28.9 us -> 24.3 us
  starting transfers between devices: 36.6 us -> 38.8 us
  local copies, waits for them, and re-layouts: 13.8 us -> 15.6 us
    ppermute x7, waiting for transfers between devices: 32.1 us -> 7.46 us  [shift(): return lax.ppermute(array, ('dp', 'tensor'), pairs)]
    all_to_all x2, waiting for transfers between devices: 2.03 us -> 21.8 us  [exchange(): lax.all_to_all(chunks, 'dp', split_axis=0, concat_axis=0, tiled=True, axi...]
    all_to_all x1, blocking collectives: 28.9 us -> 24.3 us  [exchange(): lax.all_to_all(chunks, 'dp', split_axis=0, concat_axis=0, tiled=True, axi...]
    ppermute x2, waiting for transfers between devices: 4.37 us -> 0.44 us  [swap_x_lo(): return lax.ppermute(array, 'dp', pairs)]
    unnamed x56 -> x44, local copies, waits for them, and re-layouts: 10.2 us -> 7.11 us
    ppermute x9 -> x10, waiting for transfers between devices: 10.3 us -> 13.4 us  [swap_tensor(): return lax.ppermute(array, 'tensor', [(i, i ^ mask) for i in range(size)])]
    ppermute x9 -> x10, starting transfers between devices: 7.86 us -> 10.3 us  [swap_tensor(): return lax.ppermute(array, 'tensor', [(i, i ^ mask) for i in range(size)])]
    slice x3, local copies, waits for them, and re-layouts: 0.01 us -> 2.28 us  [body(): head = jnp.concatenate([array[:, :HEAD_DIM] for array in rest])]
  transfers between devices with their start and end apart: 20 -> 21, of which waited for: 10 -> 9; matrix products, arithmetic and copies ran while one was open for 3% -> 7% of each run, Pallas kernels for 3% -> 3%
where the time goes in v3:
time: 152 us; the launch traced here: 151 us
  waiting for transfers between devices  43 us (28%)
  starting transfers between devices  38.8 us (26%)
  blocking collectives  24.3 us (16%)
  Pallas kernels  18.1 us (12%)
  local copies, waits for them, and re-layouts  15.6 us (10%)
  other arithmetic  7.74 us (5%)
  between operations  2.71 us (2%)
    all_to_all x1, blocking collectives, exchange(): lax.all_to_all(chunks, 'dp', split_axis=0, concat_axis=0, tiled=True, axi...  24.3 us
    all_to_all x2, waiting for transfers between devices, exchange(): lax.all_to_all(chunks, 'dp', split_axis=0, concat_axis=0, tiled=True, axi...  21.8 us
    all_to_all x2, starting transfers between devices, exchange(): lax.all_to_all(chunks, 'dp', split_axis=0, concat_axis=0, tiled=True, axi...  13.6 us
    ppermute x10, waiting for transfers between devices, swap_tensor(): return lax.ppermute(array, 'tensor', [(i, i ^ mask) for i in range(size)])  13.4 us
    ppermute x7, starting transfers between devices, shift(): return lax.ppermute(array, ('dp', 'tensor'), pairs)  12.8 us
    pallas_call x1, Pallas kernels, kv_attend(): pl.pallas_call(kv_attend_kernel, grid=(seq_count,), in_specs=[SMEM, SMEM]...  11.9 us
    ppermute x10, starting transfers between devices, swap_tensor(): return lax.ppermute(array, 'tensor', [(i, i ^ mask) for i in range(size)])  10.3 us
    ppermute x7, waiting for transfers between devices, shift(): return lax.ppermute(array, ('dp', 'tensor'), pairs)  7.46 us
  transfers between devices with their start and end apart: 21, of which 9 were waited for; matrix products, arithmetic and copies ran while one was open for 7% of the time, Pallas kernels for 3%

profile of v3, /device:TPU:32, one launch (start us, length us, event | category | flops | bytes accessed | tf_op | source)
XLA Modules:
  0.0 150.6 jit_solution(4893940617694547219)
XLA Ops:
  0.7 2.3 %shard_map.103.r0 = bf16[4,1024]{1,0:T(4,128)(2,1)} custom-call(s32[2,2]{1,0:T(2,128)} %len_ref.3, bf16[4,256,1024]{2,1,0:T(8,128)(2,1)} %bitcast.25), custom_call_target="tpu_custom_call" | custom-call | tf_op jit(solution)/shard_map/pallas_call | solution.py:238
  3.0 2.5 %collective-permute-start.4 = (bf16[4,1024]{1,0:T(4,128)(2,1)}, bf16[4,1024]{1,0:T(4,128)(2,1)S(1)}, u32[]{:S(2)}, u32[]{:S(2)}) collective-permute-start(bf16[4,1024]{1,0:T(4,128)(2,1)} %shard_map.103.r0), channel_id=1, source_target_pairs={{0,3},{1,2},{2,1},{3,0},{4,7},{5,6},{6,5},{7,4},{8,11},{9,10},{10,... | collective-permute-start | bytes 24584 | tf_op jit(solution)/shard_map/ppermute | solution.py:43
  5.5 0.7 collective-permute-start.3
  6.2 0.2 collective-permute-start.2
  6.4 1.6 %collective-permute-start = (bf16[64,512]{1,0:T(8,128)(2,1)S(1)}, bf16[64,512]{1,0:T(8,128)(2,1)S(1)}, u32[]{:S(2)}, u32[]{:S(2)}) collective-permute-start(bf16[64,512]{1,0:T(8,128)(2,1)S(1)} %constant_dynamic-update-slice_fusion), channel_id=1, source_target_pairs={{0,32},{4,36},{8,40},{12,44},{16,48},{20,52},{24,56},{28,60},{32,0... | collective-permute-start | bytes 196616 | tf_op jit(solution)/shard_map/ppermute | solution.py:48
  8.0 0.5 collective-permute-start.1
  8.5 0.6 pad_add_fusion.at_ref
  9.1 1.7 %collective-permute-done.3.r2 = bf16[4,1024]{1,0:T(4,128)(2,1)S(1)} collective-permute-done((bf16[4,1024]{1,0:T(4,128)(2,1)}, bf16[4,1024]{1,0:T(4,128)(2,1)S(1)}, u32[]{:S(2)}, u32[]{:S(2)}) %collective-permute-start.3) | collective-permute-done | bytes 8224 | tf_op jit(solution)/shard_map/ppermute | solution.py:43
  10.9 0.6 copy-done.19
  11.5 1.7 %shard_map.104 = bf16[8,16,384]{2,1,0:T(8,128)(2,1)} custom-call(s32[3]{0:T(128)} %pad_add_fusion.at_ref, bf16[4,1024]{1,0:T(4,128)(2,1)} %shard_map.103.r0, bf16[4,1024]{1,0:T(4,128)(2,1)} %copy-done.20, bf16[4,1024]{1,0:T(4,128)(2,1)} %copy-done.19, bf16[4,1024]{1,0:T(4,128)(2,1)} %copy-done.18, f32[1,4096]{1,0:T(1,128)} %bitcast.29), custom_call_target="tpu_custom_call" | custom-call | tf_op jit(solution)/shard_map/pallas_call | solution.py:253
  13.2 0.4 collective-permute-done.1
  13.7 2.0 %pad_maximum_fusion.1 = bf16[8,144,384]{2,1,0:T(8,128)(2,1)} fusion(bf16[8,16,384]{2,1,0:T(8,128)(2,1)} %shard_map.104, bf16[8,128,384]{2,1,0:T(8,128)(2,1)S(1)} %broadcast_in_dim.15), kind=kLoop, calls=%fused_computation.2 | loop fusion | flops 1769472 | bytes 1769472 | tf_op jit(solution)/shard_map/concatenate | solution.py:340
  15.7 8.6 %all-to-all-start = ((bf16[8,144,384]{2,1,0:T(8,128)(2,1)}), bf16[8,144,384]{2,1,0:T(8,128)(2,1)S(1)}, u32[]{:S(2)}, u32[]{:S(2)}) async-start(bf16[8,144,384]{2,1,0:T(8,128)(2,1)} %pad_maximum_fusion.1), calls=%async_computation | async-start | bytes 1769472 | tf_op jit(solution)/shard_map/all_to_all | solution.py:52
  24.3 2.9 %collective-permute-start.6 = (bf16[4,256,1024]{2,1,0:T(8,128)(2,1)S(1)}, bf16[4,256,1024]{2,1,0:T(8,128)(2,1)}, u32[]{:S(2)}, u32[]{:S(2)}) collective-permute-start(bf16[4,256,1024]{2,1,0:T(8,128)(2,1)S(1)} %bitcast.26), channel_id=1, source_target_pairs={{0,2},{1,3},{2,0},{3,1},{4,6},{5,7},{6,4},{7,5},{8,10},{9,11},{10,... | collective-permute-start | bytes 6291464 | tf_op jit(solution)/shard_map/ppermute | solution.py:43
  27.2 0.9 maximum_maximum_fusion.w0
  28.1 1.7 %collective-permute-start.9 = (bf16[128,1152]{1,0:T(8,128)(2,1)S(1)}, bf16[128,1152]{1,0:T(8,128)(2,1)}, u32[]{:S(2)}, u32[]{:S(2)}) collective-permute-start(bf16[128,1152]{1,0:T(8,128)(2,1)S(1)} %maximum_maximum_fusion.w0), channel_id=1, source_target_pairs={{0,64},{1,65},{4,68},{5,69},{8,72},{9,73},{12,76},{13,77},{16,80},... | collective-permute-start | bytes 884744 | tf_op jit(solution)/shard_map/ppermute | solution.py:38
  29.8 2.9 %collective-permute-start.8 = (bf16[128,1152]{1,0:T(8,128)(2,1)S(1)}, bf16[128,1152]{1,0:T(8,128)(2,1)}, u32[]{:S(2)}, u32[]{:S(2)}) collective-permute-start(bf16[128,1152]{1,0:T(8,128)(2,1)S(1)} %maximum_maximum_fusion.w0), channel_id=1, source_target_pairs={{0,128},{1,129},{4,132},{5,133},{8,136},{9,137},{12,140},{13,141},... | collective-permute-start | bytes 884744 | tf_op jit(solution)/shard_map/ppermute | solution.py:38
  32.7 1.3 collective-permute-start.7
  34.0 13.5 %all-to-all-done.rows_ref = bf16[8,144,384]{2,1,0:T(8,128)(2,1)S(1)} async-done(((bf16[8,144,384]{2,1,0:T(8,128)(2,1)}), bf16[8,144,384]{2,1,0:T(8,128)(2,1)S(1)}, u32[]{:S(2)}, u32[]{:S(2)}) %all-to-all-start) | async-done | bytes 884768 | tf_op jit(solution)/shard_map/all_to_all | solution.py:52
  47.6 1.2 slice.62.own_ref
  48.8 1.7 %collective-permute-start.11 = (bf16[8,128,384]{2,1,0:T(8,128)(2,1)}, bf16[8,128,384]{2,1,0:T(8,128)(2,1)}, u32[]{:S(2)}, u32[]{:S(2)}) collective-permute-start(bf16[8,128,384]{2,1,0:T(8,128)(2,1)} %slice.62.own_ref), channel_id=1, source_target_pairs={{0,64},{1,65},{4,68},{5,69},{8,72},{9,73},{12,76},{13,77},{16,80},... | collective-permute-start | bytes 2359304 | tf_op jit(solution)/shard_map/ppermute | solution.py:38
  50.4 1.7 %collective-permute-start.10 = (bf16[8,128,384]{2,1,0:T(8,128)(2,1)}, bf16[8,128,384]{2,1,0:T(8,128)(2,1)}, u32[]{:S(2)}, u32[]{:S(2)}) collective-permute-start(bf16[8,128,384]{2,1,0:T(8,128)(2,1)} %slice.62.own_ref), channel_id=1, source_target_pairs={{0,192},{1,193},{4,196},{5,197},{8,200},{9,201},{12,204},{13,205},... | collective-permute-start | bytes 2359304 | tf_op jit(solution)/shard_map/ppermute | solution.py:38
  52.1 0.8 slice.69
  52.9 0.8 slice.68
  53.6 0.8 slice.67
  54.4 0.8 slice.53
  55.2 2.3 %shard_map.105 = bf16[8,64,128]{2,1,0:T(8,128)(2,1)} custom-call(bf16[8,144,384]{2,1,0:T(8,128)(2,1)} %copy-done.12, bf16[128,1152]{1,0:T(8,128)(2,1)} %copy-done.13, bf16[128,1152]{1,0:T(8,128)(2,1)} %collective-permute-done.7.w1, bf16[128,1152]{1,0:T(8,128)(2,1)} %collective-permute-done.8.w2, bf16[128,1152]{1,0:T(8,128)(2,1)} %collective-permute-done.9.w3), custom_call_target="tpu_custom_call" | custom-call | tf_op jit(solution)/shard_map/pallas_call | solution.py:268
  57.5 0.1 broadcast_in_dim.17
  57.6 2.0 %pad_maximum_fusion = bf16[8,592,128]{2,1,0:T(8,128)(2,1)} fusion(bf16[8,16,128]{2,1,0:T(8,128)(2,1)S(1)} %collective-permute-done.15, bf16[8,64,128]{2,1,0:T(8,128)(2,1)} %shard_map.105, bf16[8,512,128]{2,1,0:T(8,128)(2,1)S(1)} %broadcast_in_dim.17), kind=kLoop, calls=%fused_computation | loop fusion | flops 3637248 | bytes 2424832 | tf_op jit(solution)/shard_map/concatenate | solution.py:360
  59.6 5.1 %all-to-all-start.1 = ((bf16[8,592,128]{2,1,0:T(8,128)(2,1)}), bf16[8,592,128]{2,1,0:T(8,128)(2,1)S(1)}, u32[]{:S(2)}, u32[]{:S(2)}) async-start(bf16[8,592,128]{2,1,0:T(8,128)(2,1)} %pad_maximum_fusion), calls=%async_computation.1 | async-start | bytes 2424832 | tf_op jit(solution)/shard_map/all_to_all | solution.py:52
  64.7 0.2 collective-permute-start.5
  64.9 7.3 %collective-permute-done.6.x2_ref = bf16[4,256,1024]{2,1,0:T(8,128)(2,1)} collective-permute-done((bf16[4,256,1024]{2,1,0:T(8,128)(2,1)S(1)}, bf16[4,256,1024]{2,1,0:T(8,128)(2,1)}, u32[]{:S(2)}, u32[]{:S(2)}) %collective-permute-start.6) | collective-permute-done | bytes 2097184 | tf_op jit(solution)/shard_map/ppermute | solution.py:43
  72.3 1.0 slice.66
  73.3 1.7 %collective-permute-start.14 = (bf16[4,128,384]{2,1,0:T(8,128)(2,1)S(1)}, bf16[4,128,384]{2,1,0:T(8,128)(2,1)S(1)}, u32[]{:S(2)}, u32[]{:S(2)}) collective-permute-start(bf16[4,128,384]{2,1,0:T(8,128)(2,1)S(1)} %slice.66), channel_id=1, source_target_pairs={{0,64},{1,65},{4,68},{5,69},{8,72},{9,73},{12,76},{13,77},{16,80},... | collective-permute-start | bytes 1179656 | tf_op jit(solution)/shard_map/ppermute | solution.py:38
  74.9 1.0 slice.65
  76.0 1.9 %collective-permute-start.13 = (bf16[4,128,384]{2,1,0:T(8,128)(2,1)S(1)}, bf16[4,128,384]{2,1,0:T(8,128)(2,1)S(1)}, u32[]{:S(2)}, u32[]{:S(2)}) collective-permute-start(bf16[4,128,384]{2,1,0:T(8,128)(2,1)S(1)} %slice.65), channel_id=1, source_target_pairs={{0,192},{1,193},{4,196},{5,197},{8,200},{9,201},{12,204},{13,205},... | collective-permute-start | bytes 1179656 | tf_op jit(solution)/shard_map/ppermute | solution.py:38
  77.9 1.4 copy-done.4
  79.3 6.9 %collective-permute-done.14.far_high_ref = bf16[4,128,384]{2,1,0:T(8,128)(2,1)S(1)} collective-permute-done((bf16[4,128,384]{2,1,0:T(8,128)(2,1)S(1)}, bf16[4,128,384]{2,1,0:T(8,128)(2,1)S(1)}, u32[]{:S(2)}, u32[]{:S(2)}) %collective-permute-start.14) | collective-permute-done | bytes 393248 | tf_op jit(solution)/shard_map/ppermute | solution.py:38
  86.2 0.8 copy-done.6
  86.9 0.6 collective-permute-done.13.far_low_ref
  87.5 0.8 copy-done.8
  88.2 8.2 %all-to-all-done.1.last_ref = bf16[8,592,128]{2,1,0:T(8,128)(2,1)S(1)} async-done(((bf16[8,592,128]{2,1,0:T(8,128)(2,1)}), bf16[8,592,128]{2,1,0:T(8,128)(2,1)S(1)}, u32[]{:S(2)}, u32[]{:S(2)}) %all-to-all-start.1) | async-done | bytes 1212448 | tf_op jit(solution)/shard_map/all_to_all | solution.py:52
  96.5 1.6 %copy-done.5 = bf16[4,256,1024]{2,1,0:T(8,128)(2,1)S(1)} copy-done((bf16[4,256,1024]{2,1,0:T(8,128)(2,1)S(1)}, bf16[4,256,1024]{2,1,0:T(8,128)(2,1)}, u32[]{:S(2)}) %copy-start.5) | copy-done | bytes 2097176
  98.1 1.0 copy-done.7
  99.1 1.0 copy-done.9
  100.1 11.9 %shard_map.106 = f32[4,8,128]{2,1,0:T(8,128)S(1)} custom-call(s32[3]{0:T(128)S(1)} %copy-done.2, s32[2,2]{1,0:T(2,128)S(1)} %copy-done.3, bf16[4,256,1024]{2,1,0:T(8,128)(2,1)S(1)} %bitcast.28, bf16[4,256,1024]{2,1,0:T(8,128)(2,1)S(1)} %copy-done.5, bf16[4,256,1024]{2,1,0:T(8,128)(2,1)} %collective-permute-done.6.x2_ref, ...), custom_call_target="tpu_custom_call" | custom-call | flops 4294967296 | bytes 12582912 | tf_op jit(solution)/shard_map/pallas_call | solution.py:285
  112.0 0.1 broadcast_in_dim.39
  112.1 24.3 %all_to_all.15 = bf16[64,4,1024]{2,1,0:T(4,128)(2,1)S(1)} all-to-all(bf16[64,4,1024]{2,1,0:T(4,128)(2,1)S(1)} %broadcast_in_dim.39), channel_id=1, replica_groups=mesh['dp'=64,'tensor'=4] {'dp'}, dimensions={0} | all-to-all | bytes 1048576 | tf_op jit(solution)/shard_map/all_to_all | solution.py:52
  136.4 0.3 multiply_reduce_fusion
  136.9 0.2 reshape.35
  137.1 0.7 fusion.12
  137.8 0.3 fusion
  138.1 2.8 %collective-permute-start.17 = (f32[130,128]{1,0:T(8,128)S(1)}, f32[130,128]{1,0:T(8,128)S(1)}, u32[]{:S(2)}, u32[]{:S(2)}) collective-permute-start(f32[130,128]{1,0:T(8,128)S(1)} %pad_maximum_fusion.4), channel_id=1, source_target_pairs={{0,2},{1,3},{2,0},{3,1},{4,6},{5,7},{6,4},{7,5},{8,10},{9,11},{10,... | collective-permute-start | bytes 199688 | tf_op jit(solution)/shard_map/ppermute | solution.py:43
  141.0 0.9 collective-permute-start.16
  141.9 2.2 %collective-permute-done.17 = f32[130,128]{1,0:T(8,128)S(1)} collective-permute-done((f32[130,128]{1,0:T(8,128)S(1)}, f32[130,128]{1,0:T(8,128)S(1)}, u32[]{:S(2)}, u32[]{:S(2)}) %collective-permute-start.17) | collective-permute-done | bytes 66592 | tf_op jit(solution)/shard_map/ppermute | solution.py:43
  144.0 2.2 %collective-permute-done.18 = f32[130,128]{1,0:T(8,128)S(1)} collective-permute-done((f32[130,128]{1,0:T(8,128)S(1)}, f32[130,128]{1,0:T(8,128)S(1)}, u32[]{:S(2)}, u32[]{:S(2)}) %collective-permute-start.18) | collective-permute-done | bytes 66592 | tf_op jit(solution)/shard_map/ppermute | solution.py:43
  146.2 0.1 dynamic-slice_bitcast_fusion
  146.3 0.1 copy.15
  146.4 0.2 fusion.10
  146.6 0.2 exponential_reduce_fusion.1
  146.8 0.1 exponential_reduce_fusion
  146.9 0.6 fusion.11
  147.5 0.6 dynamic_slice.7
  148.1 0.7 multiply_convert_fusion
  (67 shorter events, 0.4 us)
Async XLA Ops:
  0.6 5.8 %copy-start.16 = (bf16[64,256]{1,0:T(8,128)(2,1)S(1)}, bf16[64,256]{1,0:T(8,128)(2,1)}, u32[]{:S(2)}) copy-start(bf16[64,256]{1,0:T(8,128)(2,1)} %param.14) | copy-start | bytes 98308
  0.6 5.8 %copy-start.17 = (bf16[64,256]{1,0:T(8,128)(2,1)S(1)}, bf16[64,256]{1,0:T(8,128)(2,1)}, u32[]{:S(2)}) copy-start(bf16[64,256]{1,0:T(8,128)(2,1)} %param.15) | copy-start | bytes 98308
  0.7 7.4 %copy-start.14 = (bf16[64,1024]{1,0:T(8,128)(2,1)S(1)}, bf16[64,1024]{1,0:T(8,128)(2,1)}, u32[]{:S(2)}) copy-start(bf16[64,1024]{1,0:T(8,128)(2,1)} %param.13) | copy-start | bytes 393220
  3.0 6.2 %collective-permute-start.4 = (bf16[4,1024]{1,0:T(4,128)(2,1)}, bf16[4,1024]{1,0:T(4,128)(2,1)S(1)}, u32[]{:S(2)}, u32[]{:S(2)}) collective-permute-start(bf16[4,1024]{1,0:T(4,128)(2,1)} %shard_map.103.r0), channel_id=1, source_target_pairs={{0,3},{1,2},{2,1},{3,0},{4,7},{5,6},{6,5},{7,4},{8,11},{9,10},{10,... | collective-permute-start | bytes 24584 | tf_op jit(solution)/shard_map/ppermute | solution.py:43
  5.5 5.4 %collective-permute-start.3 = (bf16[4,1024]{1,0:T(4,128)(2,1)}, bf16[4,1024]{1,0:T(4,128)(2,1)S(1)}, u32[]{:S(2)}, u32[]{:S(2)}) collective-permute-start(bf16[4,1024]{1,0:T(4,128)(2,1)} %shard_map.103.r0), channel_id=1, source_target_pairs={{0,2},{1,3},{2,0},{3,1},{4,6},{5,7},{6,4},{7,5},{8,10},{9,11},{10,... | collective-permute-start | bytes 24584 | tf_op jit(solution)/shard_map/ppermute | solution.py:43
  6.2 4.7 %collective-permute-start.2 = (bf16[4,1024]{1,0:T(4,128)(2,1)}, bf16[4,1024]{1,0:T(4,128)(2,1)S(1)}, u32[]{:S(2)}, u32[]{:S(2)}) collective-permute-start(bf16[4,1024]{1,0:T(4,128)(2,1)} %shard_map.103.r0), channel_id=1, source_target_pairs={{0,1},{1,0},{2,3},{3,2},{4,5},{5,4},{6,7},{7,6},{8,9},{9,8},{10,11... | collective-permute-start | bytes 24584 | tf_op jit(solution)/shard_map/ppermute | solution.py:43
  6.4 6.7 %collective-permute-start = (bf16[64,512]{1,0:T(8,128)(2,1)S(1)}, bf16[64,512]{1,0:T(8,128)(2,1)S(1)}, u32[]{:S(2)}, u32[]{:S(2)}) collective-permute-start(bf16[64,512]{1,0:T(8,128)(2,1)S(1)} %constant_dynamic-update-slice_fusion), channel_id=1, source_target_pairs={{0,32},{4,36},{8,40},{12,44},{16,48},{20,52},{24,56},{28,60},{32,0... | collective-permute-start | bytes 196616 | tf_op jit(solution)/shard_map/ppermute | solution.py:48
  8.0 5.6 %collective-permute-start.1 = (bf16[64,1024]{1,0:T(8,128)(2,1)S(1)}, bf16[64,1024]{1,0:T(8,128)(2,1)S(1)}, u32[]{:S(2)}, u32[]{:S(2)}) collective-permute-start(bf16[64,1024]{1,0:T(8,128)(2,1)S(1)} %copy-done.14), channel_id=1, source_target_pairs={{0,32},{4,36},{8,40},{12,44},{16,48},{20,52},{24,56},{28,60},{32,0... | collective-permute-start | bytes 393224 | tf_op jit(solution)/shard_map/ppermute | solution.py:48
  9.1 1.7 %copy-start.18 = (bf16[4,1024]{1,0:T(4,128)(2,1)}, bf16[4,1024]{1,0:T(4,128)(2,1)S(1)}, u32[]{:S(2)}) copy-start(bf16[4,1024]{1,0:T(4,128)(2,1)S(1)} %collective-permute-done.4.r3) | copy-start | bytes 24580
  10.9 0.6 copy-start.19
  10.9 0.6 copy-start.20
  13.1 11.1 %copy-start = (bf16[2,2,256,1024]{3,2,1,0:T(8,128)(2,1)S(1)}, bf16[2,2,256,1024]{3,2,1,0:T(8,128)(2,1)}, u32[]{:S(2)}) copy-start(bf16[2,2,256,1024]{3,2,1,0:T(8,128)(2,1)} %param.8) | copy-start | bytes 6291460
  13.6 13.6 %copy-start.15 = (bf16[64,1024]{1,0:T(8,128)(2,1)}, bf16[64,1024]{1,0:T(8,128)(2,1)S(1)}, u32[]{:S(2)}) copy-start(bf16[64,1024]{1,0:T(8,128)(2,1)S(1)} %collective-permute-done.1) | copy-start | bytes 393220
  15.7 31.9 %all-to-all-start = ((bf16[8,144,384]{2,1,0:T(8,128)(2,1)}), bf16[8,144,384]{2,1,0:T(8,128)(2,1)S(1)}, u32[]{:S(2)}, u32[]{:S(2)}) async-start(bf16[8,144,384]{2,1,0:T(8,128)(2,1)} %pad_maximum_fusion.1), calls=%async_computation | async-start | bytes 1769472 | tf_op jit(solution)/shard_map/all_to_all | solution.py:52
  24.3 47.9 %collective-permute-start.6 = (bf16[4,256,1024]{2,1,0:T(8,128)(2,1)S(1)}, bf16[4,256,1024]{2,1,0:T(8,128)(2,1)}, u32[]{:S(2)}, u32[]{:S(2)}) collective-permute-start(bf16[4,256,1024]{2,1,0:T(8,128)(2,1)S(1)} %bitcast.26), channel_id=1, source_target_pairs={{0,2},{1,3},{2,0},{3,1},{4,6},{5,7},{6,4},{7,5},{8,10},{9,11},{10,... | collective-permute-start | bytes 6291464 | tf_op jit(solution)/shard_map/ppermute | solution.py:43
  28.1 27.1 %copy-start.13 = (bf16[128,1152]{1,0:T(8,128)(2,1)}, bf16[128,1152]{1,0:T(8,128)(2,1)S(1)}, u32[]{:S(2)}) copy-start(bf16[128,1152]{1,0:T(8,128)(2,1)S(1)} %maximum_maximum_fusion.w0) | copy-start | bytes 884740
  28.1 20.7 %collective-permute-start.9 = (bf16[128,1152]{1,0:T(8,128)(2,1)S(1)}, bf16[128,1152]{1,0:T(8,128)(2,1)}, u32[]{:S(2)}, u32[]{:S(2)}) collective-permute-start(bf16[128,1152]{1,0:T(8,128)(2,1)S(1)} %maximum_maximum_fusion.w0), channel_id=1, source_target_pairs={{0,64},{1,65},{4,68},{5,69},{8,72},{9,73},{12,76},{13,77},{16,80},... | collective-permute-start | bytes 884744 | tf_op jit(solution)/shard_map/ppermute | solution.py:38
  29.8 19.0 %collective-permute-start.8 = (bf16[128,1152]{1,0:T(8,128)(2,1)S(1)}, bf16[128,1152]{1,0:T(8,128)(2,1)}, u32[]{:S(2)}, u32[]{:S(2)}) collective-permute-start(bf16[128,1152]{1,0:T(8,128)(2,1)S(1)} %maximum_maximum_fusion.w0), channel_id=1, source_target_pairs={{0,128},{1,129},{4,132},{5,133},{8,136},{9,137},{12,140},{13,141},... | collective-permute-start | bytes 884744 | tf_op jit(solution)/shard_map/ppermute | solution.py:38
  32.7 16.1 %collective-permute-start.7 = (bf16[128,1152]{1,0:T(8,128)(2,1)S(1)}, bf16[128,1152]{1,0:T(8,128)(2,1)}, u32[]{:S(2)}, u32[]{:S(2)}) collective-permute-start(bf16[128,1152]{1,0:T(8,128)(2,1)S(1)} %maximum_maximum_fusion.w0), channel_id=1, source_target_pairs={{0,192},{1,193},{4,196},{5,197},{8,200},{9,201},{12,204},{13,205},... | collective-permute-start | bytes 884744 | tf_op jit(solution)/shard_map/ppermute | solution.py:38
  47.6 7.6 %copy-start.12 = (bf16[8,144,384]{2,1,0:T(8,128)(2,1)}, bf16[8,144,384]{2,1,0:T(8,128)(2,1)S(1)}, u32[]{:S(2)}) copy-start(bf16[8,144,384]{2,1,0:T(8,128)(2,1)S(1)} %all-to-all-done.rows_ref) | copy-start | bytes 2654212
  48.8 23.4 %collective-permute-start.11 = (bf16[8,128,384]{2,1,0:T(8,128)(2,1)}, bf16[8,128,384]{2,1,0:T(8,128)(2,1)}, u32[]{:S(2)}, u32[]{:S(2)}) collective-permute-start(bf16[8,128,384]{2,1,0:T(8,128)(2,1)} %slice.62.own_ref), channel_id=1, source_target_pairs={{0,64},{1,65},{4,68},{5,69},{8,72},{9,73},{12,76},{13,77},{16,80},... | collective-permute-start | bytes 2359304 | tf_op jit(solution)/shard_map/ppermute | solution.py:38
  50.4 21.8 %collective-permute-start.10 = (bf16[8,128,384]{2,1,0:T(8,128)(2,1)}, bf16[8,128,384]{2,1,0:T(8,128)(2,1)}, u32[]{:S(2)}, u32[]{:S(2)}) collective-permute-start(bf16[8,128,384]{2,1,0:T(8,128)(2,1)} %slice.62.own_ref), channel_id=1, source_target_pairs={{0,192},{1,193},{4,196},{5,197},{8,200},{9,201},{12,204},{13,205},... | collective-permute-start | bytes 2359304 | tf_op jit(solution)/shard_map/ppermute | solution.py:38
  55.1 2.3 %collective-permute-start.15 = (bf16[8,16,128]{2,1,0:T(8,128)(2,1)S(1)}, bf16[8,16,128]{2,1,0:T(8,128)(2,1)S(1)}, u32[]{:S(2)}, u32[]{:S(2)}) collective-permute-start(bf16[8,16,128]{2,1,0:T(8,128)(2,1)S(1)} %slice.53), channel_id=1, source_target_pairs={{0,1},{1,0},{2,3},{3,2},{4,5},{5,4},{6,7},{7,6},{8,9},{9,8},{10,11... | collective-permute-start | bytes 98312 | tf_op jit(solution)/shard_map/ppermute | solution.py:43
  59.6 36.9 %copy-start.1 = (f32[4096]{0:T(1024)S(1)}, f32[4096]{0:T(1024)}, u32[]{:S(2)}) copy-start(f32[4096]{0:T(1024)} %param.10) | copy-start | bytes 49156
  59.6 36.9 %copy-start.2 = (s32[3]{0:T(128)S(1)}, s32[3]{0:T(128)}, u32[]{:S(2)}) copy-start(s32[3]{0:T(128)} %pad_add_fusion.at_ref) | copy-start | bytes 40
  59.6 36.9 %copy-start.3 = (s32[2,2]{1,0:T(2,128)S(1)}, s32[2,2]{1,0:T(2,128)}, u32[]{:S(2)}) copy-start(s32[2,2]{1,0:T(2,128)} %len_ref.3) | copy-start | bytes 52
  59.6 36.9 %copy-start.10 = (f32[128]{0:T(128)S(1)}, f32[128]{0:T(128)}, u32[]{:S(2)}) copy-start(f32[128]{0:T(128)} %param.11) | copy-start | bytes 1540
  59.6 36.9 %copy-start.11 = (f32[128]{0:T(128)S(1)}, f32[128]{0:T(128)}, u32[]{:S(2)}) copy-start(f32[128]{0:T(128)} %param.12) | copy-start | bytes 1540
  59.6 36.8 %all-to-all-start.1 = ((bf16[8,592,128]{2,1,0:T(8,128)(2,1)}), bf16[8,592,128]{2,1,0:T(8,128)(2,1)S(1)}, u32[]{:S(2)}, u32[]{:S(2)}) async-start(bf16[8,592,128]{2,1,0:T(8,128)(2,1)} %pad_maximum_fusion), calls=%async_computation.1 | async-start | bytes 2424832 | tf_op jit(solution)/shard_map/all_to_all | solution.py:52
  64.7 13.2 %collective-permute-start.5 = (bf16[4,256,1024]{2,1,0:T(8,128)(2,1)S(1)}, bf16[4,256,1024]{2,1,0:T(8,128)(2,1)S(1)}, u32[]{:S(2)}, u32[]{:S(2)}) collective-permute-start(bf16[4,256,1024]{2,1,0:T(8,128)(2,1)S(1)} %bitcast.27), channel_id=1, source_target_pairs={{0,1},{1,0},{2,3},{3,2},{4,5},{5,4},{6,7},{7,6},{8,9},{9,8},{10,11... | collective-permute-start | bytes 6291464 | tf_op jit(solution)/shard_map/ppermute | solution.py:43
  72.2 24.2 %collective-permute-start.12 = (bf16[4,256,1024]{2,1,0:T(8,128)(2,1)}, bf16[4,256,1024]{2,1,0:T(8,128)(2,1)}, u32[]{:S(2)}, u32[]{:S(2)}) collective-permute-start(bf16[4,256,1024]{2,1,0:T(8,128)(2,1)} %collective-permute-done.6.x2_ref), channel_id=1, source_target_pairs={{0,1},{1,0},{2,3},{3,2},{4,5},{5,4},{6,7},{7,6},{8,9},{9,8},{10,11... | collective-permute-start | bytes 6291464 | tf_op jit(solution)/shard_map/ppermute | solution.py:43
  73.3 12.9 %collective-permute-start.14 = (bf16[4,128,384]{2,1,0:T(8,128)(2,1)S(1)}, bf16[4,128,384]{2,1,0:T(8,128)(2,1)S(1)}, u32[]{:S(2)}, u32[]{:S(2)}) collective-permute-start(bf16[4,128,384]{2,1,0:T(8,128)(2,1)S(1)} %slice.66), channel_id=1, source_target_pairs={{0,64},{1,65},{4,68},{5,69},{8,72},{9,73},{12,76},{13,77},{16,80},... | collective-permute-start | bytes 1179656 | tf_op jit(solution)/shard_map/ppermute | solution.py:38
  76.0 11.5 %collective-permute-start.13 = (bf16[4,128,384]{2,1,0:T(8,128)(2,1)S(1)}, bf16[4,128,384]{2,1,0:T(8,128)(2,1)S(1)}, u32[]{:S(2)}, u32[]{:S(2)}) collective-permute-start(bf16[4,128,384]{2,1,0:T(8,128)(2,1)S(1)} %slice.65), channel_id=1, source_target_pairs={{0,192},{1,193},{4,196},{5,197},{8,200},{9,201},{12,204},{13,205},... | collective-permute-start | bytes 1179656 | tf_op jit(solution)/shard_map/ppermute | solution.py:38
  77.9 1.4 copy-start.4
  86.2 0.8 copy-start.6
  87.5 0.8 copy-start.8
  96.5 1.6 %copy-start.5 = (bf16[4,256,1024]{2,1,0:T(8,128)(2,1)S(1)}, bf16[4,256,1024]{2,1,0:T(8,128)(2,1)}, u32[]{:S(2)}) copy-start(bf16[4,256,1024]{2,1,0:T(8,128)(2,1)} %copy-done.4) | copy-start | bytes 6291460
  98.1 1.0 copy-start.7
  99.1 1.0 copy-start.9
  138.1 5.9 %collective-permute-start.17 = (f32[130,128]{1,0:T(8,128)S(1)}, f32[130,128]{1,0:T(8,128)S(1)}, u32[]{:S(2)}, u32[]{:S(2)}) collective-permute-start(f32[130,128]{1,0:T(8,128)S(1)} %pad_maximum_fusion.4), channel_id=1, source_target_pairs={{0,2},{1,3},{2,0},{3,1},{4,6},{5,7},{6,4},{7,5},{8,10},{9,11},{10,... | collective-permute-start | bytes 199688 | tf_op jit(solution)/shard_map/ppermute | solution.py:43
  140.9 5.2 %collective-permute-start.18 = (f32[130,128]{1,0:T(8,128)S(1)}, f32[130,128]{1,0:T(8,128)S(1)}, u32[]{:S(2)}, u32[]{:S(2)}) collective-permute-start(f32[130,128]{1,0:T(8,128)S(1)} %pad_maximum_fusion.4), channel_id=1, source_target_pairs={{0,3},{1,2},{2,1},{3,0},{4,7},{5,6},{6,5},{7,4},{8,11},{9,10},{10,... | collective-permute-start | bytes 199688 | tf_op jit(solution)/shard_map/ppermute | solution.py:43
  141.0 5.2 %collective-permute-start.16 = (f32[130,128]{1,0:T(8,128)S(1)}, f32[130,128]{1,0:T(8,128)S(1)}, u32[]{:S(2)}, u32[]{:S(2)}) collective-permute-start(f32[130,128]{1,0:T(8,128)S(1)} %pad_maximum_fusion.4), channel_id=1, source_target_pairs={{0,1},{1,0},{2,3},{3,2},{4,5},{5,4},{6,7},{7,6},{8,9},{9,8},{10,11... | collective-permute-start | bytes 199688 | tf_op jit(solution)/shard_map/ppermute | solution.py:43

commit v4 on v3

--- a/solution.py
+++ b/solution.py
@@ -139,13 +139,13 @@
     far_low_ref,
     far_high_ref,
     last_ref,
+    part_q_ref,
     gain_ref,
     qg_ref,
     kg_ref,
     out_ref,
     wk_ref,
     wv_ref,
-    parts_ref,
     query_ref,
     sem,
 ):
@@ -167,8 +167,6 @@
             copy.start()
             copies.append(copy)
 
-        tail = pl.ds(Y * XLO * rows, parts_ref.shape[1])
-        start(last_ref.at[:, tail, :], parts_ref)
         for step, halves in enumerate(
             [[own_ref], [up_ref], [far_low_ref, far_high_ref], [down_ref]]
         ):
@@ -186,7 +184,7 @@
                 start(last_ref.at[:, block, :], wv_at)
         for copy in copies:
             copy.wait()
-        parts = jnp.sum(parts_ref[...].astype(jnp.float32), axis=0)
+        parts = jnp.sum(part_q_ref[...].astype(jnp.float32), axis=0)
         query_ref[...] = parts + pltpu.roll(parts, parts.shape[0] - 4, 0)
 
     squares = None
@@ -276,9 +274,10 @@
     )(z_all, *rest)
 
 
-def kv_attend(at, lengths, slices, pieces, last, gains, heads, qg, kg):
+def kv_attend(at, lengths, slices, pieces, last, partial_q, gains, qg, kg):
     seq_count, slots, width = slices[0].shape
     model_width = gains.size
+    heads = partial_q.shape[1] // 8
     kv_width = 2 * HEAD_DIM
     rows = model_width // (Y * XLO * Z)
     x_spec = pl.BlockSpec((1, slots, width), lambda seq: (seq, 0, 0))
@@ -288,22 +287,21 @@
         in_specs=[SMEM, SMEM]
         + [x_spec] * len(slices)
         + [pl.BlockSpec(memory_space=pltpu.HBM)] * (len(pieces) + 1)
-        + [VMEM] * 3,
+        + [VMEM] * 4,
         out_specs=pl.BlockSpec((1, heads, HEAD_DIM), lambda seq: (seq, 0, 0)),
         out_shape=jax.ShapeDtypeStruct((seq_count, heads, HEAD_DIM), jnp.float32),
         scratch_shapes=[pltpu.VMEM((Y, XLO, Z, rows, kv_width), jnp.bfloat16)] * 2
         + [
-            pltpu.VMEM((Z, heads * 8, HEAD_DIM), jnp.bfloat16),
             pltpu.VMEM((heads * 8, HEAD_DIM), jnp.float32),
-            pltpu.SemaphoreType.DMA((1 + XLO * (3 * Y + 2),)),
+            pltpu.SemaphoreType.DMA((XLO * (3 * Y + 2),)),
         ],
-        compiler_params=pltpu.CompilerParams(vmem_limit_bytes=40 * 1024 * 1024),
+        compiler_params=pltpu.CompilerParams(vmem_limit_bytes=58 * 1024 * 1024),
         cost_estimate=pl.CostEstimate(
             flops=4 * seq_count * slots * model_width * kv_width,
             bytes_accessed=2 * seq_count * slots * model_width + 4 * model_width * kv_width,
             transcendentals=seq_count * heads * slots,
         ),
-    )(at, lengths, *slices, *pieces, last, gains, qg, kg)
+    )(at, lengths, *slices, *pieces, last, partial_q, gains, qg, kg)
 
 
 def body(
@@ -320,7 +318,6 @@
     seq_count = 2 * pair_count
     own = hidden.reshape(seq_count, seq_slots, width_local)
     rows_local, kv_width = key_weight.shape
-    query_width = query_weight.shape[1]
     gains = norm_gain[None]
 
     kv_weight = jnp.concatenate([key_weight, value_weight], axis=1)
@@ -355,14 +352,9 @@
     far_high = shift(z_down[Z // 2 :], dy=1)
     pieces = [z_own, z_up, z_down, far_low, far_high]
 
-    corner = swap_tensor(z_own[:, :16, :HEAD_DIM], 1)
-    last = exchange(
-        jnp.concatenate(
-            [jnp.broadcast_to(head[None], (Z,) + head.shape), partial_q, corner], axis=1
-        ),
-        Z_GROUPS,
-    )
-    far_peer = swap_tensor(lax.optimization_barrier((far, z_up, z_down))[0], 1)
+    last = exchange(jnp.broadcast_to(head[None], (Z,) + head.shape), Z_GROUPS)
+    partial_q = exchange(lax.optimization_barrier((partial_q, last))[0], Z_GROUPS)
+    far_peer = swap_tensor(lax.optimization_barrier((far, z_up, z_down, last))[0], 1)
 
     mixed = kv_attend(
         at,
@@ -370,8 +362,8 @@
         [own, peer, far, far_peer],
         pieces,
         last,
+        partial_q,
         gains,
-        query_width // HEAD_DIM,
         q_norm_gain[None],
         k_norm_gain[None],
     ).reshape(seq_count, width_local)

time: 152 us -> 158 us (1.039)
  waiting for transfers between devices: 43 us -> 50.6 us
  local copies, waits for them, and re-layouts: 15.6 us -> 10.3 us
  starting transfers between devices: 38.8 us -> 43.8 us
  Pallas kernels: 18.1 us -> 19.8 us
    ppermute x10 -> x9, waiting for transfers between devices: 13.4 us -> 25.4 us  [swap_tensor(): return lax.ppermute(array, 'tensor', [(i, i ^ mask) for i in range(size)])]
    all_to_all x2 -> x3, starting transfers between devices: 13.6 us -> 18.9 us  [exchange(): lax.all_to_all(chunks, 'dp', split_axis=0, concat_axis=0, tiled=True, axi...]
    all_to_all x2 -> x3, waiting for transfers between devices: 21.8 us -> 17.1 us  [exchange(): lax.all_to_all(chunks, 'dp', split_axis=0, concat_axis=0, tiled=True, axi...]
    unnamed x44 -> x36, local copies, waits for them, and re-layouts: 7.11 us -> 3.75 us
    slice x3, local copies, waits for them, and re-layouts: 2.28 us -> 0.01 us  [body(): head = jnp.concatenate([array[:, :HEAD_DIM] for array in rest])]
    concatenate x1 -> x0, other arithmetic: 1.99 us -> none  [body(): jnp.concatenate([jnp.broadcast_to(head[None], (Z,) + head.shape), partial...]
    pallas_call x1, Pallas kernels: 11.9 us -> 13.5 us  [kv_attend(): pl.pallas_call(kv_attend_kernel, grid=(seq_count,), in_specs=[SMEM, SMEM]...]
    ppermute x10 -> x9, starting transfers between devices: 10.3 us -> 10.2 us  [swap_tensor(): return lax.ppermute(array, 'tensor', [(i, i ^ mask) for i in range(size)])]
  transfers between devices with their start and end apart: 21 -> 21, of which waited for: 9 -> 10; matrix products, arithmetic and copies ran while one was open for 7% -> 4% of each run, Pallas kernels for 3% -> 2%
where the time goes in v4:
time: 158 us
  waiting for transfers between devices  50.6 us (32%)
  starting transfers between devices  43.8 us (28%)
  blocking collectives  23.7 us (15%)
  Pallas kernels  19.8 us (13%)
  local copies, waits for them, and re-layouts  10.3 us (7%)
  other arithmetic  6.54 us (4%)
  between operations  2.66 us (2%)
    ppermute x9, waiting for transfers between devices, swap_tensor(): return lax.ppermute(array, 'tensor', [(i, i ^ mask) for i in range(size)])  25.4 us
    all_to_all x1, blocking collectives, exchange(): lax.all_to_all(chunks, 'dp', split_axis=0, concat_axis=0, tiled=True, axi...  23.7 us
    all_to_all x3, starting transfers between devices, exchange(): lax.all_to_all(chunks, 'dp', split_axis=0, concat_axis=0, tiled=True, axi...  18.9 us
    all_to_all x3, waiting for transfers between devices, exchange(): lax.all_to_all(chunks, 'dp', split_axis=0, concat_axis=0, tiled=True, axi...  17.1 us
    pallas_call x1, Pallas kernels, kv_attend(): pl.pallas_call(kv_attend_kernel, grid=(seq_count,), in_specs=[SMEM, SMEM]...  13.5 us
    ppermute x7, starting transfers between devices, shift(): return lax.ppermute(array, ('dp', 'tensor'), pairs)  12.5 us
    ppermute x9, starting transfers between devices, swap_tensor(): return lax.ppermute(array, 'tensor', [(i, i ^ mask) for i in range(size)])  10.2 us
    ppermute x7, waiting for transfers between devices, shift(): return lax.ppermute(array, ('dp', 'tensor'), pairs)  7.58 us
  transfers between devices with their start and end apart: 21, of which 10 were waited for; matrix products, arithmetic and copies ran while one was open for 4% of the time, Pallas kernels for 2%

profile of v4, /device:TPU:32, one launch (start us, length us, event | category | flops | bytes accessed | tf_op | source)
XLA Modules:
  0.0 157.6 jit_solution(11569060977077387535)
XLA Ops:
  0.7 2.3 %shard_map.103.r0 = bf16[4,1024]{1,0:T(4,128)(2,1)} custom-call(s32[2,2]{1,0:T(2,128)} %len_ref.3, bf16[4,256,1024]{2,1,0:T(8,128)(2,1)} %bitcast.25), custom_call_target="tpu_custom_call" | custom-call | tf_op jit(solution)/shard_map/pallas_call | solution.py:236
  3.0 2.5 %collective-permute-start.4 = (bf16[4,1024]{1,0:T(4,128)(2,1)}, bf16[4,1024]{1,0:T(4,128)(2,1)S(1)}, u32[]{:S(2)}, u32[]{:S(2)}) collective-permute-start(bf16[4,1024]{1,0:T(4,128)(2,1)} %shard_map.103.r0), channel_id=1, source_target_pairs={{0,3},{1,2},{2,1},{3,0},{4,7},{5,6},{6,5},{7,4},{8,11},{9,10},{10,... | collective-permute-start | bytes 24584 | tf_op jit(solution)/shard_map/ppermute | solution.py:43
  5.5 0.7 collective-permute-start.3
  6.2 0.2 collective-permute-start.2
  6.4 1.6 %collective-permute-start = (bf16[64,512]{1,0:T(8,128)(2,1)S(1)}, bf16[64,512]{1,0:T(8,128)(2,1)S(1)}, u32[]{:S(2)}, u32[]{:S(2)}) collective-permute-start(bf16[64,512]{1,0:T(8,128)(2,1)S(1)} %constant_dynamic-update-slice_fusion), channel_id=1, source_target_pairs={{0,32},{4,36},{8,40},{12,44},{16,48},{20,52},{24,56},{28,60},{32,0... | collective-permute-start | bytes 196616 | tf_op jit(solution)/shard_map/ppermute | solution.py:48
  8.0 0.5 collective-permute-start.1
  8.5 0.7 pad_add_fusion.at_ref
  9.2 1.7 %collective-permute-done.3.r2 = bf16[4,1024]{1,0:T(4,128)(2,1)S(1)} collective-permute-done((bf16[4,1024]{1,0:T(4,128)(2,1)}, bf16[4,1024]{1,0:T(4,128)(2,1)S(1)}, u32[]{:S(2)}, u32[]{:S(2)}) %collective-permute-start.3) | collective-permute-done | bytes 8224 | tf_op jit(solution)/shard_map/ppermute | solution.py:43
  10.9 0.6 copy-done.14
  11.5 1.7 %shard_map.104 = bf16[8,16,384]{2,1,0:T(8,128)(2,1)} custom-call(s32[3]{0:T(128)} %pad_add_fusion.at_ref, bf16[4,1024]{1,0:T(4,128)(2,1)} %shard_map.103.r0, bf16[4,1024]{1,0:T(4,128)(2,1)} %copy-done.15, bf16[4,1024]{1,0:T(4,128)(2,1)} %copy-done.14, bf16[4,1024]{1,0:T(4,128)(2,1)} %copy-done.13, f32[1,4096]{1,0:T(1,128)} %bitcast.30), custom_call_target="tpu_custom_call" | custom-call | tf_op jit(solution)/shard_map/pallas_call | solution.py:251
  13.2 0.4 collective-permute-done.1
  13.6 0.6 copy-done.9
  14.2 0.1 broadcast_in_dim.15
  14.3 2.1 %pad_maximum_fusion = bf16[8,144,384]{2,1,0:T(8,128)(2,1)} fusion(bf16[8,16,384]{2,1,0:T(8,128)(2,1)} %shard_map.104, bf16[8,128,384]{2,1,0:T(8,128)(2,1)S(1)} %broadcast_in_dim.15), kind=kLoop, calls=%fused_computation.1 | loop fusion | flops 1769472 | bytes 1769472 | tf_op jit(solution)/shard_map/concatenate | solution.py:337
  16.4 8.6 %all-to-all-start = ((bf16[8,144,384]{2,1,0:T(8,128)(2,1)}), bf16[8,144,384]{2,1,0:T(8,128)(2,1)S(1)}, u32[]{:S(2)}, u32[]{:S(2)}) async-start(bf16[8,144,384]{2,1,0:T(8,128)(2,1)} %pad_maximum_fusion), calls=%async_computation | async-start | bytes 1769472 | tf_op jit(solution)/shard_map/all_to_all | solution.py:52
  25.0 0.9 maximum_maximum_fusion.w0
  25.9 1.7 %collective-permute-start.9 = (bf16[128,1152]{1,0:T(8,128)(2,1)S(1)}, bf16[128,1152]{1,0:T(8,128)(2,1)S(1)}, u32[]{:S(2)}, u32[]{:S(2)}) collective-permute-start(bf16[128,1152]{1,0:T(8,128)(2,1)S(1)} %maximum_maximum_fusion.w0), channel_id=1, source_target_pairs={{0,64},{1,65},{4,68},{5,69},{8,72},{9,73},{12,76},{13,77},{16,80},... | collective-permute-start | bytes 884744 | tf_op jit(solution)/shard_map/ppermute | solution.py:38
  27.6 2.9 %collective-permute-start.8 = (bf16[128,1152]{1,0:T(8,128)(2,1)S(1)}, bf16[128,1152]{1,0:T(8,128)(2,1)S(1)}, u32[]{:S(2)}, u32[]{:S(2)}) collective-permute-start(bf16[128,1152]{1,0:T(8,128)(2,1)S(1)} %maximum_maximum_fusion.w0), channel_id=1, source_target_pairs={{0,128},{1,129},{4,132},{5,133},{8,136},{9,137},{12,140},{13,141},... | collective-permute-start | bytes 884744 | tf_op jit(solution)/shard_map/ppermute | solution.py:38
  30.5 1.3 collective-permute-start.7
  31.8 3.0 %collective-permute-start.6 = (bf16[4,256,1024]{2,1,0:T(8,128)(2,1)S(1)}, bf16[4,256,1024]{2,1,0:T(8,128)(2,1)}, u32[]{:S(2)}, u32[]{:S(2)}) collective-permute-start(bf16[4,256,1024]{2,1,0:T(8,128)(2,1)S(1)} %bitcast.27), channel_id=1, source_target_pairs={{0,2},{1,3},{2,0},{3,1},{4,6},{5,7},{6,4},{7,5},{8,10},{9,11},{10,... | collective-permute-start | bytes 6291464 | tf_op jit(solution)/shard_map/ppermute | solution.py:43
  34.8 1.2 collective-permute-done.9.w3
  36.0 6.4 %collective-permute-done.8.w2 = bf16[128,1152]{1,0:T(8,128)(2,1)S(1)} collective-permute-done((bf16[128,1152]{1,0:T(8,128)(2,1)S(1)}, bf16[128,1152]{1,0:T(8,128)(2,1)S(1)}, u32[]{:S(2)}, u32[]{:S(2)}) %collective-permute-start.8) | collective-permute-done | bytes 294944 | tf_op jit(solution)/shard_map/ppermute | solution.py:38
  42.4 0.7 copy-done.4
  43.1 0.1 copy-done.5
  43.2 4.9 %all-to-all-done.rows_ref = bf16[8,144,384]{2,1,0:T(8,128)(2,1)S(1)} async-done(((bf16[8,144,384]{2,1,0:T(8,128)(2,1)}), bf16[8,144,384]{2,1,0:T(8,128)(2,1)S(1)}, u32[]{:S(2)}, u32[]{:S(2)}) %all-to-all-start) | async-done | bytes 884768 | tf_op jit(solution)/shard_map/all_to_all | solution.py:52
  48.2 1.3 broadcast_in_dim.17
  49.5 5.6 %all-to-all-start.1 = ((bf16[8,512,128]{2,1,0:T(8,128)(2,1)}), bf16[8,512,128]{2,1,0:T(8,128)(2,1)}, u32[]{:S(2)}, u32[]{:S(2)}) async-start(bf16[8,512,128]{2,1,0:T(8,128)(2,1)} %broadcast_in_dim.17), calls=%async_computation.1 | async-start | bytes 2097152 | tf_op jit(solution)/shard_map/all_to_all | solution.py:52
  55.1 1.1 slice.58.own_ref
  56.2 1.6 %collective-permute-start.11 = (bf16[8,128,384]{2,1,0:T(8,128)(2,1)}, bf16[8,128,384]{2,1,0:T(8,128)(2,1)}, u32[]{:S(2)}, u32[]{:S(2)}) collective-permute-start(bf16[8,128,384]{2,1,0:T(8,128)(2,1)} %slice.58.own_ref), channel_id=1, source_target_pairs={{0,64},{1,65},{4,68},{5,69},{8,72},{9,73},{12,76},{13,77},{16,80},... | collective-permute-start | bytes 2359304 | tf_op jit(solution)/shard_map/ppermute | solution.py:38
  57.7 1.7 %collective-permute-start.10 = (bf16[8,128,384]{2,1,0:T(8,128)(2,1)}, bf16[8,128,384]{2,1,0:T(8,128)(2,1)S(1)}, u32[]{:S(2)}, u32[]{:S(2)}) collective-permute-start(bf16[8,128,384]{2,1,0:T(8,128)(2,1)} %slice.58.own_ref), channel_id=1, source_target_pairs={{0,192},{1,193},{4,196},{5,197},{8,200},{9,201},{12,204},{13,205},... | collective-permute-start | bytes 2359304 | tf_op jit(solution)/shard_map/ppermute | solution.py:38
  59.4 19.5 %collective-permute-done.6.x2_ref = bf16[4,256,1024]{2,1,0:T(8,128)(2,1)} collective-permute-done((bf16[4,256,1024]{2,1,0:T(8,128)(2,1)S(1)}, bf16[4,256,1024]{2,1,0:T(8,128)(2,1)}, u32[]{:S(2)}, u32[]{:S(2)}) %collective-permute-start.6) | collective-permute-done | bytes 2097184 | tf_op jit(solution)/shard_map/ppermute | solution.py:43
  78.9 4.1 %all-to-all-done.1.last_ref = bf16[8,512,128]{2,1,0:T(8,128)(2,1)} async-done(((bf16[8,512,128]{2,1,0:T(8,128)(2,1)}), bf16[8,512,128]{2,1,0:T(8,128)(2,1)}, u32[]{:S(2)}, u32[]{:S(2)}) %all-to-all-start.1) | async-done | bytes 1048608 | tf_op jit(solution)/shard_map/all_to_all | solution.py:52
  83.0 0.9 copy-done.6
  83.9 1.0 slice.65
  84.9 1.7 %collective-permute-start.14 = (bf16[4,128,384]{2,1,0:T(8,128)(2,1)S(1)}, bf16[4,128,384]{2,1,0:T(8,128)(2,1)S(1)}, u32[]{:S(2)}, u32[]{:S(2)}) collective-permute-start(bf16[4,128,384]{2,1,0:T(8,128)(2,1)S(1)} %slice.65), channel_id=1, source_target_pairs={{0,64},{1,65},{4,68},{5,69},{8,72},{9,73},{12,76},{13,77},{16,80},... | collective-permute-start | bytes 1179656 | tf_op jit(solution)/shard_map/ppermute | solution.py:38
  86.6 1.0 slice.64
  87.6 1.7 %collective-permute-start.13 = (bf16[4,128,384]{2,1,0:T(8,128)(2,1)S(1)}, bf16[4,128,384]{2,1,0:T(8,128)(2,1)}, u32[]{:S(2)}, u32[]{:S(2)}) collective-permute-start(bf16[4,128,384]{2,1,0:T(8,128)(2,1)S(1)} %slice.64), channel_id=1, source_target_pairs={{0,192},{1,193},{4,196},{5,197},{8,200},{9,201},{12,204},{13,205},... | collective-permute-start | bytes 1179656 | tf_op jit(solution)/shard_map/ppermute | solution.py:38
  89.3 2.3 %shard_map.105 = bf16[8,64,128]{2,1,0:T(8,128)(2,1)} custom-call(bf16[8,144,384]{2,1,0:T(8,128)(2,1)} %copy-done, bf16[128,1152]{1,0:T(8,128)(2,1)} %copy-done.2, bf16[128,1152]{1,0:T(8,128)(2,1)} %copy-done.5, bf16[128,1152]{1,0:T(8,128)(2,1)} %copy-done.4, bf16[128,1152]{1,0:T(8,128)(2,1)} %copy-done.3), custom_call_target="tpu_custom_call" | custom-call | tf_op jit(solution)/shard_map/pallas_call | solution.py:266
  91.6 4.8 %all-to-all-start.2 = ((bf16[8,64,128]{2,1,0:T(8,128)(2,1)}), bf16[8,64,128]{2,1,0:T(8,128)(2,1)S(1)}, u32[]{:S(2)}, u32[]{:S(2)}) async-start(bf16[8,64,128]{2,1,0:T(8,128)(2,1)} %shard_map.105), calls=%async_computation.2 | async-start | bytes 262144 | tf_op jit(solution)/shard_map/all_to_all | solution.py:52
  96.4 8.1 %all-to-all-done.2.part_q_ref = bf16[8,64,128]{2,1,0:T(8,128)(2,1)S(1)} async-done(((bf16[8,64,128]{2,1,0:T(8,128)(2,1)}), bf16[8,64,128]{2,1,0:T(8,128)(2,1)S(1)}, u32[]{:S(2)}, u32[]{:S(2)}) %all-to-all-start.2) | async-done | bytes 131104 | tf_op jit(solution)/shard_map/all_to_all | solution.py:52
  104.5 0.6 copy-done.7
  105.1 0.2 copy-done.16
  105.3 13.5 %shard_map.106 = f32[4,8,128]{2,1,0:T(8,128)} custom-call(s32[3]{0:T(128)} %pad_add_fusion.at_ref, s32[2,2]{1,0:T(2,128)} %len_ref.3, bf16[4,256,1024]{2,1,0:T(8,128)(2,1)} %bitcast.26, bf16[4,256,1024]{2,1,0:T(8,128)(2,1)} %collective-permute-done.5.x1_ref, bf16[4,256,1024]{2,1,0:T(8,128)(2,1)} %collective-permute-done.6.x2_ref, ...), custom_call_target="tpu_custom_call" | custom-call | flops 4294967296 | bytes 12582912 | tf_op jit(solution)/shard_map/pallas_call | solution.py:284
  118.8 0.7 convert_bitcast_fusion
  119.6 0.1 broadcast_in_dim.39
  119.7 23.7 %all_to_all.20 = bf16[64,4,1024]{2,1,0:T(4,128)(2,1)S(1)} all-to-all(bf16[64,4,1024]{2,1,0:T(4,128)(2,1)S(1)} %broadcast_in_dim.39), channel_id=1, replica_groups=mesh['dp'=64,'tensor'=4] {'dp'}, dimensions={0} | all-to-all | bytes 1048576 | tf_op jit(solution)/shard_map/all_to_all | solution.py:52
  143.4 0.3 multiply_reduce_fusion
  143.8 0.1 reduce_sum.48
  143.9 0.1 copy.14
  143.9 0.2 reshape.35
  144.2 0.7 fusion.12
  144.9 0.3 fusion
  145.2 2.8 %collective-permute-start.16 = (f32[130,128]{1,0:T(8,128)S(1)}, f32[130,128]{1,0:T(8,128)S(1)}, u32[]{:S(2)}, u32[]{:S(2)}) collective-permute-start(f32[130,128]{1,0:T(8,128)S(1)} %pad_maximum_fusion.3), channel_id=1, source_target_pairs={{0,2},{1,3},{2,0},{3,1},{4,6},{5,7},{6,4},{7,5},{8,10},{9,11},{10,... | collective-permute-start | bytes 199688 | tf_op jit(solution)/shard_map/ppermute | solution.py:43
  148.0 0.9 collective-permute-start.15
  148.9 2.2 %collective-permute-done.16 = f32[130,128]{1,0:T(8,128)S(1)} collective-permute-done((f32[130,128]{1,0:T(8,128)S(1)}, f32[130,128]{1,0:T(8,128)S(1)}, u32[]{:S(2)}, u32[]{:S(2)}) %collective-permute-start.16) | collective-permute-done | bytes 66592 | tf_op jit(solution)/shard_map/ppermute | solution.py:43
  151.1 2.2 %collective-permute-done.17 = f32[130,128]{1,0:T(8,128)S(1)} collective-permute-done((f32[130,128]{1,0:T(8,128)S(1)}, f32[130,128]{1,0:T(8,128)S(1)}, u32[]{:S(2)}, u32[]{:S(2)}) %collective-permute-start.17) | collective-permute-done | bytes 66592 | tf_op jit(solution)/shard_map/ppermute | solution.py:43
  153.3 0.1 dynamic-slice_bitcast_fusion
  153.3 0.1 copy.15
  153.4 0.2 fusion.10
  153.6 0.2 exponential_reduce_fusion.1
  153.8 0.1 exponential_reduce_fusion
  153.9 0.6 fusion.11
  154.6 0.6 dynamic_slice.7
  155.1 0.7 multiply_convert_fusion
  (57 shorter events, 0.2 us)
Async XLA Ops:
  0.6 5.8 %copy-start.11 = (bf16[64,256]{1,0:T(8,128)(2,1)S(1)}, bf16[64,256]{1,0:T(8,128)(2,1)}, u32[]{:S(2)}) copy-start(bf16[64,256]{1,0:T(8,128)(2,1)} %param.14) | copy-start | bytes 98308
  0.6 5.8 %copy-start.12 = (bf16[64,256]{1,0:T(8,128)(2,1)S(1)}, bf16[64,256]{1,0:T(8,128)(2,1)}, u32[]{:S(2)}) copy-start(bf16[64,256]{1,0:T(8,128)(2,1)} %param.15) | copy-start | bytes 98308
  0.7 7.4 %copy-start.8 = (bf16[64,1024]{1,0:T(8,128)(2,1)S(1)}, bf16[64,1024]{1,0:T(8,128)(2,1)}, u32[]{:S(2)}) copy-start(bf16[64,1024]{1,0:T(8,128)(2,1)} %param.13) | copy-start | bytes 393220
  3.0 6.3 %collective-permute-start.4 = (bf16[4,1024]{1,0:T(4,128)(2,1)}, bf16[4,1024]{1,0:T(4,128)(2,1)S(1)}, u32[]{:S(2)}, u32[]{:S(2)}) collective-permute-start(bf16[4,1024]{1,0:T(4,128)(2,1)} %shard_map.103.r0), channel_id=1, source_target_pairs={{0,3},{1,2},{2,1},{3,0},{4,7},{5,6},{6,5},{7,4},{8,11},{9,10},{10,... | collective-permute-start | bytes 24584 | tf_op jit(solution)/shard_map/ppermute | solution.py:43
  5.5 5.4 %collective-permute-start.3 = (bf16[4,1024]{1,0:T(4,128)(2,1)}, bf16[4,1024]{1,0:T(4,128)(2,1)S(1)}, u32[]{:S(2)}, u32[]{:S(2)}) collective-permute-start(bf16[4,1024]{1,0:T(4,128)(2,1)} %shard_map.103.r0), channel_id=1, source_target_pairs={{0,2},{1,3},{2,0},{3,1},{4,6},{5,7},{6,4},{7,5},{8,10},{9,11},{10,... | collective-permute-start | bytes 24584 | tf_op jit(solution)/shard_map/ppermute | solution.py:43
  6.2 4.7 %collective-permute-start.2 = (bf16[4,1024]{1,0:T(4,128)(2,1)}, bf16[4,1024]{1,0:T(4,128)(2,1)S(1)}, u32[]{:S(2)}, u32[]{:S(2)}) collective-permute-start(bf16[4,1024]{1,0:T(4,128)(2,1)} %shard_map.103.r0), channel_id=1, source_target_pairs={{0,1},{1,0},{2,3},{3,2},{4,5},{5,4},{6,7},{7,6},{8,9},{9,8},{10,11... | collective-permute-start | bytes 24584 | tf_op jit(solution)/shard_map/ppermute | solution.py:43
  6.4 6.7 %collective-permute-start = (bf16[64,512]{1,0:T(8,128)(2,1)S(1)}, bf16[64,512]{1,0:T(8,128)(2,1)S(1)}, u32[]{:S(2)}, u32[]{:S(2)}) collective-permute-start(bf16[64,512]{1,0:T(8,128)(2,1)S(1)} %constant_dynamic-update-slice_fusion), channel_id=1, source_target_pairs={{0,32},{4,36},{8,40},{12,44},{16,48},{20,52},{24,56},{28,60},{32,0... | collective-permute-start | bytes 196616 | tf_op jit(solution)/shard_map/ppermute | solution.py:48
  8.0 5.6 %collective-permute-start.1 = (bf16[64,1024]{1,0:T(8,128)(2,1)S(1)}, bf16[64,1024]{1,0:T(8,128)(2,1)S(1)}, u32[]{:S(2)}, u32[]{:S(2)}) collective-permute-start(bf16[64,1024]{1,0:T(8,128)(2,1)S(1)} %copy-done.8), channel_id=1, source_target_pairs={{0,32},{4,36},{8,40},{12,44},{16,48},{20,52},{24,56},{28,60},{32,0... | collective-permute-start | bytes 393224 | tf_op jit(solution)/shard_map/ppermute | solution.py:48
  9.2 1.7 %copy-start.13 = (bf16[4,1024]{1,0:T(4,128)(2,1)}, bf16[4,1024]{1,0:T(4,128)(2,1)S(1)}, u32[]{:S(2)}) copy-start(bf16[4,1024]{1,0:T(4,128)(2,1)S(1)} %collective-permute-done.4.r3) | copy-start | bytes 24580
  10.9 0.6 copy-start.14
  10.9 0.6 copy-start.15
  13.6 0.6 copy-start.9
  14.3 17.5 %copy-start.1 = (bf16[2,2,256,1024]{3,2,1,0:T(8,128)(2,1)S(1)}, bf16[2,2,256,1024]{3,2,1,0:T(8,128)(2,1)}, u32[]{:S(2)}) copy-start(bf16[2,2,256,1024]{3,2,1,0:T(8,128)(2,1)} %param.8) | copy-start | bytes 6291460
  16.4 31.8 %all-to-all-start = ((bf16[8,144,384]{2,1,0:T(8,128)(2,1)}), bf16[8,144,384]{2,1,0:T(8,128)(2,1)S(1)}, u32[]{:S(2)}, u32[]{:S(2)}) async-start(bf16[8,144,384]{2,1,0:T(8,128)(2,1)} %pad_maximum_fusion), calls=%async_computation | async-start | bytes 1769472 | tf_op jit(solution)/shard_map/all_to_all | solution.py:52
  25.9 30.3 %copy-start.2 = (bf16[128,1152]{1,0:T(8,128)(2,1)}, bf16[128,1152]{1,0:T(8,128)(2,1)S(1)}, u32[]{:S(2)}) copy-start(bf16[128,1152]{1,0:T(8,128)(2,1)S(1)} %maximum_maximum_fusion.w0) | copy-start | bytes 884740
  25.9 10.1 %collective-permute-start.9 = (bf16[128,1152]{1,0:T(8,128)(2,1)S(1)}, bf16[128,1152]{1,0:T(8,128)(2,1)S(1)}, u32[]{:S(2)}, u32[]{:S(2)}) collective-permute-start(bf16[128,1152]{1,0:T(8,128)(2,1)S(1)} %maximum_maximum_fusion.w0), channel_id=1, source_target_pairs={{0,64},{1,65},{4,68},{5,69},{8,72},{9,73},{12,76},{13,77},{16,80},... | collective-permute-start | bytes 884744 | tf_op jit(solution)/shard_map/ppermute | solution.py:38
  27.6 14.8 %collective-permute-start.8 = (bf16[128,1152]{1,0:T(8,128)(2,1)S(1)}, bf16[128,1152]{1,0:T(8,128)(2,1)S(1)}, u32[]{:S(2)}, u32[]{:S(2)}) collective-permute-start(bf16[128,1152]{1,0:T(8,128)(2,1)S(1)} %maximum_maximum_fusion.w0), channel_id=1, source_target_pairs={{0,128},{1,129},{4,132},{5,133},{8,136},{9,137},{12,140},{13,141},... | collective-permute-start | bytes 884744 | tf_op jit(solution)/shard_map/ppermute | solution.py:38
  30.5 12.0 %collective-permute-start.7 = (bf16[128,1152]{1,0:T(8,128)(2,1)S(1)}, bf16[128,1152]{1,0:T(8,128)(2,1)S(1)}, u32[]{:S(2)}, u32[]{:S(2)}) collective-permute-start(bf16[128,1152]{1,0:T(8,128)(2,1)S(1)} %maximum_maximum_fusion.w0), channel_id=1, source_target_pairs={{0,192},{1,193},{4,196},{5,197},{8,200},{9,201},{12,204},{13,205},... | collective-permute-start | bytes 884744 | tf_op jit(solution)/shard_map/ppermute | solution.py:38
  31.8 47.0 %collective-permute-start.6 = (bf16[4,256,1024]{2,1,0:T(8,128)(2,1)S(1)}, bf16[4,256,1024]{2,1,0:T(8,128)(2,1)}, u32[]{:S(2)}, u32[]{:S(2)}) collective-permute-start(bf16[4,256,1024]{2,1,0:T(8,128)(2,1)S(1)} %bitcast.27), channel_id=1, source_target_pairs={{0,2},{1,3},{2,0},{3,1},{4,6},{5,7},{6,4},{7,5},{8,10},{9,11},{10,... | collective-permute-start | bytes 6291464 | tf_op jit(solution)/shard_map/ppermute | solution.py:43
  36.0 6.4 %copy-start.3 = (bf16[128,1152]{1,0:T(8,128)(2,1)}, bf16[128,1152]{1,0:T(8,128)(2,1)S(1)}, u32[]{:S(2)}) copy-start(bf16[128,1152]{1,0:T(8,128)(2,1)S(1)} %collective-permute-done.9.w3) | copy-start | bytes 884740
  42.4 0.7 copy-start.4
  42.4 0.8 copy-start.5
  48.2 8.0 %copy-start = (bf16[8,144,384]{2,1,0:T(8,128)(2,1)}, bf16[8,144,384]{2,1,0:T(8,128)(2,1)S(1)}, u32[]{:S(2)}) copy-start(bf16[8,144,384]{2,1,0:T(8,128)(2,1)S(1)} %all-to-all-done.rows_ref) | copy-start | bytes 2654212
  49.5 33.5 %all-to-all-start.1 = ((bf16[8,512,128]{2,1,0:T(8,128)(2,1)}), bf16[8,512,128]{2,1,0:T(8,128)(2,1)}, u32[]{:S(2)}, u32[]{:S(2)}) async-start(bf16[8,512,128]{2,1,0:T(8,128)(2,1)} %broadcast_in_dim.17), calls=%async_computation.1 | async-start | bytes 2097152 | tf_op jit(solution)/shard_map/all_to_all | solution.py:52
  56.2 26.8 %collective-permute-start.11 = (bf16[8,128,384]{2,1,0:T(8,128)(2,1)}, bf16[8,128,384]{2,1,0:T(8,128)(2,1)}, u32[]{:S(2)}, u32[]{:S(2)}) collective-permute-start(bf16[8,128,384]{2,1,0:T(8,128)(2,1)} %slice.58.own_ref), channel_id=1, source_target_pairs={{0,64},{1,65},{4,68},{5,69},{8,72},{9,73},{12,76},{13,77},{16,80},... | collective-permute-start | bytes 2359304 | tf_op jit(solution)/shard_map/ppermute | solution.py:38
  57.7 25.2 %collective-permute-start.10 = (bf16[8,128,384]{2,1,0:T(8,128)(2,1)}, bf16[8,128,384]{2,1,0:T(8,128)(2,1)S(1)}, u32[]{:S(2)}, u32[]{:S(2)}) collective-permute-start(bf16[8,128,384]{2,1,0:T(8,128)(2,1)} %slice.58.own_ref), channel_id=1, source_target_pairs={{0,192},{1,193},{4,196},{5,197},{8,200},{9,201},{12,204},{13,205},... | collective-permute-start | bytes 2359304 | tf_op jit(solution)/shard_map/ppermute | solution.py:38
  59.4 37.0 %collective-permute-start.5 = (bf16[4,256,1024]{2,1,0:T(8,128)(2,1)S(1)}, bf16[4,256,1024]{2,1,0:T(8,128)(2,1)}, u32[]{:S(2)}, u32[]{:S(2)}) collective-permute-start(bf16[4,256,1024]{2,1,0:T(8,128)(2,1)S(1)} %bitcast.28), channel_id=1, source_target_pairs={{0,1},{1,0},{2,3},{3,2},{4,5},{5,4},{6,7},{7,6},{8,9},{9,8},{10,11... | collective-permute-start | bytes 6291464 | tf_op jit(solution)/shard_map/ppermute | solution.py:43
  83.0 0.9 copy-start.6
  83.9 20.6 %collective-permute-start.12 = (bf16[4,256,1024]{2,1,0:T(8,128)(2,1)}, bf16[4,256,1024]{2,1,0:T(8,128)(2,1)}, u32[]{:S(2)}, u32[]{:S(2)}) collective-permute-start(bf16[4,256,1024]{2,1,0:T(8,128)(2,1)} %collective-permute-done.6.x2_ref), channel_id=1, source_target_pairs={{0,1},{1,0},{2,3},{3,2},{4,5},{5,4},{6,7},{7,6},{8,9},{9,8},{10,11... | collective-permute-start | bytes 6291464 | tf_op jit(solution)/shard_map/ppermute | solution.py:43
  84.9 19.6 %collective-permute-start.14 = (bf16[4,128,384]{2,1,0:T(8,128)(2,1)S(1)}, bf16[4,128,384]{2,1,0:T(8,128)(2,1)S(1)}, u32[]{:S(2)}, u32[]{:S(2)}) collective-permute-start(bf16[4,128,384]{2,1,0:T(8,128)(2,1)S(1)} %slice.65), channel_id=1, source_target_pairs={{0,64},{1,65},{4,68},{5,69},{8,72},{9,73},{12,76},{13,77},{16,80},... | collective-permute-start | bytes 1179656 | tf_op jit(solution)/shard_map/ppermute | solution.py:38
  87.6 16.9 %collective-permute-start.13 = (bf16[4,128,384]{2,1,0:T(8,128)(2,1)S(1)}, bf16[4,128,384]{2,1,0:T(8,128)(2,1)}, u32[]{:S(2)}, u32[]{:S(2)}) collective-permute-start(bf16[4,128,384]{2,1,0:T(8,128)(2,1)S(1)} %slice.64), channel_id=1, source_target_pairs={{0,192},{1,193},{4,196},{5,197},{8,200},{9,201},{12,204},{13,205},... | collective-permute-start | bytes 1179656 | tf_op jit(solution)/shard_map/ppermute | solution.py:38
  91.6 12.9 %all-to-all-start.2 = ((bf16[8,64,128]{2,1,0:T(8,128)(2,1)}), bf16[8,64,128]{2,1,0:T(8,128)(2,1)S(1)}, u32[]{:S(2)}, u32[]{:S(2)}) async-start(bf16[8,64,128]{2,1,0:T(8,128)(2,1)} %shard_map.105), calls=%async_computation.2 | async-start | bytes 262144 | tf_op jit(solution)/shard_map/all_to_all | solution.py:52
  104.5 0.7 copy-start.7
  104.5 0.8 copy-start.16
  143.8 5.1 %copy-start.10 = (f32[4,8,128]{2,1,0:T(8,128)S(1)}, f32[4,8,128]{2,1,0:T(8,128)}, u32[]{:S(2)}) copy-start(f32[4,8,128]{2,1,0:T(8,128)} %shard_map.106) | copy-start | bytes 49156
  145.2 5.9 %collective-permute-start.16 = (f32[130,128]{1,0:T(8,128)S(1)}, f32[130,128]{1,0:T(8,128)S(1)}, u32[]{:S(2)}, u32[]{:S(2)}) collective-permute-start(f32[130,128]{1,0:T(8,128)S(1)} %pad_maximum_fusion.3), channel_id=1, source_target_pairs={{0,2},{1,3},{2,0},{3,1},{4,6},{5,7},{6,4},{7,5},{8,10},{9,11},{10,... | collective-permute-start | bytes 199688 | tf_op jit(solution)/shard_map/ppermute | solution.py:43
  148.0 5.2 %collective-permute-start.17 = (f32[130,128]{1,0:T(8,128)S(1)}, f32[130,128]{1,0:T(8,128)S(1)}, u32[]{:S(2)}, u32[]{:S(2)}) collective-permute-start(f32[130,128]{1,0:T(8,128)S(1)} %pad_maximum_fusion.3), channel_id=1, source_target_pairs={{0,3},{1,2},{2,1},{3,0},{4,7},{5,6},{6,5},{7,4},{8,11},{9,10},{10,... | collective-permute-start | bytes 199688 | tf_op jit(solution)/shard_map/ppermute | solution.py:43
  148.0 5.2 %collective-permute-start.15 = (f32[130,128]{1,0:T(8,128)S(1)}, f32[130,128]{1,0:T(8,128)S(1)}, u32[]{:S(2)}, u32[]{:S(2)}) collective-permute-start(f32[130,128]{1,0:T(8,128)S(1)} %pad_maximum_fusion.3), channel_id=1, source_target_pairs={{0,1},{1,0},{2,3},{3,2},{4,5},{5,4},{6,7},{7,6},{8,9},{9,8},{10,11... | collective-permute-start | bytes 199688 | tf_op jit(solution)/shard_map/ppermute | solution.py:43

commit v5 on v4

--- a/solution.py
+++ b/solution.py
@@ -75,7 +75,9 @@
     out_ref[...] = rows.astype(jnp.bfloat16)
 
 
-def last_rows_kernel(at_ref, r0, r1, r2, r3, gain_ref, out_ref, raw_ref, row_ref):
+def payload_kernel(
+    at_ref, r0, r1, r2, r3, gain_ref, kv_ref, other_ref, out_ref, raw_ref, row_ref
+):
     y_at, x_lo_at, tensor_at = at_ref[0], at_ref[1], at_ref[2]
     refs = [r0, r1, r2, r3]
     seq_count, width = r0.shape
@@ -95,15 +97,16 @@
         ]
         normed = normed.astype(jnp.bfloat16).astype(jnp.float32)
         halves = [normed[:, : Z * rows], normed[:, Z * rows :]]
-        row, lane = (0, step * XLO * rows) if step < Y - 1 else (8, 0)
         for x in range(XLO):
             half = jnp.where(x_lo_at == x, halves[0], halves[1])
             for z in range(Z):
-                at = lane + x * rows
-                row_ref[z, row : row + seq_count, at : at + rows] = half[
-                    :, z * rows : (z + 1) * rows
-                ]
-    out_ref[...] = row_ref[...].astype(jnp.bfloat16)
+                at = (step * XLO + x) * rows
+                row_ref[z, :seq_count, at : at + rows] = half[:, z * rows : (z + 1) * rows]
+    depth = kv_ref.shape[0]
+    for z in range(Z):
+        out_ref[z, :depth, :] = kv_ref[...]
+        out_ref[z, depth : XLO * depth, :] = other_ref[...]
+        out_ref[z, XLO * depth :, :] = row_ref[z].astype(jnp.bfloat16)
 
 
 def query_kernel(rows_ref, w0, w1, w2, w3, out_ref, acc_ref):
@@ -111,11 +114,8 @@
     rows = rows_ref[...].astype(jnp.float32)
     total = None
     for step, w_ref in enumerate([w0, w1, w2, w3]):
-        row, lane = (0, step * depth) if step < Y - 1 else (8, 0)
-        lhs = rows[:, row : row + 8, lane : lane + depth].reshape(Z * 8, depth)
-        part = jnp.dot(
-            lhs.astype(jnp.bfloat16), w_ref[:, HEAD_DIM:], preferred_element_type=jnp.float32
-        )
+        lhs = rows[:, :8, step * depth : (step + 1) * depth].reshape(Z * 8, depth)
+        part = jnp.dot(lhs.astype(jnp.bfloat16), w_ref[...], preferred_element_type=jnp.float32)
         total = part if total is None else total + part
     high = total.astype(jnp.bfloat16).astype(jnp.float32)
     low = (total - high).astype(jnp.bfloat16).astype(jnp.float32)
@@ -134,11 +134,12 @@
     x2_ref,
     x3_ref,
     own_ref,
-    up_ref,
-    down_ref,
+    up_low_ref,
+    up_high_ref,
+    down_low_ref,
+    down_high_ref,
     far_low_ref,
     far_high_ref,
-    last_ref,
     part_q_ref,
     gain_ref,
     qg_ref,
@@ -159,33 +160,26 @@
 
     @pl.when(seq == 0)
     def _():
-        low = Z // 2
-        copies = []
-
-        def start(source, target):
-            copy = pltpu.make_async_copy(source, target, sem.at[len(copies)])
-            copy.start()
-            copies.append(copy)
-
         for step, halves in enumerate(
-            [[own_ref], [up_ref], [far_low_ref, far_high_ref], [down_ref]]
+            [
+                [own_ref],
+                [up_low_ref, up_high_ref],
+                [far_low_ref, far_high_ref],
+                [down_low_ref, down_high_ref],
+            ]
         ):
             y = (y_at + step) & (Y - 1)
-            for x in range(XLO):
-                block = pl.ds(x * rows, rows)
-                for half, piece in enumerate(halves):
-                    zs = pl.ds(half * low, piece.shape[0])
-                    wk_at = wk_ref.at[y, x_lo_at ^ x, zs]
-                    start(piece.at[:, block, pl.ds(0, 2 * HEAD_DIM)], wk_at)
-                    wv_at = wv_ref.at[y, x_lo_at ^ x, zs, :, pl.ds(0, HEAD_DIM)]
-                    start(piece.at[:, block, pl.ds(2 * HEAD_DIM, HEAD_DIM)], wv_at)
-                block = pl.ds((step * XLO + x) * rows, rows)
-                wv_at = wv_ref.at[y, x_lo_at ^ x, :, :, pl.ds(HEAD_DIM, HEAD_DIM)]
-                start(last_ref.at[:, block, :], wv_at)
-        for copy in copies:
-            copy.wait()
-        parts = jnp.sum(part_q_ref[...].astype(jnp.float32), axis=0)
-        query_ref[...] = parts + pltpu.roll(parts, parts.shape[0] - 4, 0)
+            for half, piece in enumerate(halves):
+                zs = pl.ds(half * (Z // 2), piece.shape[0])
+                for x in range(XLO):
+                    block = pl.ds(x * rows, rows)
+                    for i, w_ref in enumerate([wk_ref, wv_ref]):
+                        columns = pl.ds(i * 2 * HEAD_DIM, 2 * HEAD_DIM)
+                        pltpu.make_async_copy(
+                            piece.at[:, block, columns],
+                            w_ref.at[y, x_lo_at ^ x, zs],
+                            sem.at[i],
+                        ).start()
 
     squares = None
     for k in range(slices):
@@ -193,6 +187,14 @@
         part = jnp.sum(x * x, axis=-1, keepdims=True)
         squares = part if squares is None else squares + part
     scale = lax.rsqrt(squares / (slices * width) + EPS)
+
+    @pl.when(seq == 0)
+    def _():
+        for i, w_ref in enumerate([wk_ref, wv_ref]):
+            pltpu.make_async_copy(w_ref, w_ref, sem.at[i]).wait()
+        parts = jnp.sum(part_q_ref[...].astype(jnp.float32), axis=0)
+        query_ref[...] = parts + pltpu.roll(parts, parts.shape[0] - 4, 0)
+
     key_proj = value_proj = None
     for k in range(slices):
         x = x_refs[k][0].astype(jnp.float32)
@@ -229,6 +231,7 @@
 
 SMEM = pl.BlockSpec(memory_space=pltpu.SMEM)
 VMEM = pl.BlockSpec(memory_space=pltpu.VMEM)
+ANY = pl.BlockSpec(memory_space=pl.ANY)
 
 
 def take_last_call(lengths, own):
@@ -245,23 +248,23 @@
     )(lengths, own)
 
 
-def last_rows_call(at, raw, gains):
+def payload_call(at, raw, gains, kv_own, kv_other):
     seq_count, width = raw[0].shape
-    shape = (Z, 16, (Y - 1) * XLO * (width // (XLO * Z)))
+    rows, columns = kv_own.shape
     return pl.pallas_call(
-        last_rows_kernel,
-        in_specs=[SMEM] + [VMEM] * (len(raw) + 1),
+        payload_kernel,
+        in_specs=[SMEM] + [VMEM] * (len(raw) + 3),
         out_specs=VMEM,
-        out_shape=jax.ShapeDtypeStruct(shape, jnp.bfloat16),
+        out_shape=jax.ShapeDtypeStruct((Z, XLO * rows + 16, columns), jnp.bfloat16),
         scratch_shapes=[
             pltpu.VMEM((len(raw), seq_count, width), jnp.float32),
-            pltpu.VMEM(shape, jnp.float32),
+            pltpu.VMEM((Z, 16, columns), jnp.float32),
         ],
-    )(at, *raw, gains)
+    )(at, *raw, gains, kv_own, kv_other)
 
 
 def query_call(z_all, rest):
-    shape = (Z, (rest[0].shape[1] // HEAD_DIM - 1) * 8, HEAD_DIM)
+    shape = (Z, (rest[0].shape[1] // HEAD_DIM) * 8, HEAD_DIM)
     tail = z_all.shape[1] // 16 - 1
     return pl.pallas_call(
         query_kernel,
@@ -274,7 +277,7 @@
     )(z_all, *rest)
 
 
-def kv_attend(at, lengths, slices, pieces, last, partial_q, gains, qg, kg):
+def kv_attend(at, lengths, slices, pieces, partial_q, gains, qg, kg):
     seq_count, slots, width = slices[0].shape
     model_width = gains.size
     heads = partial_q.shape[1] // 8
@@ -286,14 +289,14 @@
         grid=(seq_count,),
         in_specs=[SMEM, SMEM]
         + [x_spec] * len(slices)
-        + [pl.BlockSpec(memory_space=pltpu.HBM)] * (len(pieces) + 1)
+        + [pl.BlockSpec(memory_space=pltpu.HBM)] * len(pieces)
         + [VMEM] * 4,
         out_specs=pl.BlockSpec((1, heads, HEAD_DIM), lambda seq: (seq, 0, 0)),
         out_shape=jax.ShapeDtypeStruct((seq_count, heads, HEAD_DIM), jnp.float32),
         scratch_shapes=[pltpu.VMEM((Y, XLO, Z, rows, kv_width), jnp.bfloat16)] * 2
         + [
             pltpu.VMEM((heads * 8, HEAD_DIM), jnp.float32),
-            pltpu.SemaphoreType.DMA((XLO * (3 * Y + 2),)),
+            pltpu.SemaphoreType.DMA((2,)),
         ],
         compiler_params=pltpu.CompilerParams(vmem_limit_bytes=58 * 1024 * 1024),
         cost_estimate=pl.CostEstimate(
@@ -301,7 +304,7 @@
             bytes_accessed=2 * seq_count * slots * model_width + 4 * model_width * kv_width,
             transcendentals=seq_count * heads * slots,
         ),
-    )(at, lengths, *slices, *pieces, last, partial_q, gains, qg, kg)
+    )(at, lengths, *slices, *pieces, partial_q, gains, qg, kg)
 
 
 def body(
@@ -317,51 +320,43 @@
     pair_count, _, seq_slots, width_local = hidden.shape
     seq_count = 2 * pair_count
     own = hidden.reshape(seq_count, seq_slots, width_local)
-    rows_local, kv_width = key_weight.shape
     gains = norm_gain[None]
 
     kv_weight = jnp.concatenate([key_weight, value_weight], axis=1)
-    kv_both = jnp.concatenate([kv_weight, swap_x_lo(kv_weight)])
+    kv_other = swap_x_lo(kv_weight)
     query_other = swap_x_lo(query_weight)
     last_own = take_last_call(lengths, own)
     last_raw = [last_own] + [swap_tensor(last_own, k) for k in range(1, tensor_size)]
 
-    sent_own = lax.optimization_barrier((own, kv_both, query_other, *last_raw))[0]
+    sent_own = lax.optimization_barrier((own, kv_other, query_other, *last_raw))[0]
     far = swap_tensor(sent_own, 2)
     peer = swap_tensor(sent_own, 1)
 
-    block = kv_both[:, : kv_width + HEAD_DIM]
-    rows = last_rows_call(at, last_raw, gains)
-    rows, _ = lax.optimization_barrier((rows, query_other))
-    z_all = exchange(
-        jnp.concatenate([jnp.broadcast_to(block[None], (Z,) + block.shape), rows], axis=1),
-        Z_GROUPS,
-    )
-
-    rest = jnp.concatenate(
-        [kv_both[:, kv_width + HEAD_DIM :], jnp.concatenate([query_weight, query_other])], axis=1
-    )
+    payload = payload_call(at, last_raw, gains, kv_weight, kv_other)
+    payload, _ = lax.optimization_barrier((payload, query_other))
+    z_all = exchange(payload, Z_GROUPS)
+
+    rest = jnp.concatenate([query_weight, query_other])
     rest = [rest] + [shift(rest, dy=-step) for step in range(1, Y)]
-    partial_q = query_call(z_all, rest)
-    head = jnp.concatenate([array[:, :HEAD_DIM] for array in rest])
-
-    z_own = lax.optimization_barrier((z_all[:, : block.shape[0]], *rest))[0]
-    z_up = shift(z_own, dy=-1)
-    z_down = shift(z_own, dy=1)
-    far_low = shift(z_up[: Z // 2], dy=-1)
-    far_high = shift(z_down[Z // 2 :], dy=1)
-    pieces = [z_own, z_up, z_down, far_low, far_high]
-
-    last = exchange(jnp.broadcast_to(head[None], (Z,) + head.shape), Z_GROUPS)
-    partial_q = exchange(lax.optimization_barrier((partial_q, last))[0], Z_GROUPS)
-    far_peer = swap_tensor(lax.optimization_barrier((far, z_up, z_down, last))[0], 1)
+
+    z_sent = lax.optimization_barrier((z_all, *rest))[0][:, :-16]
+    z_low, z_high = z_sent[: Z // 2], z_sent[Z // 2 :]
+    up_low = shift(z_low, dy=-1)
+    down_high = shift(z_high, dy=1)
+    up_high = shift(z_high, dy=-1)
+    down_low = shift(z_low, dy=1)
+    far_low = shift(up_low, dy=-1)
+    far_high = shift(down_high, dy=1)
+    pieces = [z_all, up_low, up_high, down_low, down_high, far_low, far_high]
+
+    partial_q = exchange(query_call(z_all, rest), Z_GROUPS)
+    far_peer = swap_tensor(lax.optimization_barrier((far, up_low, down_high, up_high, down_low))[0], 1)
 
     mixed = kv_attend(
         at,
         lengths,
         [own, peer, far, far_peer],
         pieces,
-        last,
         partial_q,
         gains,
         q_norm_gain[None],

time: 158 us -> 155 us (0.981)
  waiting for transfers between devices: 50.6 us -> 53.9 us
  other arithmetic: 6.54 us -> 3.54 us
  local copies, waits for them, and re-layouts: 10.3 us -> 7.31 us
  blocking collectives: 23.7 us -> 21.8 us
    ppermute x7 -> x9, waiting for transfers between devices: 7.58 us -> 16.3 us  [shift(): return lax.ppermute(array, ('dp', 'tensor'), pairs)]
    ppermute x9, waiting for transfers between devices: 25.4 us -> 17.7 us  [swap_tensor(): return lax.ppermute(array, 'tensor', [(i, i ^ mask) for i in range(size)])]
    slice x6 -> x1, local copies, waits for them, and re-layouts: 3.15 us -> 0.09 us  [body(): z_low, z_high = (z_sent[:Z // 2], z_sent[Z // 2:])]
    concatenate x5 -> x0, other arithmetic: 3.01 us -> none  [the longest x1 2.05 us: body(): jnp.concatenate([jnp.broadcast_to(block[None], (Z,) + block.shape), rows]...]
    ppermute x7 -> x9, starting transfers between devices: 12.5 us -> 15.5 us  [shift(): return lax.ppermute(array, ('dp', 'tensor'), pairs)]
    ppermute x2, waiting for transfers between devices: 0.44 us -> 2.68 us  [swap_x_lo(): return lax.ppermute(array, 'dp', pairs)]
    all_to_all x3 -> x2, starting transfers between devices: 18.9 us -> 16.9 us  [exchange(): lax.all_to_all(chunks, 'dp', split_axis=0, concat_axis=0, tiled=True, axi...]
    all_to_all x1, blocking collectives: 23.7 us -> 21.8 us  [exchange(): lax.all_to_all(chunks, 'dp', split_axis=0, concat_axis=0, tiled=True, axi...]
  transfers between devices with their start and end apart: 21 -> 22, of which waited for: 10 -> 11; matrix products, arithmetic and copies ran while one was open for 4% -> 2% of each run, Pallas kernels for 2% -> 3%
where the time goes in v5:
time: 155 us; the launch traced here: 154 us
  waiting for transfers between devices  53.9 us (35%)
  starting transfers between devices  44.6 us (29%)
  blocking collectives  21.8 us (14%)
  Pallas kernels  19.9 us (13%)
  local copies, waits for them, and re-layouts  7.31 us (5%)
  other arithmetic  3.54 us (2%)
  between operations  2.64 us (2%)
    all_to_all x1, blocking collectives, exchange(): lax.all_to_all(chunks, 'dp', split_axis=0, concat_axis=0, tiled=True, axi...  21.8 us
    ppermute x9, waiting for transfers between devices, swap_tensor(): return lax.ppermute(array, 'tensor', [(i, i ^ mask) for i in range(size)])  17.7 us
    all_to_all x2, waiting for transfers between devices, exchange(): lax.all_to_all(chunks, 'dp', split_axis=0, concat_axis=0, tiled=True, axi...  17.3 us
    all_to_all x2, starting transfers between devices, exchange(): lax.all_to_all(chunks, 'dp', split_axis=0, concat_axis=0, tiled=True, axi...  16.9 us
    ppermute x9, waiting for transfers between devices, shift(): return lax.ppermute(array, ('dp', 'tensor'), pairs)  16.3 us
    ppermute x9, starting transfers between devices, shift(): return lax.ppermute(array, ('dp', 'tensor'), pairs)  15.5 us
    pallas_call x1, Pallas kernels, kv_attend(): pl.pallas_call(kv_attend_kernel, grid=(seq_count,), in_specs=[SMEM, SMEM]...  13.1 us
    ppermute x9, starting transfers between devices, swap_tensor(): return lax.ppermute(array, 'tensor', [(i, i ^ mask) for i in range(size)])  10.1 us
  transfers between devices with their start and end apart: 22, of which 11 were waited for; matrix products, arithmetic and copies ran while one was open for 2% of the time, Pallas kernels for 3%

profile of v5, /device:TPU:32, one launch (start us, length us, event | category | flops | bytes accessed | tf_op | source)
XLA Modules:
  0.0 154.0 jit_solution(1372666362433141684)
XLA Ops:
  0.6 0.0 copy-start.6
  0.7 2.3 %shard_map.103.r0 = bf16[4,1024]{1,0:T(4,128)(2,1)} custom-call(s32[2,2]{1,0:T(2,128)} %len_ref.3, bf16[4,256,1024]{2,1,0:T(8,128)(2,1)} %bitcast.25), custom_call_target="tpu_custom_call" | custom-call | tf_op jit(solution)/shard_map/pallas_call | solution.py:239
  3.0 0.0 copy-start.1
  3.0 2.5 %collective-permute-start.4 = (bf16[4,1024]{1,0:T(4,128)(2,1)}, bf16[4,1024]{1,0:T(4,128)(2,1)S(1)}, u32[]{:S(2)}, u32[]{:S(2)}) collective-permute-start(bf16[4,1024]{1,0:T(4,128)(2,1)} %shard_map.103.r0), channel_id=1, source_target_pairs={{0,3},{1,2},{2,1},{3,0},{4,7},{5,6},{6,5},{7,4},{8,11},{9,10},{10,... | collective-permute-start | bytes 24584 | tf_op jit(solution)/shard_map/ppermute | solution.py:43
  5.5 0.7 collective-permute-start.3
  6.2 0.2 collective-permute-start.2
  6.4 1.5 collective-permute-start.1
  7.9 0.6 collective-permute-start
  8.6 0.7 pad_add_fusion.at_ref
  9.2 0.0 collective-permute-done.4.r3
  9.2 1.6 %collective-permute-done.3.r2 = bf16[4,1024]{1,0:T(4,128)(2,1)S(1)} collective-permute-done((bf16[4,1024]{1,0:T(4,128)(2,1)}, bf16[4,1024]{1,0:T(4,128)(2,1)S(1)}, u32[]{:S(2)}, u32[]{:S(2)}) %collective-permute-start.3) | collective-permute-done | bytes 8224 | tf_op jit(solution)/shard_map/ppermute | solution.py:43
  10.9 2.7 %collective-permute-done.other_ref = bf16[64,512]{1,0:T(8,128)(2,1)S(1)} collective-permute-done((bf16[64,512]{1,0:T(8,128)(2,1)S(1)}, bf16[64,512]{1,0:T(8,128)(2,1)S(1)}, u32[]{:S(2)}, u32[]{:S(2)}) %collective-permute-start) | collective-permute-done | bytes 65568 | tf_op jit(solution)/shard_map/ppermute | solution.py:48
  13.6 0.6 copy-done.9
  14.2 2.2 %shard_map.104 = bf16[8,144,512]{2,1,0:T(8,128)(2,1)} custom-call(s32[3]{0:T(128)} %pad_add_fusion.at_ref, bf16[4,1024]{1,0:T(4,128)(2,1)} %shard_map.103.r0, bf16[4,1024]{1,0:T(4,128)(2,1)} %copy-done.15, bf16[4,1024]{1,0:T(4,128)(2,1)} %copy-done.14, bf16[4,1024]{1,0:T(4,128)(2,1)} %copy-done.13, f32[1,4096]{1,0:T(1,128)} %bitcast.30, ...), custom_call_target="tpu_custom_call" | custom-call | tf_op jit(solution)/shard_map/pallas_call | solution.py:254
  16.4 0.0 collective-permute-done.1
  16.4 0.7 copy-done.7
  17.1 8.6 %all-to-all-start = ((bf16[8,144,512]{2,1,0:T(8,128)(2,1)}), bf16[8,144,512]{2,1,0:T(8,128)(2,1)S(1)}, u32[]{:S(2)}, u32[]{:S(2)}) async-start(bf16[8,144,512]{2,1,0:T(8,128)(2,1)} %shard_map.104), calls=%async_computation | async-start | bytes 2359296 | tf_op jit(solution)/shard_map/all_to_all | solution.py:52
  25.6 2.8 %collective-permute-start.6 = (bf16[4,256,1024]{2,1,0:T(8,128)(2,1)S(1)}, bf16[4,256,1024]{2,1,0:T(8,128)(2,1)}, u32[]{:S(2)}, u32[]{:S(2)}) collective-permute-start(bf16[4,256,1024]{2,1,0:T(8,128)(2,1)S(1)} %bitcast.27), channel_id=1, source_target_pairs={{0,2},{1,3},{2,0},{3,1},{4,6},{5,7},{6,4},{7,5},{8,10},{9,11},{10,... | collective-permute-start | bytes 6291464 | tf_op jit(solution)/shard_map/ppermute | solution.py:43
  28.5 0.9 constant_dynamic-update-slice_fusion.3
  29.4 0.9 constant_dynamic-update-slice_fusion.2.w0
  30.3 1.7 %collective-permute-start.9 = (bf16[128,1024]{1,0:T(8,128)(2,1)S(1)}, bf16[128,1024]{1,0:T(8,128)(2,1)S(1)}, u32[]{:S(2)}, u32[]{:S(2)}) collective-permute-start(bf16[128,1024]{1,0:T(8,128)(2,1)S(1)} %constant_dynamic-update-slice_fusion.2.w0), channel_id=1, source_target_pairs={{0,64},{1,65},{4,68},{5,69},{8,72},{9,73},{12,76},{13,77},{16,80},... | collective-permute-start | bytes 786440 | tf_op jit(solution)/shard_map/ppermute | solution.py:38
  32.0 2.9 %collective-permute-start.8 = (bf16[128,1024]{1,0:T(8,128)(2,1)S(1)}, bf16[128,1024]{1,0:T(8,128)(2,1)S(1)}, u32[]{:S(2)}, u32[]{:S(2)}) collective-permute-start(bf16[128,1024]{1,0:T(8,128)(2,1)S(1)} %constant_dynamic-update-slice_fusion.2.w0), channel_id=1, source_target_pairs={{0,128},{1,129},{4,132},{5,133},{8,136},{9,137},{12,140},{13,141},... | collective-permute-start | bytes 786440 | tf_op jit(solution)/shard_map/ppermute | solution.py:38
  34.9 1.3 collective-permute-start.7
  36.2 3.5 %collective-permute-done.9.w3 = bf16[128,1024]{1,0:T(8,128)(2,1)S(1)} collective-permute-done((bf16[128,1024]{1,0:T(8,128)(2,1)S(1)}, bf16[128,1024]{1,0:T(8,128)(2,1)S(1)}, u32[]{:S(2)}, u32[]{:S(2)}) %collective-permute-start.9) | collective-permute-done | bytes 262176 | tf_op jit(solution)/shard_map/ppermute | solution.py:38
  39.7 5.4 %collective-permute-done.8.w2 = bf16[128,1024]{1,0:T(8,128)(2,1)S(1)} collective-permute-done((bf16[128,1024]{1,0:T(8,128)(2,1)S(1)}, bf16[128,1024]{1,0:T(8,128)(2,1)S(1)}, u32[]{:S(2)}, u32[]{:S(2)}) %collective-permute-start.8) | collective-permute-done | bytes 262176 | tf_op jit(solution)/shard_map/ppermute | solution.py:38
  45.1 0.7 copy-done.4
  45.8 0.0 collective-permute-done.7.w1
  45.8 9.6 %all-to-all-done.rows_ref.own_ref = bf16[8,144,512]{2,1,0:T(8,128)(2,1)S(1)} async-done(((bf16[8,144,512]{2,1,0:T(8,128)(2,1)}), bf16[8,144,512]{2,1,0:T(8,128)(2,1)S(1)}, u32[]{:S(2)}, u32[]{:S(2)}) %all-to-all-start) | async-done | bytes 1179680 | tf_op jit(solution)/shard_map/all_to_all | solution.py:52
  55.4 0.1 fusion.10
  55.5 3.1 %collective-permute-start.12 = (bf16[4,128,512]{2,1,0:T(8,128)(2,1)S(1)}, bf16[4,128,512]{2,1,0:T(8,128)(2,1)S(1)}, u32[]{:S(2)}, u32[]{:S(2)}) collective-permute-start(bf16[4,128,512]{2,1,0:T(8,128)(2,1)S(1)} %get-tuple-element.16), channel_id=1, source_target_pairs={{0,192},{1,193},{4,196},{5,197},{8,200},{9,201},{12,204},{13,205},... | collective-permute-start | bytes 1572872 | tf_op jit(solution)/shard_map/ppermute | solution.py:38
  58.6 0.6 collective-permute-start.13
  59.2 2.7 %collective-permute-start.10 = (bf16[4,128,512]{2,1,0:T(8,128)(2,1)S(1)}, bf16[4,128,512]{2,1,0:T(8,128)(2,1)}, u32[]{:S(2)}, u32[]{:S(2)}) collective-permute-start(bf16[4,128,512]{2,1,0:T(8,128)(2,1)S(1)} %get-tuple-element.17), channel_id=1, source_target_pairs={{0,192},{1,193},{4,196},{5,197},{8,200},{9,201},{12,204},{13,205},... | collective-permute-start | bytes 1572872 | tf_op jit(solution)/shard_map/ppermute | solution.py:38
  61.9 11.9 %collective-permute-done.6.x2_ref = bf16[4,256,1024]{2,1,0:T(8,128)(2,1)} collective-permute-done((bf16[4,256,1024]{2,1,0:T(8,128)(2,1)S(1)}, bf16[4,256,1024]{2,1,0:T(8,128)(2,1)}, u32[]{:S(2)}, u32[]{:S(2)}) %collective-permute-start.6) | collective-permute-done | bytes 2097184 | tf_op jit(solution)/shard_map/ppermute | solution.py:43
  73.8 1.0 collective-permute-done.11.down_high_ref
  74.8 6.4 %collective-permute-done.13.down_low_ref = bf16[4,128,512]{2,1,0:T(8,128)(2,1)S(1)} collective-permute-done((bf16[4,128,512]{2,1,0:T(8,128)(2,1)S(1)}, bf16[4,128,512]{2,1,0:T(8,128)(2,1)S(1)}, u32[]{:S(2)}, u32[]{:S(2)}) %collective-permute-start.13) | collective-permute-done | bytes 524320 | tf_op jit(solution)/shard_map/ppermute | solution.py:38
  81.2 0.1 collective-permute-start.14
  81.3 0.7 copy-done.17
  82.0 3.2 %collective-permute-start.15 = (bf16[4,128,512]{2,1,0:T(8,128)(2,1)}, bf16[4,128,512]{2,1,0:T(8,128)(2,1)}, u32[]{:S(2)}, u32[]{:S(2)}) collective-permute-start(bf16[4,128,512]{2,1,0:T(8,128)(2,1)} %collective-permute-done.10.up_low_ref), channel_id=1, source_target_pairs={{0,192},{1,193},{4,196},{5,197},{8,200},{9,201},{12,204},{13,205},... | collective-permute-start | bytes 1572872 | tf_op jit(solution)/shard_map/ppermute | solution.py:38
  85.3 2.2 %shard_map.105 = bf16[8,64,128]{2,1,0:T(8,128)(2,1)} custom-call(bf16[8,144,512]{2,1,0:T(8,128)(2,1)} %copy-done, bf16[128,1024]{1,0:T(8,128)(2,1)} %copy-done.2, bf16[128,1024]{1,0:T(8,128)(2,1)} %collective-permute-done.7.w1, bf16[128,1024]{1,0:T(8,128)(2,1)} %copy-done.4, bf16[128,1024]{1,0:T(8,128)(2,1)} %copy-done.3), custom_call_target="tpu_custom_call" | custom-call | tf_op jit(solution)/shard_map/pallas_call | solution.py:269
  87.5 8.4 %all-to-all-start.1 = ((bf16[8,64,128]{2,1,0:T(8,128)(2,1)}), bf16[8,64,128]{2,1,0:T(8,128)(2,1)S(1)}, u32[]{:S(2)}, u32[]{:S(2)}) async-start(bf16[8,64,128]{2,1,0:T(8,128)(2,1)} %shard_map.105), calls=%async_computation.1 | async-start | bytes 262144 | tf_op jit(solution)/shard_map/all_to_all | solution.py:52
  95.9 7.6 %all-to-all-done.1.part_q_ref = bf16[8,64,128]{2,1,0:T(8,128)(2,1)S(1)} async-done(((bf16[8,64,128]{2,1,0:T(8,128)(2,1)}), bf16[8,64,128]{2,1,0:T(8,128)(2,1)S(1)}, u32[]{:S(2)}, u32[]{:S(2)}) %all-to-all-start.1) | async-done | bytes 131104 | tf_op jit(solution)/shard_map/all_to_all | solution.py:52
  103.5 0.6 copy-done.8
  104.2 13.1 %shard_map.106 = f32[4,8,128]{2,1,0:T(8,128)} custom-call(s32[3]{0:T(128)} %pad_add_fusion.at_ref, s32[2,2]{1,0:T(2,128)} %len_ref.3, bf16[4,256,1024]{2,1,0:T(8,128)(2,1)} %bitcast.26, bf16[4,256,1024]{2,1,0:T(8,128)(2,1)} %collective-permute-done.5.x1_ref, bf16[4,256,1024]{2,1,0:T(8,128)(2,1)} %collective-permute-done.6.x2_ref, ...), custom_call_target="tpu_custom_call" | custom-call | flops 4294967296 | bytes 12582912 | tf_op jit(solution)/shard_map/pallas_call | solution.py:287
  117.3 0.7 convert_bitcast_fusion
  118.1 0.1 broadcast_in_dim.25
  118.2 21.8 %all_to_all.15 = bf16[64,4,1024]{2,1,0:T(4,128)(2,1)S(1)} all-to-all(bf16[64,4,1024]{2,1,0:T(4,128)(2,1)S(1)} %broadcast_in_dim.25), channel_id=1, replica_groups=mesh['dp'=64,'tensor'=4] {'dp'}, dimensions={0} | all-to-all | bytes 1048576 | tf_op jit(solution)/shard_map/all_to_all | solution.py:52
  140.0 0.3 multiply_reduce_fusion
  140.3 0.1 reduce_sum.48
  140.4 0.1 copy.14
  140.5 0.2 reshape.33
  140.7 0.7 fusion.11
  141.4 0.3 fusion
  141.7 2.6 %collective-permute-start.18 = (f32[130,128]{1,0:T(8,128)S(1)}, f32[130,128]{1,0:T(8,128)S(1)}, u32[]{:S(2)}, u32[]{:S(2)}) collective-permute-start(f32[130,128]{1,0:T(8,128)S(1)} %pad_maximum_fusion), channel_id=1, source_target_pairs={{0,2},{1,3},{2,0},{3,1},{4,6},{5,7},{6,4},{7,5},{8,10},{9,11},{10,... | collective-permute-start | bytes 199688 | tf_op jit(solution)/shard_map/ppermute | solution.py:43
  144.3 1.1 collective-permute-start.17
  145.4 2.2 %collective-permute-done.18 = f32[130,128]{1,0:T(8,128)S(1)} collective-permute-done((f32[130,128]{1,0:T(8,128)S(1)}, f32[130,128]{1,0:T(8,128)S(1)}, u32[]{:S(2)}, u32[]{:S(2)}) %collective-permute-start.18) | collective-permute-done | bytes 66592 | tf_op jit(solution)/shard_map/ppermute | solution.py:43
  147.6 2.0 %collective-permute-done.19 = f32[130,128]{1,0:T(8,128)S(1)} collective-permute-done((f32[130,128]{1,0:T(8,128)S(1)}, f32[130,128]{1,0:T(8,128)S(1)}, u32[]{:S(2)}, u32[]{:S(2)}) %collective-permute-start.19) | collective-permute-done | bytes 66592 | tf_op jit(solution)/shard_map/ppermute | solution.py:43
  149.6 0.1 dynamic-slice_bitcast_fusion
  149.7 0.1 copy.15
  149.8 0.2 fusion.8
  150.0 0.2 exponential_reduce_fusion.1
  150.2 0.1 exponential_reduce_fusion
  150.3 0.6 fusion.9
  150.9 0.6 dynamic_slice.7
  151.5 0.7 multiply_convert_fusion
  (51 shorter events, 0.2 us)
Async XLA Ops:
  0.6 5.8 %copy-start.6 = (bf16[64,1024]{1,0:T(8,128)(2,1)S(1)}, bf16[64,1024]{1,0:T(8,128)(2,1)}, u32[]{:S(2)}) copy-start(bf16[64,1024]{1,0:T(8,128)(2,1)} %param.13) | copy-start | bytes 393220
  0.6 7.3 %copy-start.11 = (bf16[64,256]{1,0:T(8,128)(2,1)S(1)}, bf16[64,256]{1,0:T(8,128)(2,1)}, u32[]{:S(2)}) copy-start(bf16[64,256]{1,0:T(8,128)(2,1)} %param.14) | copy-start | bytes 98308
  0.7 7.3 %copy-start.12 = (bf16[64,256]{1,0:T(8,128)(2,1)S(1)}, bf16[64,256]{1,0:T(8,128)(2,1)}, u32[]{:S(2)}) copy-start(bf16[64,256]{1,0:T(8,128)(2,1)} %param.15) | copy-start | bytes 98308
  3.0 22.7 %copy-start.1 = (bf16[2,2,256,1024]{3,2,1,0:T(8,128)(2,1)S(1)}, bf16[2,2,256,1024]{3,2,1,0:T(8,128)(2,1)}, u32[]{:S(2)}) copy-start(bf16[2,2,256,1024]{3,2,1,0:T(8,128)(2,1)} %param.8) | copy-start | bytes 6291460
  3.0 6.3 %collective-permute-start.4 = (bf16[4,1024]{1,0:T(4,128)(2,1)}, bf16[4,1024]{1,0:T(4,128)(2,1)S(1)}, u32[]{:S(2)}, u32[]{:S(2)}) collective-permute-start(bf16[4,1024]{1,0:T(4,128)(2,1)} %shard_map.103.r0), channel_id=1, source_target_pairs={{0,3},{1,2},{2,1},{3,0},{4,7},{5,6},{6,5},{7,4},{8,11},{9,10},{10,... | collective-permute-start | bytes 24584 | tf_op jit(solution)/shard_map/ppermute | solution.py:43
  5.5 5.4 %collective-permute-start.3 = (bf16[4,1024]{1,0:T(4,128)(2,1)}, bf16[4,1024]{1,0:T(4,128)(2,1)S(1)}, u32[]{:S(2)}, u32[]{:S(2)}) collective-permute-start(bf16[4,1024]{1,0:T(4,128)(2,1)} %shard_map.103.r0), channel_id=1, source_target_pairs={{0,2},{1,3},{2,0},{3,1},{4,6},{5,7},{6,4},{7,5},{8,10},{9,11},{10,... | collective-permute-start | bytes 24584 | tf_op jit(solution)/shard_map/ppermute | solution.py:43
  6.2 4.7 %collective-permute-start.2 = (bf16[4,1024]{1,0:T(4,128)(2,1)}, bf16[4,1024]{1,0:T(4,128)(2,1)S(1)}, u32[]{:S(2)}, u32[]{:S(2)}) collective-permute-start(bf16[4,1024]{1,0:T(4,128)(2,1)} %shard_map.103.r0), channel_id=1, source_target_pairs={{0,1},{1,0},{2,3},{3,2},{4,5},{5,4},{6,7},{7,6},{8,9},{9,8},{10,11... | collective-permute-start | bytes 24584 | tf_op jit(solution)/shard_map/ppermute | solution.py:43
  6.4 10.0 %collective-permute-start.1 = (bf16[64,1024]{1,0:T(8,128)(2,1)S(1)}, bf16[64,1024]{1,0:T(8,128)(2,1)S(1)}, u32[]{:S(2)}, u32[]{:S(2)}) collective-permute-start(bf16[64,1024]{1,0:T(8,128)(2,1)S(1)} %copy-done.6), channel_id=1, source_target_pairs={{0,32},{4,36},{8,40},{12,44},{16,48},{20,52},{24,56},{28,60},{32,0... | collective-permute-start | bytes 393224 | tf_op jit(solution)/shard_map/ppermute | solution.py:48
  7.9 5.6 %copy-start.5 = (bf16[64,512]{1,0:T(8,128)(2,1)}, bf16[64,512]{1,0:T(8,128)(2,1)S(1)}, u32[]{:S(2)}) copy-start(bf16[64,512]{1,0:T(8,128)(2,1)S(1)} %constant_dynamic-update-slice_fusion.kv_ref) | copy-start | bytes 196612
  7.9 5.6 %collective-permute-start = (bf16[64,512]{1,0:T(8,128)(2,1)S(1)}, bf16[64,512]{1,0:T(8,128)(2,1)S(1)}, u32[]{:S(2)}, u32[]{:S(2)}) collective-permute-start(bf16[64,512]{1,0:T(8,128)(2,1)S(1)} %constant_dynamic-update-slice_fusion.kv_ref), channel_id=1, source_target_pairs={{0,32},{4,36},{8,40},{12,44},{16,48},{20,52},{24,56},{28,60},{32,0... | collective-permute-start | bytes 196616 | tf_op jit(solution)/shard_map/ppermute | solution.py:48
  9.2 4.3 %copy-start.13 = (bf16[4,1024]{1,0:T(4,128)(2,1)}, bf16[4,1024]{1,0:T(4,128)(2,1)S(1)}, u32[]{:S(2)}) copy-start(bf16[4,1024]{1,0:T(4,128)(2,1)S(1)} %collective-permute-done.4.r3) | copy-start | bytes 24580
  10.9 2.7 %copy-start.14 = (bf16[4,1024]{1,0:T(4,128)(2,1)}, bf16[4,1024]{1,0:T(4,128)(2,1)S(1)}, u32[]{:S(2)}) copy-start(bf16[4,1024]{1,0:T(4,128)(2,1)S(1)} %collective-permute-done.3.r2) | copy-start | bytes 24580
  10.9 2.7 %copy-start.15 = (bf16[4,1024]{1,0:T(4,128)(2,1)}, bf16[4,1024]{1,0:T(4,128)(2,1)S(1)}, u32[]{:S(2)}) copy-start(bf16[4,1024]{1,0:T(4,128)(2,1)S(1)} %collective-permute-done.2.r1) | copy-start | bytes 24580
  13.6 0.6 copy-start.9
  16.4 0.7 copy-start.7
  17.1 38.3 %all-to-all-start = ((bf16[8,144,512]{2,1,0:T(8,128)(2,1)}), bf16[8,144,512]{2,1,0:T(8,128)(2,1)S(1)}, u32[]{:S(2)}, u32[]{:S(2)}) async-start(bf16[8,144,512]{2,1,0:T(8,128)(2,1)} %shard_map.104), calls=%async_computation | async-start | bytes 2359296 | tf_op jit(solution)/shard_map/all_to_all | solution.py:52
  25.6 48.1 %collective-permute-start.6 = (bf16[4,256,1024]{2,1,0:T(8,128)(2,1)S(1)}, bf16[4,256,1024]{2,1,0:T(8,128)(2,1)}, u32[]{:S(2)}, u32[]{:S(2)}) collective-permute-start(bf16[4,256,1024]{2,1,0:T(8,128)(2,1)S(1)} %bitcast.27), channel_id=1, source_target_pairs={{0,2},{1,3},{2,0},{3,1},{4,6},{5,7},{6,4},{7,5},{8,10},{9,11},{10,... | collective-permute-start | bytes 6291464 | tf_op jit(solution)/shard_map/ppermute | solution.py:43
  30.3 55.0 %copy-start.2 = (bf16[128,1024]{1,0:T(8,128)(2,1)}, bf16[128,1024]{1,0:T(8,128)(2,1)S(1)}, u32[]{:S(2)}) copy-start(bf16[128,1024]{1,0:T(8,128)(2,1)S(1)} %constant_dynamic-update-slice_fusion.2.w0) | copy-start | bytes 786436
  30.3 9.4 %collective-permute-start.9 = (bf16[128,1024]{1,0:T(8,128)(2,1)S(1)}, bf16[128,1024]{1,0:T(8,128)(2,1)S(1)}, u32[]{:S(2)}, u32[]{:S(2)}) collective-permute-start(bf16[128,1024]{1,0:T(8,128)(2,1)S(1)} %constant_dynamic-update-slice_fusion.2.w0), channel_id=1, source_target_pairs={{0,64},{1,65},{4,68},{5,69},{8,72},{9,73},{12,76},{13,77},{16,80},... | collective-permute-start | bytes 786440 | tf_op jit(solution)/shard_map/ppermute | solution.py:38
  32.0 13.1 %collective-permute-start.8 = (bf16[128,1024]{1,0:T(8,128)(2,1)S(1)}, bf16[128,1024]{1,0:T(8,128)(2,1)S(1)}, u32[]{:S(2)}, u32[]{:S(2)}) collective-permute-start(bf16[128,1024]{1,0:T(8,128)(2,1)S(1)} %constant_dynamic-update-slice_fusion.2.w0), channel_id=1, source_target_pairs={{0,128},{1,129},{4,132},{5,133},{8,136},{9,137},{12,140},{13,141},... | collective-permute-start | bytes 786440 | tf_op jit(solution)/shard_map/ppermute | solution.py:38
  34.9 10.9 %collective-permute-start.7 = (bf16[128,1024]{1,0:T(8,128)(2,1)S(1)}, bf16[128,1024]{1,0:T(8,128)(2,1)}, u32[]{:S(2)}, u32[]{:S(2)}) collective-permute-start(bf16[128,1024]{1,0:T(8,128)(2,1)S(1)} %constant_dynamic-update-slice_fusion.2.w0), channel_id=1, source_target_pairs={{0,192},{1,193},{4,196},{5,197},{8,200},{9,201},{12,204},{13,205},... | collective-permute-start | bytes 786440 | tf_op jit(solution)/shard_map/ppermute | solution.py:38
  39.7 5.4 %copy-start.3 = (bf16[128,1024]{1,0:T(8,128)(2,1)}, bf16[128,1024]{1,0:T(8,128)(2,1)S(1)}, u32[]{:S(2)}) copy-start(bf16[128,1024]{1,0:T(8,128)(2,1)S(1)} %collective-permute-done.9.w3) | copy-start | bytes 786436
  45.1 0.7 copy-start.4
  55.4 29.8 %copy-start = (bf16[8,144,512]{2,1,0:T(8,128)(2,1)}, bf16[8,144,512]{2,1,0:T(8,128)(2,1)S(1)}, u32[]{:S(2)}) copy-start(bf16[8,144,512]{2,1,0:T(8,128)(2,1)S(1)} %all-to-all-done.rows_ref.own_ref) | copy-start | bytes 3538948
  55.5 18.2 %collective-permute-start.12 = (bf16[4,128,512]{2,1,0:T(8,128)(2,1)S(1)}, bf16[4,128,512]{2,1,0:T(8,128)(2,1)S(1)}, u32[]{:S(2)}, u32[]{:S(2)}) collective-permute-start(bf16[4,128,512]{2,1,0:T(8,128)(2,1)S(1)} %get-tuple-element.16), channel_id=1, source_target_pairs={{0,192},{1,193},{4,196},{5,197},{8,200},{9,201},{12,204},{13,205},... | collective-permute-start | bytes 1572872 | tf_op jit(solution)/shard_map/ppermute | solution.py:38
  58.6 16.2 %collective-permute-start.11 = (bf16[4,128,512]{2,1,0:T(8,128)(2,1)S(1)}, bf16[4,128,512]{2,1,0:T(8,128)(2,1)}, u32[]{:S(2)}, u32[]{:S(2)}) collective-permute-start(bf16[4,128,512]{2,1,0:T(8,128)(2,1)S(1)} %get-tuple-element.16), channel_id=1, source_target_pairs={{0,64},{1,65},{4,68},{5,69},{8,72},{9,73},{12,76},{13,77},{16,80},... | collective-permute-start | bytes 1572872 | tf_op jit(solution)/shard_map/ppermute | solution.py:38
  58.6 22.6 %collective-permute-start.13 = (bf16[4,128,512]{2,1,0:T(8,128)(2,1)S(1)}, bf16[4,128,512]{2,1,0:T(8,128)(2,1)S(1)}, u32[]{:S(2)}, u32[]{:S(2)}) collective-permute-start(bf16[4,128,512]{2,1,0:T(8,128)(2,1)S(1)} %get-tuple-element.17), channel_id=1, source_target_pairs={{0,64},{1,65},{4,68},{5,69},{8,72},{9,73},{12,76},{13,77},{16,80},... | collective-permute-start | bytes 1572872 | tf_op jit(solution)/shard_map/ppermute | solution.py:38
  59.2 22.0 %collective-permute-start.10 = (bf16[4,128,512]{2,1,0:T(8,128)(2,1)S(1)}, bf16[4,128,512]{2,1,0:T(8,128)(2,1)}, u32[]{:S(2)}, u32[]{:S(2)}) collective-permute-start(bf16[4,128,512]{2,1,0:T(8,128)(2,1)S(1)} %get-tuple-element.17), channel_id=1, source_target_pairs={{0,192},{1,193},{4,196},{5,197},{8,200},{9,201},{12,204},{13,205},... | collective-permute-start | bytes 1572872 | tf_op jit(solution)/shard_map/ppermute | solution.py:38
  73.8 22.1 %collective-permute-start.5 = (bf16[4,256,1024]{2,1,0:T(8,128)(2,1)S(1)}, bf16[4,256,1024]{2,1,0:T(8,128)(2,1)}, u32[]{:S(2)}, u32[]{:S(2)}) collective-permute-start(bf16[4,256,1024]{2,1,0:T(8,128)(2,1)S(1)} %bitcast.28), channel_id=1, source_target_pairs={{0,1},{1,0},{2,3},{3,2},{4,5},{5,4},{6,7},{7,6},{8,9},{9,8},{10,11... | collective-permute-start | bytes 6291464 | tf_op jit(solution)/shard_map/ppermute | solution.py:43
  73.8 7.4 %copy-start.16 = (bf16[4,128,512]{2,1,0:T(8,128)(2,1)}, bf16[4,128,512]{2,1,0:T(8,128)(2,1)S(1)}, u32[]{:S(2)}) copy-start(bf16[4,128,512]{2,1,0:T(8,128)(2,1)S(1)} %collective-permute-done.12.up_high_ref) | copy-start | bytes 1572868
  81.2 0.8 copy-start.17
  81.2 22.3 %collective-permute-start.14 = (bf16[4,256,1024]{2,1,0:T(8,128)(2,1)}, bf16[4,256,1024]{2,1,0:T(8,128)(2,1)}, u32[]{:S(2)}, u32[]{:S(2)}) collective-permute-start(bf16[4,256,1024]{2,1,0:T(8,128)(2,1)} %collective-permute-done.6.x2_ref), channel_id=1, source_target_pairs={{0,1},{1,0},{2,3},{3,2},{4,5},{5,4},{6,7},{7,6},{8,9},{9,8},{10,11... | collective-permute-start | bytes 6291464 | tf_op jit(solution)/shard_map/ppermute | solution.py:43
  82.0 21.5 %collective-permute-start.16 = (bf16[4,128,512]{2,1,0:T(8,128)(2,1)}, bf16[4,128,512]{2,1,0:T(8,128)(2,1)}, u32[]{:S(2)}, u32[]{:S(2)}) collective-permute-start(bf16[4,128,512]{2,1,0:T(8,128)(2,1)} %collective-permute-done.11.down_high_ref), channel_id=1, source_target_pairs={{0,64},{1,65},{4,68},{5,69},{8,72},{9,73},{12,76},{13,77},{16,80},... | collective-permute-start | bytes 1572872 | tf_op jit(solution)/shard_map/ppermute | solution.py:38
  82.0 21.5 %collective-permute-start.15 = (bf16[4,128,512]{2,1,0:T(8,128)(2,1)}, bf16[4,128,512]{2,1,0:T(8,128)(2,1)}, u32[]{:S(2)}, u32[]{:S(2)}) collective-permute-start(bf16[4,128,512]{2,1,0:T(8,128)(2,1)} %collective-permute-done.10.up_low_ref), channel_id=1, source_target_pairs={{0,192},{1,193},{4,196},{5,197},{8,200},{9,201},{12,204},{13,205},... | collective-permute-start | bytes 1572872 | tf_op jit(solution)/shard_map/ppermute | solution.py:38
  87.5 16.0 %all-to-all-start.1 = ((bf16[8,64,128]{2,1,0:T(8,128)(2,1)}), bf16[8,64,128]{2,1,0:T(8,128)(2,1)S(1)}, u32[]{:S(2)}, u32[]{:S(2)}) async-start(bf16[8,64,128]{2,1,0:T(8,128)(2,1)} %shard_map.105), calls=%async_computation.1 | async-start | bytes 262144 | tf_op jit(solution)/shard_map/all_to_all | solution.py:52
  103.5 0.7 copy-start.8
  140.3 5.1 %copy-start.10 = (f32[4,8,128]{2,1,0:T(8,128)S(1)}, f32[4,8,128]{2,1,0:T(8,128)}, u32[]{:S(2)}) copy-start(f32[4,8,128]{2,1,0:T(8,128)} %shard_map.106) | copy-start | bytes 49156
  141.7 5.9 %collective-permute-start.18 = (f32[130,128]{1,0:T(8,128)S(1)}, f32[130,128]{1,0:T(8,128)S(1)}, u32[]{:S(2)}, u32[]{:S(2)}) collective-permute-start(f32[130,128]{1,0:T(8,128)S(1)} %pad_maximum_fusion), channel_id=1, source_target_pairs={{0,2},{1,3},{2,0},{3,1},{4,6},{5,7},{6,4},{7,5},{8,10},{9,11},{10,... | collective-permute-start | bytes 199688 | tf_op jit(solution)/shard_map/ppermute | solution.py:43
  144.3 5.2 %collective-permute-start.19 = (f32[130,128]{1,0:T(8,128)S(1)}, f32[130,128]{1,0:T(8,128)S(1)}, u32[]{:S(2)}, u32[]{:S(2)}) collective-permute-start(f32[130,128]{1,0:T(8,128)S(1)} %pad_maximum_fusion), channel_id=1, source_target_pairs={{0,3},{1,2},{2,1},{3,0},{4,7},{5,6},{6,5},{7,4},{8,11},{9,10},{10,... | collective-permute-start | bytes 199688 | tf_op jit(solution)/shard_map/ppermute | solution.py:43
  144.3 5.2 %collective-permute-start.17 = (f32[130,128]{1,0:T(8,128)S(1)}, f32[130,128]{1,0:T(8,128)S(1)}, u32[]{:S(2)}, u32[]{:S(2)}) collective-permute-start(f32[130,128]{1,0:T(8,128)S(1)} %pad_maximum_fusion), channel_id=1, source_target_pairs={{0,1},{1,0},{2,3},{3,2},{4,5},{5,4},{6,7},{7,6},{8,9},{9,8},{10,11... | collective-permute-start | bytes 199688 | tf_op jit(solution)/shard_map/ppermute | solution.py:43

commit v6 on v3

--- a/solution.py
+++ b/solution.py
@@ -160,15 +160,11 @@
     @pl.when(seq == 0)
     def _():
         low = Z // 2
-        copies = []
-
-        def start(source, target):
-            copy = pltpu.make_async_copy(source, target, sem.at[len(copies)])
-            copy.start()
-            copies.append(copy)
-
-        tail = pl.ds(Y * XLO * rows, parts_ref.shape[1])
-        start(last_ref.at[:, tail, :], parts_ref)
+
+        def start(source, target, at):
+            pltpu.make_async_copy(source, target, sem.at[at]).start()
+
+        start(last_ref.at[:, pl.ds(Y * XLO * rows, parts_ref.shape[1]), :], parts_ref, 2)
         for step, halves in enumerate(
             [[own_ref], [up_ref], [far_low_ref, far_high_ref], [down_ref]]
         ):
@@ -178,16 +174,12 @@
                 for half, piece in enumerate(halves):
                     zs = pl.ds(half * low, piece.shape[0])
                     wk_at = wk_ref.at[y, x_lo_at ^ x, zs]
-                    start(piece.at[:, block, pl.ds(0, 2 * HEAD_DIM)], wk_at)
+                    start(piece.at[:, block, pl.ds(0, 2 * HEAD_DIM)], wk_at, 0)
                     wv_at = wv_ref.at[y, x_lo_at ^ x, zs, :, pl.ds(0, HEAD_DIM)]
-                    start(piece.at[:, block, pl.ds(2 * HEAD_DIM, HEAD_DIM)], wv_at)
+                    start(piece.at[:, block, pl.ds(2 * HEAD_DIM, HEAD_DIM)], wv_at, 1)
                 block = pl.ds((step * XLO + x) * rows, rows)
                 wv_at = wv_ref.at[y, x_lo_at ^ x, :, :, pl.ds(HEAD_DIM, HEAD_DIM)]
-                start(last_ref.at[:, block, :], wv_at)
-        for copy in copies:
-            copy.wait()
-        parts = jnp.sum(parts_ref[...].astype(jnp.float32), axis=0)
-        query_ref[...] = parts + pltpu.roll(parts, parts.shape[0] - 4, 0)
+                start(last_ref.at[:, block, :], wv_at, 1)
 
     squares = None
     for k in range(slices):
@@ -195,6 +187,14 @@
         part = jnp.sum(x * x, axis=-1, keepdims=True)
         squares = part if squares is None else squares + part
     scale = lax.rsqrt(squares / (slices * width) + EPS)
+
+    @pl.when(seq == 0)
+    def _():
+        for at, ref in enumerate([wk_ref, wv_ref, parts_ref]):
+            pltpu.make_async_copy(ref, ref, sem.at[at]).wait()
+        parts = jnp.sum(parts_ref[...].astype(jnp.float32), axis=0)
+        query_ref[...] = parts + pltpu.roll(parts, parts.shape[0] - 4, 0)
+
     key_proj = value_proj = None
     for k in range(slices):
         x = x_refs[k][0].astype(jnp.float32)
@@ -295,9 +295,9 @@
         + [
             pltpu.VMEM((Z, heads * 8, HEAD_DIM), jnp.bfloat16),
             pltpu.VMEM((heads * 8, HEAD_DIM), jnp.float32),
-            pltpu.SemaphoreType.DMA((1 + XLO * (3 * Y + 2),)),
+            pltpu.SemaphoreType.DMA((3,)),
         ],
-        compiler_params=pltpu.CompilerParams(vmem_limit_bytes=40 * 1024 * 1024),
+        compiler_params=pltpu.CompilerParams(vmem_limit_bytes=58 * 1024 * 1024),
         cost_estimate=pl.CostEstimate(
             flops=4 * seq_count * slots * model_width * kv_width,
             bytes_accessed=2 * seq_count * slots * model_width + 4 * model_width * kv_width,
@@ -346,9 +346,10 @@
     )
     rest = [rest] + [shift(rest, dy=-step) for step in range(1, Y)]
     partial_q = query_call(z_all, rest)
-    head = jnp.concatenate([array[:, :HEAD_DIM] for array in rest])
-
-    z_own = lax.optimization_barrier((z_all[:, : block.shape[0]], *rest))[0]
+    heads = [array[:, :HEAD_DIM] for array in rest]
+
+    z_own, *heads = lax.optimization_barrier((z_all[:, : block.shape[0]], *heads))
+    head = jnp.concatenate(heads)
     z_up = shift(z_own, dy=-1)
     z_down = shift(z_own, dy=1)
     far_low = shift(z_up[: Z // 2], dy=-1)

time: 152 us -> 148 us (0.974)
  local copies, waits for them, and re-layouts: 15.6 us -> 8.82 us
    ppermute x7, waiting for transfers between devices: 7.46 us -> 20.1 us  [shift(): return lax.ppermute(array, ('dp', 'tensor'), pairs)]
    all_to_all x2, waiting for transfers between devices: 21.8 us -> 9.52 us  [exchange(): lax.all_to_all(chunks, 'dp', split_axis=0, concat_axis=0, tiled=True, axi...]
    unnamed x44 -> x36, local copies, waits for them, and re-layouts: 7.11 us -> 2.05 us
    slice x4, local copies, waits for them, and re-layouts: 3.48 us -> 1.11 us  [the longest x1 1.1 us: body(): z_all[:, :block.shape[0]]]
  transfers between devices with their start and end apart: 21 -> 21, of which waited for: 9 -> 11; matrix products, arithmetic and copies ran while one was open for 7% -> 6% of each run, Pallas kernels for 3% -> 3%
where the time goes in v6:
time: 148 us
  waiting for transfers between devices  44.5 us (30%)
  starting transfers between devices  39.3 us (27%)
  blocking collectives  24.3 us (16%)
  Pallas kernels  19.2 us (13%)
  local copies, waits for them, and re-layouts  8.82 us (6%)
  other arithmetic  8.68 us (6%)
  between operations  2.66 us (2%)
    all_to_all x1, blocking collectives, exchange(): lax.all_to_all(chunks, 'dp', split_axis=0, concat_axis=0, tiled=True, axi...  24.3 us
    ppermute x7, waiting for transfers between devices, shift(): return lax.ppermute(array, ('dp', 'tensor'), pairs)  20.1 us
    ppermute x10, waiting for transfers between devices, swap_tensor(): return lax.ppermute(array, 'tensor', [(i, i ^ mask) for i in range(size)])  14.5 us
    all_to_all x2, starting transfers between devices, exchange(): lax.all_to_all(chunks, 'dp', split_axis=0, concat_axis=0, tiled=True, axi...  14.2 us
    pallas_call x1, Pallas kernels, kv_attend(): pl.pallas_call(kv_attend_kernel, grid=(seq_count,), in_specs=[SMEM, SMEM]...  13 us
    ppermute x7, starting transfers between devices, shift(): return lax.ppermute(array, ('dp', 'tensor'), pairs)  12.7 us
    ppermute x10, starting transfers between devices, swap_tensor(): return lax.ppermute(array, 'tensor', [(i, i ^ mask) for i in range(size)])  10.3 us
    all_to_all x2, waiting for transfers between devices, exchange(): lax.all_to_all(chunks, 'dp', split_axis=0, concat_axis=0, tiled=True, axi...  9.52 us
  transfers between devices with their start and end apart: 21, of which 11 were waited for; matrix products, arithmetic and copies ran while one was open for 6% of the time, Pallas kernels for 3%

profile of v6, /device:TPU:32, one launch (start us, length us, event | category | flops | bytes accessed | tf_op | source)
XLA Modules:
  0.0 147.7 jit_solution(14784808693718698310)
XLA Ops:
  0.7 2.3 %shard_map.103.r0 = bf16[4,1024]{1,0:T(4,128)(2,1)} custom-call(s32[2,2]{1,0:T(2,128)} %len_ref.3, bf16[4,256,1024]{2,1,0:T(8,128)(2,1)} %bitcast.25), custom_call_target="tpu_custom_call" | custom-call | tf_op jit(solution)/shard_map/pallas_call | solution.py:238
  3.0 2.5 %collective-permute-start.4 = (bf16[4,1024]{1,0:T(4,128)(2,1)}, bf16[4,1024]{1,0:T(4,128)(2,1)S(1)}, u32[]{:S(2)}, u32[]{:S(2)}) collective-permute-start(bf16[4,1024]{1,0:T(4,128)(2,1)} %shard_map.103.r0), channel_id=1, source_target_pairs={{0,3},{1,2},{2,1},{3,0},{4,7},{5,6},{6,5},{7,4},{8,11},{9,10},{10,... | collective-permute-start | bytes 24584 | tf_op jit(solution)/shard_map/ppermute | solution.py:43
  5.5 0.7 collective-permute-start.3
  6.2 0.2 collective-permute-start.2
  6.4 1.6 %collective-permute-start = (bf16[64,512]{1,0:T(8,128)(2,1)S(1)}, bf16[64,512]{1,0:T(8,128)(2,1)S(1)}, u32[]{:S(2)}, u32[]{:S(2)}) collective-permute-start(bf16[64,512]{1,0:T(8,128)(2,1)S(1)} %constant_dynamic-update-slice_fusion), channel_id=1, source_target_pairs={{0,32},{4,36},{8,40},{12,44},{16,48},{20,52},{24,56},{28,60},{32,0... | collective-permute-start | bytes 196616 | tf_op jit(solution)/shard_map/ppermute | solution.py:48
  8.0 0.5 collective-permute-start.1
  8.5 0.7 pad_add_fusion.at_ref
  9.2 1.7 %collective-permute-done.3.r2 = bf16[4,1024]{1,0:T(4,128)(2,1)S(1)} collective-permute-done((bf16[4,1024]{1,0:T(4,128)(2,1)}, bf16[4,1024]{1,0:T(4,128)(2,1)S(1)}, u32[]{:S(2)}, u32[]{:S(2)}) %collective-permute-start.3) | collective-permute-done | bytes 8224 | tf_op jit(solution)/shard_map/ppermute | solution.py:43
  10.9 0.6 copy-done.12
  11.5 0.0 copy-done.13
  11.5 1.7 %shard_map.104 = bf16[8,16,384]{2,1,0:T(8,128)(2,1)} custom-call(s32[3]{0:T(128)} %pad_add_fusion.at_ref, bf16[4,1024]{1,0:T(4,128)(2,1)} %shard_map.103.r0, bf16[4,1024]{1,0:T(4,128)(2,1)} %copy-done.13, bf16[4,1024]{1,0:T(4,128)(2,1)} %copy-done.12, bf16[4,1024]{1,0:T(4,128)(2,1)} %copy-done.11, f32[1,4096]{1,0:T(1,128)} %bitcast.30), custom_call_target="tpu_custom_call" | custom-call | tf_op jit(solution)/shard_map/pallas_call | solution.py:253
  13.2 0.4 collective-permute-done.1
  13.6 0.1 broadcast_in_dim.15
  13.7 2.0 %pad_maximum_fusion.1 = bf16[8,144,384]{2,1,0:T(8,128)(2,1)} fusion(bf16[8,16,384]{2,1,0:T(8,128)(2,1)} %shard_map.104, bf16[8,128,384]{2,1,0:T(8,128)(2,1)S(1)} %broadcast_in_dim.15), kind=kLoop, calls=%fused_computation.2 | loop fusion | flops 1769472 | bytes 1769472 | tf_op jit(solution)/shard_map/concatenate | solution.py:340
  15.7 8.6 %all-to-all-start = ((bf16[8,144,384]{2,1,0:T(8,128)(2,1)}), bf16[8,144,384]{2,1,0:T(8,128)(2,1)S(1)}, u32[]{:S(2)}, u32[]{:S(2)}) async-start(bf16[8,144,384]{2,1,0:T(8,128)(2,1)} %pad_maximum_fusion.1), calls=%async_computation | async-start | bytes 1769472 | tf_op jit(solution)/shard_map/all_to_all | solution.py:52
  24.3 2.9 %collective-permute-start.6 = (bf16[4,256,1024]{2,1,0:T(8,128)(2,1)S(1)}, bf16[4,256,1024]{2,1,0:T(8,128)(2,1)}, u32[]{:S(2)}, u32[]{:S(2)}) collective-permute-start(bf16[4,256,1024]{2,1,0:T(8,128)(2,1)S(1)} %bitcast.27), channel_id=1, source_target_pairs={{0,2},{1,3},{2,0},{3,1},{4,6},{5,7},{6,4},{7,5},{8,10},{9,11},{10,... | collective-permute-start | bytes 6291464 | tf_op jit(solution)/shard_map/ppermute | solution.py:43
  27.2 0.9 maximum_maximum_fusion.w0
  28.1 1.7 %collective-permute-start.9 = (bf16[128,1152]{1,0:T(8,128)(2,1)S(1)}, bf16[128,1152]{1,0:T(8,128)(2,1)S(1)}, u32[]{:S(2)}, u32[]{:S(2)}) collective-permute-start(bf16[128,1152]{1,0:T(8,128)(2,1)S(1)} %maximum_maximum_fusion.w0), channel_id=1, source_target_pairs={{0,64},{1,65},{4,68},{5,69},{8,72},{9,73},{12,76},{13,77},{16,80},... | collective-permute-start | bytes 884744 | tf_op jit(solution)/shard_map/ppermute | solution.py:38
  29.8 2.9 %collective-permute-start.8 = (bf16[128,1152]{1,0:T(8,128)(2,1)S(1)}, bf16[128,1152]{1,0:T(8,128)(2,1)S(1)}, u32[]{:S(2)}, u32[]{:S(2)}) collective-permute-start(bf16[128,1152]{1,0:T(8,128)(2,1)S(1)} %maximum_maximum_fusion.w0), channel_id=1, source_target_pairs={{0,128},{1,129},{4,132},{5,133},{8,136},{9,137},{12,140},{13,141},... | collective-permute-start | bytes 884744 | tf_op jit(solution)/shard_map/ppermute | solution.py:38
  32.7 1.3 collective-permute-start.7
  34.0 4.2 %collective-permute-done.9.w3 = bf16[128,1152]{1,0:T(8,128)(2,1)S(1)} collective-permute-done((bf16[128,1152]{1,0:T(8,128)(2,1)S(1)}, bf16[128,1152]{1,0:T(8,128)(2,1)S(1)}, u32[]{:S(2)}, u32[]{:S(2)}) %collective-permute-start.9) | collective-permute-done | bytes 294944 | tf_op jit(solution)/shard_map/ppermute | solution.py:38
  38.2 6.3 %collective-permute-done.8.w2 = bf16[128,1152]{1,0:T(8,128)(2,1)S(1)} collective-permute-done((bf16[128,1152]{1,0:T(8,128)(2,1)S(1)}, bf16[128,1152]{1,0:T(8,128)(2,1)S(1)}, u32[]{:S(2)}, u32[]{:S(2)}) %collective-permute-start.8) | collective-permute-done | bytes 294944 | tf_op jit(solution)/shard_map/ppermute | solution.py:38
  44.5 0.7 copy-done.4
  45.2 0.7 copy-done.5
  45.9 1.6 %all-to-all-done.rows_ref = bf16[8,144,384]{2,1,0:T(8,128)(2,1)S(1)} async-done(((bf16[8,144,384]{2,1,0:T(8,128)(2,1)}), bf16[8,144,384]{2,1,0:T(8,128)(2,1)S(1)}, u32[]{:S(2)}, u32[]{:S(2)}) %all-to-all-start) | async-done | bytes 884768 | tf_op jit(solution)/shard_map/all_to_all | solution.py:52
  47.6 1.1 slice.62.own_ref
  48.7 1.6 %collective-permute-start.11 = (bf16[8,128,384]{2,1,0:T(8,128)(2,1)}, bf16[8,128,384]{2,1,0:T(8,128)(2,1)}, u32[]{:S(2)}, u32[]{:S(2)}) collective-permute-start(bf16[8,128,384]{2,1,0:T(8,128)(2,1)} %slice.62.own_ref), channel_id=1, source_target_pairs={{0,64},{1,65},{4,68},{5,69},{8,72},{9,73},{12,76},{13,77},{16,80},... | collective-permute-start | bytes 2359304 | tf_op jit(solution)/shard_map/ppermute | solution.py:38
  50.3 1.7 %collective-permute-start.10 = (bf16[8,128,384]{2,1,0:T(8,128)(2,1)}, bf16[8,128,384]{2,1,0:T(8,128)(2,1)}, u32[]{:S(2)}, u32[]{:S(2)}) collective-permute-start(bf16[8,128,384]{2,1,0:T(8,128)(2,1)} %slice.62.own_ref), channel_id=1, source_target_pairs={{0,192},{1,193},{4,196},{5,197},{8,200},{9,201},{12,204},{13,205},... | collective-permute-start | bytes 2359304 | tf_op jit(solution)/shard_map/ppermute | solution.py:38
  51.9 1.4 slice.53
  53.3 2.3 %shard_map.105 = bf16[8,64,128]{2,1,0:T(8,128)(2,1)} custom-call(bf16[8,144,384]{2,1,0:T(8,128)(2,1)} %copy-done, bf16[128,1152]{1,0:T(8,128)(2,1)} %copy-done.2, bf16[128,1152]{1,0:T(8,128)(2,1)} %copy-done.5, bf16[128,1152]{1,0:T(8,128)(2,1)} %copy-done.4, bf16[128,1152]{1,0:T(8,128)(2,1)} %copy-done.3), custom_call_target="tpu_custom_call" | custom-call | tf_op jit(solution)/shard_map/pallas_call | solution.py:268
  55.6 0.1 broadcast_in_dim.17
  55.8 2.1 %pad_maximum_fusion = bf16[8,592,128]{2,1,0:T(8,128)(2,1)} fusion(bf16[8,16,128]{2,1,0:T(8,128)(2,1)} %collective-permute-done.15, bf16[8,64,128]{2,1,0:T(8,128)(2,1)} %shard_map.105, bf16[8,512,128]{2,1,0:T(8,128)(2,1)S(1)} %broadcast_in_dim.17), kind=kLoop, calls=%fused_computation | loop fusion | flops 3637248 | bytes 2424832 | tf_op jit(solution)/shard_map/concatenate | solution.py:361
  57.9 5.6 %all-to-all-start.1 = ((bf16[8,592,128]{2,1,0:T(8,128)(2,1)}), bf16[8,592,128]{2,1,0:T(8,128)(2,1)}, u32[]{:S(2)}, u32[]{:S(2)}) async-start(bf16[8,592,128]{2,1,0:T(8,128)(2,1)} %pad_maximum_fusion), calls=%async_computation.1 | async-start | bytes 2424832 | tf_op jit(solution)/shard_map/all_to_all | solution.py:52
  63.5 0.2 collective-permute-start.5
  63.7 8.5 %collective-permute-done.6.x2_ref = bf16[4,256,1024]{2,1,0:T(8,128)(2,1)} collective-permute-done((bf16[4,256,1024]{2,1,0:T(8,128)(2,1)S(1)}, bf16[4,256,1024]{2,1,0:T(8,128)(2,1)}, u32[]{:S(2)}, u32[]{:S(2)}) %collective-permute-start.6) | collective-permute-done | bytes 2097184 | tf_op jit(solution)/shard_map/ppermute | solution.py:43
  72.3 1.0 slice.69
  73.3 1.7 %collective-permute-start.14 = (bf16[4,128,384]{2,1,0:T(8,128)(2,1)S(1)}, bf16[4,128,384]{2,1,0:T(8,128)(2,1)S(1)}, u32[]{:S(2)}, u32[]{:S(2)}) collective-permute-start(bf16[4,128,384]{2,1,0:T(8,128)(2,1)S(1)} %slice.69), channel_id=1, source_target_pairs={{0,64},{1,65},{4,68},{5,69},{8,72},{9,73},{12,76},{13,77},{16,80},... | collective-permute-start | bytes 1179656 | tf_op jit(solution)/shard_map/ppermute | solution.py:38
  74.9 1.0 slice.68
  76.0 1.9 %collective-permute-start.13 = (bf16[4,128,384]{2,1,0:T(8,128)(2,1)S(1)}, bf16[4,128,384]{2,1,0:T(8,128)(2,1)S(1)}, u32[]{:S(2)}, u32[]{:S(2)}) collective-permute-start(bf16[4,128,384]{2,1,0:T(8,128)(2,1)S(1)} %slice.68), channel_id=1, source_target_pairs={{0,192},{1,193},{4,196},{5,197},{8,200},{9,201},{12,204},{13,205},... | collective-permute-start | bytes 1179656 | tf_op jit(solution)/shard_map/ppermute | solution.py:38
  77.9 8.3 %collective-permute-done.14.far_high_ref = bf16[4,128,384]{2,1,0:T(8,128)(2,1)S(1)} collective-permute-done((bf16[4,128,384]{2,1,0:T(8,128)(2,1)S(1)}, bf16[4,128,384]{2,1,0:T(8,128)(2,1)S(1)}, u32[]{:S(2)}, u32[]{:S(2)}) %collective-permute-start.14) | collective-permute-done | bytes 393248 | tf_op jit(solution)/shard_map/ppermute | solution.py:38
  86.2 1.3 collective-permute-done.13.far_low_ref
  87.5 7.9 %all-to-all-done.1.last_ref = bf16[8,592,128]{2,1,0:T(8,128)(2,1)} async-done(((bf16[8,592,128]{2,1,0:T(8,128)(2,1)}), bf16[8,592,128]{2,1,0:T(8,128)(2,1)}, u32[]{:S(2)}, u32[]{:S(2)}) %all-to-all-start.1) | async-done | bytes 1212448 | tf_op jit(solution)/shard_map/all_to_all | solution.py:52
  95.4 13.0 %shard_map.106 = f32[4,8,128]{2,1,0:T(8,128)} custom-call(s32[3]{0:T(128)} %pad_add_fusion.at_ref, s32[2,2]{1,0:T(2,128)} %len_ref.3, bf16[4,256,1024]{2,1,0:T(8,128)(2,1)} %bitcast.26, bf16[4,256,1024]{2,1,0:T(8,128)(2,1)} %copy-done.14, bf16[4,256,1024]{2,1,0:T(8,128)(2,1)} %collective-permute-done.6.x2_ref, ...), custom_call_target="tpu_custom_call" | custom-call | flops 4294967296 | bytes 12582912 | tf_op jit(solution)/shard_map/pallas_call | solution.py:285
  108.4 0.7 convert_bitcast_fusion
  109.1 0.1 broadcast_in_dim.39
  109.2 24.3 %all_to_all.15 = bf16[64,4,1024]{2,1,0:T(4,128)(2,1)S(1)} all-to-all(bf16[64,4,1024]{2,1,0:T(4,128)(2,1)S(1)} %broadcast_in_dim.39), channel_id=1, replica_groups=mesh['dp'=64,'tensor'=4] {'dp'}, dimensions={0} | all-to-all | bytes 1048576 | tf_op jit(solution)/shard_map/all_to_all | solution.py:52
  133.5 0.3 multiply_reduce_fusion
  133.9 0.1 reduce_sum.48
  133.9 0.1 copy.14
  134.0 0.2 reshape.35
  134.2 0.7 fusion.12
  135.0 0.3 fusion
  135.2 2.8 %collective-permute-start.17 = (f32[130,128]{1,0:T(8,128)S(1)}, f32[130,128]{1,0:T(8,128)S(1)}, u32[]{:S(2)}, u32[]{:S(2)}) collective-permute-start(f32[130,128]{1,0:T(8,128)S(1)} %pad_maximum_fusion.4), channel_id=1, source_target_pairs={{0,2},{1,3},{2,0},{3,1},{4,6},{5,7},{6,4},{7,5},{8,10},{9,11},{10,... | collective-permute-start | bytes 199688 | tf_op jit(solution)/shard_map/ppermute | solution.py:43
  138.1 0.9 collective-permute-start.16
  139.0 2.2 %collective-permute-done.17 = f32[130,128]{1,0:T(8,128)S(1)} collective-permute-done((f32[130,128]{1,0:T(8,128)S(1)}, f32[130,128]{1,0:T(8,128)S(1)}, u32[]{:S(2)}, u32[]{:S(2)}) %collective-permute-start.17) | collective-permute-done | bytes 66592 | tf_op jit(solution)/shard_map/ppermute | solution.py:43
  141.1 2.2 %collective-permute-done.18 = f32[130,128]{1,0:T(8,128)S(1)} collective-permute-done((f32[130,128]{1,0:T(8,128)S(1)}, f32[130,128]{1,0:T(8,128)S(1)}, u32[]{:S(2)}, u32[]{:S(2)}) %collective-permute-start.18) | collective-permute-done | bytes 66592 | tf_op jit(solution)/shard_map/ppermute | solution.py:43
  143.4 0.1 dynamic-slice_bitcast_fusion
  143.4 0.1 copy.15
  143.5 0.2 fusion.10
  143.7 0.2 exponential_reduce_fusion.1
  143.9 0.1 exponential_reduce_fusion
  144.0 0.6 fusion.11
  144.7 0.6 dynamic_slice.7
  145.2 0.7 multiply_convert_fusion
  (59 shorter events, 0.2 us)
Async XLA Ops:
  0.6 5.8 %copy-start.9 = (bf16[64,256]{1,0:T(8,128)(2,1)S(1)}, bf16[64,256]{1,0:T(8,128)(2,1)}, u32[]{:S(2)}) copy-start(bf16[64,256]{1,0:T(8,128)(2,1)} %param.14) | copy-start | bytes 98308
  0.6 5.8 %copy-start.10 = (bf16[64,256]{1,0:T(8,128)(2,1)S(1)}, bf16[64,256]{1,0:T(8,128)(2,1)}, u32[]{:S(2)}) copy-start(bf16[64,256]{1,0:T(8,128)(2,1)} %param.15) | copy-start | bytes 98308
  0.7 7.4 %copy-start.6 = (bf16[64,1024]{1,0:T(8,128)(2,1)S(1)}, bf16[64,1024]{1,0:T(8,128)(2,1)}, u32[]{:S(2)}) copy-start(bf16[64,1024]{1,0:T(8,128)(2,1)} %param.13) | copy-start | bytes 393220
  3.0 6.3 %collective-permute-start.4 = (bf16[4,1024]{1,0:T(4,128)(2,1)}, bf16[4,1024]{1,0:T(4,128)(2,1)S(1)}, u32[]{:S(2)}, u32[]{:S(2)}) collective-permute-start(bf16[4,1024]{1,0:T(4,128)(2,1)} %shard_map.103.r0), channel_id=1, source_target_pairs={{0,3},{1,2},{2,1},{3,0},{4,7},{5,6},{6,5},{7,4},{8,11},{9,10},{10,... | collective-permute-start | bytes 24584 | tf_op jit(solution)/shard_map/ppermute | solution.py:43
  5.5 5.4 %collective-permute-start.3 = (bf16[4,1024]{1,0:T(4,128)(2,1)}, bf16[4,1024]{1,0:T(4,128)(2,1)S(1)}, u32[]{:S(2)}, u32[]{:S(2)}) collective-permute-start(bf16[4,1024]{1,0:T(4,128)(2,1)} %shard_map.103.r0), channel_id=1, source_target_pairs={{0,2},{1,3},{2,0},{3,1},{4,6},{5,7},{6,4},{7,5},{8,10},{9,11},{10,... | collective-permute-start | bytes 24584 | tf_op jit(solution)/shard_map/ppermute | solution.py:43
  6.2 4.7 %collective-permute-start.2 = (bf16[4,1024]{1,0:T(4,128)(2,1)}, bf16[4,1024]{1,0:T(4,128)(2,1)S(1)}, u32[]{:S(2)}, u32[]{:S(2)}) collective-permute-start(bf16[4,1024]{1,0:T(4,128)(2,1)} %shard_map.103.r0), channel_id=1, source_target_pairs={{0,1},{1,0},{2,3},{3,2},{4,5},{5,4},{6,7},{7,6},{8,9},{9,8},{10,11... | collective-permute-start | bytes 24584 | tf_op jit(solution)/shard_map/ppermute | solution.py:43
  6.4 6.7 %collective-permute-start = (bf16[64,512]{1,0:T(8,128)(2,1)S(1)}, bf16[64,512]{1,0:T(8,128)(2,1)S(1)}, u32[]{:S(2)}, u32[]{:S(2)}) collective-permute-start(bf16[64,512]{1,0:T(8,128)(2,1)S(1)} %constant_dynamic-update-slice_fusion), channel_id=1, source_target_pairs={{0,32},{4,36},{8,40},{12,44},{16,48},{20,52},{24,56},{28,60},{32,0... | collective-permute-start | bytes 196616 | tf_op jit(solution)/shard_map/ppermute | solution.py:48
  8.0 5.6 %collective-permute-start.1 = (bf16[64,1024]{1,0:T(8,128)(2,1)S(1)}, bf16[64,1024]{1,0:T(8,128)(2,1)S(1)}, u32[]{:S(2)}, u32[]{:S(2)}) collective-permute-start(bf16[64,1024]{1,0:T(8,128)(2,1)S(1)} %copy-done.6), channel_id=1, source_target_pairs={{0,32},{4,36},{8,40},{12,44},{16,48},{20,52},{24,56},{28,60},{32,0... | collective-permute-start | bytes 393224 | tf_op jit(solution)/shard_map/ppermute | solution.py:48
  9.2 1.7 %copy-start.11 = (bf16[4,1024]{1,0:T(4,128)(2,1)}, bf16[4,1024]{1,0:T(4,128)(2,1)S(1)}, u32[]{:S(2)}) copy-start(bf16[4,1024]{1,0:T(4,128)(2,1)S(1)} %collective-permute-done.4.r3) | copy-start | bytes 24580
  10.9 0.6 copy-start.12
  10.9 0.6 copy-start.13
  13.1 11.1 %copy-start.1 = (bf16[2,2,256,1024]{3,2,1,0:T(8,128)(2,1)S(1)}, bf16[2,2,256,1024]{3,2,1,0:T(8,128)(2,1)}, u32[]{:S(2)}) copy-start(bf16[2,2,256,1024]{3,2,1,0:T(8,128)(2,1)} %param.8) | copy-start | bytes 6291460
  13.6 13.6 %copy-start.7 = (bf16[64,1024]{1,0:T(8,128)(2,1)}, bf16[64,1024]{1,0:T(8,128)(2,1)S(1)}, u32[]{:S(2)}) copy-start(bf16[64,1024]{1,0:T(8,128)(2,1)S(1)} %collective-permute-done.1) | copy-start | bytes 393220
  15.7 31.9 %all-to-all-start = ((bf16[8,144,384]{2,1,0:T(8,128)(2,1)}), bf16[8,144,384]{2,1,0:T(8,128)(2,1)S(1)}, u32[]{:S(2)}, u32[]{:S(2)}) async-start(bf16[8,144,384]{2,1,0:T(8,128)(2,1)} %pad_maximum_fusion.1), calls=%async_computation | async-start | bytes 1769472 | tf_op jit(solution)/shard_map/all_to_all | solution.py:52
  24.3 47.9 %collective-permute-start.6 = (bf16[4,256,1024]{2,1,0:T(8,128)(2,1)S(1)}, bf16[4,256,1024]{2,1,0:T(8,128)(2,1)}, u32[]{:S(2)}, u32[]{:S(2)}) collective-permute-start(bf16[4,256,1024]{2,1,0:T(8,128)(2,1)S(1)} %bitcast.27), channel_id=1, source_target_pairs={{0,2},{1,3},{2,0},{3,1},{4,6},{5,7},{6,4},{7,5},{8,10},{9,11},{10,... | collective-permute-start | bytes 6291464 | tf_op jit(solution)/shard_map/ppermute | solution.py:43
  28.1 25.2 %copy-start.2 = (bf16[128,1152]{1,0:T(8,128)(2,1)}, bf16[128,1152]{1,0:T(8,128)(2,1)S(1)}, u32[]{:S(2)}) copy-start(bf16[128,1152]{1,0:T(8,128)(2,1)S(1)} %maximum_maximum_fusion.w0) | copy-start | bytes 884740
  28.1 10.1 %collective-permute-start.9 = (bf16[128,1152]{1,0:T(8,128)(2,1)S(1)}, bf16[128,1152]{1,0:T(8,128)(2,1)S(1)}, u32[]{:S(2)}, u32[]{:S(2)}) collective-permute-start(bf16[128,1152]{1,0:T(8,128)(2,1)S(1)} %maximum_maximum_fusion.w0), channel_id=1, source_target_pairs={{0,64},{1,65},{4,68},{5,69},{8,72},{9,73},{12,76},{13,77},{16,80},... | collective-permute-start | bytes 884744 | tf_op jit(solution)/shard_map/ppermute | solution.py:38
  29.8 14.7 %collective-permute-start.8 = (bf16[128,1152]{1,0:T(8,128)(2,1)S(1)}, bf16[128,1152]{1,0:T(8,128)(2,1)S(1)}, u32[]{:S(2)}, u32[]{:S(2)}) collective-permute-start(bf16[128,1152]{1,0:T(8,128)(2,1)S(1)} %maximum_maximum_fusion.w0), channel_id=1, source_target_pairs={{0,128},{1,129},{4,132},{5,133},{8,136},{9,137},{12,140},{13,141},... | collective-permute-start | bytes 884744 | tf_op jit(solution)/shard_map/ppermute | solution.py:38
  32.7 11.8 %collective-permute-start.7 = (bf16[128,1152]{1,0:T(8,128)(2,1)S(1)}, bf16[128,1152]{1,0:T(8,128)(2,1)S(1)}, u32[]{:S(2)}, u32[]{:S(2)}) collective-permute-start(bf16[128,1152]{1,0:T(8,128)(2,1)S(1)} %maximum_maximum_fusion.w0), channel_id=1, source_target_pairs={{0,192},{1,193},{4,196},{5,197},{8,200},{9,201},{12,204},{13,205},... | collective-permute-start | bytes 884744 | tf_op jit(solution)/shard_map/ppermute | solution.py:38
  38.2 6.3 %copy-start.3 = (bf16[128,1152]{1,0:T(8,128)(2,1)}, bf16[128,1152]{1,0:T(8,128)(2,1)S(1)}, u32[]{:S(2)}) copy-start(bf16[128,1152]{1,0:T(8,128)(2,1)S(1)} %collective-permute-done.9.w3) | copy-start | bytes 884740
  44.5 0.7 copy-start.4
  45.2 0.7 copy-start.5
  47.6 5.8 %copy-start = (bf16[8,144,384]{2,1,0:T(8,128)(2,1)}, bf16[8,144,384]{2,1,0:T(8,128)(2,1)S(1)}, u32[]{:S(2)}) copy-start(bf16[8,144,384]{2,1,0:T(8,128)(2,1)S(1)} %all-to-all-done.rows_ref) | copy-start | bytes 2654212
  48.7 23.6 %collective-permute-start.11 = (bf16[8,128,384]{2,1,0:T(8,128)(2,1)}, bf16[8,128,384]{2,1,0:T(8,128)(2,1)}, u32[]{:S(2)}, u32[]{:S(2)}) collective-permute-start(bf16[8,128,384]{2,1,0:T(8,128)(2,1)} %slice.62.own_ref), channel_id=1, source_target_pairs={{0,64},{1,65},{4,68},{5,69},{8,72},{9,73},{12,76},{13,77},{16,80},... | collective-permute-start | bytes 2359304 | tf_op jit(solution)/shard_map/ppermute | solution.py:38
  50.3 22.0 %collective-permute-start.10 = (bf16[8,128,384]{2,1,0:T(8,128)(2,1)}, bf16[8,128,384]{2,1,0:T(8,128)(2,1)}, u32[]{:S(2)}, u32[]{:S(2)}) collective-permute-start(bf16[8,128,384]{2,1,0:T(8,128)(2,1)} %slice.62.own_ref), channel_id=1, source_target_pairs={{0,192},{1,193},{4,196},{5,197},{8,200},{9,201},{12,204},{13,205},... | collective-permute-start | bytes 2359304 | tf_op jit(solution)/shard_map/ppermute | solution.py:38
  53.3 2.3 %collective-permute-start.15 = (bf16[8,16,128]{2,1,0:T(8,128)(2,1)}, bf16[8,16,128]{2,1,0:T(8,128)(2,1)}, u32[]{:S(2)}, u32[]{:S(2)}) collective-permute-start(bf16[8,16,128]{2,1,0:T(8,128)(2,1)} %slice.53), channel_id=1, source_target_pairs={{0,1},{1,0},{2,3},{3,2},{4,5},{5,4},{6,7},{7,6},{8,9},{9,8},{10,11... | collective-permute-start | bytes 98312 | tf_op jit(solution)/shard_map/ppermute | solution.py:43
  57.9 37.5 %all-to-all-start.1 = ((bf16[8,592,128]{2,1,0:T(8,128)(2,1)}), bf16[8,592,128]{2,1,0:T(8,128)(2,1)}, u32[]{:S(2)}, u32[]{:S(2)}) async-start(bf16[8,592,128]{2,1,0:T(8,128)(2,1)} %pad_maximum_fusion), calls=%async_computation.1 | async-start | bytes 2424832 | tf_op jit(solution)/shard_map/all_to_all | solution.py:52
  63.5 14.4 %collective-permute-start.5 = (bf16[4,256,1024]{2,1,0:T(8,128)(2,1)S(1)}, bf16[4,256,1024]{2,1,0:T(8,128)(2,1)S(1)}, u32[]{:S(2)}, u32[]{:S(2)}) collective-permute-start(bf16[4,256,1024]{2,1,0:T(8,128)(2,1)S(1)} %bitcast.28), channel_id=1, source_target_pairs={{0,1},{1,0},{2,3},{3,2},{4,5},{5,4},{6,7},{7,6},{8,9},{9,8},{10,11... | collective-permute-start | bytes 6291464 | tf_op jit(solution)/shard_map/ppermute | solution.py:43
  72.2 23.1 %collective-permute-start.12 = (bf16[4,256,1024]{2,1,0:T(8,128)(2,1)}, bf16[4,256,1024]{2,1,0:T(8,128)(2,1)}, u32[]{:S(2)}, u32[]{:S(2)}) collective-permute-start(bf16[4,256,1024]{2,1,0:T(8,128)(2,1)} %collective-permute-done.6.x2_ref), channel_id=1, source_target_pairs={{0,1},{1,0},{2,3},{3,2},{4,5},{5,4},{6,7},{7,6},{8,9},{9,8},{10,11... | collective-permute-start | bytes 6291464 | tf_op jit(solution)/shard_map/ppermute | solution.py:43
  73.3 12.9 %collective-permute-start.14 = (bf16[4,128,384]{2,1,0:T(8,128)(2,1)S(1)}, bf16[4,128,384]{2,1,0:T(8,128)(2,1)S(1)}, u32[]{:S(2)}, u32[]{:S(2)}) collective-permute-start(bf16[4,128,384]{2,1,0:T(8,128)(2,1)S(1)} %slice.69), channel_id=1, source_target_pairs={{0,64},{1,65},{4,68},{5,69},{8,72},{9,73},{12,76},{13,77},{16,80},... | collective-permute-start | bytes 1179656 | tf_op jit(solution)/shard_map/ppermute | solution.py:38
  76.0 11.5 %collective-permute-start.13 = (bf16[4,128,384]{2,1,0:T(8,128)(2,1)S(1)}, bf16[4,128,384]{2,1,0:T(8,128)(2,1)S(1)}, u32[]{:S(2)}, u32[]{:S(2)}) collective-permute-start(bf16[4,128,384]{2,1,0:T(8,128)(2,1)S(1)} %slice.68), channel_id=1, source_target_pairs={{0,192},{1,193},{4,196},{5,197},{8,200},{9,201},{12,204},{13,205},... | collective-permute-start | bytes 1179656 | tf_op jit(solution)/shard_map/ppermute | solution.py:38
  77.9 8.3 %copy-start.14 = (bf16[4,256,1024]{2,1,0:T(8,128)(2,1)}, bf16[4,256,1024]{2,1,0:T(8,128)(2,1)S(1)}, u32[]{:S(2)}) copy-start(bf16[4,256,1024]{2,1,0:T(8,128)(2,1)S(1)} %collective-permute-done.5.x1_ref) | copy-start | bytes 6291460
  86.2 9.2 %copy-start.15 = (bf16[4,128,384]{2,1,0:T(8,128)(2,1)}, bf16[4,128,384]{2,1,0:T(8,128)(2,1)S(1)}, u32[]{:S(2)}) copy-start(bf16[4,128,384]{2,1,0:T(8,128)(2,1)S(1)} %collective-permute-done.14.far_high_ref) | copy-start | bytes 1179652
  87.5 7.9 %copy-start.16 = (bf16[4,128,384]{2,1,0:T(8,128)(2,1)}, bf16[4,128,384]{2,1,0:T(8,128)(2,1)S(1)}, u32[]{:S(2)}) copy-start(bf16[4,128,384]{2,1,0:T(8,128)(2,1)S(1)} %collective-permute-done.13.far_low_ref) | copy-start | bytes 1179652
  133.9 5.1 %copy-start.8 = (f32[4,8,128]{2,1,0:T(8,128)S(1)}, f32[4,8,128]{2,1,0:T(8,128)}, u32[]{:S(2)}) copy-start(f32[4,8,128]{2,1,0:T(8,128)} %shard_map.106) | copy-start | bytes 49156
  135.2 5.9 %collective-permute-start.17 = (f32[130,128]{1,0:T(8,128)S(1)}, f32[130,128]{1,0:T(8,128)S(1)}, u32[]{:S(2)}, u32[]{:S(2)}) collective-permute-start(f32[130,128]{1,0:T(8,128)S(1)} %pad_maximum_fusion.4), channel_id=1, source_target_pairs={{0,2},{1,3},{2,0},{3,1},{4,6},{5,7},{6,4},{7,5},{8,10},{9,11},{10,... | collective-permute-start | bytes 199688 | tf_op jit(solution)/shard_map/ppermute | solution.py:43
  138.1 5.2 %collective-permute-start.18 = (f32[130,128]{1,0:T(8,128)S(1)}, f32[130,128]{1,0:T(8,128)S(1)}, u32[]{:S(2)}, u32[]{:S(2)}) collective-permute-start(f32[130,128]{1,0:T(8,128)S(1)} %pad_maximum_fusion.4), channel_id=1, source_target_pairs={{0,3},{1,2},{2,1},{3,0},{4,7},{5,6},{6,5},{7,4},{8,11},{9,10},{10,... | collective-permute-start | bytes 199688 | tf_op jit(solution)/shard_map/ppermute | solution.py:43
  138.1 5.2 %collective-permute-start.16 = (f32[130,128]{1,0:T(8,128)S(1)}, f32[130,128]{1,0:T(8,128)S(1)}, u32[]{:S(2)}, u32[]{:S(2)}) collective-permute-start(f32[130,128]{1,0:T(8,128)S(1)} %pad_maximum_fusion.4), channel_id=1, source_target_pairs={{0,1},{1,0},{2,3},{3,2},{4,5},{5,4},{6,7},{7,6},{8,9},{9,8},{10,11... | collective-permute-start | bytes 199688 | tf_op jit(solution)/shard_map/ppermute | solution.py:43

commit v7 on v6

--- a/solution.py
+++ b/solution.py
@@ -106,7 +106,7 @@
     out_ref[...] = row_ref[...].astype(jnp.bfloat16)
 
 
-def query_kernel(rows_ref, w0, w1, w2, w3, out_ref, acc_ref):
+def second_payload_kernel(rows_ref, w0, w1, w2, w3, out_ref, acc_ref):
     depth, _ = w0.shape
     rows = rows_ref[...].astype(jnp.float32)
     total = None
@@ -123,7 +123,12 @@
     for head in range(both.shape[1] // HEAD_DIM):
         block = both[:, head * HEAD_DIM : (head + 1) * HEAD_DIM]
         acc_ref[:, head * 8 : (head + 1) * 8, :] = block.reshape(Z, 8, HEAD_DIM)
-    out_ref[...] = acc_ref[...].astype(jnp.bfloat16)
+    for z in range(Z):
+        for step, w_ref in enumerate([w0, w1, w2, w3]):
+            out_ref[z, step * depth : (step + 1) * depth, :] = w_ref[:, :HEAD_DIM]
+        tail = slice(Y * depth, Y * depth + acc_ref.shape[1])
+        out_ref[z, tail, :] = acc_ref[z].astype(jnp.bfloat16)
+        out_ref[z, tail.stop :, :] = jnp.zeros((16, HEAD_DIM), jnp.bfloat16)
 
 
 def kv_attend_kernel(
@@ -139,6 +144,7 @@
     far_low_ref,
     far_high_ref,
     last_ref,
+    corner_ref,
     gain_ref,
     qg_ref,
     kg_ref,
@@ -149,15 +155,16 @@
     query_ref,
     sem,
 ):
+    del corner_ref
     x_refs = [x0_ref, x1_ref, x2_ref, x3_ref]
-    _, slots, width = x0_ref.shape
+    per_step, slots, width = x0_ref.shape
     slices = len(x_refs)
     rows = width // (XLO * Z)
-    seq = pl.program_id(0)
+    step_at = pl.program_id(0)
     heads = out_ref.shape[1]
     y_at, x_lo_at, tensor_at = at_ref[0], at_ref[1], at_ref[2]
 
-    @pl.when(seq == 0)
+    @pl.when(step_at == 0)
     def _():
         low = Z // 2
 
@@ -183,12 +190,12 @@
 
     squares = None
     for k in range(slices):
-        x = x_refs[k][0].astype(jnp.float32)
+        x = x_refs[k][...].reshape(-1, width).astype(jnp.float32)
         part = jnp.sum(x * x, axis=-1, keepdims=True)
         squares = part if squares is None else squares + part
     scale = lax.rsqrt(squares / (slices * width) + EPS)
 
-    @pl.when(seq == 0)
+    @pl.when(step_at == 0)
     def _():
         for at, ref in enumerate([wk_ref, wv_ref, parts_ref]):
             pltpu.make_async_copy(ref, ref, sem.at[at]).wait()
@@ -197,7 +204,7 @@
 
     key_proj = value_proj = None
     for k in range(slices):
-        x = x_refs[k][0].astype(jnp.float32)
+        x = x_refs[k][...].reshape(-1, width).astype(jnp.float32)
         slice_at = tensor_at ^ k
         at = pl.ds(pl.multiple_of(slice_at * width, width), width)
         normed = (x * scale * gain_ref[:, at]).astype(jnp.bfloat16)
@@ -207,26 +214,30 @@
         vp = jnp.dot(normed, wv, preferred_element_type=jnp.float32)
         key_proj = kp if key_proj is None else key_proj + kp
         value_proj = vp if value_proj is None else value_proj + vp
-    query = query_ref[pl.ds(seq, heads, stride=8), :]
-    query = (rms_rows(query) * qg_ref[...]).astype(jnp.bfloat16)
     first = lax.broadcasted_iota(jnp.int32, (heads, 1), 0) < heads // 2
-    scores = []
+    positions = lax.broadcasted_iota(jnp.int32, (1, slots), 1)
+    keys = []
     for h in range(2):
         key = key_proj[:, h * HEAD_DIM : (h + 1) * HEAD_DIM]
-        key = (rms_rows(key) * kg_ref[...]).astype(jnp.bfloat16)
-        scores.append(
+        keys.append((rms_rows(key) * kg_ref[...]).astype(jnp.bfloat16))
+    value = value_proj.astype(jnp.bfloat16)
+    for j in range(per_step):
+        seq = step_at * per_step + j
+        own = slice(j * slots, (j + 1) * slots)
+        query = query_ref[pl.ds(seq, heads, stride=8), :]
+        query = (rms_rows(query) * qg_ref[...]).astype(jnp.bfloat16)
+        scores = [
             lax.dot_general(
-                query, key, (((1,), (1,)), ((), ())), preferred_element_type=jnp.float32
+                query, key[own], (((1,), (1,)), ((), ())), preferred_element_type=jnp.float32
             )
-        )
-    scores = jnp.where(first, scores[0], scores[1]) / math.sqrt(HEAD_DIM)
-    positions = lax.broadcasted_iota(jnp.int32, (1, slots), 1)
-    scores = jnp.where(positions < len_ref[seq >> 1, seq & 1], scores, -1e30)
-    expo = jnp.exp(scores - jnp.max(scores, axis=-1, keepdims=True))
-    weights = (expo / jnp.sum(expo, axis=-1, keepdims=True)).astype(jnp.bfloat16)
-    value = value_proj.astype(jnp.bfloat16)
-    mixed = jnp.dot(weights, value, preferred_element_type=jnp.float32)
-    out_ref[0] = jnp.where(first, mixed[:, :HEAD_DIM], mixed[:, HEAD_DIM:])
+            for key in keys
+        ]
+        scores = jnp.where(first, scores[0], scores[1]) / math.sqrt(HEAD_DIM)
+        scores = jnp.where(positions < len_ref[seq >> 1, seq & 1], scores, -1e30)
+        expo = jnp.exp(scores - jnp.max(scores, axis=-1, keepdims=True))
+        weights = (expo / jnp.sum(expo, axis=-1, keepdims=True)).astype(jnp.bfloat16)
+        mixed = jnp.dot(weights, value[own], preferred_element_type=jnp.float32)
+        out_ref[j] = jnp.where(first, mixed[:, :HEAD_DIM], mixed[:, HEAD_DIM:])
 
 
 SMEM = pl.BlockSpec(memory_space=pltpu.SMEM)
@@ -262,34 +273,36 @@
     )(at, *raw, gains)
 
 
-def query_call(z_all, rest):
-    shape = (Z, (rest[0].shape[1] // HEAD_DIM - 1) * 8, HEAD_DIM)
+def second_payload_call(z_all, rest):
+    depth, width = rest[0].shape
+    tail_rows = (width // HEAD_DIM - 1) * 8
     tail = z_all.shape[1] // 16 - 1
     return pl.pallas_call(
-        query_kernel,
+        second_payload_kernel,
         grid=(1,),
         in_specs=[pl.BlockSpec((Z, 16, z_all.shape[2]), lambda i: (0, tail, 0))]
         + [VMEM] * len(rest),
         out_specs=VMEM,
-        out_shape=jax.ShapeDtypeStruct(shape, jnp.bfloat16),
-        scratch_shapes=[pltpu.VMEM(shape, jnp.float32)],
+        out_shape=jax.ShapeDtypeStruct((Z, Y * depth + tail_rows + 16, HEAD_DIM), jnp.bfloat16),
+        scratch_shapes=[pltpu.VMEM((Z, tail_rows, HEAD_DIM), jnp.float32)],
     )(z_all, *rest)
 
 
-def kv_attend(at, lengths, slices, pieces, last, gains, heads, qg, kg):
+def kv_attend(at, lengths, slices, pieces, last, corner, gains, heads, qg, kg):
     seq_count, slots, width = slices[0].shape
     model_width = gains.size
     kv_width = 2 * HEAD_DIM
     rows = model_width // (Y * XLO * Z)
-    x_spec = pl.BlockSpec((1, slots, width), lambda seq: (seq, 0, 0))
+    per_step = 2
+    x_spec = pl.BlockSpec((per_step, slots, width), lambda step: (step, 0, 0))
     return pl.pallas_call(
         kv_attend_kernel,
-        grid=(seq_count,),
+        grid=(seq_count // per_step,),
         in_specs=[SMEM, SMEM]
         + [x_spec] * len(slices)
-        + [pl.BlockSpec(memory_space=pltpu.HBM)] * (len(pieces) + 1)
+        + [pl.BlockSpec(memory_space=pltpu.HBM)] * (len(pieces) + 2)
         + [VMEM] * 3,
-        out_specs=pl.BlockSpec((1, heads, HEAD_DIM), lambda seq: (seq, 0, 0)),
+        out_specs=pl.BlockSpec((per_step, heads, HEAD_DIM), lambda step: (step, 0, 0)),
         out_shape=jax.ShapeDtypeStruct((seq_count, heads, HEAD_DIM), jnp.float32),
         scratch_shapes=[pltpu.VMEM((Y, XLO, Z, rows, kv_width), jnp.bfloat16)] * 2
         + [
@@ -303,7 +316,7 @@
             bytes_accessed=2 * seq_count * slots * model_width + 4 * model_width * kv_width,
             transcendentals=seq_count * heads * slots,
         ),
-    )(at, lengths, *slices, *pieces, last, gains, qg, kg)
+    )(at, lengths, *slices, *pieces, last, corner, gains, qg, kg)
 
 
 def body(
@@ -345,24 +358,17 @@
         [kv_both[:, kv_width + HEAD_DIM :], jnp.concatenate([query_weight, query_other])], axis=1
     )
     rest = [rest] + [shift(rest, dy=-step) for step in range(1, Y)]
-    partial_q = query_call(z_all, rest)
-    heads = [array[:, :HEAD_DIM] for array in rest]
-
-    z_own, *heads = lax.optimization_barrier((z_all[:, : block.shape[0]], *heads))
-    head = jnp.concatenate(heads)
+
+    z_own = lax.optimization_barrier((z_all[:, : block.shape[0]], *rest))[0]
     z_up = shift(z_own, dy=-1)
     z_down = shift(z_own, dy=1)
     far_low = shift(z_up[: Z // 2], dy=-1)
     far_high = shift(z_down[Z // 2 :], dy=1)
     pieces = [z_own, z_up, z_down, far_low, far_high]
 
-    corner = swap_tensor(z_own[:, :16, :HEAD_DIM], 1)
-    last = exchange(
-        jnp.concatenate(
-            [jnp.broadcast_to(head[None], (Z,) + head.shape), partial_q, corner], axis=1
-        ),
-        Z_GROUPS,
-    )
+    corner = swap_tensor(z_own[0, :16], 1)
+    second, corner = lax.optimization_barrier((second_payload_call(z_all, rest), corner))
+    last = exchange(second, Z_GROUPS)
     far_peer = swap_tensor(lax.optimization_barrier((far, z_up, z_down))[0], 1)
 
     mixed = kv_attend(
@@ -371,6 +377,7 @@
         [own, peer, far, far_peer],
         pieces,
         last,
+        corner,
         gains,
         query_width // HEAD_DIM,
         q_norm_gain[None],

time: 148 us -> 146 us (0.986)
  other arithmetic: 8.68 us -> 5.63 us
  waiting for transfers between devices: 44.5 us -> 46.7 us
  local copies, waits for them, and re-layouts: 8.82 us -> 6.63 us
    ppermute x7, waiting for transfers between devices: 20.1 us -> 9.58 us  [shift(): return lax.ppermute(array, ('dp', 'tensor'), pairs)]
    all_to_all x2, waiting for transfers between devices: 9.52 us -> 19.8 us  [exchange(): lax.all_to_all(chunks, 'dp', split_axis=0, concat_axis=0, tiled=True, axi...]
    ppermute x10, waiting for transfers between devices: 14.5 us -> 16.8 us  [swap_tensor(): return lax.ppermute(array, 'tensor', [(i, i ^ mask) for i in range(size)])]
    concatenate x2 -> x0, other arithmetic: 2.15 us -> none  [the longest x1 2.14 us: body(): jnp.concatenate([jnp.broadcast_to(head[None], (Z,) + head.shape), partial...]
  transfers between devices with their start and end apart: 21 -> 21, of which waited for: 11 -> 9; matrix products, arithmetic and copies ran while one was open for 6% -> 3% of each run, Pallas kernels for 3% -> 3%
where the time goes in v7:
time: 146 us; the launch traced here: 145 us
  waiting for transfers between devices  46.7 us (32%)
  starting transfers between devices  39.5 us (27%)
  blocking collectives  24.5 us (17%)
  Pallas kernels  19.3 us (13%)
  local copies, waits for them, and re-layouts  6.63 us (5%)
  other arithmetic  5.63 us (4%)
  between operations  2.63 us (2%)
    all_to_all x1, blocking collectives, exchange(): lax.all_to_all(chunks, 'dp', split_axis=0, concat_axis=0, tiled=True, axi...  24.5 us
    all_to_all x2, waiting for transfers between devices, exchange(): lax.all_to_all(chunks, 'dp', split_axis=0, concat_axis=0, tiled=True, axi...  19.8 us
    ppermute x10, waiting for transfers between devices, swap_tensor(): return lax.ppermute(array, 'tensor', [(i, i ^ mask) for i in range(size)])  16.8 us
    all_to_all x2, starting transfers between devices, exchange(): lax.all_to_all(chunks, 'dp', split_axis=0, concat_axis=0, tiled=True, axi...  14.2 us
    ppermute x7, starting transfers between devices, shift(): return lax.ppermute(array, ('dp', 'tensor'), pairs)  12.8 us
    pallas_call x1, Pallas kernels, kv_attend(): pl.pallas_call(kv_attend_kernel, grid=(seq_count // per_step,), in_specs=...  12.6 us
    ppermute x10, starting transfers between devices, swap_tensor(): return lax.ppermute(array, 'tensor', [(i, i ^ mask) for i in range(size)])  10.4 us
    ppermute x7, waiting for transfers between devices, shift(): return lax.ppermute(array, ('dp', 'tensor'), pairs)  9.58 us
  transfers between devices with their start and end apart: 21, of which 9 were waited for; matrix products, arithmetic and copies ran while one was open for 3% of the time, Pallas kernels for 3%

profile of v7, /device:TPU:32, one launch (start us, length us, event | category | flops | bytes accessed | tf_op | source)
XLA Modules:
  0.0 145.1 jit_solution(1525829477915763630)
XLA Ops:
  0.7 2.3 %shard_map.103.r0 = bf16[4,1024]{1,0:T(4,128)(2,1)} custom-call(s32[2,2]{1,0:T(2,128)} %len_ref.3, bf16[4,256,1024]{2,1,0:T(8,128)(2,1)} %bitcast.27), custom_call_target="tpu_custom_call" | custom-call | tf_op jit(solution)/shard_map/pallas_call | solution.py:249
  3.0 2.5 %collective-permute-start.4 = (bf16[4,1024]{1,0:T(4,128)(2,1)}, bf16[4,1024]{1,0:T(4,128)(2,1)S(1)}, u32[]{:S(2)}, u32[]{:S(2)}) collective-permute-start(bf16[4,1024]{1,0:T(4,128)(2,1)} %shard_map.103.r0), channel_id=1, source_target_pairs={{0,3},{1,2},{2,1},{3,0},{4,7},{5,6},{6,5},{7,4},{8,11},{9,10},{10,... | collective-permute-start | bytes 24584 | tf_op jit(solution)/shard_map/ppermute | solution.py:43
  5.5 0.7 collective-permute-start.3
  6.2 0.2 collective-permute-start.2
  6.4 1.6 %collective-permute-start = (bf16[64,512]{1,0:T(8,128)(2,1)S(1)}, bf16[64,512]{1,0:T(8,128)(2,1)S(1)}, u32[]{:S(2)}, u32[]{:S(2)}) collective-permute-start(bf16[64,512]{1,0:T(8,128)(2,1)S(1)} %constant_dynamic-update-slice_fusion), channel_id=1, source_target_pairs={{0,32},{4,36},{8,40},{12,44},{16,48},{20,52},{24,56},{28,60},{32,0... | collective-permute-start | bytes 196616 | tf_op jit(solution)/shard_map/ppermute | solution.py:48
  8.0 0.5 collective-permute-start.1
  8.5 0.7 pad_add_fusion.at_ref
  9.2 1.7 %collective-permute-done.3.r2 = bf16[4,1024]{1,0:T(4,128)(2,1)S(1)} collective-permute-done((bf16[4,1024]{1,0:T(4,128)(2,1)}, bf16[4,1024]{1,0:T(4,128)(2,1)S(1)}, u32[]{:S(2)}, u32[]{:S(2)}) %collective-permute-start.3) | collective-permute-done | bytes 8224 | tf_op jit(solution)/shard_map/ppermute | solution.py:43
  10.9 0.0 collective-permute-done.2.r1
  10.9 0.6 copy-done.8
  11.5 0.0 copy-done.9
  11.5 1.7 %shard_map.104 = bf16[8,16,384]{2,1,0:T(8,128)(2,1)} custom-call(s32[3]{0:T(128)} %pad_add_fusion.at_ref, bf16[4,1024]{1,0:T(4,128)(2,1)} %shard_map.103.r0, bf16[4,1024]{1,0:T(4,128)(2,1)} %copy-done.9, bf16[4,1024]{1,0:T(4,128)(2,1)} %copy-done.8, bf16[4,1024]{1,0:T(4,128)(2,1)} %copy-done.7, f32[1,4096]{1,0:T(1,128)} %bitcast.32), custom_call_target="tpu_custom_call" | custom-call | tf_op jit(solution)/shard_map/pallas_call | solution.py:264
  13.2 0.4 collective-permute-done.1
  13.6 0.1 broadcast_in_dim.13
  13.7 0.0 copy-start.1
  13.7 2.1 %pad_maximum_fusion = bf16[8,144,384]{2,1,0:T(8,128)(2,1)} fusion(bf16[8,16,384]{2,1,0:T(8,128)(2,1)} %shard_map.104, bf16[8,128,384]{2,1,0:T(8,128)(2,1)S(1)} %broadcast_in_dim.13), kind=kLoop, calls=%fused_computation.1 | loop fusion | flops 1769472 | bytes 1769472 | tf_op jit(solution)/shard_map/concatenate | solution.py:353
  15.7 8.6 %all-to-all-start = ((bf16[8,144,384]{2,1,0:T(8,128)(2,1)}), bf16[8,144,384]{2,1,0:T(8,128)(2,1)S(1)}, u32[]{:S(2)}, u32[]{:S(2)}) async-start(bf16[8,144,384]{2,1,0:T(8,128)(2,1)} %pad_maximum_fusion), calls=%async_computation | async-start | bytes 1769472 | tf_op jit(solution)/shard_map/all_to_all | solution.py:52
  24.3 3.0 %collective-permute-start.6 = (bf16[4,256,1024]{2,1,0:T(8,128)(2,1)S(1)}, bf16[4,256,1024]{2,1,0:T(8,128)(2,1)}, u32[]{:S(2)}, u32[]{:S(2)}) collective-permute-start(bf16[4,256,1024]{2,1,0:T(8,128)(2,1)S(1)} %bitcast.29), channel_id=1, source_target_pairs={{0,2},{1,3},{2,0},{3,1},{4,6},{5,7},{6,4},{7,5},{8,10},{9,11},{10,... | collective-permute-start | bytes 6291464 | tf_op jit(solution)/shard_map/ppermute | solution.py:43
  27.4 1.7 %collective-permute-start.9 = (bf16[128,1152]{1,0:T(8,128)(2,1)S(1)}, bf16[128,1152]{1,0:T(8,128)(2,1)}, u32[]{:S(2)}, u32[]{:S(2)}) collective-permute-start(bf16[128,1152]{1,0:T(8,128)(2,1)S(1)} %maximum_maximum_fusion.w0), channel_id=1, source_target_pairs={{0,64},{1,65},{4,68},{5,69},{8,72},{9,73},{12,76},{13,77},{16,80},... | collective-permute-start | bytes 884744 | tf_op jit(solution)/shard_map/ppermute | solution.py:38
  29.0 2.9 %collective-permute-start.8 = (bf16[128,1152]{1,0:T(8,128)(2,1)S(1)}, bf16[128,1152]{1,0:T(8,128)(2,1)}, u32[]{:S(2)}, u32[]{:S(2)}) collective-permute-start(bf16[128,1152]{1,0:T(8,128)(2,1)S(1)} %maximum_maximum_fusion.w0), channel_id=1, source_target_pairs={{0,128},{1,129},{4,132},{5,133},{8,136},{9,137},{12,140},{13,141},... | collective-permute-start | bytes 884744 | tf_op jit(solution)/shard_map/ppermute | solution.py:38
  31.9 1.3 collective-permute-start.7
  33.3 14.3 %all-to-all-done.rows_ref = bf16[8,144,384]{2,1,0:T(8,128)(2,1)S(1)} async-done(((bf16[8,144,384]{2,1,0:T(8,128)(2,1)}), bf16[8,144,384]{2,1,0:T(8,128)(2,1)S(1)}, u32[]{:S(2)}, u32[]{:S(2)}) %all-to-all-start) | async-done | bytes 884768 | tf_op jit(solution)/shard_map/all_to_all | solution.py:52
  47.5 1.1 slice.50.own_ref
  48.6 1.7 %collective-permute-start.11 = (bf16[8,128,384]{2,1,0:T(8,128)(2,1)}, bf16[8,128,384]{2,1,0:T(8,128)(2,1)}, u32[]{:S(2)}, u32[]{:S(2)}) collective-permute-start(bf16[8,128,384]{2,1,0:T(8,128)(2,1)} %slice.50.own_ref), channel_id=1, source_target_pairs={{0,64},{1,65},{4,68},{5,69},{8,72},{9,73},{12,76},{13,77},{16,80},... | collective-permute-start | bytes 2359304 | tf_op jit(solution)/shard_map/ppermute | solution.py:38
  50.3 1.7 %collective-permute-start.10 = (bf16[8,128,384]{2,1,0:T(8,128)(2,1)}, bf16[8,128,384]{2,1,0:T(8,128)(2,1)}, u32[]{:S(2)}, u32[]{:S(2)}) collective-permute-start(bf16[8,128,384]{2,1,0:T(8,128)(2,1)} %slice.50.own_ref), channel_id=1, source_target_pairs={{0,192},{1,193},{4,196},{5,197},{8,200},{9,201},{12,204},{13,205},... | collective-permute-start | bytes 2359304 | tf_op jit(solution)/shard_map/ppermute | solution.py:38
  52.0 0.7 slice_bitcast_fusion
  52.7 0.0 collective-permute-start.15
  52.7 2.8 %shard_map.105 = bf16[8,592,128]{2,1,0:T(8,128)(2,1)} custom-call(bf16[8,144,384]{2,1,0:T(8,128)(2,1)} %copy-done, bf16[128,1152]{1,0:T(8,128)(2,1)} %copy-done.2, bf16[128,1152]{1,0:T(8,128)(2,1)} %collective-permute-done.7.w1, bf16[128,1152]{1,0:T(8,128)(2,1)} %collective-permute-done.8.w2, bf16[128,1152]{1,0:T(8,128)(2,1)} %collective-permute-done.9.w3), custom_call_target="tpu_custom_call" | custom-call | tf_op jit(solution)/shard_map/pallas_call | solution.py:280
  55.5 0.0 collective-permute-done.15.corner_ref
  55.5 5.6 %all-to-all-start.1 = ((bf16[8,592,128]{2,1,0:T(8,128)(2,1)}), bf16[8,592,128]{2,1,0:T(8,128)(2,1)}, u32[]{:S(2)}, u32[]{:S(2)}) async-start(bf16[8,592,128]{2,1,0:T(8,128)(2,1)} %shard_map.105), calls=%async_computation.1 | async-start | bytes 2424832 | tf_op jit(solution)/shard_map/all_to_all | solution.py:52
  61.1 0.2 collective-permute-start.5
  61.3 10.8 %collective-permute-done.6.x2_ref = bf16[4,256,1024]{2,1,0:T(8,128)(2,1)} collective-permute-done((bf16[4,256,1024]{2,1,0:T(8,128)(2,1)S(1)}, bf16[4,256,1024]{2,1,0:T(8,128)(2,1)}, u32[]{:S(2)}, u32[]{:S(2)}) %collective-permute-start.6) | collective-permute-done | bytes 2097184 | tf_op jit(solution)/shard_map/ppermute | solution.py:43
  72.2 0.0 collective-permute-done.11.down_ref
  72.2 0.0 collective-permute-done.10.up_ref
  72.2 1.0 slice.54
  73.3 1.7 %collective-permute-start.14 = (bf16[4,128,384]{2,1,0:T(8,128)(2,1)S(1)}, bf16[4,128,384]{2,1,0:T(8,128)(2,1)S(1)}, u32[]{:S(2)}, u32[]{:S(2)}) collective-permute-start(bf16[4,128,384]{2,1,0:T(8,128)(2,1)S(1)} %slice.54), channel_id=1, source_target_pairs={{0,64},{1,65},{4,68},{5,69},{8,72},{9,73},{12,76},{13,77},{16,80},... | collective-permute-start | bytes 1179656 | tf_op jit(solution)/shard_map/ppermute | solution.py:38
  74.9 1.0 slice.53
  76.0 1.9 %collective-permute-start.13 = (bf16[4,128,384]{2,1,0:T(8,128)(2,1)S(1)}, bf16[4,128,384]{2,1,0:T(8,128)(2,1)S(1)}, u32[]{:S(2)}, u32[]{:S(2)}) collective-permute-start(bf16[4,128,384]{2,1,0:T(8,128)(2,1)S(1)} %slice.53), channel_id=1, source_target_pairs={{0,192},{1,193},{4,196},{5,197},{8,200},{9,201},{12,204},{13,205},... | collective-permute-start | bytes 1179656 | tf_op jit(solution)/shard_map/ppermute | solution.py:38
  77.9 8.2 %collective-permute-done.14.far_high_ref = bf16[4,128,384]{2,1,0:T(8,128)(2,1)S(1)} collective-permute-done((bf16[4,128,384]{2,1,0:T(8,128)(2,1)S(1)}, bf16[4,128,384]{2,1,0:T(8,128)(2,1)S(1)}, u32[]{:S(2)}, u32[]{:S(2)}) %collective-permute-start.14) | collective-permute-done | bytes 393248 | tf_op jit(solution)/shard_map/ppermute | solution.py:38
  86.1 1.3 collective-permute-done.13.far_low_ref
  87.5 5.5 %all-to-all-done.1.last_ref = bf16[8,592,128]{2,1,0:T(8,128)(2,1)} async-done(((bf16[8,592,128]{2,1,0:T(8,128)(2,1)}), bf16[8,592,128]{2,1,0:T(8,128)(2,1)}, u32[]{:S(2)}, u32[]{:S(2)}) %all-to-all-start.1) | async-done | bytes 1212448 | tf_op jit(solution)/shard_map/all_to_all | solution.py:52
  93.0 0.0 collective-permute-done.12.x3_ref
  93.0 12.6 %shard_map.106 = f32[4,8,128]{2,1,0:T(8,128)} custom-call(s32[3]{0:T(128)} %pad_add_fusion.at_ref, s32[2,2]{1,0:T(2,128)} %len_ref.3, bf16[4,256,1024]{2,1,0:T(8,128)(2,1)} %bitcast.28, bf16[4,256,1024]{2,1,0:T(8,128)(2,1)} %copy-done.10, bf16[4,256,1024]{2,1,0:T(8,128)(2,1)} %collective-permute-done.6.x2_ref, ...), custom_call_target="tpu_custom_call" | custom-call | flops 4294967296 | bytes 12582912 | tf_op jit(solution)/shard_map/pallas_call | solution.py:298
  105.6 0.7 convert_bitcast_fusion
  106.3 0.1 broadcast_in_dim.32
  106.5 24.5 %all_to_all.15 = bf16[64,4,1024]{2,1,0:T(4,128)(2,1)S(1)} all-to-all(bf16[64,4,1024]{2,1,0:T(4,128)(2,1)S(1)} %broadcast_in_dim.32), channel_id=1, replica_groups=mesh['dp'=64,'tensor'=4] {'dp'}, dimensions={0} | all-to-all | bytes 1048576 | tf_op jit(solution)/shard_map/all_to_all | solution.py:52
  130.9 0.3 multiply_reduce_fusion
  131.3 0.1 reduce_sum.48
  131.4 0.1 copy.14
  131.4 0.2 reshape.34
  131.6 0.7 fusion.12
  132.4 0.3 fusion
  132.7 2.8 %collective-permute-start.17 = (f32[130,128]{1,0:T(8,128)S(1)}, f32[130,128]{1,0:T(8,128)S(1)}, u32[]{:S(2)}, u32[]{:S(2)}) collective-permute-start(f32[130,128]{1,0:T(8,128)S(1)} %pad_maximum_fusion.2), channel_id=1, source_target_pairs={{0,2},{1,3},{2,0},{3,1},{4,6},{5,7},{6,4},{7,5},{8,10},{9,11},{10,... | collective-permute-start | bytes 199688 | tf_op jit(solution)/shard_map/ppermute | solution.py:43
  135.5 0.9 collective-permute-start.16
  136.4 2.2 %collective-permute-done.17 = f32[130,128]{1,0:T(8,128)S(1)} collective-permute-done((f32[130,128]{1,0:T(8,128)S(1)}, f32[130,128]{1,0:T(8,128)S(1)}, u32[]{:S(2)}, u32[]{:S(2)}) %collective-permute-start.17) | collective-permute-done | bytes 66592 | tf_op jit(solution)/shard_map/ppermute | solution.py:43
  138.6 2.2 %collective-permute-done.18 = f32[130,128]{1,0:T(8,128)S(1)} collective-permute-done((f32[130,128]{1,0:T(8,128)S(1)}, f32[130,128]{1,0:T(8,128)S(1)}, u32[]{:S(2)}, u32[]{:S(2)}) %collective-permute-start.18) | collective-permute-done | bytes 66592 | tf_op jit(solution)/shard_map/ppermute | solution.py:43
  140.8 0.1 dynamic-slice_bitcast_fusion
  140.9 0.1 copy.15
  141.0 0.2 fusion.10
  141.1 0.2 exponential_reduce_fusion.1
  141.3 0.1 exponential_reduce_fusion
  141.5 0.6 fusion.11
  142.1 0.6 dynamic_slice.7
  142.7 0.7 multiply_convert_fusion
  (47 shorter events, 0.2 us)
Async XLA Ops:
  0.6 5.8 %copy-start.5 = (bf16[64,256]{1,0:T(8,128)(2,1)S(1)}, bf16[64,256]{1,0:T(8,128)(2,1)}, u32[]{:S(2)}) copy-start(bf16[64,256]{1,0:T(8,128)(2,1)} %param.14) | copy-start | bytes 98308
  0.6 5.8 %copy-start.6 = (bf16[64,256]{1,0:T(8,128)(2,1)S(1)}, bf16[64,256]{1,0:T(8,128)(2,1)}, u32[]{:S(2)}) copy-start(bf16[64,256]{1,0:T(8,128)(2,1)} %param.15) | copy-start | bytes 98308
  0.7 7.4 %copy-start.3 = (bf16[64,1024]{1,0:T(8,128)(2,1)S(1)}, bf16[64,1024]{1,0:T(8,128)(2,1)}, u32[]{:S(2)}) copy-start(bf16[64,1024]{1,0:T(8,128)(2,1)} %param.13) | copy-start | bytes 393220
  3.0 6.2 %collective-permute-start.4 = (bf16[4,1024]{1,0:T(4,128)(2,1)}, bf16[4,1024]{1,0:T(4,128)(2,1)S(1)}, u32[]{:S(2)}, u32[]{:S(2)}) collective-permute-start(bf16[4,1024]{1,0:T(4,128)(2,1)} %shard_map.103.r0), channel_id=1, source_target_pairs={{0,3},{1,2},{2,1},{3,0},{4,7},{5,6},{6,5},{7,4},{8,11},{9,10},{10,... | collective-permute-start | bytes 24584 | tf_op jit(solution)/shard_map/ppermute | solution.py:43
  5.5 5.4 %collective-permute-start.3 = (bf16[4,1024]{1,0:T(4,128)(2,1)}, bf16[4,1024]{1,0:T(4,128)(2,1)S(1)}, u32[]{:S(2)}, u32[]{:S(2)}) collective-permute-start(bf16[4,1024]{1,0:T(4,128)(2,1)} %shard_map.103.r0), channel_id=1, source_target_pairs={{0,2},{1,3},{2,0},{3,1},{4,6},{5,7},{6,4},{7,5},{8,10},{9,11},{10,... | collective-permute-start | bytes 24584 | tf_op jit(solution)/shard_map/ppermute | solution.py:43
  6.2 4.7 %collective-permute-start.2 = (bf16[4,1024]{1,0:T(4,128)(2,1)}, bf16[4,1024]{1,0:T(4,128)(2,1)S(1)}, u32[]{:S(2)}, u32[]{:S(2)}) collective-permute-start(bf16[4,1024]{1,0:T(4,128)(2,1)} %shard_map.103.r0), channel_id=1, source_target_pairs={{0,1},{1,0},{2,3},{3,2},{4,5},{5,4},{6,7},{7,6},{8,9},{9,8},{10,11... | collective-permute-start | bytes 24584 | tf_op jit(solution)/shard_map/ppermute | solution.py:43
  6.4 6.7 %collective-permute-start = (bf16[64,512]{1,0:T(8,128)(2,1)S(1)}, bf16[64,512]{1,0:T(8,128)(2,1)S(1)}, u32[]{:S(2)}, u32[]{:S(2)}) collective-permute-start(bf16[64,512]{1,0:T(8,128)(2,1)S(1)} %constant_dynamic-update-slice_fusion), channel_id=1, source_target_pairs={{0,32},{4,36},{8,40},{12,44},{16,48},{20,52},{24,56},{28,60},{32,0... | collective-permute-start | bytes 196616 | tf_op jit(solution)/shard_map/ppermute | solution.py:48
  8.0 5.6 %collective-permute-start.1 = (bf16[64,1024]{1,0:T(8,128)(2,1)S(1)}, bf16[64,1024]{1,0:T(8,128)(2,1)S(1)}, u32[]{:S(2)}, u32[]{:S(2)}) collective-permute-start(bf16[64,1024]{1,0:T(8,128)(2,1)S(1)} %copy-done.3), channel_id=1, source_target_pairs={{0,32},{4,36},{8,40},{12,44},{16,48},{20,52},{24,56},{28,60},{32,0... | collective-permute-start | bytes 393224 | tf_op jit(solution)/shard_map/ppermute | solution.py:48
  9.2 1.7 %copy-start.7 = (bf16[4,1024]{1,0:T(4,128)(2,1)}, bf16[4,1024]{1,0:T(4,128)(2,1)S(1)}, u32[]{:S(2)}) copy-start(bf16[4,1024]{1,0:T(4,128)(2,1)S(1)} %collective-permute-done.4.r3) | copy-start | bytes 24580
  10.9 0.6 copy-start.8
  10.9 0.6 copy-start.9
  13.7 10.6 %copy-start.1 = (bf16[2,2,256,1024]{3,2,1,0:T(8,128)(2,1)S(1)}, bf16[2,2,256,1024]{3,2,1,0:T(8,128)(2,1)}, u32[]{:S(2)}) copy-start(bf16[2,2,256,1024]{3,2,1,0:T(8,128)(2,1)} %param.8) | copy-start | bytes 6291460
  15.7 31.8 %all-to-all-start = ((bf16[8,144,384]{2,1,0:T(8,128)(2,1)}), bf16[8,144,384]{2,1,0:T(8,128)(2,1)S(1)}, u32[]{:S(2)}, u32[]{:S(2)}) async-start(bf16[8,144,384]{2,1,0:T(8,128)(2,1)} %pad_maximum_fusion), calls=%async_computation | async-start | bytes 1769472 | tf_op jit(solution)/shard_map/all_to_all | solution.py:52
  24.3 47.9 %collective-permute-start.6 = (bf16[4,256,1024]{2,1,0:T(8,128)(2,1)S(1)}, bf16[4,256,1024]{2,1,0:T(8,128)(2,1)}, u32[]{:S(2)}, u32[]{:S(2)}) collective-permute-start(bf16[4,256,1024]{2,1,0:T(8,128)(2,1)S(1)} %bitcast.29), channel_id=1, source_target_pairs={{0,2},{1,3},{2,0},{3,1},{4,6},{5,7},{6,4},{7,5},{8,10},{9,11},{10,... | collective-permute-start | bytes 6291464 | tf_op jit(solution)/shard_map/ppermute | solution.py:43
  27.4 25.3 %copy-start.2 = (bf16[128,1152]{1,0:T(8,128)(2,1)}, bf16[128,1152]{1,0:T(8,128)(2,1)S(1)}, u32[]{:S(2)}) copy-start(bf16[128,1152]{1,0:T(8,128)(2,1)S(1)} %maximum_maximum_fusion.w0) | copy-start | bytes 884740
  27.4 21.3 %collective-permute-start.9 = (bf16[128,1152]{1,0:T(8,128)(2,1)S(1)}, bf16[128,1152]{1,0:T(8,128)(2,1)}, u32[]{:S(2)}, u32[]{:S(2)}) collective-permute-start(bf16[128,1152]{1,0:T(8,128)(2,1)S(1)} %maximum_maximum_fusion.w0), channel_id=1, source_target_pairs={{0,64},{1,65},{4,68},{5,69},{8,72},{9,73},{12,76},{13,77},{16,80},... | collective-permute-start | bytes 884744 | tf_op jit(solution)/shard_map/ppermute | solution.py:38
  29.0 19.6 %collective-permute-start.8 = (bf16[128,1152]{1,0:T(8,128)(2,1)S(1)}, bf16[128,1152]{1,0:T(8,128)(2,1)}, u32[]{:S(2)}, u32[]{:S(2)}) collective-permute-start(bf16[128,1152]{1,0:T(8,128)(2,1)S(1)} %maximum_maximum_fusion.w0), channel_id=1, source_target_pairs={{0,128},{1,129},{4,132},{5,133},{8,136},{9,137},{12,140},{13,141},... | collective-permute-start | bytes 884744 | tf_op jit(solution)/shard_map/ppermute | solution.py:38
  31.9 16.7 %collective-permute-start.7 = (bf16[128,1152]{1,0:T(8,128)(2,1)S(1)}, bf16[128,1152]{1,0:T(8,128)(2,1)}, u32[]{:S(2)}, u32[]{:S(2)}) collective-permute-start(bf16[128,1152]{1,0:T(8,128)(2,1)S(1)} %maximum_maximum_fusion.w0), channel_id=1, source_target_pairs={{0,192},{1,193},{4,196},{5,197},{8,200},{9,201},{12,204},{13,205},... | collective-permute-start | bytes 884744 | tf_op jit(solution)/shard_map/ppermute | solution.py:38
  47.5 5.2 %copy-start = (bf16[8,144,384]{2,1,0:T(8,128)(2,1)}, bf16[8,144,384]{2,1,0:T(8,128)(2,1)S(1)}, u32[]{:S(2)}) copy-start(bf16[8,144,384]{2,1,0:T(8,128)(2,1)S(1)} %all-to-all-done.rows_ref) | copy-start | bytes 2654212
  48.6 23.6 %collective-permute-start.11 = (bf16[8,128,384]{2,1,0:T(8,128)(2,1)}, bf16[8,128,384]{2,1,0:T(8,128)(2,1)}, u32[]{:S(2)}, u32[]{:S(2)}) collective-permute-start(bf16[8,128,384]{2,1,0:T(8,128)(2,1)} %slice.50.own_ref), channel_id=1, source_target_pairs={{0,64},{1,65},{4,68},{5,69},{8,72},{9,73},{12,76},{13,77},{16,80},... | collective-permute-start | bytes 2359304 | tf_op jit(solution)/shard_map/ppermute | solution.py:38
  50.3 21.9 %collective-permute-start.10 = (bf16[8,128,384]{2,1,0:T(8,128)(2,1)}, bf16[8,128,384]{2,1,0:T(8,128)(2,1)}, u32[]{:S(2)}, u32[]{:S(2)}) collective-permute-start(bf16[8,128,384]{2,1,0:T(8,128)(2,1)} %slice.50.own_ref), channel_id=1, source_target_pairs={{0,192},{1,193},{4,196},{5,197},{8,200},{9,201},{12,204},{13,205},... | collective-permute-start | bytes 2359304 | tf_op jit(solution)/shard_map/ppermute | solution.py:38
  52.7 2.8 %collective-permute-start.15 = (bf16[16,384]{1,0:T(8,128)(2,1)S(1)}, bf16[16,384]{1,0:T(8,128)(2,1)S(1)}, u32[]{:S(2)}, u32[]{:S(2)}) collective-permute-start(bf16[16,384]{1,0:T(8,128)(2,1)S(1)} %slice_bitcast_fusion), channel_id=1, source_target_pairs={{0,1},{1,0},{2,3},{3,2},{4,5},{5,4},{6,7},{7,6},{8,9},{9,8},{10,11... | collective-permute-start | bytes 36872 | tf_op jit(solution)/shard_map/ppermute | solution.py:43
  55.5 20.4 %copy-start.13 = (bf16[16,384]{1,0:T(8,128)(2,1)}, bf16[16,384]{1,0:T(8,128)(2,1)S(1)}, u32[]{:S(2)}) copy-start(bf16[16,384]{1,0:T(8,128)(2,1)S(1)} %collective-permute-done.15.corner_ref) | copy-start | bytes 36868
  55.5 37.5 %all-to-all-start.1 = ((bf16[8,592,128]{2,1,0:T(8,128)(2,1)}), bf16[8,592,128]{2,1,0:T(8,128)(2,1)}, u32[]{:S(2)}, u32[]{:S(2)}) async-start(bf16[8,592,128]{2,1,0:T(8,128)(2,1)} %shard_map.105), calls=%async_computation.1 | async-start | bytes 2424832 | tf_op jit(solution)/shard_map/all_to_all | solution.py:52
  61.1 16.7 %collective-permute-start.5 = (bf16[4,256,1024]{2,1,0:T(8,128)(2,1)S(1)}, bf16[4,256,1024]{2,1,0:T(8,128)(2,1)S(1)}, u32[]{:S(2)}, u32[]{:S(2)}) collective-permute-start(bf16[4,256,1024]{2,1,0:T(8,128)(2,1)S(1)} %bitcast.30), channel_id=1, source_target_pairs={{0,1},{1,0},{2,3},{3,2},{4,5},{5,4},{6,7},{7,6},{8,9},{9,8},{10,11... | collective-permute-start | bytes 6291464 | tf_op jit(solution)/shard_map/ppermute | solution.py:43
  72.2 20.8 %collective-permute-start.12 = (bf16[4,256,1024]{2,1,0:T(8,128)(2,1)}, bf16[4,256,1024]{2,1,0:T(8,128)(2,1)}, u32[]{:S(2)}, u32[]{:S(2)}) collective-permute-start(bf16[4,256,1024]{2,1,0:T(8,128)(2,1)} %collective-permute-done.6.x2_ref), channel_id=1, source_target_pairs={{0,1},{1,0},{2,3},{3,2},{4,5},{5,4},{6,7},{7,6},{8,9},{9,8},{10,11... | collective-permute-start | bytes 6291464 | tf_op jit(solution)/shard_map/ppermute | solution.py:43
  73.3 12.9 %collective-permute-start.14 = (bf16[4,128,384]{2,1,0:T(8,128)(2,1)S(1)}, bf16[4,128,384]{2,1,0:T(8,128)(2,1)S(1)}, u32[]{:S(2)}, u32[]{:S(2)}) collective-permute-start(bf16[4,128,384]{2,1,0:T(8,128)(2,1)S(1)} %slice.54), channel_id=1, source_target_pairs={{0,64},{1,65},{4,68},{5,69},{8,72},{9,73},{12,76},{13,77},{16,80},... | collective-permute-start | bytes 1179656 | tf_op jit(solution)/shard_map/ppermute | solution.py:38
  76.0 11.5 %collective-permute-start.13 = (bf16[4,128,384]{2,1,0:T(8,128)(2,1)S(1)}, bf16[4,128,384]{2,1,0:T(8,128)(2,1)S(1)}, u32[]{:S(2)}, u32[]{:S(2)}) collective-permute-start(bf16[4,128,384]{2,1,0:T(8,128)(2,1)S(1)} %slice.53), channel_id=1, source_target_pairs={{0,192},{1,193},{4,196},{5,197},{8,200},{9,201},{12,204},{13,205},... | collective-permute-start | bytes 1179656 | tf_op jit(solution)/shard_map/ppermute | solution.py:38
  77.9 8.2 %copy-start.10 = (bf16[4,256,1024]{2,1,0:T(8,128)(2,1)}, bf16[4,256,1024]{2,1,0:T(8,128)(2,1)S(1)}, u32[]{:S(2)}) copy-start(bf16[4,256,1024]{2,1,0:T(8,128)(2,1)S(1)} %collective-permute-done.5.x1_ref) | copy-start | bytes 6291460
  86.1 6.9 %copy-start.11 = (bf16[4,128,384]{2,1,0:T(8,128)(2,1)}, bf16[4,128,384]{2,1,0:T(8,128)(2,1)S(1)}, u32[]{:S(2)}) copy-start(bf16[4,128,384]{2,1,0:T(8,128)(2,1)S(1)} %collective-permute-done.14.far_high_ref) | copy-start | bytes 1179652
  87.5 5.5 %copy-start.12 = (bf16[4,128,384]{2,1,0:T(8,128)(2,1)}, bf16[4,128,384]{2,1,0:T(8,128)(2,1)S(1)}, u32[]{:S(2)}) copy-start(bf16[4,128,384]{2,1,0:T(8,128)(2,1)S(1)} %collective-permute-done.13.far_low_ref) | copy-start | bytes 1179652
  131.4 5.0 %copy-start.4 = (f32[4,8,128]{2,1,0:T(8,128)S(1)}, f32[4,8,128]{2,1,0:T(8,128)}, u32[]{:S(2)}) copy-start(f32[4,8,128]{2,1,0:T(8,128)} %shard_map.106) | copy-start | bytes 49156
  132.7 5.9 %collective-permute-start.17 = (f32[130,128]{1,0:T(8,128)S(1)}, f32[130,128]{1,0:T(8,128)S(1)}, u32[]{:S(2)}, u32[]{:S(2)}) collective-permute-start(f32[130,128]{1,0:T(8,128)S(1)} %pad_maximum_fusion.2), channel_id=1, source_target_pairs={{0,2},{1,3},{2,0},{3,1},{4,6},{5,7},{6,4},{7,5},{8,10},{9,11},{10,... | collective-permute-start | bytes 199688 | tf_op jit(solution)/shard_map/ppermute | solution.py:43
  135.5 5.2 %collective-permute-start.18 = (f32[130,128]{1,0:T(8,128)S(1)}, f32[130,128]{1,0:T(8,128)S(1)}, u32[]{:S(2)}, u32[]{:S(2)}) collective-permute-start(f32[130,128]{1,0:T(8,128)S(1)} %pad_maximum_fusion.2), channel_id=1, source_target_pairs={{0,3},{1,2},{2,1},{3,0},{4,7},{5,6},{6,5},{7,4},{8,11},{9,10},{10,... | collective-permute-start | bytes 199688 | tf_op jit(solution)/shard_map/ppermute | solution.py:43
  135.5 5.2 %collective-permute-start.16 = (f32[130,128]{1,0:T(8,128)S(1)}, f32[130,128]{1,0:T(8,128)S(1)}, u32[]{:S(2)}, u32[]{:S(2)}) collective-permute-start(f32[130,128]{1,0:T(8,128)S(1)} %pad_maximum_fusion.2), channel_id=1, source_target_pairs={{0,1},{1,0},{2,3},{3,2},{4,5},{5,4},{6,7},{7,6},{8,9},{9,8},{10,11... | collective-permute-start | bytes 199688 | tf_op jit(solution)/shard_map/ppermute | solution.py:43

commit v8 on v7

--- a/solution.py
+++ b/solution.py
@@ -153,6 +153,7 @@
     wv_ref,
     parts_ref,
     query_ref,
+    normed_ref,
     sem,
 ):
     del corner_ref
@@ -171,22 +172,26 @@
         def start(source, target, at):
             pltpu.make_async_copy(source, target, sem.at[at]).start()
 
+        sources = [[own_ref], [up_ref], [far_low_ref, far_high_ref], [down_ref]]
+        for values in range(2):
+            for step, halves in enumerate(sources):
+                y = (y_at + step) & (Y - 1)
+                for x in range(XLO):
+                    block = pl.ds(x * rows, rows)
+                    for half, piece in enumerate(halves):
+                        zs = pl.ds(half * low, piece.shape[0])
+                        if values:
+                            columns = pl.ds(2 * HEAD_DIM, HEAD_DIM)
+                            target = wv_ref.at[y, x_lo_at ^ x, zs, :, pl.ds(0, HEAD_DIM)]
+                        else:
+                            columns = pl.ds(0, 2 * HEAD_DIM)
+                            target = wk_ref.at[y, x_lo_at ^ x, zs]
+                        start(piece.at[:, block, columns], target, values)
+                    if values:
+                        block = pl.ds((step * XLO + x) * rows, rows)
+                        target = wv_ref.at[y, x_lo_at ^ x, :, :, pl.ds(HEAD_DIM, HEAD_DIM)]
+                        start(last_ref.at[:, block, :], target, values)
         start(last_ref.at[:, pl.ds(Y * XLO * rows, parts_ref.shape[1]), :], parts_ref, 2)
-        for step, halves in enumerate(
-            [[own_ref], [up_ref], [far_low_ref, far_high_ref], [down_ref]]
-        ):
-            y = (y_at + step) & (Y - 1)
-            for x in range(XLO):
-                block = pl.ds(x * rows, rows)
-                for half, piece in enumerate(halves):
-                    zs = pl.ds(half * low, piece.shape[0])
-                    wk_at = wk_ref.at[y, x_lo_at ^ x, zs]
-                    start(piece.at[:, block, pl.ds(0, 2 * HEAD_DIM)], wk_at, 0)
-                    wv_at = wv_ref.at[y, x_lo_at ^ x, zs, :, pl.ds(0, HEAD_DIM)]
-                    start(piece.at[:, block, pl.ds(2 * HEAD_DIM, HEAD_DIM)], wv_at, 1)
-                block = pl.ds((step * XLO + x) * rows, rows)
-                wv_at = wv_ref.at[y, x_lo_at ^ x, :, :, pl.ds(HEAD_DIM, HEAD_DIM)]
-                start(last_ref.at[:, block, :], wv_at, 1)
 
     squares = None
     for k in range(slices):
@@ -197,10 +202,7 @@
 
     @pl.when(step_at == 0)
     def _():
-        for at, ref in enumerate([wk_ref, wv_ref, parts_ref]):
-            pltpu.make_async_copy(ref, ref, sem.at[at]).wait()
-        parts = jnp.sum(parts_ref[...].astype(jnp.float32), axis=0)
-        query_ref[...] = parts + pltpu.roll(parts, parts.shape[0] - 4, 0)
+        pltpu.make_async_copy(wk_ref, wk_ref, sem.at[0]).wait()
 
     key_proj = value_proj = None
     for k in range(slices):
@@ -208,12 +210,22 @@
         slice_at = tensor_at ^ k
         at = pl.ds(pl.multiple_of(slice_at * width, width), width)
         normed = (x * scale * gain_ref[:, at]).astype(jnp.bfloat16)
+        normed_ref[k] = normed
         wk = wk_ref[slice_at].reshape(width, -1)
-        wv = wv_ref[slice_at].reshape(width, -1)
-        kp = jnp.dot(normed, wk, preferred_element_type=jnp.float32)
-        vp = jnp.dot(normed, wv, preferred_element_type=jnp.float32)
-        key_proj = kp if key_proj is None else key_proj + kp
-        value_proj = vp if value_proj is None else value_proj + vp
+        part = jnp.dot(normed, wk, preferred_element_type=jnp.float32)
+        key_proj = part if key_proj is None else key_proj + part
+
+    @pl.when(step_at == 0)
+    def _():
+        pltpu.make_async_copy(wv_ref, wv_ref, sem.at[1]).wait()
+        pltpu.make_async_copy(parts_ref, parts_ref, sem.at[2]).wait()
+        parts = jnp.sum(parts_ref[...].astype(jnp.float32), axis=0)
+        query_ref[...] = parts + pltpu.roll(parts, parts.shape[0] - 4, 0)
+
+    for k in range(slices):
+        wv = wv_ref[tensor_at ^ k].reshape(width, -1)
+        part = jnp.dot(normed_ref[k], wv, preferred_element_type=jnp.float32)
+        value_proj = part if value_proj is None else value_proj + part
     first = lax.broadcasted_iota(jnp.int32, (heads, 1), 0) < heads // 2
     positions = lax.broadcasted_iota(jnp.int32, (1, slots), 1)
     keys = []
@@ -308,6 +320,7 @@
         + [
             pltpu.VMEM((Z, heads * 8, HEAD_DIM), jnp.bfloat16),
             pltpu.VMEM((heads * 8, HEAD_DIM), jnp.float32),
+            pltpu.VMEM((len(slices), per_step * slots, width), jnp.bfloat16),
             pltpu.SemaphoreType.DMA((3,)),
         ],
         compiler_params=pltpu.CompilerParams(vmem_limit_bytes=58 * 1024 * 1024),
@@ -348,11 +361,9 @@
 
     block = kv_both[:, : kv_width + HEAD_DIM]
     rows = last_rows_call(at, last_raw, gains)
-    rows, _ = lax.optimization_barrier((rows, query_other))
-    z_all = exchange(
-        jnp.concatenate([jnp.broadcast_to(block[None], (Z,) + block.shape), rows], axis=1),
-        Z_GROUPS,
-    )
+    payload = jnp.concatenate([jnp.broadcast_to(block[None], (Z,) + block.shape), rows], axis=1)
+    payload, _ = lax.optimization_barrier((payload, query_other))
+    z_all = exchange(payload, Z_GROUPS)
 
     rest = jnp.concatenate(
         [kv_both[:, kv_width + HEAD_DIM :], jnp.concatenate([query_weight, query_other])], axis=1

time: 146 us -> 148 us (1.014)
  Pallas kernels: 19.3 us -> 23 us
  starting transfers between devices: 39.5 us -> 37.9 us
    pallas_call x1, Pallas kernels: 12.6 us -> 16.3 us  [kv_attend(): pl.pallas_call(kv_attend_kernel, grid=(seq_count // per_step,), in_specs=...]
    all_to_all x2, waiting for transfers between devices: 19.8 us -> 21.6 us  [exchange(): lax.all_to_all(chunks, 'dp', split_axis=0, concat_axis=0, tiled=True, axi...]
    ppermute x10, starting transfers between devices: 10.4 us -> 8.78 us  [swap_tensor(): return lax.ppermute(array, 'tensor', [(i, i ^ mask) for i in range(size)])]
  transfers between devices with their start and end apart: 21 -> 21, of which waited for: 9 -> 8; matrix products, arithmetic and copies ran while one was open for 3% -> 5% of each run, Pallas kernels for 3% -> 3%
where the time goes in v8:
time: 148 us; the launch traced here: 147 us
  waiting for transfers between devices  47.4 us (32%)
  starting transfers between devices  37.9 us (26%)
  blocking collectives  23.8 us (16%)
  Pallas kernels  23 us (16%)
  local copies, waits for them, and re-layouts  6.63 us (4%)
  other arithmetic  5.63 us (4%)
  between operations  2.63 us (2%)
    all_to_all x1, blocking collectives, exchange(): lax.all_to_all(chunks, 'dp', split_axis=0, concat_axis=0, tiled=True, axi...  23.8 us
    all_to_all x2, waiting for transfers between devices, exchange(): lax.all_to_all(chunks, 'dp', split_axis=0, concat_axis=0, tiled=True, axi...  21.6 us
    pallas_call x1, Pallas kernels, kv_attend(): pl.pallas_call(kv_attend_kernel, grid=(seq_count // per_step,), in_specs=...  16.3 us
    ppermute x10, waiting for transfers between devices, swap_tensor(): return lax.ppermute(array, 'tensor', [(i, i ^ mask) for i in range(size)])  16.2 us
    all_to_all x2, starting transfers between devices, exchange(): lax.all_to_all(chunks, 'dp', split_axis=0, concat_axis=0, tiled=True, axi...  14.2 us
    ppermute x7, starting transfers between devices, shift(): return lax.ppermute(array, ('dp', 'tensor'), pairs)  12.8 us
    ppermute x7, waiting for transfers between devices, shift(): return lax.ppermute(array, ('dp', 'tensor'), pairs)  9.58 us
    ppermute x10, starting transfers between devices, swap_tensor(): return lax.ppermute(array, 'tensor', [(i, i ^ mask) for i in range(size)])  8.78 us
  transfers between devices with their start and end apart: 21, of which 8 were waited for; matrix products, arithmetic and copies ran while one was open for 5% of the time, Pallas kernels for 3%

profile of v8, /device:TPU:32, one launch (start us, length us, event | category | flops | bytes accessed | tf_op | source)
XLA Modules:
  0.0 147.2 jit_solution(17872441603650596762)
XLA Ops:
  0.7 2.3 %shard_map.103.r0 = bf16[4,1024]{1,0:T(4,128)(2,1)} custom-call(s32[2,2]{1,0:T(2,128)} %len_ref.3, bf16[4,256,1024]{2,1,0:T(8,128)(2,1)} %bitcast.27), custom_call_target="tpu_custom_call" | custom-call | tf_op jit(solution)/shard_map/pallas_call | solution.py:261
  3.0 2.5 %collective-permute-start.4 = (bf16[4,1024]{1,0:T(4,128)(2,1)}, bf16[4,1024]{1,0:T(4,128)(2,1)S(1)}, u32[]{:S(2)}, u32[]{:S(2)}) collective-permute-start(bf16[4,1024]{1,0:T(4,128)(2,1)} %shard_map.103.r0), channel_id=1, source_target_pairs={{0,3},{1,2},{2,1},{3,0},{4,7},{5,6},{6,5},{7,4},{8,11},{9,10},{10,... | collective-permute-start | bytes 24584 | tf_op jit(solution)/shard_map/ppermute | solution.py:43
  5.5 0.7 collective-permute-start.3
  6.2 0.2 collective-permute-start.2
  6.4 1.6 %collective-permute-start = (bf16[64,512]{1,0:T(8,128)(2,1)S(1)}, bf16[64,512]{1,0:T(8,128)(2,1)S(1)}, u32[]{:S(2)}, u32[]{:S(2)}) collective-permute-start(bf16[64,512]{1,0:T(8,128)(2,1)S(1)} %constant_dynamic-update-slice_fusion), channel_id=1, source_target_pairs={{0,32},{4,36},{8,40},{12,44},{16,48},{20,52},{24,56},{28,60},{32,0... | collective-permute-start | bytes 196616 | tf_op jit(solution)/shard_map/ppermute | solution.py:48
  8.0 0.5 collective-permute-start.1
  8.5 0.7 pad_add_fusion.at_ref
  9.2 1.7 %collective-permute-done.3.r2 = bf16[4,1024]{1,0:T(4,128)(2,1)S(1)} collective-permute-done((bf16[4,1024]{1,0:T(4,128)(2,1)}, bf16[4,1024]{1,0:T(4,128)(2,1)S(1)}, u32[]{:S(2)}, u32[]{:S(2)}) %collective-permute-start.3) | collective-permute-done | bytes 8224 | tf_op jit(solution)/shard_map/ppermute | solution.py:43
  10.9 0.0 collective-permute-done.2.r1
  10.9 0.6 copy-done.8
  11.5 0.0 copy-done.9
  11.5 1.7 %shard_map.104 = bf16[8,16,384]{2,1,0:T(8,128)(2,1)} custom-call(s32[3]{0:T(128)} %pad_add_fusion.at_ref, bf16[4,1024]{1,0:T(4,128)(2,1)} %shard_map.103.r0, bf16[4,1024]{1,0:T(4,128)(2,1)} %copy-done.9, bf16[4,1024]{1,0:T(4,128)(2,1)} %copy-done.8, bf16[4,1024]{1,0:T(4,128)(2,1)} %copy-done.7, f32[1,4096]{1,0:T(1,128)} %bitcast.32), custom_call_target="tpu_custom_call" | custom-call | tf_op jit(solution)/shard_map/pallas_call | solution.py:276
  13.2 0.1 broadcast_in_dim.13
  13.2 0.0 copy-start.1
  13.2 2.1 %pad_maximum_fusion = bf16[8,144,384]{2,1,0:T(8,128)(2,1)} fusion(bf16[8,16,384]{2,1,0:T(8,128)(2,1)} %shard_map.104, bf16[8,128,384]{2,1,0:T(8,128)(2,1)S(1)} %broadcast_in_dim.13), kind=kLoop, calls=%fused_computation.1 | loop fusion | flops 1769472 | bytes 1769472 | tf_op jit(solution)/shard_map/concatenate | solution.py:364
  15.3 0.0 collective-permute-done.1
  15.3 8.6 %all-to-all-start = ((bf16[8,144,384]{2,1,0:T(8,128)(2,1)}), bf16[8,144,384]{2,1,0:T(8,128)(2,1)S(1)}, u32[]{:S(2)}, u32[]{:S(2)}) async-start(bf16[8,144,384]{2,1,0:T(8,128)(2,1)} %pad_maximum_fusion), calls=%async_computation | async-start | bytes 1769472 | tf_op jit(solution)/shard_map/all_to_all | solution.py:52
  23.9 1.4 collective-permute-start.6
  25.3 1.7 %collective-permute-start.9 = (bf16[128,1152]{1,0:T(8,128)(2,1)S(1)}, bf16[128,1152]{1,0:T(8,128)(2,1)}, u32[]{:S(2)}, u32[]{:S(2)}) collective-permute-start(bf16[128,1152]{1,0:T(8,128)(2,1)S(1)} %maximum_maximum_fusion.w0), channel_id=1, source_target_pairs={{0,64},{1,65},{4,68},{5,69},{8,72},{9,73},{12,76},{13,77},{16,80},... | collective-permute-start | bytes 884744 | tf_op jit(solution)/shard_map/ppermute | solution.py:38
  27.0 2.9 %collective-permute-start.8 = (bf16[128,1152]{1,0:T(8,128)(2,1)S(1)}, bf16[128,1152]{1,0:T(8,128)(2,1)}, u32[]{:S(2)}, u32[]{:S(2)}) collective-permute-start(bf16[128,1152]{1,0:T(8,128)(2,1)S(1)} %maximum_maximum_fusion.w0), channel_id=1, source_target_pairs={{0,128},{1,129},{4,132},{5,133},{8,136},{9,137},{12,140},{13,141},... | collective-permute-start | bytes 884744 | tf_op jit(solution)/shard_map/ppermute | solution.py:38
  29.9 1.3 collective-permute-start.7
  31.2 16.1 %all-to-all-done.rows_ref = bf16[8,144,384]{2,1,0:T(8,128)(2,1)S(1)} async-done(((bf16[8,144,384]{2,1,0:T(8,128)(2,1)}), bf16[8,144,384]{2,1,0:T(8,128)(2,1)S(1)}, u32[]{:S(2)}, u32[]{:S(2)}) %all-to-all-start) | async-done | bytes 884768 | tf_op jit(solution)/shard_map/all_to_all | solution.py:52
  47.3 1.1 slice.50.own_ref
  48.4 0.0 collective-permute-done.7.w1
  48.4 1.7 %collective-permute-start.11 = (bf16[8,128,384]{2,1,0:T(8,128)(2,1)}, bf16[8,128,384]{2,1,0:T(8,128)(2,1)}, u32[]{:S(2)}, u32[]{:S(2)}) collective-permute-start(bf16[8,128,384]{2,1,0:T(8,128)(2,1)} %slice.50.own_ref), channel_id=1, source_target_pairs={{0,64},{1,65},{4,68},{5,69},{8,72},{9,73},{12,76},{13,77},{16,80},... | collective-permute-start | bytes 2359304 | tf_op jit(solution)/shard_map/ppermute | solution.py:38
  50.1 1.7 %collective-permute-start.10 = (bf16[8,128,384]{2,1,0:T(8,128)(2,1)}, bf16[8,128,384]{2,1,0:T(8,128)(2,1)}, u32[]{:S(2)}, u32[]{:S(2)}) collective-permute-start(bf16[8,128,384]{2,1,0:T(8,128)(2,1)} %slice.50.own_ref), channel_id=1, source_target_pairs={{0,192},{1,193},{4,196},{5,197},{8,200},{9,201},{12,204},{13,205},... | collective-permute-start | bytes 2359304 | tf_op jit(solution)/shard_map/ppermute | solution.py:38
  51.8 0.7 slice_bitcast_fusion
  52.5 0.0 collective-permute-start.15
  52.5 2.8 %shard_map.105 = bf16[8,592,128]{2,1,0:T(8,128)(2,1)} custom-call(bf16[8,144,384]{2,1,0:T(8,128)(2,1)} %copy-done, bf16[128,1152]{1,0:T(8,128)(2,1)} %copy-done.2, bf16[128,1152]{1,0:T(8,128)(2,1)} %collective-permute-done.7.w1, bf16[128,1152]{1,0:T(8,128)(2,1)} %collective-permute-done.8.w2, bf16[128,1152]{1,0:T(8,128)(2,1)} %collective-permute-done.9.w3), custom_call_target="tpu_custom_call" | custom-call | tf_op jit(solution)/shard_map/pallas_call | solution.py:292
  55.3 0.0 collective-permute-done.15.corner_ref
  55.3 5.6 %all-to-all-start.1 = ((bf16[8,592,128]{2,1,0:T(8,128)(2,1)}), bf16[8,592,128]{2,1,0:T(8,128)(2,1)}, u32[]{:S(2)}, u32[]{:S(2)}) async-start(bf16[8,592,128]{2,1,0:T(8,128)(2,1)} %shard_map.105), calls=%async_computation.1 | async-start | bytes 2424832 | tf_op jit(solution)/shard_map/all_to_all | solution.py:52
  60.9 0.2 collective-permute-start.5
  61.1 10.8 %collective-permute-done.6.x2_ref = bf16[4,256,1024]{2,1,0:T(8,128)(2,1)} collective-permute-done((bf16[4,256,1024]{2,1,0:T(8,128)(2,1)S(1)}, bf16[4,256,1024]{2,1,0:T(8,128)(2,1)}, u32[]{:S(2)}, u32[]{:S(2)}) %collective-permute-start.6) | collective-permute-done | bytes 2097184 | tf_op jit(solution)/shard_map/ppermute | solution.py:43
  72.0 0.0 collective-permute-done.11.down_ref
  72.0 1.0 slice.54
  73.0 1.7 %collective-permute-start.14 = (bf16[4,128,384]{2,1,0:T(8,128)(2,1)S(1)}, bf16[4,128,384]{2,1,0:T(8,128)(2,1)S(1)}, u32[]{:S(2)}, u32[]{:S(2)}) collective-permute-start(bf16[4,128,384]{2,1,0:T(8,128)(2,1)S(1)} %slice.54), channel_id=1, source_target_pairs={{0,64},{1,65},{4,68},{5,69},{8,72},{9,73},{12,76},{13,77},{16,80},... | collective-permute-start | bytes 1179656 | tf_op jit(solution)/shard_map/ppermute | solution.py:38
  74.7 1.0 slice.53
  75.7 1.9 %collective-permute-start.13 = (bf16[4,128,384]{2,1,0:T(8,128)(2,1)S(1)}, bf16[4,128,384]{2,1,0:T(8,128)(2,1)S(1)}, u32[]{:S(2)}, u32[]{:S(2)}) collective-permute-start(bf16[4,128,384]{2,1,0:T(8,128)(2,1)S(1)} %slice.53), channel_id=1, source_target_pairs={{0,192},{1,193},{4,196},{5,197},{8,200},{9,201},{12,204},{13,205},... | collective-permute-start | bytes 1179656 | tf_op jit(solution)/shard_map/ppermute | solution.py:38
  77.7 8.2 %collective-permute-done.14.far_high_ref = bf16[4,128,384]{2,1,0:T(8,128)(2,1)S(1)} collective-permute-done((bf16[4,128,384]{2,1,0:T(8,128)(2,1)S(1)}, bf16[4,128,384]{2,1,0:T(8,128)(2,1)S(1)}, u32[]{:S(2)}, u32[]{:S(2)}) %collective-permute-start.14) | collective-permute-done | bytes 393248 | tf_op jit(solution)/shard_map/ppermute | solution.py:38
  85.9 1.3 collective-permute-done.13.far_low_ref
  87.2 5.5 %all-to-all-done.1.last_ref = bf16[8,592,128]{2,1,0:T(8,128)(2,1)} async-done(((bf16[8,592,128]{2,1,0:T(8,128)(2,1)}), bf16[8,592,128]{2,1,0:T(8,128)(2,1)}, u32[]{:S(2)}, u32[]{:S(2)}) %all-to-all-start.1) | async-done | bytes 1212448 | tf_op jit(solution)/shard_map/all_to_all | solution.py:52
  92.8 16.3 %shard_map.106 = f32[4,8,128]{2,1,0:T(8,128)} custom-call(s32[3]{0:T(128)} %pad_add_fusion.at_ref, s32[2,2]{1,0:T(2,128)} %len_ref.3, bf16[4,256,1024]{2,1,0:T(8,128)(2,1)} %bitcast.28, bf16[4,256,1024]{2,1,0:T(8,128)(2,1)} %copy-done.10, bf16[4,256,1024]{2,1,0:T(8,128)(2,1)} %collective-permute-done.6.x2_ref, ...), custom_call_target="tpu_custom_call" | custom-call | flops 4294967296 | bytes 12582912 | tf_op jit(solution)/shard_map/pallas_call | solution.py:310
  109.0 0.7 convert_bitcast_fusion
  109.8 0.1 broadcast_in_dim.32
  109.9 23.8 %all_to_all.15 = bf16[64,4,1024]{2,1,0:T(4,128)(2,1)S(1)} all-to-all(bf16[64,4,1024]{2,1,0:T(4,128)(2,1)S(1)} %broadcast_in_dim.32), channel_id=1, replica_groups=mesh['dp'=64,'tensor'=4] {'dp'}, dimensions={0} | all-to-all | bytes 1048576 | tf_op jit(solution)/shard_map/all_to_all | solution.py:52
  133.7 0.3 multiply_reduce_fusion
  134.0 0.1 reduce_sum.48
  134.1 0.1 copy.14
  134.2 0.2 reshape.34
  134.4 0.7 fusion.12
  135.1 0.3 fusion
  135.4 2.1 %collective-permute-start.17 = (f32[130,128]{1,0:T(8,128)S(1)}, f32[130,128]{1,0:T(8,128)S(1)}, u32[]{:S(2)}, u32[]{:S(2)}) collective-permute-start(f32[130,128]{1,0:T(8,128)S(1)} %pad_maximum_fusion.2), channel_id=1, source_target_pairs={{0,2},{1,3},{2,0},{3,1},{4,6},{5,7},{6,4},{7,5},{8,10},{9,11},{10,... | collective-permute-start | bytes 199688 | tf_op jit(solution)/shard_map/ppermute | solution.py:43
  137.5 0.0 collective-permute-start.18
  137.5 1.6 %collective-permute-start.16 = (f32[130,128]{1,0:T(8,128)S(1)}, f32[130,128]{1,0:T(8,128)S(1)}, u32[]{:S(2)}, u32[]{:S(2)}) collective-permute-start(f32[130,128]{1,0:T(8,128)S(1)} %pad_maximum_fusion.2), channel_id=1, source_target_pairs={{0,1},{1,0},{2,3},{3,2},{4,5},{5,4},{6,7},{7,6},{8,9},{9,8},{10,11... | collective-permute-start | bytes 199688 | tf_op jit(solution)/shard_map/ppermute | solution.py:43
  139.2 2.2 %collective-permute-done.17 = f32[130,128]{1,0:T(8,128)S(1)} collective-permute-done((f32[130,128]{1,0:T(8,128)S(1)}, f32[130,128]{1,0:T(8,128)S(1)}, u32[]{:S(2)}, u32[]{:S(2)}) %collective-permute-start.17) | collective-permute-done | bytes 66592 | tf_op jit(solution)/shard_map/ppermute | solution.py:43
  141.3 1.5 %collective-permute-done.18 = f32[130,128]{1,0:T(8,128)S(1)} collective-permute-done((f32[130,128]{1,0:T(8,128)S(1)}, f32[130,128]{1,0:T(8,128)S(1)}, u32[]{:S(2)}, u32[]{:S(2)}) %collective-permute-start.18) | collective-permute-done | bytes 66592 | tf_op jit(solution)/shard_map/ppermute | solution.py:43
  142.9 0.1 dynamic-slice_bitcast_fusion
  142.9 0.1 copy.15
  143.0 0.2 fusion.10
  143.2 0.2 exponential_reduce_fusion.1
  143.4 0.1 exponential_reduce_fusion
  143.5 0.6 fusion.11
  144.1 0.6 dynamic_slice.7
  144.7 0.7 multiply_convert_fusion
  (47 shorter events, 0.2 us)
Async XLA Ops:
  0.6 5.8 %copy-start.5 = (bf16[64,256]{1,0:T(8,128)(2,1)S(1)}, bf16[64,256]{1,0:T(8,128)(2,1)}, u32[]{:S(2)}) copy-start(bf16[64,256]{1,0:T(8,128)(2,1)} %param.14) | copy-start | bytes 98308
  0.6 5.8 %copy-start.6 = (bf16[64,256]{1,0:T(8,128)(2,1)S(1)}, bf16[64,256]{1,0:T(8,128)(2,1)}, u32[]{:S(2)}) copy-start(bf16[64,256]{1,0:T(8,128)(2,1)} %param.15) | copy-start | bytes 98308
  0.7 7.4 %copy-start.3 = (bf16[64,1024]{1,0:T(8,128)(2,1)S(1)}, bf16[64,1024]{1,0:T(8,128)(2,1)}, u32[]{:S(2)}) copy-start(bf16[64,1024]{1,0:T(8,128)(2,1)} %param.13) | copy-start | bytes 393220
  3.0 6.2 %collective-permute-start.4 = (bf16[4,1024]{1,0:T(4,128)(2,1)}, bf16[4,1024]{1,0:T(4,128)(2,1)S(1)}, u32[]{:S(2)}, u32[]{:S(2)}) collective-permute-start(bf16[4,1024]{1,0:T(4,128)(2,1)} %shard_map.103.r0), channel_id=1, source_target_pairs={{0,3},{1,2},{2,1},{3,0},{4,7},{5,6},{6,5},{7,4},{8,11},{9,10},{10,... | collective-permute-start | bytes 24584 | tf_op jit(solution)/shard_map/ppermute | solution.py:43
  5.5 5.4 %collective-permute-start.3 = (bf16[4,1024]{1,0:T(4,128)(2,1)}, bf16[4,1024]{1,0:T(4,128)(2,1)S(1)}, u32[]{:S(2)}, u32[]{:S(2)}) collective-permute-start(bf16[4,1024]{1,0:T(4,128)(2,1)} %shard_map.103.r0), channel_id=1, source_target_pairs={{0,2},{1,3},{2,0},{3,1},{4,6},{5,7},{6,4},{7,5},{8,10},{9,11},{10,... | collective-permute-start | bytes 24584 | tf_op jit(solution)/shard_map/ppermute | solution.py:43
  6.2 4.7 %collective-permute-start.2 = (bf16[4,1024]{1,0:T(4,128)(2,1)}, bf16[4,1024]{1,0:T(4,128)(2,1)S(1)}, u32[]{:S(2)}, u32[]{:S(2)}) collective-permute-start(bf16[4,1024]{1,0:T(4,128)(2,1)} %shard_map.103.r0), channel_id=1, source_target_pairs={{0,1},{1,0},{2,3},{3,2},{4,5},{5,4},{6,7},{7,6},{8,9},{9,8},{10,11... | collective-permute-start | bytes 24584 | tf_op jit(solution)/shard_map/ppermute | solution.py:43
  6.4 6.7 %collective-permute-start = (bf16[64,512]{1,0:T(8,128)(2,1)S(1)}, bf16[64,512]{1,0:T(8,128)(2,1)S(1)}, u32[]{:S(2)}, u32[]{:S(2)}) collective-permute-start(bf16[64,512]{1,0:T(8,128)(2,1)S(1)} %constant_dynamic-update-slice_fusion), channel_id=1, source_target_pairs={{0,32},{4,36},{8,40},{12,44},{16,48},{20,52},{24,56},{28,60},{32,0... | collective-permute-start | bytes 196616 | tf_op jit(solution)/shard_map/ppermute | solution.py:48
  8.0 7.3 %collective-permute-start.1 = (bf16[64,1024]{1,0:T(8,128)(2,1)S(1)}, bf16[64,1024]{1,0:T(8,128)(2,1)S(1)}, u32[]{:S(2)}, u32[]{:S(2)}) collective-permute-start(bf16[64,1024]{1,0:T(8,128)(2,1)S(1)} %copy-done.3), channel_id=1, source_target_pairs={{0,32},{4,36},{8,40},{12,44},{16,48},{20,52},{24,56},{28,60},{32,0... | collective-permute-start | bytes 393224 | tf_op jit(solution)/shard_map/ppermute | solution.py:48
  9.2 1.7 %copy-start.7 = (bf16[4,1024]{1,0:T(4,128)(2,1)}, bf16[4,1024]{1,0:T(4,128)(2,1)S(1)}, u32[]{:S(2)}) copy-start(bf16[4,1024]{1,0:T(4,128)(2,1)S(1)} %collective-permute-done.4.r3) | copy-start | bytes 24580
  10.9 0.6 copy-start.8
  10.9 0.6 copy-start.9
  13.2 10.6 %copy-start.1 = (bf16[2,2,256,1024]{3,2,1,0:T(8,128)(2,1)S(1)}, bf16[2,2,256,1024]{3,2,1,0:T(8,128)(2,1)}, u32[]{:S(2)}) copy-start(bf16[2,2,256,1024]{3,2,1,0:T(8,128)(2,1)} %param.8) | copy-start | bytes 6291460
  15.3 32.0 %all-to-all-start = ((bf16[8,144,384]{2,1,0:T(8,128)(2,1)}), bf16[8,144,384]{2,1,0:T(8,128)(2,1)S(1)}, u32[]{:S(2)}, u32[]{:S(2)}) async-start(bf16[8,144,384]{2,1,0:T(8,128)(2,1)} %pad_maximum_fusion), calls=%async_computation | async-start | bytes 1769472 | tf_op jit(solution)/shard_map/all_to_all | solution.py:52
  23.9 48.1 %collective-permute-start.6 = (bf16[4,256,1024]{2,1,0:T(8,128)(2,1)S(1)}, bf16[4,256,1024]{2,1,0:T(8,128)(2,1)}, u32[]{:S(2)}, u32[]{:S(2)}) collective-permute-start(bf16[4,256,1024]{2,1,0:T(8,128)(2,1)S(1)} %bitcast.29), channel_id=1, source_target_pairs={{0,2},{1,3},{2,0},{3,1},{4,6},{5,7},{6,4},{7,5},{8,10},{9,11},{10,... | collective-permute-start | bytes 6291464 | tf_op jit(solution)/shard_map/ppermute | solution.py:43
  25.3 27.2 %copy-start.2 = (bf16[128,1152]{1,0:T(8,128)(2,1)}, bf16[128,1152]{1,0:T(8,128)(2,1)S(1)}, u32[]{:S(2)}) copy-start(bf16[128,1152]{1,0:T(8,128)(2,1)S(1)} %maximum_maximum_fusion.w0) | copy-start | bytes 884740
  25.3 23.1 %collective-permute-start.9 = (bf16[128,1152]{1,0:T(8,128)(2,1)S(1)}, bf16[128,1152]{1,0:T(8,128)(2,1)}, u32[]{:S(2)}, u32[]{:S(2)}) collective-permute-start(bf16[128,1152]{1,0:T(8,128)(2,1)S(1)} %maximum_maximum_fusion.w0), channel_id=1, source_target_pairs={{0,64},{1,65},{4,68},{5,69},{8,72},{9,73},{12,76},{13,77},{16,80},... | collective-permute-start | bytes 884744 | tf_op jit(solution)/shard_map/ppermute | solution.py:38
  27.0 21.5 %collective-permute-start.8 = (bf16[128,1152]{1,0:T(8,128)(2,1)S(1)}, bf16[128,1152]{1,0:T(8,128)(2,1)}, u32[]{:S(2)}, u32[]{:S(2)}) collective-permute-start(bf16[128,1152]{1,0:T(8,128)(2,1)S(1)} %maximum_maximum_fusion.w0), channel_id=1, source_target_pairs={{0,128},{1,129},{4,132},{5,133},{8,136},{9,137},{12,140},{13,141},... | collective-permute-start | bytes 884744 | tf_op jit(solution)/shard_map/ppermute | solution.py:38
  29.9 18.6 %collective-permute-start.7 = (bf16[128,1152]{1,0:T(8,128)(2,1)S(1)}, bf16[128,1152]{1,0:T(8,128)(2,1)}, u32[]{:S(2)}, u32[]{:S(2)}) collective-permute-start(bf16[128,1152]{1,0:T(8,128)(2,1)S(1)} %maximum_maximum_fusion.w0), channel_id=1, source_target_pairs={{0,192},{1,193},{4,196},{5,197},{8,200},{9,201},{12,204},{13,205},... | collective-permute-start | bytes 884744 | tf_op jit(solution)/shard_map/ppermute | solution.py:38
  47.3 5.2 %copy-start = (bf16[8,144,384]{2,1,0:T(8,128)(2,1)}, bf16[8,144,384]{2,1,0:T(8,128)(2,1)S(1)}, u32[]{:S(2)}) copy-start(bf16[8,144,384]{2,1,0:T(8,128)(2,1)S(1)} %all-to-all-done.rows_ref) | copy-start | bytes 2654212
  48.4 23.6 %collective-permute-start.11 = (bf16[8,128,384]{2,1,0:T(8,128)(2,1)}, bf16[8,128,384]{2,1,0:T(8,128)(2,1)}, u32[]{:S(2)}, u32[]{:S(2)}) collective-permute-start(bf16[8,128,384]{2,1,0:T(8,128)(2,1)} %slice.50.own_ref), channel_id=1, source_target_pairs={{0,64},{1,65},{4,68},{5,69},{8,72},{9,73},{12,76},{13,77},{16,80},... | collective-permute-start | bytes 2359304 | tf_op jit(solution)/shard_map/ppermute | solution.py:38
  50.1 21.9 %collective-permute-start.10 = (bf16[8,128,384]{2,1,0:T(8,128)(2,1)}, bf16[8,128,384]{2,1,0:T(8,128)(2,1)}, u32[]{:S(2)}, u32[]{:S(2)}) collective-permute-start(bf16[8,128,384]{2,1,0:T(8,128)(2,1)} %slice.50.own_ref), channel_id=1, source_target_pairs={{0,192},{1,193},{4,196},{5,197},{8,200},{9,201},{12,204},{13,205},... | collective-permute-start | bytes 2359304 | tf_op jit(solution)/shard_map/ppermute | solution.py:38
  52.5 2.8 %collective-permute-start.15 = (bf16[16,384]{1,0:T(8,128)(2,1)S(1)}, bf16[16,384]{1,0:T(8,128)(2,1)S(1)}, u32[]{:S(2)}, u32[]{:S(2)}) collective-permute-start(bf16[16,384]{1,0:T(8,128)(2,1)S(1)} %slice_bitcast_fusion), channel_id=1, source_target_pairs={{0,1},{1,0},{2,3},{3,2},{4,5},{5,4},{6,7},{7,6},{8,9},{9,8},{10,11... | collective-permute-start | bytes 36872 | tf_op jit(solution)/shard_map/ppermute | solution.py:43
  55.3 20.4 %copy-start.13 = (bf16[16,384]{1,0:T(8,128)(2,1)}, bf16[16,384]{1,0:T(8,128)(2,1)S(1)}, u32[]{:S(2)}) copy-start(bf16[16,384]{1,0:T(8,128)(2,1)S(1)} %collective-permute-done.15.corner_ref) | copy-start | bytes 36868
  55.3 37.5 %all-to-all-start.1 = ((bf16[8,592,128]{2,1,0:T(8,128)(2,1)}), bf16[8,592,128]{2,1,0:T(8,128)(2,1)}, u32[]{:S(2)}, u32[]{:S(2)}) async-start(bf16[8,592,128]{2,1,0:T(8,128)(2,1)} %shard_map.105), calls=%async_computation.1 | async-start | bytes 2424832 | tf_op jit(solution)/shard_map/all_to_all | solution.py:52
  60.9 16.7 %collective-permute-start.5 = (bf16[4,256,1024]{2,1,0:T(8,128)(2,1)S(1)}, bf16[4,256,1024]{2,1,0:T(8,128)(2,1)S(1)}, u32[]{:S(2)}, u32[]{:S(2)}) collective-permute-start(bf16[4,256,1024]{2,1,0:T(8,128)(2,1)S(1)} %bitcast.30), channel_id=1, source_target_pairs={{0,1},{1,0},{2,3},{3,2},{4,5},{5,4},{6,7},{7,6},{8,9},{9,8},{10,11... | collective-permute-start | bytes 6291464 | tf_op jit(solution)/shard_map/ppermute | solution.py:43
  72.0 20.8 %collective-permute-start.12 = (bf16[4,256,1024]{2,1,0:T(8,128)(2,1)}, bf16[4,256,1024]{2,1,0:T(8,128)(2,1)}, u32[]{:S(2)}, u32[]{:S(2)}) collective-permute-start(bf16[4,256,1024]{2,1,0:T(8,128)(2,1)} %collective-permute-done.6.x2_ref), channel_id=1, source_target_pairs={{0,1},{1,0},{2,3},{3,2},{4,5},{5,4},{6,7},{7,6},{8,9},{9,8},{10,11... | collective-permute-start | bytes 6291464 | tf_op jit(solution)/shard_map/ppermute | solution.py:43
  73.0 12.9 %collective-permute-start.14 = (bf16[4,128,384]{2,1,0:T(8,128)(2,1)S(1)}, bf16[4,128,384]{2,1,0:T(8,128)(2,1)S(1)}, u32[]{:S(2)}, u32[]{:S(2)}) collective-permute-start(bf16[4,128,384]{2,1,0:T(8,128)(2,1)S(1)} %slice.54), channel_id=1, source_target_pairs={{0,64},{1,65},{4,68},{5,69},{8,72},{9,73},{12,76},{13,77},{16,80},... | collective-permute-start | bytes 1179656 | tf_op jit(solution)/shard_map/ppermute | solution.py:38
  75.7 11.5 %collective-permute-start.13 = (bf16[4,128,384]{2,1,0:T(8,128)(2,1)S(1)}, bf16[4,128,384]{2,1,0:T(8,128)(2,1)S(1)}, u32[]{:S(2)}, u32[]{:S(2)}) collective-permute-start(bf16[4,128,384]{2,1,0:T(8,128)(2,1)S(1)} %slice.53), channel_id=1, source_target_pairs={{0,192},{1,193},{4,196},{5,197},{8,200},{9,201},{12,204},{13,205},... | collective-permute-start | bytes 1179656 | tf_op jit(solution)/shard_map/ppermute | solution.py:38
  77.7 8.3 %copy-start.10 = (bf16[4,256,1024]{2,1,0:T(8,128)(2,1)}, bf16[4,256,1024]{2,1,0:T(8,128)(2,1)S(1)}, u32[]{:S(2)}) copy-start(bf16[4,256,1024]{2,1,0:T(8,128)(2,1)S(1)} %collective-permute-done.5.x1_ref) | copy-start | bytes 6291460
  85.9 6.9 %copy-start.11 = (bf16[4,128,384]{2,1,0:T(8,128)(2,1)}, bf16[4,128,384]{2,1,0:T(8,128)(2,1)S(1)}, u32[]{:S(2)}) copy-start(bf16[4,128,384]{2,1,0:T(8,128)(2,1)S(1)} %collective-permute-done.14.far_high_ref) | copy-start | bytes 1179652
  87.2 5.5 %copy-start.12 = (bf16[4,128,384]{2,1,0:T(8,128)(2,1)}, bf16[4,128,384]{2,1,0:T(8,128)(2,1)S(1)}, u32[]{:S(2)}) copy-start(bf16[4,128,384]{2,1,0:T(8,128)(2,1)S(1)} %collective-permute-done.13.far_low_ref) | copy-start | bytes 1179652
  134.2 5.0 %copy-start.4 = (f32[4,8,128]{2,1,0:T(8,128)S(1)}, f32[4,8,128]{2,1,0:T(8,128)}, u32[]{:S(2)}) copy-start(f32[4,8,128]{2,1,0:T(8,128)} %shard_map.106) | copy-start | bytes 49156
  135.4 5.9 %collective-permute-start.17 = (f32[130,128]{1,0:T(8,128)S(1)}, f32[130,128]{1,0:T(8,128)S(1)}, u32[]{:S(2)}, u32[]{:S(2)}) collective-permute-start(f32[130,128]{1,0:T(8,128)S(1)} %pad_maximum_fusion.2), channel_id=1, source_target_pairs={{0,2},{1,3},{2,0},{3,1},{4,6},{5,7},{6,4},{7,5},{8,10},{9,11},{10,... | collective-permute-start | bytes 199688 | tf_op jit(solution)/shard_map/ppermute | solution.py:43
  137.5 5.3 %collective-permute-start.18 = (f32[130,128]{1,0:T(8,128)S(1)}, f32[130,128]{1,0:T(8,128)S(1)}, u32[]{:S(2)}, u32[]{:S(2)}) collective-permute-start(f32[130,128]{1,0:T(8,128)S(1)} %pad_maximum_fusion.2), channel_id=1, source_target_pairs={{0,3},{1,2},{2,1},{3,0},{4,7},{5,6},{6,5},{7,4},{8,11},{9,10},{10,... | collective-permute-start | bytes 199688 | tf_op jit(solution)/shard_map/ppermute | solution.py:43
  137.5 5.3 %collective-permute-start.16 = (f32[130,128]{1,0:T(8,128)S(1)}, f32[130,128]{1,0:T(8,128)S(1)}, u32[]{:S(2)}, u32[]{:S(2)}) collective-permute-start(f32[130,128]{1,0:T(8,128)S(1)} %pad_maximum_fusion.2), channel_id=1, source_target_pairs={{0,1},{1,0},{2,3},{3,2},{4,5},{5,4},{6,7},{7,6},{8,9},{9,8},{10,11... | collective-permute-start | bytes 199688 | tf_op jit(solution)/shard_map/ppermute | solution.py:43

commit v9 on v7

--- a/solution.py
+++ b/solution.py
@@ -359,7 +359,7 @@
     )
     rest = [rest] + [shift(rest, dy=-step) for step in range(1, Y)]
 
-    z_own = lax.optimization_barrier((z_all[:, : block.shape[0]], *rest))[0]
+    z_own = lax.optimization_barrier((z_all, *rest))[0]
     z_up = shift(z_own, dy=-1)
     z_down = shift(z_own, dy=1)
     far_low = shift(z_up[: Z // 2], dy=-1)

time: 146 us -> 146 us (level)
  blocking collectives: 24.5 us -> 27 us
    all_to_all x2, waiting for transfers between devices: 19.8 us -> 5.54 us  [exchange(): lax.all_to_all(chunks, 'dp', split_axis=0, concat_axis=0, tiled=True, axi...]
    ppermute x7, waiting for transfers between devices: 9.58 us -> 21.1 us  [shift(): return lax.ppermute(array, ('dp', 'tensor'), pairs)]
    all_to_all x1, blocking collectives: 24.5 us -> 27 us  [exchange(): lax.all_to_all(chunks, 'dp', split_axis=0, concat_axis=0, tiled=True, axi...]
    ppermute x10, waiting for transfers between devices: 16.8 us -> 18.8 us  [swap_tensor(): return lax.ppermute(array, 'tensor', [(i, i ^ mask) for i in range(size)])]
  transfers between devices with their start and end apart: 21 -> 21, of which waited for: 9 -> 11; matrix products, arithmetic and copies ran while one was open for 3% -> 2% of each run, Pallas kernels for 3% -> 3%
where the time goes in v9:
time: 146 us
  waiting for transfers between devices  45.9 us (31%)
  starting transfers between devices  39.4 us (27%)
  blocking collectives  27 us (18%)
  Pallas kernels  19.3 us (13%)
  other arithmetic  5.59 us (4%)
  local copies, waits for them, and re-layouts  5.55 us (4%)
  between operations  2.63 us (2%)
    all_to_all x1, blocking collectives, exchange(): lax.all_to_all(chunks, 'dp', split_axis=0, concat_axis=0, tiled=True, axi...  27 us
    ppermute x7, waiting for transfers between devices, shift(): return lax.ppermute(array, ('dp', 'tensor'), pairs)  21.1 us
    ppermute x10, waiting for transfers between devices, swap_tensor(): return lax.ppermute(array, 'tensor', [(i, i ^ mask) for i in range(size)])  18.8 us
    all_to_all x2, starting transfers between devices, exchange(): lax.all_to_all(chunks, 'dp', split_axis=0, concat_axis=0, tiled=True, axi...  14.2 us
    ppermute x7, starting transfers between devices, shift(): return lax.ppermute(array, ('dp', 'tensor'), pairs)  12.7 us
    pallas_call x1, Pallas kernels, kv_attend(): pl.pallas_call(kv_attend_kernel, grid=(seq_count // per_step,), in_specs=...  12.6 us
    ppermute x10, starting transfers between devices, swap_tensor(): return lax.ppermute(array, 'tensor', [(i, i ^ mask) for i in range(size)])  10.4 us
    all_to_all x2, waiting for transfers between devices, exchange(): lax.all_to_all(chunks, 'dp', split_axis=0, concat_axis=0, tiled=True, axi...  5.54 us
  transfers between devices with their start and end apart: 21, of which 11 were waited for; matrix products, arithmetic and copies ran while one was open for 2% of the time, Pallas kernels for 3%

profile of v9, /device:TPU:32, one launch (start us, length us, event | category | flops | bytes accessed | tf_op | source)
XLA Modules:
  0.0 145.7 jit_solution(4152182955929447966)
XLA Ops:
  0.7 2.3 %shard_map.103.r0 = bf16[4,1024]{1,0:T(4,128)(2,1)} custom-call(s32[2,2]{1,0:T(2,128)} %len_ref.3, bf16[4,256,1024]{2,1,0:T(8,128)(2,1)} %bitcast.27), custom_call_target="tpu_custom_call" | custom-call | tf_op jit(solution)/shard_map/pallas_call | solution.py:249
  3.0 2.5 %collective-permute-start.4 = (bf16[4,1024]{1,0:T(4,128)(2,1)}, bf16[4,1024]{1,0:T(4,128)(2,1)S(1)}, u32[]{:S(2)}, u32[]{:S(2)}) collective-permute-start(bf16[4,1024]{1,0:T(4,128)(2,1)} %shard_map.103.r0), channel_id=1, source_target_pairs={{0,3},{1,2},{2,1},{3,0},{4,7},{5,6},{6,5},{7,4},{8,11},{9,10},{10,... | collective-permute-start | bytes 24584 | tf_op jit(solution)/shard_map/ppermute | solution.py:43
  5.5 0.7 collective-permute-start.3
  6.2 0.2 collective-permute-start.2
  6.4 1.6 %collective-permute-start = (bf16[64,512]{1,0:T(8,128)(2,1)S(1)}, bf16[64,512]{1,0:T(8,128)(2,1)S(1)}, u32[]{:S(2)}, u32[]{:S(2)}) collective-permute-start(bf16[64,512]{1,0:T(8,128)(2,1)S(1)} %constant_dynamic-update-slice_fusion), channel_id=1, source_target_pairs={{0,32},{4,36},{8,40},{12,44},{16,48},{20,52},{24,56},{28,60},{32,0... | collective-permute-start | bytes 196616 | tf_op jit(solution)/shard_map/ppermute | solution.py:48
  8.0 0.5 collective-permute-start.1
  8.5 0.6 pad_add_fusion.at_ref
  9.2 1.7 %collective-permute-done.3.r2 = bf16[4,1024]{1,0:T(4,128)(2,1)S(1)} collective-permute-done((bf16[4,1024]{1,0:T(4,128)(2,1)}, bf16[4,1024]{1,0:T(4,128)(2,1)S(1)}, u32[]{:S(2)}, u32[]{:S(2)}) %collective-permute-start.3) | collective-permute-done | bytes 8224 | tf_op jit(solution)/shard_map/ppermute | solution.py:43
  10.9 0.0 collective-permute-done.2.r1
  10.9 0.6 copy-done.10
  11.5 0.0 copy-done.11
  11.5 1.7 %shard_map.104 = bf16[8,16,384]{2,1,0:T(8,128)(2,1)} custom-call(s32[3]{0:T(128)} %pad_add_fusion.at_ref, bf16[4,1024]{1,0:T(4,128)(2,1)} %shard_map.103.r0, bf16[4,1024]{1,0:T(4,128)(2,1)} %copy-done.11, bf16[4,1024]{1,0:T(4,128)(2,1)} %copy-done.10, bf16[4,1024]{1,0:T(4,128)(2,1)} %copy-done.9, f32[1,4096]{1,0:T(1,128)} %bitcast.32), custom_call_target="tpu_custom_call" | custom-call | tf_op jit(solution)/shard_map/pallas_call | solution.py:264
  13.1 0.4 collective-permute-done.1
  13.6 0.1 broadcast_in_dim.13
  13.7 0.0 copy-start.1
  13.7 2.1 %pad_maximum_fusion = bf16[8,144,384]{2,1,0:T(8,128)(2,1)} fusion(bf16[8,16,384]{2,1,0:T(8,128)(2,1)} %shard_map.104, bf16[8,128,384]{2,1,0:T(8,128)(2,1)S(1)} %broadcast_in_dim.13), kind=kLoop, calls=%fused_computation.1 | loop fusion | flops 1769472 | bytes 1769472 | tf_op jit(solution)/shard_map/concatenate | solution.py:353
  15.7 8.6 %all-to-all-start = ((bf16[8,144,384]{2,1,0:T(8,128)(2,1)}), bf16[8,144,384]{2,1,0:T(8,128)(2,1)S(1)}, u32[]{:S(2)}, u32[]{:S(2)}) async-start(bf16[8,144,384]{2,1,0:T(8,128)(2,1)} %pad_maximum_fusion), calls=%async_computation | async-start | bytes 1769472 | tf_op jit(solution)/shard_map/all_to_all | solution.py:52
  24.3 3.0 %collective-permute-start.6 = (bf16[4,256,1024]{2,1,0:T(8,128)(2,1)S(1)}, bf16[4,256,1024]{2,1,0:T(8,128)(2,1)}, u32[]{:S(2)}, u32[]{:S(2)}) collective-permute-start(bf16[4,256,1024]{2,1,0:T(8,128)(2,1)S(1)} %bitcast.29), channel_id=1, source_target_pairs={{0,2},{1,3},{2,0},{3,1},{4,6},{5,7},{6,4},{7,5},{8,10},{9,11},{10,... | collective-permute-start | bytes 6291464 | tf_op jit(solution)/shard_map/ppermute | solution.py:43
  27.4 1.7 %collective-permute-start.9 = (bf16[128,1152]{1,0:T(8,128)(2,1)S(1)}, bf16[128,1152]{1,0:T(8,128)(2,1)S(1)}, u32[]{:S(2)}, u32[]{:S(2)}) collective-permute-start(bf16[128,1152]{1,0:T(8,128)(2,1)S(1)} %maximum_maximum_fusion.w0), channel_id=1, source_target_pairs={{0,64},{1,65},{4,68},{5,69},{8,72},{9,73},{12,76},{13,77},{16,80},... | collective-permute-start | bytes 884744 | tf_op jit(solution)/shard_map/ppermute | solution.py:38
  29.0 2.9 %collective-permute-start.8 = (bf16[128,1152]{1,0:T(8,128)(2,1)S(1)}, bf16[128,1152]{1,0:T(8,128)(2,1)S(1)}, u32[]{:S(2)}, u32[]{:S(2)}) collective-permute-start(bf16[128,1152]{1,0:T(8,128)(2,1)S(1)} %maximum_maximum_fusion.w0), channel_id=1, source_target_pairs={{0,128},{1,129},{4,132},{5,133},{8,136},{9,137},{12,140},{13,141},... | collective-permute-start | bytes 884744 | tf_op jit(solution)/shard_map/ppermute | solution.py:38
  31.9 1.3 collective-permute-start.7
  33.3 4.2 %collective-permute-done.9.w3 = bf16[128,1152]{1,0:T(8,128)(2,1)S(1)} collective-permute-done((bf16[128,1152]{1,0:T(8,128)(2,1)S(1)}, bf16[128,1152]{1,0:T(8,128)(2,1)S(1)}, u32[]{:S(2)}, u32[]{:S(2)}) %collective-permute-start.9) | collective-permute-done | bytes 294944 | tf_op jit(solution)/shard_map/ppermute | solution.py:38
  37.5 6.3 %collective-permute-done.8.w2 = bf16[128,1152]{1,0:T(8,128)(2,1)S(1)} collective-permute-done((bf16[128,1152]{1,0:T(8,128)(2,1)S(1)}, bf16[128,1152]{1,0:T(8,128)(2,1)S(1)}, u32[]{:S(2)}, u32[]{:S(2)}) %collective-permute-start.8) | collective-permute-done | bytes 294944 | tf_op jit(solution)/shard_map/ppermute | solution.py:38
  43.8 0.7 copy-done.4
  44.5 0.0 collective-permute-done.7.w1
  44.5 3.0 %all-to-all-done.rows_ref.own_ref = bf16[8,144,384]{2,1,0:T(8,128)(2,1)S(1)} async-done(((bf16[8,144,384]{2,1,0:T(8,128)(2,1)}), bf16[8,144,384]{2,1,0:T(8,128)(2,1)S(1)}, u32[]{:S(2)}, u32[]{:S(2)}) %all-to-all-start) | async-done | bytes 884768 | tf_op jit(solution)/shard_map/all_to_all | solution.py:52
  47.5 1.6 %collective-permute-start.11 = (bf16[8,144,384]{2,1,0:T(8,128)(2,1)S(1)}, bf16[8,144,384]{2,1,0:T(8,128)(2,1)}, u32[]{:S(2)}, u32[]{:S(2)}) collective-permute-start(bf16[8,144,384]{2,1,0:T(8,128)(2,1)S(1)} %all-to-all-done.rows_ref.own_ref), channel_id=1, source_target_pairs={{0,64},{1,65},{4,68},{5,69},{8,72},{9,73},{12,76},{13,77},{16,80},... | collective-permute-start | bytes 2654216 | tf_op jit(solution)/shard_map/ppermute | solution.py:38
  49.1 1.7 %collective-permute-start.10 = (bf16[8,144,384]{2,1,0:T(8,128)(2,1)S(1)}, bf16[8,144,384]{2,1,0:T(8,128)(2,1)}, u32[]{:S(2)}, u32[]{:S(2)}) collective-permute-start(bf16[8,144,384]{2,1,0:T(8,128)(2,1)S(1)} %all-to-all-done.rows_ref.own_ref), channel_id=1, source_target_pairs={{0,192},{1,193},{4,196},{5,197},{8,200},{9,201},{12,204},{13,205},... | collective-permute-start | bytes 2654216 | tf_op jit(solution)/shard_map/ppermute | solution.py:38
  50.8 2.8 %shard_map.105 = bf16[8,592,128]{2,1,0:T(8,128)(2,1)} custom-call(bf16[8,144,384]{2,1,0:T(8,128)(2,1)} %copy-done, bf16[128,1152]{1,0:T(8,128)(2,1)} %copy-done.2, bf16[128,1152]{1,0:T(8,128)(2,1)} %collective-permute-done.7.w1, bf16[128,1152]{1,0:T(8,128)(2,1)} %copy-done.4, bf16[128,1152]{1,0:T(8,128)(2,1)} %copy-done.3), custom_call_target="tpu_custom_call" | custom-call | tf_op jit(solution)/shard_map/pallas_call | solution.py:280
  53.6 0.0 collective-permute-done.15.corner_ref
  53.6 5.6 %all-to-all-start.1 = ((bf16[8,592,128]{2,1,0:T(8,128)(2,1)}), bf16[8,592,128]{2,1,0:T(8,128)(2,1)}, u32[]{:S(2)}, u32[]{:S(2)}) async-start(bf16[8,592,128]{2,1,0:T(8,128)(2,1)} %shard_map.105), calls=%async_computation.1 | async-start | bytes 2424832 | tf_op jit(solution)/shard_map/all_to_all | solution.py:52
  59.2 0.2 collective-permute-start.5
  59.4 12.8 %collective-permute-done.6.x2_ref = bf16[4,256,1024]{2,1,0:T(8,128)(2,1)} collective-permute-done((bf16[4,256,1024]{2,1,0:T(8,128)(2,1)S(1)}, bf16[4,256,1024]{2,1,0:T(8,128)(2,1)}, u32[]{:S(2)}, u32[]{:S(2)}) %collective-permute-start.6) | collective-permute-done | bytes 2097184 | tf_op jit(solution)/shard_map/ppermute | solution.py:43
  72.2 0.0 collective-permute-done.11.down_ref
  72.2 0.0 collective-permute-done.10.up_ref
  72.2 1.1 slice.49
  73.3 1.7 %collective-permute-start.14 = (bf16[4,144,384]{2,1,0:T(8,128)(2,1)S(1)}, bf16[4,144,384]{2,1,0:T(8,128)(2,1)S(1)}, u32[]{:S(2)}, u32[]{:S(2)}) collective-permute-start(bf16[4,144,384]{2,1,0:T(8,128)(2,1)S(1)} %slice.49), channel_id=1, source_target_pairs={{0,64},{1,65},{4,68},{5,69},{8,72},{9,73},{12,76},{13,77},{16,80},... | collective-permute-start | bytes 1327112 | tf_op jit(solution)/shard_map/ppermute | solution.py:38
  74.9 1.1 slice.48
  76.0 1.9 %collective-permute-start.13 = (bf16[4,144,384]{2,1,0:T(8,128)(2,1)S(1)}, bf16[4,144,384]{2,1,0:T(8,128)(2,1)S(1)}, u32[]{:S(2)}, u32[]{:S(2)}) collective-permute-start(bf16[4,144,384]{2,1,0:T(8,128)(2,1)S(1)} %slice.48), channel_id=1, source_target_pairs={{0,192},{1,193},{4,196},{5,197},{8,200},{9,201},{12,204},{13,205},... | collective-permute-start | bytes 1327112 | tf_op jit(solution)/shard_map/ppermute | solution.py:38
  77.9 9.3 %collective-permute-done.14.far_high_ref = bf16[4,144,384]{2,1,0:T(8,128)(2,1)S(1)} collective-permute-done((bf16[4,144,384]{2,1,0:T(8,128)(2,1)S(1)}, bf16[4,144,384]{2,1,0:T(8,128)(2,1)S(1)}, u32[]{:S(2)}, u32[]{:S(2)}) %collective-permute-start.14) | collective-permute-done | bytes 442400 | tf_op jit(solution)/shard_map/ppermute | solution.py:38
  87.2 1.3 collective-permute-done.13.far_low_ref
  88.6 2.5 %all-to-all-done.1.last_ref = bf16[8,592,128]{2,1,0:T(8,128)(2,1)} async-done(((bf16[8,592,128]{2,1,0:T(8,128)(2,1)}), bf16[8,592,128]{2,1,0:T(8,128)(2,1)}, u32[]{:S(2)}, u32[]{:S(2)}) %all-to-all-start.1) | async-done | bytes 1212448 | tf_op jit(solution)/shard_map/all_to_all | solution.py:52
  91.1 12.6 %shard_map.106 = f32[4,8,128]{2,1,0:T(8,128)} custom-call(s32[3]{0:T(128)} %pad_add_fusion.at_ref, s32[2,2]{1,0:T(2,128)} %len_ref.3, bf16[4,256,1024]{2,1,0:T(8,128)(2,1)} %bitcast.28, bf16[4,256,1024]{2,1,0:T(8,128)(2,1)} %copy-done.12, bf16[4,256,1024]{2,1,0:T(8,128)(2,1)} %collective-permute-done.6.x2_ref, ...), custom_call_target="tpu_custom_call" | custom-call | flops 4294967296 | bytes 12582912 | tf_op jit(solution)/shard_map/pallas_call | solution.py:298
  103.7 0.7 convert_bitcast_fusion
  104.4 0.1 broadcast_in_dim.32
  104.5 27.0 %all_to_all.15 = bf16[64,4,1024]{2,1,0:T(4,128)(2,1)S(1)} all-to-all(bf16[64,4,1024]{2,1,0:T(4,128)(2,1)S(1)} %broadcast_in_dim.32), channel_id=1, replica_groups=mesh['dp'=64,'tensor'=4] {'dp'}, dimensions={0} | all-to-all | bytes 1048576 | tf_op jit(solution)/shard_map/all_to_all | solution.py:52
  131.5 0.3 multiply_reduce_fusion
  131.8 0.1 reduce_sum.48
  131.9 0.1 copy.14
  132.0 0.2 reshape.34
  132.2 0.7 fusion.12
  132.9 0.3 fusion
  133.2 2.8 %collective-permute-start.17 = (f32[130,128]{1,0:T(8,128)S(1)}, f32[130,128]{1,0:T(8,128)S(1)}, u32[]{:S(2)}, u32[]{:S(2)}) collective-permute-start(f32[130,128]{1,0:T(8,128)S(1)} %pad_maximum_fusion.2), channel_id=1, source_target_pairs={{0,2},{1,3},{2,0},{3,1},{4,6},{5,7},{6,4},{7,5},{8,10},{9,11},{10,... | collective-permute-start | bytes 199688 | tf_op jit(solution)/shard_map/ppermute | solution.py:43
  136.0 0.9 collective-permute-start.16
  137.0 2.2 %collective-permute-done.17 = f32[130,128]{1,0:T(8,128)S(1)} collective-permute-done((f32[130,128]{1,0:T(8,128)S(1)}, f32[130,128]{1,0:T(8,128)S(1)}, u32[]{:S(2)}, u32[]{:S(2)}) %collective-permute-start.17) | collective-permute-done | bytes 66592 | tf_op jit(solution)/shard_map/ppermute | solution.py:43
  139.1 2.2 %collective-permute-done.18 = f32[130,128]{1,0:T(8,128)S(1)} collective-permute-done((f32[130,128]{1,0:T(8,128)S(1)}, f32[130,128]{1,0:T(8,128)S(1)}, u32[]{:S(2)}, u32[]{:S(2)}) %collective-permute-start.18) | collective-permute-done | bytes 66592 | tf_op jit(solution)/shard_map/ppermute | solution.py:43
  141.3 0.1 dynamic-slice_bitcast_fusion
  141.4 0.1 copy.15
  141.5 0.2 fusion.10
  141.7 0.2 exponential_reduce_fusion.1
  141.9 0.1 exponential_reduce_fusion
  142.0 0.6 fusion.11
  142.6 0.6 dynamic_slice.7
  143.2 0.7 multiply_convert_fusion
  (50 shorter events, 0.2 us)
Async XLA Ops:
  0.6 5.8 %copy-start.7 = (bf16[64,256]{1,0:T(8,128)(2,1)S(1)}, bf16[64,256]{1,0:T(8,128)(2,1)}, u32[]{:S(2)}) copy-start(bf16[64,256]{1,0:T(8,128)(2,1)} %param.14) | copy-start | bytes 98308
  0.6 5.8 %copy-start.8 = (bf16[64,256]{1,0:T(8,128)(2,1)S(1)}, bf16[64,256]{1,0:T(8,128)(2,1)}, u32[]{:S(2)}) copy-start(bf16[64,256]{1,0:T(8,128)(2,1)} %param.15) | copy-start | bytes 98308
  0.7 7.4 %copy-start.5 = (bf16[64,1024]{1,0:T(8,128)(2,1)S(1)}, bf16[64,1024]{1,0:T(8,128)(2,1)}, u32[]{:S(2)}) copy-start(bf16[64,1024]{1,0:T(8,128)(2,1)} %param.13) | copy-start | bytes 393220
  3.0 6.2 %collective-permute-start.4 = (bf16[4,1024]{1,0:T(4,128)(2,1)}, bf16[4,1024]{1,0:T(4,128)(2,1)S(1)}, u32[]{:S(2)}, u32[]{:S(2)}) collective-permute-start(bf16[4,1024]{1,0:T(4,128)(2,1)} %shard_map.103.r0), channel_id=1, source_target_pairs={{0,3},{1,2},{2,1},{3,0},{4,7},{5,6},{6,5},{7,4},{8,11},{9,10},{10,... | collective-permute-start | bytes 24584 | tf_op jit(solution)/shard_map/ppermute | solution.py:43
  5.5 5.4 %collective-permute-start.3 = (bf16[4,1024]{1,0:T(4,128)(2,1)}, bf16[4,1024]{1,0:T(4,128)(2,1)S(1)}, u32[]{:S(2)}, u32[]{:S(2)}) collective-permute-start(bf16[4,1024]{1,0:T(4,128)(2,1)} %shard_map.103.r0), channel_id=1, source_target_pairs={{0,2},{1,3},{2,0},{3,1},{4,6},{5,7},{6,4},{7,5},{8,10},{9,11},{10,... | collective-permute-start | bytes 24584 | tf_op jit(solution)/shard_map/ppermute | solution.py:43
  6.2 4.7 %collective-permute-start.2 = (bf16[4,1024]{1,0:T(4,128)(2,1)}, bf16[4,1024]{1,0:T(4,128)(2,1)S(1)}, u32[]{:S(2)}, u32[]{:S(2)}) collective-permute-start(bf16[4,1024]{1,0:T(4,128)(2,1)} %shard_map.103.r0), channel_id=1, source_target_pairs={{0,1},{1,0},{2,3},{3,2},{4,5},{5,4},{6,7},{7,6},{8,9},{9,8},{10,11... | collective-permute-start | bytes 24584 | tf_op jit(solution)/shard_map/ppermute | solution.py:43
  6.4 6.7 %collective-permute-start = (bf16[64,512]{1,0:T(8,128)(2,1)S(1)}, bf16[64,512]{1,0:T(8,128)(2,1)S(1)}, u32[]{:S(2)}, u32[]{:S(2)}) collective-permute-start(bf16[64,512]{1,0:T(8,128)(2,1)S(1)} %constant_dynamic-update-slice_fusion), channel_id=1, source_target_pairs={{0,32},{4,36},{8,40},{12,44},{16,48},{20,52},{24,56},{28,60},{32,0... | collective-permute-start | bytes 196616 | tf_op jit(solution)/shard_map/ppermute | solution.py:48
  8.0 5.6 %collective-permute-start.1 = (bf16[64,1024]{1,0:T(8,128)(2,1)S(1)}, bf16[64,1024]{1,0:T(8,128)(2,1)S(1)}, u32[]{:S(2)}, u32[]{:S(2)}) collective-permute-start(bf16[64,1024]{1,0:T(8,128)(2,1)S(1)} %copy-done.5), channel_id=1, source_target_pairs={{0,32},{4,36},{8,40},{12,44},{16,48},{20,52},{24,56},{28,60},{32,0... | collective-permute-start | bytes 393224 | tf_op jit(solution)/shard_map/ppermute | solution.py:48
  9.2 1.7 %copy-start.9 = (bf16[4,1024]{1,0:T(4,128)(2,1)}, bf16[4,1024]{1,0:T(4,128)(2,1)S(1)}, u32[]{:S(2)}) copy-start(bf16[4,1024]{1,0:T(4,128)(2,1)S(1)} %collective-permute-done.4.r3) | copy-start | bytes 24580
  10.9 0.6 copy-start.10
  10.9 0.6 copy-start.11
  13.7 10.6 %copy-start.1 = (bf16[2,2,256,1024]{3,2,1,0:T(8,128)(2,1)S(1)}, bf16[2,2,256,1024]{3,2,1,0:T(8,128)(2,1)}, u32[]{:S(2)}) copy-start(bf16[2,2,256,1024]{3,2,1,0:T(8,128)(2,1)} %param.8) | copy-start | bytes 6291460
  15.7 31.8 %all-to-all-start = ((bf16[8,144,384]{2,1,0:T(8,128)(2,1)}), bf16[8,144,384]{2,1,0:T(8,128)(2,1)S(1)}, u32[]{:S(2)}, u32[]{:S(2)}) async-start(bf16[8,144,384]{2,1,0:T(8,128)(2,1)} %pad_maximum_fusion), calls=%async_computation | async-start | bytes 1769472 | tf_op jit(solution)/shard_map/all_to_all | solution.py:52
  24.3 47.9 %collective-permute-start.6 = (bf16[4,256,1024]{2,1,0:T(8,128)(2,1)S(1)}, bf16[4,256,1024]{2,1,0:T(8,128)(2,1)}, u32[]{:S(2)}, u32[]{:S(2)}) collective-permute-start(bf16[4,256,1024]{2,1,0:T(8,128)(2,1)S(1)} %bitcast.29), channel_id=1, source_target_pairs={{0,2},{1,3},{2,0},{3,1},{4,6},{5,7},{6,4},{7,5},{8,10},{9,11},{10,... | collective-permute-start | bytes 6291464 | tf_op jit(solution)/shard_map/ppermute | solution.py:43
  27.4 23.4 %copy-start.2 = (bf16[128,1152]{1,0:T(8,128)(2,1)}, bf16[128,1152]{1,0:T(8,128)(2,1)S(1)}, u32[]{:S(2)}) copy-start(bf16[128,1152]{1,0:T(8,128)(2,1)S(1)} %maximum_maximum_fusion.w0) | copy-start | bytes 884740
  27.4 10.1 %collective-permute-start.9 = (bf16[128,1152]{1,0:T(8,128)(2,1)S(1)}, bf16[128,1152]{1,0:T(8,128)(2,1)S(1)}, u32[]{:S(2)}, u32[]{:S(2)}) collective-permute-start(bf16[128,1152]{1,0:T(8,128)(2,1)S(1)} %maximum_maximum_fusion.w0), channel_id=1, source_target_pairs={{0,64},{1,65},{4,68},{5,69},{8,72},{9,73},{12,76},{13,77},{16,80},... | collective-permute-start | bytes 884744 | tf_op jit(solution)/shard_map/ppermute | solution.py:38
  29.0 14.7 %collective-permute-start.8 = (bf16[128,1152]{1,0:T(8,128)(2,1)S(1)}, bf16[128,1152]{1,0:T(8,128)(2,1)S(1)}, u32[]{:S(2)}, u32[]{:S(2)}) collective-permute-start(bf16[128,1152]{1,0:T(8,128)(2,1)S(1)} %maximum_maximum_fusion.w0), channel_id=1, source_target_pairs={{0,128},{1,129},{4,132},{5,133},{8,136},{9,137},{12,140},{13,141},... | collective-permute-start | bytes 884744 | tf_op jit(solution)/shard_map/ppermute | solution.py:38
  31.9 12.6 %collective-permute-start.7 = (bf16[128,1152]{1,0:T(8,128)(2,1)S(1)}, bf16[128,1152]{1,0:T(8,128)(2,1)}, u32[]{:S(2)}, u32[]{:S(2)}) collective-permute-start(bf16[128,1152]{1,0:T(8,128)(2,1)S(1)} %maximum_maximum_fusion.w0), channel_id=1, source_target_pairs={{0,192},{1,193},{4,196},{5,197},{8,200},{9,201},{12,204},{13,205},... | collective-permute-start | bytes 884744 | tf_op jit(solution)/shard_map/ppermute | solution.py:38
  37.5 6.3 %copy-start.3 = (bf16[128,1152]{1,0:T(8,128)(2,1)}, bf16[128,1152]{1,0:T(8,128)(2,1)S(1)}, u32[]{:S(2)}) copy-start(bf16[128,1152]{1,0:T(8,128)(2,1)S(1)} %collective-permute-done.9.w3) | copy-start | bytes 884740
  43.8 0.7 copy-start.4
  47.5 3.3 %copy-start = (bf16[8,144,384]{2,1,0:T(8,128)(2,1)}, bf16[8,144,384]{2,1,0:T(8,128)(2,1)S(1)}, u32[]{:S(2)}) copy-start(bf16[8,144,384]{2,1,0:T(8,128)(2,1)S(1)} %all-to-all-done.rows_ref.own_ref) | copy-start | bytes 2654212
  47.5 24.7 %collective-permute-start.11 = (bf16[8,144,384]{2,1,0:T(8,128)(2,1)S(1)}, bf16[8,144,384]{2,1,0:T(8,128)(2,1)}, u32[]{:S(2)}, u32[]{:S(2)}) collective-permute-start(bf16[8,144,384]{2,1,0:T(8,128)(2,1)S(1)} %all-to-all-done.rows_ref.own_ref), channel_id=1, source_target_pairs={{0,64},{1,65},{4,68},{5,69},{8,72},{9,73},{12,76},{13,77},{16,80},... | collective-permute-start | bytes 2654216 | tf_op jit(solution)/shard_map/ppermute | solution.py:38
  49.1 23.1 %collective-permute-start.10 = (bf16[8,144,384]{2,1,0:T(8,128)(2,1)S(1)}, bf16[8,144,384]{2,1,0:T(8,128)(2,1)}, u32[]{:S(2)}, u32[]{:S(2)}) collective-permute-start(bf16[8,144,384]{2,1,0:T(8,128)(2,1)S(1)} %all-to-all-done.rows_ref.own_ref), channel_id=1, source_target_pairs={{0,192},{1,193},{4,196},{5,197},{8,200},{9,201},{12,204},{13,205},... | collective-permute-start | bytes 2654216 | tf_op jit(solution)/shard_map/ppermute | solution.py:38
  50.8 2.8 %collective-permute-start.15 = (bf16[16,384]{1,0:T(8,128)(2,1)S(1)}, bf16[16,384]{1,0:T(8,128)(2,1)S(1)}, u32[]{:S(2)}, u32[]{:S(2)}) collective-permute-start(bf16[16,384]{1,0:T(8,128)(2,1)S(1)} %slice_bitcast_fusion), channel_id=1, source_target_pairs={{0,1},{1,0},{2,3},{3,2},{4,5},{5,4},{6,7},{7,6},{8,9},{9,8},{10,11... | collective-permute-start | bytes 36872 | tf_op jit(solution)/shard_map/ppermute | solution.py:43
  53.6 22.4 %copy-start.15 = (bf16[16,384]{1,0:T(8,128)(2,1)}, bf16[16,384]{1,0:T(8,128)(2,1)S(1)}, u32[]{:S(2)}) copy-start(bf16[16,384]{1,0:T(8,128)(2,1)S(1)} %collective-permute-done.15.corner_ref) | copy-start | bytes 36868
  53.6 37.4 %all-to-all-start.1 = ((bf16[8,592,128]{2,1,0:T(8,128)(2,1)}), bf16[8,592,128]{2,1,0:T(8,128)(2,1)}, u32[]{:S(2)}, u32[]{:S(2)}) async-start(bf16[8,592,128]{2,1,0:T(8,128)(2,1)} %shard_map.105), calls=%async_computation.1 | async-start | bytes 2424832 | tf_op jit(solution)/shard_map/all_to_all | solution.py:52
  59.2 18.7 %collective-permute-start.5 = (bf16[4,256,1024]{2,1,0:T(8,128)(2,1)S(1)}, bf16[4,256,1024]{2,1,0:T(8,128)(2,1)S(1)}, u32[]{:S(2)}, u32[]{:S(2)}) collective-permute-start(bf16[4,256,1024]{2,1,0:T(8,128)(2,1)S(1)} %bitcast.30), channel_id=1, source_target_pairs={{0,1},{1,0},{2,3},{3,2},{4,5},{5,4},{6,7},{7,6},{8,9},{9,8},{10,11... | collective-permute-start | bytes 6291464 | tf_op jit(solution)/shard_map/ppermute | solution.py:43
  72.2 18.9 %collective-permute-start.12 = (bf16[4,256,1024]{2,1,0:T(8,128)(2,1)}, bf16[4,256,1024]{2,1,0:T(8,128)(2,1)}, u32[]{:S(2)}, u32[]{:S(2)}) collective-permute-start(bf16[4,256,1024]{2,1,0:T(8,128)(2,1)} %collective-permute-done.6.x2_ref), channel_id=1, source_target_pairs={{0,1},{1,0},{2,3},{3,2},{4,5},{5,4},{6,7},{7,6},{8,9},{9,8},{10,11... | collective-permute-start | bytes 6291464 | tf_op jit(solution)/shard_map/ppermute | solution.py:43
  73.3 13.9 %collective-permute-start.14 = (bf16[4,144,384]{2,1,0:T(8,128)(2,1)S(1)}, bf16[4,144,384]{2,1,0:T(8,128)(2,1)S(1)}, u32[]{:S(2)}, u32[]{:S(2)}) collective-permute-start(bf16[4,144,384]{2,1,0:T(8,128)(2,1)S(1)} %slice.49), channel_id=1, source_target_pairs={{0,64},{1,65},{4,68},{5,69},{8,72},{9,73},{12,76},{13,77},{16,80},... | collective-permute-start | bytes 1327112 | tf_op jit(solution)/shard_map/ppermute | solution.py:38
  76.0 12.6 %collective-permute-start.13 = (bf16[4,144,384]{2,1,0:T(8,128)(2,1)S(1)}, bf16[4,144,384]{2,1,0:T(8,128)(2,1)S(1)}, u32[]{:S(2)}, u32[]{:S(2)}) collective-permute-start(bf16[4,144,384]{2,1,0:T(8,128)(2,1)S(1)} %slice.48), channel_id=1, source_target_pairs={{0,192},{1,193},{4,196},{5,197},{8,200},{9,201},{12,204},{13,205},... | collective-permute-start | bytes 1327112 | tf_op jit(solution)/shard_map/ppermute | solution.py:38
  77.9 9.3 %copy-start.12 = (bf16[4,256,1024]{2,1,0:T(8,128)(2,1)}, bf16[4,256,1024]{2,1,0:T(8,128)(2,1)S(1)}, u32[]{:S(2)}) copy-start(bf16[4,256,1024]{2,1,0:T(8,128)(2,1)S(1)} %collective-permute-done.5.x1_ref) | copy-start | bytes 6291460
  87.2 3.9 %copy-start.13 = (bf16[4,144,384]{2,1,0:T(8,128)(2,1)}, bf16[4,144,384]{2,1,0:T(8,128)(2,1)S(1)}, u32[]{:S(2)}) copy-start(bf16[4,144,384]{2,1,0:T(8,128)(2,1)S(1)} %collective-permute-done.14.far_high_ref) | copy-start | bytes 1327108
  88.5 2.5 %copy-start.14 = (bf16[4,144,384]{2,1,0:T(8,128)(2,1)}, bf16[4,144,384]{2,1,0:T(8,128)(2,1)S(1)}, u32[]{:S(2)}) copy-start(bf16[4,144,384]{2,1,0:T(8,128)(2,1)S(1)} %collective-permute-done.13.far_low_ref) | copy-start | bytes 1327108
  132.0 5.0 %copy-start.6 = (f32[4,8,128]{2,1,0:T(8,128)S(1)}, f32[4,8,128]{2,1,0:T(8,128)}, u32[]{:S(2)}) copy-start(f32[4,8,128]{2,1,0:T(8,128)} %shard_map.106) | copy-start | bytes 49156
  133.2 5.9 %collective-permute-start.17 = (f32[130,128]{1,0:T(8,128)S(1)}, f32[130,128]{1,0:T(8,128)S(1)}, u32[]{:S(2)}, u32[]{:S(2)}) collective-permute-start(f32[130,128]{1,0:T(8,128)S(1)} %pad_maximum_fusion.2), channel_id=1, source_target_pairs={{0,2},{1,3},{2,0},{3,1},{4,6},{5,7},{6,4},{7,5},{8,10},{9,11},{10,... | collective-permute-start | bytes 199688 | tf_op jit(solution)/shard_map/ppermute | solution.py:43
  136.0 5.2 %collective-permute-start.18 = (f32[130,128]{1,0:T(8,128)S(1)}, f32[130,128]{1,0:T(8,128)S(1)}, u32[]{:S(2)}, u32[]{:S(2)}) collective-permute-start(f32[130,128]{1,0:T(8,128)S(1)} %pad_maximum_fusion.2), channel_id=1, source_target_pairs={{0,3},{1,2},{2,1},{3,0},{4,7},{5,6},{6,5},{7,4},{8,11},{9,10},{10,... | collective-permute-start | bytes 199688 | tf_op jit(solution)/shard_map/ppermute | solution.py:43
  136.0 5.2 %collective-permute-start.16 = (f32[130,128]{1,0:T(8,128)S(1)}, f32[130,128]{1,0:T(8,128)S(1)}, u32[]{:S(2)}, u32[]{:S(2)}) collective-permute-start(f32[130,128]{1,0:T(8,128)S(1)} %pad_maximum_fusion.2), channel_id=1, source_target_pairs={{0,1},{1,0},{2,3},{3,2},{4,5},{5,4},{6,7},{7,6},{8,9},{9,8},{10,11... | collective-permute-start | bytes 199688 | tf_op jit(solution)/shard_map/ppermute | solution.py:43

commit v10 on v7

--- a/solution.py
+++ b/solution.py
@@ -14,6 +14,8 @@
 Y, XLO, Z = 4, 2, 8
 XHI, CORES = 2, 2
 GROUPS = Y * XLO
+XZ_GROUPS = [[y * XLO * Z + i for i in range(XLO * Z)] for y in range(Y)]
+Y_GROUPS = [[y * XLO * Z + i for y in range(Y)] for i in range(XLO * Z)]
 Z_GROUPS = [[g * Z + z for z in range(Z)] for g in range(GROUPS)]
 
 
@@ -385,7 +387,8 @@
     ).reshape(seq_count, width_local)
 
     sent = mixed.astype(jnp.bfloat16)
-    every = exchange(jnp.broadcast_to(sent[None], (GROUPS * Z,) + sent.shape), None)
+    near = exchange(jnp.broadcast_to(sent[None], (XLO * Z,) + sent.shape), XZ_GROUPS)
+    every = exchange(jnp.broadcast_to(near[None], (Y,) + near.shape), Y_GROUPS)
     every = every.reshape(-1, 2, width_local)
     dots = jnp.dot(every[:, 0], every[:, 1].T, preferred_element_type=jnp.float32)
     every_f32 = every.astype(jnp.float32)

time: 146 us -> 146 us (level)
    all_to_all x1 -> x2, blocking collectives: 24.5 us -> 23.9 us  [exchange(): lax.all_to_all(chunks, 'dp', split_axis=0, concat_axis=0, tiled=True, axi...]
where the time goes in v10:
time: 146 us; the launch traced here: 145 us
  waiting for transfers between devices  47.1 us (32%)
  starting transfers between devices  39.5 us (27%)
  blocking collectives  23.9 us (16%)
  Pallas kernels  19.3 us (13%)
  local copies, waits for them, and re-layouts  6.68 us (5%)
  other arithmetic  5.63 us (4%)
  between operations  2.64 us (2%)
    all_to_all x2, blocking collectives, exchange(): lax.all_to_all(chunks, 'dp', split_axis=0, concat_axis=0, tiled=True, axi...  23.9 us
    all_to_all x2, waiting for transfers between devices, exchange(): lax.all_to_all(chunks, 'dp', split_axis=0, concat_axis=0, tiled=True, axi...  19.8 us
    ppermute x10, waiting for transfers between devices, swap_tensor(): return lax.ppermute(array, 'tensor', [(i, i ^ mask) for i in range(size)])  17.3 us
    all_to_all x2, starting transfers between devices, exchange(): lax.all_to_all(chunks, 'dp', split_axis=0, concat_axis=0, tiled=True, axi...  14.2 us
    ppermute x7, starting transfers between devices, shift(): return lax.ppermute(array, ('dp', 'tensor'), pairs)  12.8 us
    pallas_call x1, Pallas kernels, kv_attend(): pl.pallas_call(kv_attend_kernel, grid=(seq_count // per_step,), in_specs=...  12.6 us
    ppermute x10, starting transfers between devices, swap_tensor(): return lax.ppermute(array, 'tensor', [(i, i ^ mask) for i in range(size)])  10.4 us
    ppermute x7, waiting for transfers between devices, shift(): return lax.ppermute(array, ('dp', 'tensor'), pairs)  9.58 us
  transfers between devices with their start and end apart: 21, of which 9 were waited for; matrix products, arithmetic and copies ran while one was open for 3% of the time, Pallas kernels for 3%

profile of v10, /device:TPU:32, one launch (start us, length us, event | category | flops | bytes accessed | tf_op | source)
XLA Modules:
  0.0 145.0 jit_solution(7613804545473593806)
XLA Ops:
  0.7 2.3 %shard_map.103.r0 = bf16[4,1024]{1,0:T(4,128)(2,1)} custom-call(s32[2,2]{1,0:T(2,128)} %len_ref.3, bf16[4,256,1024]{2,1,0:T(8,128)(2,1)} %bitcast.27), custom_call_target="tpu_custom_call" | custom-call | tf_op jit(solution)/shard_map/pallas_call | solution.py:251
  3.0 2.5 %collective-permute-start.4 = (bf16[4,1024]{1,0:T(4,128)(2,1)}, bf16[4,1024]{1,0:T(4,128)(2,1)S(1)}, u32[]{:S(2)}, u32[]{:S(2)}) collective-permute-start(bf16[4,1024]{1,0:T(4,128)(2,1)} %shard_map.103.r0), channel_id=1, source_target_pairs={{0,3},{1,2},{2,1},{3,0},{4,7},{5,6},{6,5},{7,4},{8,11},{9,10},{10,... | collective-permute-start | bytes 24584 | tf_op jit(solution)/shard_map/ppermute | solution.py:45
  5.5 0.7 collective-permute-start.3
  6.2 0.2 collective-permute-start.2
  6.4 1.6 %collective-permute-start = (bf16[64,512]{1,0:T(8,128)(2,1)S(1)}, bf16[64,512]{1,0:T(8,128)(2,1)S(1)}, u32[]{:S(2)}, u32[]{:S(2)}) collective-permute-start(bf16[64,512]{1,0:T(8,128)(2,1)S(1)} %constant_dynamic-update-slice_fusion), channel_id=1, source_target_pairs={{0,32},{4,36},{8,40},{12,44},{16,48},{20,52},{24,56},{28,60},{32,0... | collective-permute-start | bytes 196616 | tf_op jit(solution)/shard_map/ppermute | solution.py:50
  8.0 0.5 collective-permute-start.1
  8.5 0.7 pad_add_fusion.at_ref
  9.2 1.7 %collective-permute-done.3.r2 = bf16[4,1024]{1,0:T(4,128)(2,1)S(1)} collective-permute-done((bf16[4,1024]{1,0:T(4,128)(2,1)}, bf16[4,1024]{1,0:T(4,128)(2,1)S(1)}, u32[]{:S(2)}, u32[]{:S(2)}) %collective-permute-start.3) | collective-permute-done | bytes 8224 | tf_op jit(solution)/shard_map/ppermute | solution.py:45
  10.9 0.0 collective-permute-done.2.r1
  10.9 0.6 copy-done.8
  11.5 0.0 copy-done.9
  11.5 1.7 %shard_map.104 = bf16[8,16,384]{2,1,0:T(8,128)(2,1)} custom-call(s32[3]{0:T(128)} %pad_add_fusion.at_ref, bf16[4,1024]{1,0:T(4,128)(2,1)} %shard_map.103.r0, bf16[4,1024]{1,0:T(4,128)(2,1)} %copy-done.9, bf16[4,1024]{1,0:T(4,128)(2,1)} %copy-done.8, bf16[4,1024]{1,0:T(4,128)(2,1)} %copy-done.7, f32[1,4096]{1,0:T(1,128)} %bitcast.32), custom_call_target="tpu_custom_call" | custom-call | tf_op jit(solution)/shard_map/pallas_call | solution.py:266
  13.2 0.4 collective-permute-done.1
  13.6 0.1 broadcast_in_dim.15
  13.7 0.0 copy-start.1
  13.7 2.1 %pad_maximum_fusion = bf16[8,144,384]{2,1,0:T(8,128)(2,1)} fusion(bf16[8,16,384]{2,1,0:T(8,128)(2,1)} %shard_map.104, bf16[8,128,384]{2,1,0:T(8,128)(2,1)S(1)} %broadcast_in_dim.15), kind=kLoop, calls=%fused_computation.1 | loop fusion | flops 1769472 | bytes 1769472 | tf_op jit(solution)/shard_map/concatenate | solution.py:355
  15.7 8.6 %all-to-all-start = ((bf16[8,144,384]{2,1,0:T(8,128)(2,1)}), bf16[8,144,384]{2,1,0:T(8,128)(2,1)S(1)}, u32[]{:S(2)}, u32[]{:S(2)}) async-start(bf16[8,144,384]{2,1,0:T(8,128)(2,1)} %pad_maximum_fusion), calls=%async_computation | async-start | bytes 1769472 | tf_op jit(solution)/shard_map/all_to_all | solution.py:54
  24.3 3.0 %collective-permute-start.6 = (bf16[4,256,1024]{2,1,0:T(8,128)(2,1)S(1)}, bf16[4,256,1024]{2,1,0:T(8,128)(2,1)}, u32[]{:S(2)}, u32[]{:S(2)}) collective-permute-start(bf16[4,256,1024]{2,1,0:T(8,128)(2,1)S(1)} %bitcast.29), channel_id=1, source_target_pairs={{0,2},{1,3},{2,0},{3,1},{4,6},{5,7},{6,4},{7,5},{8,10},{9,11},{10,... | collective-permute-start | bytes 6291464 | tf_op jit(solution)/shard_map/ppermute | solution.py:45
  27.4 1.7 %collective-permute-start.9 = (bf16[128,1152]{1,0:T(8,128)(2,1)S(1)}, bf16[128,1152]{1,0:T(8,128)(2,1)}, u32[]{:S(2)}, u32[]{:S(2)}) collective-permute-start(bf16[128,1152]{1,0:T(8,128)(2,1)S(1)} %maximum_maximum_fusion.w0), channel_id=1, source_target_pairs={{0,64},{1,65},{4,68},{5,69},{8,72},{9,73},{12,76},{13,77},{16,80},... | collective-permute-start | bytes 884744 | tf_op jit(solution)/shard_map/ppermute | solution.py:40
  29.0 2.9 %collective-permute-start.8 = (bf16[128,1152]{1,0:T(8,128)(2,1)S(1)}, bf16[128,1152]{1,0:T(8,128)(2,1)}, u32[]{:S(2)}, u32[]{:S(2)}) collective-permute-start(bf16[128,1152]{1,0:T(8,128)(2,1)S(1)} %maximum_maximum_fusion.w0), channel_id=1, source_target_pairs={{0,128},{1,129},{4,132},{5,133},{8,136},{9,137},{12,140},{13,141},... | collective-permute-start | bytes 884744 | tf_op jit(solution)/shard_map/ppermute | solution.py:40
  31.9 1.3 collective-permute-start.7
  33.3 14.3 %all-to-all-done.rows_ref = bf16[8,144,384]{2,1,0:T(8,128)(2,1)S(1)} async-done(((bf16[8,144,384]{2,1,0:T(8,128)(2,1)}), bf16[8,144,384]{2,1,0:T(8,128)(2,1)S(1)}, u32[]{:S(2)}, u32[]{:S(2)}) %all-to-all-start) | async-done | bytes 884768 | tf_op jit(solution)/shard_map/all_to_all | solution.py:54
  47.5 1.1 slice.50.own_ref
  48.6 1.7 %collective-permute-start.11 = (bf16[8,128,384]{2,1,0:T(8,128)(2,1)}, bf16[8,128,384]{2,1,0:T(8,128)(2,1)}, u32[]{:S(2)}, u32[]{:S(2)}) collective-permute-start(bf16[8,128,384]{2,1,0:T(8,128)(2,1)} %slice.50.own_ref), channel_id=1, source_target_pairs={{0,64},{1,65},{4,68},{5,69},{8,72},{9,73},{12,76},{13,77},{16,80},... | collective-permute-start | bytes 2359304 | tf_op jit(solution)/shard_map/ppermute | solution.py:40
  50.3 1.7 %collective-permute-start.10 = (bf16[8,128,384]{2,1,0:T(8,128)(2,1)}, bf16[8,128,384]{2,1,0:T(8,128)(2,1)}, u32[]{:S(2)}, u32[]{:S(2)}) collective-permute-start(bf16[8,128,384]{2,1,0:T(8,128)(2,1)} %slice.50.own_ref), channel_id=1, source_target_pairs={{0,192},{1,193},{4,196},{5,197},{8,200},{9,201},{12,204},{13,205},... | collective-permute-start | bytes 2359304 | tf_op jit(solution)/shard_map/ppermute | solution.py:40
  52.0 0.7 slice_bitcast_fusion
  52.7 0.0 collective-permute-start.15
  52.7 2.8 %shard_map.105 = bf16[8,592,128]{2,1,0:T(8,128)(2,1)} custom-call(bf16[8,144,384]{2,1,0:T(8,128)(2,1)} %copy-done, bf16[128,1152]{1,0:T(8,128)(2,1)} %copy-done.2, bf16[128,1152]{1,0:T(8,128)(2,1)} %collective-permute-done.7.w1, bf16[128,1152]{1,0:T(8,128)(2,1)} %collective-permute-done.8.w2, bf16[128,1152]{1,0:T(8,128)(2,1)} %collective-permute-done.9.w3), custom_call_target="tpu_custom_call" | custom-call | tf_op jit(solution)/shard_map/pallas_call | solution.py:282
  55.5 0.0 collective-permute-done.15.corner_ref
  55.5 5.6 %all-to-all-start.1 = ((bf16[8,592,128]{2,1,0:T(8,128)(2,1)}), bf16[8,592,128]{2,1,0:T(8,128)(2,1)}, u32[]{:S(2)}, u32[]{:S(2)}) async-start(bf16[8,592,128]{2,1,0:T(8,128)(2,1)} %shard_map.105), calls=%async_computation.1 | async-start | bytes 2424832 | tf_op jit(solution)/shard_map/all_to_all | solution.py:54
  61.1 0.2 collective-permute-start.5
  61.3 10.8 %collective-permute-done.6.x2_ref = bf16[4,256,1024]{2,1,0:T(8,128)(2,1)} collective-permute-done((bf16[4,256,1024]{2,1,0:T(8,128)(2,1)S(1)}, bf16[4,256,1024]{2,1,0:T(8,128)(2,1)}, u32[]{:S(2)}, u32[]{:S(2)}) %collective-permute-start.6) | collective-permute-done | bytes 2097184 | tf_op jit(solution)/shard_map/ppermute | solution.py:45
  72.2 0.0 collective-permute-done.11.down_ref
  72.2 0.0 collective-permute-done.10.up_ref
  72.2 1.0 slice.54
  73.3 1.7 %collective-permute-start.14 = (bf16[4,128,384]{2,1,0:T(8,128)(2,1)S(1)}, bf16[4,128,384]{2,1,0:T(8,128)(2,1)S(1)}, u32[]{:S(2)}, u32[]{:S(2)}) collective-permute-start(bf16[4,128,384]{2,1,0:T(8,128)(2,1)S(1)} %slice.54), channel_id=1, source_target_pairs={{0,64},{1,65},{4,68},{5,69},{8,72},{9,73},{12,76},{13,77},{16,80},... | collective-permute-start | bytes 1179656 | tf_op jit(solution)/shard_map/ppermute | solution.py:40
  74.9 1.0 slice.53
  76.0 1.9 %collective-permute-start.13 = (bf16[4,128,384]{2,1,0:T(8,128)(2,1)S(1)}, bf16[4,128,384]{2,1,0:T(8,128)(2,1)S(1)}, u32[]{:S(2)}, u32[]{:S(2)}) collective-permute-start(bf16[4,128,384]{2,1,0:T(8,128)(2,1)S(1)} %slice.53), channel_id=1, source_target_pairs={{0,192},{1,193},{4,196},{5,197},{8,200},{9,201},{12,204},{13,205},... | collective-permute-start | bytes 1179656 | tf_op jit(solution)/shard_map/ppermute | solution.py:40
  77.9 8.2 %collective-permute-done.14.far_high_ref = bf16[4,128,384]{2,1,0:T(8,128)(2,1)S(1)} collective-permute-done((bf16[4,128,384]{2,1,0:T(8,128)(2,1)S(1)}, bf16[4,128,384]{2,1,0:T(8,128)(2,1)S(1)}, u32[]{:S(2)}, u32[]{:S(2)}) %collective-permute-start.14) | collective-permute-done | bytes 393248 | tf_op jit(solution)/shard_map/ppermute | solution.py:40
  86.1 1.3 collective-permute-done.13.far_low_ref
  87.5 5.5 %all-to-all-done.1.last_ref = bf16[8,592,128]{2,1,0:T(8,128)(2,1)} async-done(((bf16[8,592,128]{2,1,0:T(8,128)(2,1)}), bf16[8,592,128]{2,1,0:T(8,128)(2,1)}, u32[]{:S(2)}, u32[]{:S(2)}) %all-to-all-start.1) | async-done | bytes 1212448 | tf_op jit(solution)/shard_map/all_to_all | solution.py:54
  93.0 12.6 %shard_map.106 = f32[4,8,128]{2,1,0:T(8,128)} custom-call(s32[3]{0:T(128)} %pad_add_fusion.at_ref, s32[2,2]{1,0:T(2,128)} %len_ref.3, bf16[4,256,1024]{2,1,0:T(8,128)(2,1)} %bitcast.28, bf16[4,256,1024]{2,1,0:T(8,128)(2,1)} %copy-done.10, bf16[4,256,1024]{2,1,0:T(8,128)(2,1)} %collective-permute-done.6.x2_ref, ...), custom_call_target="tpu_custom_call" | custom-call | flops 4294967296 | bytes 12582912 | tf_op jit(solution)/shard_map/pallas_call | solution.py:300
  105.6 0.7 convert_bitcast_fusion
  106.4 12.4 %all_to_all.20 = bf16[16,4,1024]{2,1,0:T(4,128)(2,1)S(1)} all-to-all(bf16[16,4,1024]{2,1,0:T(4,128)(2,1)S(1)} %broadcast_in_dim.38), channel_id=1, replica_groups={{0,4,8,12,16,20,24,28,32,36,40,44,48,52,56,60},{64,68,72,76,80,84,88,92..., dimensions={0} | all-to-all | bytes 262144 | tf_op jit(solution)/shard_map/all_to_all | solution.py:54
  118.8 0.2 broadcast_in_dim.39
  119.0 11.4 %all_to_all.21 = bf16[4,16,4,1024]{3,2,1,0:T(4,128)(2,1)S(1)} all-to-all(bf16[4,16,4,1024]{3,2,1,0:T(4,128)(2,1)S(1)} %broadcast_in_dim.39), channel_id=1, replica_groups={{0,64,128,192},{4,68,132,196},{8,72,136,200},{12,76,140,204},{16,80,144..., dimensions={0} | all-to-all | bytes 1048576 | tf_op jit(solution)/shard_map/all_to_all | solution.py:54
  130.4 0.3 multiply_reduce_fusion
  130.7 0.1 reduce_sum.48
  130.8 0.1 copy.14
  130.9 0.2 reshape.35
  131.1 0.7 fusion.12
  131.8 0.3 fusion
  132.1 3.3 %collective-permute-start.17 = (f32[130,128]{1,0:T(8,128)S(1)}, f32[130,128]{1,0:T(8,128)S(1)}, u32[]{:S(2)}, u32[]{:S(2)}) collective-permute-start(f32[130,128]{1,0:T(8,128)S(1)} %pad_maximum_fusion.2), channel_id=1, source_target_pairs={{0,2},{1,3},{2,0},{3,1},{4,6},{5,7},{6,4},{7,5},{8,10},{9,11},{10,... | collective-permute-start | bytes 199688 | tf_op jit(solution)/shard_map/ppermute | solution.py:45
  135.4 0.4 collective-permute-start.16
  135.9 2.2 %collective-permute-done.17 = f32[130,128]{1,0:T(8,128)S(1)} collective-permute-done((f32[130,128]{1,0:T(8,128)S(1)}, f32[130,128]{1,0:T(8,128)S(1)}, u32[]{:S(2)}, u32[]{:S(2)}) %collective-permute-start.17) | collective-permute-done | bytes 66592 | tf_op jit(solution)/shard_map/ppermute | solution.py:45
  138.0 2.6 %collective-permute-done.18 = f32[130,128]{1,0:T(8,128)S(1)} collective-permute-done((f32[130,128]{1,0:T(8,128)S(1)}, f32[130,128]{1,0:T(8,128)S(1)}, u32[]{:S(2)}, u32[]{:S(2)}) %collective-permute-start.18) | collective-permute-done | bytes 66592 | tf_op jit(solution)/shard_map/ppermute | solution.py:45
  140.7 0.1 dynamic-slice_bitcast_fusion
  140.8 0.1 copy.15
  140.9 0.2 fusion.10
  141.0 0.2 exponential_reduce_fusion.1
  141.2 0.1 exponential_reduce_fusion
  141.4 0.6 fusion.11
  142.0 0.6 dynamic_slice.7
  142.6 0.7 multiply_convert_fusion
  (49 shorter events, 0.2 us)
Async XLA Ops:
  0.6 5.8 %copy-start.5 = (bf16[64,256]{1,0:T(8,128)(2,1)S(1)}, bf16[64,256]{1,0:T(8,128)(2,1)}, u32[]{:S(2)}) copy-start(bf16[64,256]{1,0:T(8,128)(2,1)} %param.14) | copy-start | bytes 98308
  0.6 5.8 %copy-start.6 = (bf16[64,256]{1,0:T(8,128)(2,1)S(1)}, bf16[64,256]{1,0:T(8,128)(2,1)}, u32[]{:S(2)}) copy-start(bf16[64,256]{1,0:T(8,128)(2,1)} %param.15) | copy-start | bytes 98308
  0.7 7.4 %copy-start.3 = (bf16[64,1024]{1,0:T(8,128)(2,1)S(1)}, bf16[64,1024]{1,0:T(8,128)(2,1)}, u32[]{:S(2)}) copy-start(bf16[64,1024]{1,0:T(8,128)(2,1)} %param.13) | copy-start | bytes 393220
  3.0 6.2 %collective-permute-start.4 = (bf16[4,1024]{1,0:T(4,128)(2,1)}, bf16[4,1024]{1,0:T(4,128)(2,1)S(1)}, u32[]{:S(2)}, u32[]{:S(2)}) collective-permute-start(bf16[4,1024]{1,0:T(4,128)(2,1)} %shard_map.103.r0), channel_id=1, source_target_pairs={{0,3},{1,2},{2,1},{3,0},{4,7},{5,6},{6,5},{7,4},{8,11},{9,10},{10,... | collective-permute-start | bytes 24584 | tf_op jit(solution)/shard_map/ppermute | solution.py:45
  5.5 5.4 %collective-permute-start.3 = (bf16[4,1024]{1,0:T(4,128)(2,1)}, bf16[4,1024]{1,0:T(4,128)(2,1)S(1)}, u32[]{:S(2)}, u32[]{:S(2)}) collective-permute-start(bf16[4,1024]{1,0:T(4,128)(2,1)} %shard_map.103.r0), channel_id=1, source_target_pairs={{0,2},{1,3},{2,0},{3,1},{4,6},{5,7},{6,4},{7,5},{8,10},{9,11},{10,... | collective-permute-start | bytes 24584 | tf_op jit(solution)/shard_map/ppermute | solution.py:45
  6.2 4.7 %collective-permute-start.2 = (bf16[4,1024]{1,0:T(4,128)(2,1)}, bf16[4,1024]{1,0:T(4,128)(2,1)S(1)}, u32[]{:S(2)}, u32[]{:S(2)}) collective-permute-start(bf16[4,1024]{1,0:T(4,128)(2,1)} %shard_map.103.r0), channel_id=1, source_target_pairs={{0,1},{1,0},{2,3},{3,2},{4,5},{5,4},{6,7},{7,6},{8,9},{9,8},{10,11... | collective-permute-start | bytes 24584 | tf_op jit(solution)/shard_map/ppermute | solution.py:45
  6.4 6.7 %collective-permute-start = (bf16[64,512]{1,0:T(8,128)(2,1)S(1)}, bf16[64,512]{1,0:T(8,128)(2,1)S(1)}, u32[]{:S(2)}, u32[]{:S(2)}) collective-permute-start(bf16[64,512]{1,0:T(8,128)(2,1)S(1)} %constant_dynamic-update-slice_fusion), channel_id=1, source_target_pairs={{0,32},{4,36},{8,40},{12,44},{16,48},{20,52},{24,56},{28,60},{32,0... | collective-permute-start | bytes 196616 | tf_op jit(solution)/shard_map/ppermute | solution.py:50
  8.0 5.6 %collective-permute-start.1 = (bf16[64,1024]{1,0:T(8,128)(2,1)S(1)}, bf16[64,1024]{1,0:T(8,128)(2,1)S(1)}, u32[]{:S(2)}, u32[]{:S(2)}) collective-permute-start(bf16[64,1024]{1,0:T(8,128)(2,1)S(1)} %copy-done.3), channel_id=1, source_target_pairs={{0,32},{4,36},{8,40},{12,44},{16,48},{20,52},{24,56},{28,60},{32,0... | collective-permute-start | bytes 393224 | tf_op jit(solution)/shard_map/ppermute | solution.py:50
  9.2 1.7 %copy-start.7 = (bf16[4,1024]{1,0:T(4,128)(2,1)}, bf16[4,1024]{1,0:T(4,128)(2,1)S(1)}, u32[]{:S(2)}) copy-start(bf16[4,1024]{1,0:T(4,128)(2,1)S(1)} %collective-permute-done.4.r3) | copy-start | bytes 24580
  10.9 0.6 copy-start.8
  10.9 0.6 copy-start.9
  13.7 10.6 %copy-start.1 = (bf16[2,2,256,1024]{3,2,1,0:T(8,128)(2,1)S(1)}, bf16[2,2,256,1024]{3,2,1,0:T(8,128)(2,1)}, u32[]{:S(2)}) copy-start(bf16[2,2,256,1024]{3,2,1,0:T(8,128)(2,1)} %param.8) | copy-start | bytes 6291460
  15.7 31.8 %all-to-all-start = ((bf16[8,144,384]{2,1,0:T(8,128)(2,1)}), bf16[8,144,384]{2,1,0:T(8,128)(2,1)S(1)}, u32[]{:S(2)}, u32[]{:S(2)}) async-start(bf16[8,144,384]{2,1,0:T(8,128)(2,1)} %pad_maximum_fusion), calls=%async_computation | async-start | bytes 1769472 | tf_op jit(solution)/shard_map/all_to_all | solution.py:54
  24.3 47.9 %collective-permute-start.6 = (bf16[4,256,1024]{2,1,0:T(8,128)(2,1)S(1)}, bf16[4,256,1024]{2,1,0:T(8,128)(2,1)}, u32[]{:S(2)}, u32[]{:S(2)}) collective-permute-start(bf16[4,256,1024]{2,1,0:T(8,128)(2,1)S(1)} %bitcast.29), channel_id=1, source_target_pairs={{0,2},{1,3},{2,0},{3,1},{4,6},{5,7},{6,4},{7,5},{8,10},{9,11},{10,... | collective-permute-start | bytes 6291464 | tf_op jit(solution)/shard_map/ppermute | solution.py:45
  27.4 25.3 %copy-start.2 = (bf16[128,1152]{1,0:T(8,128)(2,1)}, bf16[128,1152]{1,0:T(8,128)(2,1)S(1)}, u32[]{:S(2)}) copy-start(bf16[128,1152]{1,0:T(8,128)(2,1)S(1)} %maximum_maximum_fusion.w0) | copy-start | bytes 884740
  27.4 21.3 %collective-permute-start.9 = (bf16[128,1152]{1,0:T(8,128)(2,1)S(1)}, bf16[128,1152]{1,0:T(8,128)(2,1)}, u32[]{:S(2)}, u32[]{:S(2)}) collective-permute-start(bf16[128,1152]{1,0:T(8,128)(2,1)S(1)} %maximum_maximum_fusion.w0), channel_id=1, source_target_pairs={{0,64},{1,65},{4,68},{5,69},{8,72},{9,73},{12,76},{13,77},{16,80},... | collective-permute-start | bytes 884744 | tf_op jit(solution)/shard_map/ppermute | solution.py:40
  29.0 19.6 %collective-permute-start.8 = (bf16[128,1152]{1,0:T(8,128)(2,1)S(1)}, bf16[128,1152]{1,0:T(8,128)(2,1)}, u32[]{:S(2)}, u32[]{:S(2)}) collective-permute-start(bf16[128,1152]{1,0:T(8,128)(2,1)S(1)} %maximum_maximum_fusion.w0), channel_id=1, source_target_pairs={{0,128},{1,129},{4,132},{5,133},{8,136},{9,137},{12,140},{13,141},... | collective-permute-start | bytes 884744 | tf_op jit(solution)/shard_map/ppermute | solution.py:40
  31.9 16.7 %collective-permute-start.7 = (bf16[128,1152]{1,0:T(8,128)(2,1)S(1)}, bf16[128,1152]{1,0:T(8,128)(2,1)}, u32[]{:S(2)}, u32[]{:S(2)}) collective-permute-start(bf16[128,1152]{1,0:T(8,128)(2,1)S(1)} %maximum_maximum_fusion.w0), channel_id=1, source_target_pairs={{0,192},{1,193},{4,196},{5,197},{8,200},{9,201},{12,204},{13,205},... | collective-permute-start | bytes 884744 | tf_op jit(solution)/shard_map/ppermute | solution.py:40
  47.5 5.2 %copy-start = (bf16[8,144,384]{2,1,0:T(8,128)(2,1)}, bf16[8,144,384]{2,1,0:T(8,128)(2,1)S(1)}, u32[]{:S(2)}) copy-start(bf16[8,144,384]{2,1,0:T(8,128)(2,1)S(1)} %all-to-all-done.rows_ref) | copy-start | bytes 2654212
  48.6 23.6 %collective-permute-start.11 = (bf16[8,128,384]{2,1,0:T(8,128)(2,1)}, bf16[8,128,384]{2,1,0:T(8,128)(2,1)}, u32[]{:S(2)}, u32[]{:S(2)}) collective-permute-start(bf16[8,128,384]{2,1,0:T(8,128)(2,1)} %slice.50.own_ref), channel_id=1, source_target_pairs={{0,64},{1,65},{4,68},{5,69},{8,72},{9,73},{12,76},{13,77},{16,80},... | collective-permute-start | bytes 2359304 | tf_op jit(solution)/shard_map/ppermute | solution.py:40
  50.3 21.9 %collective-permute-start.10 = (bf16[8,128,384]{2,1,0:T(8,128)(2,1)}, bf16[8,128,384]{2,1,0:T(8,128)(2,1)}, u32[]{:S(2)}, u32[]{:S(2)}) collective-permute-start(bf16[8,128,384]{2,1,0:T(8,128)(2,1)} %slice.50.own_ref), channel_id=1, source_target_pairs={{0,192},{1,193},{4,196},{5,197},{8,200},{9,201},{12,204},{13,205},... | collective-permute-start | bytes 2359304 | tf_op jit(solution)/shard_map/ppermute | solution.py:40
  52.7 2.8 %collective-permute-start.15 = (bf16[16,384]{1,0:T(8,128)(2,1)S(1)}, bf16[16,384]{1,0:T(8,128)(2,1)S(1)}, u32[]{:S(2)}, u32[]{:S(2)}) collective-permute-start(bf16[16,384]{1,0:T(8,128)(2,1)S(1)} %slice_bitcast_fusion), channel_id=1, source_target_pairs={{0,1},{1,0},{2,3},{3,2},{4,5},{5,4},{6,7},{7,6},{8,9},{9,8},{10,11... | collective-permute-start | bytes 36872 | tf_op jit(solution)/shard_map/ppermute | solution.py:45
  55.5 20.4 %copy-start.13 = (bf16[16,384]{1,0:T(8,128)(2,1)}, bf16[16,384]{1,0:T(8,128)(2,1)S(1)}, u32[]{:S(2)}) copy-start(bf16[16,384]{1,0:T(8,128)(2,1)S(1)} %collective-permute-done.15.corner_ref) | copy-start | bytes 36868
  55.5 37.5 %all-to-all-start.1 = ((bf16[8,592,128]{2,1,0:T(8,128)(2,1)}), bf16[8,592,128]{2,1,0:T(8,128)(2,1)}, u32[]{:S(2)}, u32[]{:S(2)}) async-start(bf16[8,592,128]{2,1,0:T(8,128)(2,1)} %shard_map.105), calls=%async_computation.1 | async-start | bytes 2424832 | tf_op jit(solution)/shard_map/all_to_all | solution.py:54
  61.1 16.7 %collective-permute-start.5 = (bf16[4,256,1024]{2,1,0:T(8,128)(2,1)S(1)}, bf16[4,256,1024]{2,1,0:T(8,128)(2,1)S(1)}, u32[]{:S(2)}, u32[]{:S(2)}) collective-permute-start(bf16[4,256,1024]{2,1,0:T(8,128)(2,1)S(1)} %bitcast.30), channel_id=1, source_target_pairs={{0,1},{1,0},{2,3},{3,2},{4,5},{5,4},{6,7},{7,6},{8,9},{9,8},{10,11... | collective-permute-start | bytes 6291464 | tf_op jit(solution)/shard_map/ppermute | solution.py:45
  72.2 20.8 %collective-permute-start.12 = (bf16[4,256,1024]{2,1,0:T(8,128)(2,1)}, bf16[4,256,1024]{2,1,0:T(8,128)(2,1)}, u32[]{:S(2)}, u32[]{:S(2)}) collective-permute-start(bf16[4,256,1024]{2,1,0:T(8,128)(2,1)} %collective-permute-done.6.x2_ref), channel_id=1, source_target_pairs={{0,1},{1,0},{2,3},{3,2},{4,5},{5,4},{6,7},{7,6},{8,9},{9,8},{10,11... | collective-permute-start | bytes 6291464 | tf_op jit(solution)/shard_map/ppermute | solution.py:45
  73.3 12.9 %collective-permute-start.14 = (bf16[4,128,384]{2,1,0:T(8,128)(2,1)S(1)}, bf16[4,128,384]{2,1,0:T(8,128)(2,1)S(1)}, u32[]{:S(2)}, u32[]{:S(2)}) collective-permute-start(bf16[4,128,384]{2,1,0:T(8,128)(2,1)S(1)} %slice.54), channel_id=1, source_target_pairs={{0,64},{1,65},{4,68},{5,69},{8,72},{9,73},{12,76},{13,77},{16,80},... | collective-permute-start | bytes 1179656 | tf_op jit(solution)/shard_map/ppermute | solution.py:40
  76.0 11.5 %collective-permute-start.13 = (bf16[4,128,384]{2,1,0:T(8,128)(2,1)S(1)}, bf16[4,128,384]{2,1,0:T(8,128)(2,1)S(1)}, u32[]{:S(2)}, u32[]{:S(2)}) collective-permute-start(bf16[4,128,384]{2,1,0:T(8,128)(2,1)S(1)} %slice.53), channel_id=1, source_target_pairs={{0,192},{1,193},{4,196},{5,197},{8,200},{9,201},{12,204},{13,205},... | collective-permute-start | bytes 1179656 | tf_op jit(solution)/shard_map/ppermute | solution.py:40
  77.9 8.2 %copy-start.10 = (bf16[4,256,1024]{2,1,0:T(8,128)(2,1)}, bf16[4,256,1024]{2,1,0:T(8,128)(2,1)S(1)}, u32[]{:S(2)}) copy-start(bf16[4,256,1024]{2,1,0:T(8,128)(2,1)S(1)} %collective-permute-done.5.x1_ref) | copy-start | bytes 6291460
  86.1 6.9 %copy-start.11 = (bf16[4,128,384]{2,1,0:T(8,128)(2,1)}, bf16[4,128,384]{2,1,0:T(8,128)(2,1)S(1)}, u32[]{:S(2)}) copy-start(bf16[4,128,384]{2,1,0:T(8,128)(2,1)S(1)} %collective-permute-done.14.far_high_ref) | copy-start | bytes 1179652
  87.5 5.5 %copy-start.12 = (bf16[4,128,384]{2,1,0:T(8,128)(2,1)}, bf16[4,128,384]{2,1,0:T(8,128)(2,1)S(1)}, u32[]{:S(2)}) copy-start(bf16[4,128,384]{2,1,0:T(8,128)(2,1)S(1)} %collective-permute-done.13.far_low_ref) | copy-start | bytes 1179652
  130.9 5.0 %copy-start.4 = (f32[4,8,128]{2,1,0:T(8,128)S(1)}, f32[4,8,128]{2,1,0:T(8,128)}, u32[]{:S(2)}) copy-start(f32[4,8,128]{2,1,0:T(8,128)} %shard_map.106) | copy-start | bytes 49156
  132.1 5.9 %collective-permute-start.17 = (f32[130,128]{1,0:T(8,128)S(1)}, f32[130,128]{1,0:T(8,128)S(1)}, u32[]{:S(2)}, u32[]{:S(2)}) collective-permute-start(f32[130,128]{1,0:T(8,128)S(1)} %pad_maximum_fusion.2), channel_id=1, source_target_pairs={{0,2},{1,3},{2,0},{3,1},{4,6},{5,7},{6,4},{7,5},{8,10},{9,11},{10,... | collective-permute-start | bytes 199688 | tf_op jit(solution)/shard_map/ppermute | solution.py:45
  135.4 5.2 %collective-permute-start.18 = (f32[130,128]{1,0:T(8,128)S(1)}, f32[130,128]{1,0:T(8,128)S(1)}, u32[]{:S(2)}, u32[]{:S(2)}) collective-permute-start(f32[130,128]{1,0:T(8,128)S(1)} %pad_maximum_fusion.2), channel_id=1, source_target_pairs={{0,3},{1,2},{2,1},{3,0},{4,7},{5,6},{6,5},{7,4},{8,11},{9,10},{10,... | collective-permute-start | bytes 199688 | tf_op jit(solution)/shard_map/ppermute | solution.py:45
  135.4 5.2 %collective-permute-start.16 = (f32[130,128]{1,0:T(8,128)S(1)}, f32[130,128]{1,0:T(8,128)S(1)}, u32[]{:S(2)}, u32[]{:S(2)}) collective-permute-start(f32[130,128]{1,0:T(8,128)S(1)} %pad_maximum_fusion.2), channel_id=1, source_target_pairs={{0,1},{1,0},{2,3},{3,2},{4,5},{5,4},{6,7},{7,6},{8,9},{9,8},{10,11... | collective-permute-start | bytes 199688 | tf_op jit(solution)/shard_map/ppermute | solution.py:45
